TPU v7x, 32 devices: a whole 2x2x4 slice. The times are simulated.
32 devices in a mesh: row: 4 (over y, core), col: 8 (over z, x).
Axes of the slice: x: 2, y: 2, z: 4, core: 2. Of those that a mesh axis runs over, the one named last changes fastest.
Arguments:
- stored_inverse: bfloat16 [6, 4, 3, 8, 256, 256], P(None, 'row', None, 'col'), may hold values from -6 to 6
- panel_first: bfloat16 [6, 4, 256, 256], P(None, 'row', 'col'), may hold values from -0.09375 to 0.09375
- panel_second: bfloat16 [6, 4, 256, 256], P(None, 'row', 'col'), may hold values from -0.109375 to 0.109375
- panel_link: bfloat16 [256, 256], replicated, may hold values from -0.375 to 0.375
- inv_first: float32 [256, 256], replicated, as said below
- inv_second: float32 [256, 256], replicated, as said below
- struct_first: int32 [18], replicated, may hold values from 0 to 23, as said below
- struct_second: int32 [12], replicated, may hold values from 0 to 23, as said below
Outputs:
- column_first: float32 [6, 4, 256, 256], P(None, 'row', 'col')
- column_second: float32 [6, 4, 256, 256], P(None, 'row', 'col')
- diag_first: float32 [256, 256], P('col')
- link_block: float32 [256, 256], P('col')
- diag_second: float32 [256, 256], P('col')
Inputs may be any that keep to these rules, and one draw needn't show every extreme that they name: `struct_first`: 18 distinct block indices in increasing order; the last is always 24 - 1. `struct_second`: 12 distinct block indices in increasing order, each also listed in struct_first; the last is always 24 - 1; the second supernode's whole structure is the first supernode together with these blocks. `inv_first`: lower triangular with a positive diagonal. `inv_second`: lower triangular with a positive diagonal.
All inputs are finite; a program needn't handle non-finite values.
Results may differ from a plain program's by a relative error of at most 0.0041.
Values may be sent and summed in bfloat16 or wider, within the bound.
No kernel may reach another device: no remote copies, remote signals or barrier semaphores. Data moves between devices by JAX's collectives and lax.ppermute only.
A program may use at most 64 MiB of HBM per device.

v0:
```python
import functools

import jax
import jax.numpy as jnp
from jax import lax
from jax.experimental import pallas as pl
from jax.experimental.pallas import tpu as pltpu
from jax.sharding import PartitionSpec as P

precise = lax.Precision.HIGHEST
SMEM = pl.BlockSpec(memory_space=pltpu.SMEM)
VMEM = pl.BlockSpec(memory_space=pltpu.VMEM)
HBM = pl.BlockSpec(memory_space=pltpu.HBM)
ANY = pl.BlockSpec(memory_space=pl.ANY)


def exact_dot(left, right, left_dim=1):
    dims = (((left_dim,), (0,)), ((), ()))
    return lax.dot_general(left, right, dims, precision=precise, preferred_element_type=jnp.float32)


def split_dot(left, right, left_dim=1):
    def halves(value):
        if value.dtype == jnp.bfloat16:
            return [value]
        high = value.astype(jnp.bfloat16)
        return [high, (value - high.astype(jnp.float32)).astype(jnp.bfloat16)]

    dims = (((left_dim,), (0,)), ((), ()))
    total = None
    for i, a in enumerate(halves(left)):
        for j, b in enumerate(halves(right)):
            if i + j < 2:
                term = lax.dot_general(a, b, dims, preferred_element_type=jnp.float32)
                total = term if total is None else total + term
    return total


def listed(struct_ref, blocks, n_row):
    ids = lax.broadcasted_iota(jnp.int32, (blocks, 1, 1), 0) * n_row + lax.axis_index("row")

    def look(place, found):
        return jnp.where(ids == struct_ref[place], 1, found)

    found = lax.fori_loop(0, struct_ref.shape[0], look, jnp.zeros((blocks, 1, 1), jnp.int32))
    return found == 1


def slice_of(row, turn, n_row):
    return turn * n_row + row


def place_of(piece, n_row):
    return piece % n_row, piece // n_row


def product_kernel(n_row, n_col, first_bits, struct1, struct2, inv1, inv2, stored, pieces, *rest):
    cycle = n_col // n_row
    keeps, sends = rest[:2], rest[2:4]
    loose, factor = rest[4:]
    row_blocks = stored.shape[0]
    _, col_blocks, _, slab, width = loose.shape
    here_row, here_col = lax.axis_index("row"), lax.axis_index("col")

    group = here_col // n_row
    for m in range(n_row):
        row = here_row ^ m
        for s in range(cycle):
            slot = slice_of(row, lax.rem(s - group + cycle, cycle), n_row)
            for p in range(2):
                for b in range(col_blocks):
                    loose[p, b, slot] = pieces[m, s, p, b].astype(loose.dtype)
    for p, (struct, inverse) in enumerate(((struct1, inv1), (struct2, inv2))):

        def look(place, found):
            return tuple(f | (struct[place] == b * n_col + here_col).astype(jnp.int32) for b, f in enumerate(found))

        found = lax.fori_loop(0, struct.shape[0], look, (jnp.int32(0),) * col_blocks)
        blocks = loose[p].reshape(col_blocks * width, width).astype(jnp.bfloat16)
        product = split_dot(blocks, inverse[...])
        for b in range(col_blocks):
            place = slice(b * width, (b + 1) * width)
            factor[place, p * width : (p + 1) * width] = jnp.where(found[b] == 1, product[place], 0.0).astype(jnp.bfloat16)

    half = row_blocks // 2
    step = 2 if row_blocks % 2 == 0 else 1
    for a in range(0, row_blocks, step):
        wide = [jnp.concatenate([stored[a + i, b] for b in range(col_blocks)], axis=1) for i in range(step)]
        totals = jnp.dot(jnp.concatenate(wide, axis=0), factor[...], preferred_element_type=jnp.float32)
        for i in range(step):
            total = totals[i * width : (i + 1) * width]
            group, place = divmod(a + i, half)
            bit = first_bits[group]
            upper = ((here_col >> bit) & 1) == 1
            for p in range(2):
                for j in range(n_col // 2):
                    low = ((j >> bit) << (bit + 1)) | (j & ((1 << bit) - 1))
                    high = low | (1 << bit)
                    x = total[low * slab : (low + 1) * slab, p * width : (p + 1) * width]
                    y = total[high * slab : (high + 1) * slab, p * width : (p + 1) * width]
                    keeps[group][j, p, place] = jnp.where(upper, y, x)
                    sends[group][j, p, place] = jnp.where(upper, x, y).astype(jnp.bfloat16)


def prepare_kernel(link, inv1, inv2, after, linked, out, whole):
    slab = out.shape[1]
    linked[...] = exact_dot(link[...].astype(jnp.float32), inv2[...])
    link = linked[...]
    gram1 = exact_dot(inv1[...], inv1[...], 0)
    across = exact_dot(gram1, link)
    whole[0] = gram1
    whole[1] = -across
    whole[2] = exact_dot(inv2[...], inv2[...], 0) + exact_dot(link, across, 0)
    place = pl.ds(pl.multiple_of(lax.axis_index("col") * slab, slab), slab)
    out[...] = whole[:, place, :]


def form_kernel(n_row, struct1, struct2, inv1, inv2, base, rows):
    slices, _, blocks, slab, width = base.shape
    for p, (struct, inverse) in enumerate(((struct1, inv1), (struct2, inv2))):
        keep = listed(struct, blocks, n_row)
        flat = base[:, p].astype(jnp.float32).reshape(slices * blocks * slab, width).astype(jnp.bfloat16)
        product = split_dot(flat, inverse[...]).reshape(slices, blocks, slab, width)
        rows[:, p] = jnp.where(keep[None], product, 0.0).astype(jnp.bfloat16)


def sum_kernel(last_bit, rows, total_low, total_high, linked, after, out):
    _, _, half, slab, width = total_low.shape
    mine = (lax.axis_index("col") >> last_bit) & 1

    def gathered(p):
        parts = [total[place, p].reshape(half * slab, width) for place in (mine, 1 - mine) for total in (total_low, total_high)]
        return jnp.concatenate(parts, axis=0)

    def factor(p):
        return rows[:, p].astype(jnp.float32).reshape(-1, width).astype(jnp.bfloat16)

    link = linked[...]
    sum1 = gathered(0)
    u2 = factor(1)
    first = split_dot(factor(0), sum1, 0)
    cross = split_dot(u2, sum1, 0)
    top = cross.T - split_dot(first, link)
    second = split_dot(u2, gathered(1), 0) - split_dot(cross, link) - split_dot(link, top, 0)
    across = width // 2
    for i, part in enumerate((first, top, second)):
        part = part.reshape(width // slab, slab, width)
        for h in range(2):
            out[h, :, i] = part[:, :, h * across : (h + 1) * across]


def column_kernel(n_row, struct1, struct2, kept_low, came_low, kept_high, came_high, linked, column1, column2):
    blocks, slab, width = column1.shape
    sums = []
    for p in range(2):
        parts = [k[p] + c[p].astype(jnp.float32) for k, c in ((kept_low, came_low), (kept_high, came_high))]
        sums.append(jnp.concatenate(parts, axis=0))
    col1 = jnp.where(listed(struct1, blocks, n_row), -sums[0], 0.0)
    column1[...] = col1
    carried = split_dot(col1.reshape(blocks * slab, width), linked[...]).reshape(col1.shape)
    column2[...] = jnp.where(listed(struct2, blocks, n_row), -(sums[1] + carried), 0.0)


def swapped(value, axis, size, mask):
    return lax.ppermute(value, axis, [(i, i ^ mask) for i in range(size)])


def halves(value, axis, ways):
    kept, sent = (lax.dynamic_index_in_dim(value, way, axis, keepdims=False) for way in ways)
    return kept, sent


def body(stored_inverse, panel_first, panel_second, panel_link, inv_first, inv_second, struct_first, struct_second):
    n_row, n_col = lax.axis_size("row"), lax.axis_size("col")
    here_col = lax.axis_index("col")
    row_blocks, _, col_blocks, _, width, _ = stored_inverse.shape
    slab = width // n_col
    cycle = n_col // n_row
    n_bits = n_col.bit_length() - 1
    f32, bf16 = jnp.float32, jnp.bfloat16
    shape = jax.ShapeDtypeStruct
    big = pltpu.CompilerParams(vmem_limit_bytes=12 * 1024 * 1024)
    stored = stored_inverse.reshape(row_blocks, col_blocks, width, width)
    panel = (row_blocks, slab, width)

    panels = [panel_first.reshape(panel), panel_second.reshape(panel)]
    _, turn = place_of(here_col, n_row)
    picks = [((s - turn + cycle) % cycle).astype(jnp.uint32) for s in range(cycle)]
    ways = [(here_col >> bit) & 1 for bit in range(n_bits)]
    ways = [(way.astype(jnp.uint32), (1 - way).astype(jnp.uint32)) for way in ways]
    core = lax.axis_index("row") & 1
    cores = (core.astype(jnp.uint32), (1 - core).astype(jnp.uint32))
    panels, picks, ways, cores = lax.optimization_barrier((panels, picks, ways, cores))

    raw = lax.optimization_barrier(jnp.stack(panels))
    turns = raw.reshape(2, col_blocks, cycle, slab, width)
    got = []
    for s in range(cycle):
        moves = []
        for r in range(n_row):
            for c in range(n_col):
                row, t = place_of(c, n_row)
                moves.append((r * n_col + c, row * n_col + r + (s - t) % cycle * n_row))
        part = lax.dynamic_index_in_dim(turns, picks[s], 2, keepdims=False)
        got.append(lax.ppermute(part, ("row", "col"), moves))
    base = jnp.stack([raw, swapped(raw, "col", n_col, n_col // 2)])

    pieces = {0: got}
    bit = n_row // 2
    while bit > 1:
        for m, parts in list(pieces.items()):
            pieces[m ^ bit] = [swapped(part, "row", n_row, bit) for part in parts]
        bit //= 2
    pieces = jnp.stack([jnp.stack(pieces[m]) for m in sorted(pieces)])
    pieces, base = lax.optimization_barrier((pieces, base))
    rows = pl.pallas_call(
        functools.partial(form_kernel, n_row),
        out_shape=shape(base.shape, bf16),
        in_specs=[SMEM, SMEM] + [VMEM] * 3,
        out_specs=VMEM,
        compiler_params=big,
        name="form",
        cost_estimate=pl.CostEstimate(flops=8 * width**3, bytes_accessed=4 * width**2, transcendentals=0),
    )(struct_first, struct_second, inv_first, inv_second, base)
    beside, rows = lax.optimization_barrier((swapped(pieces, "row", n_row, 1), rows))
    pieces = jnp.stack([pieces, beside], axis=1).reshape((n_row,) + pieces.shape[1:])

    orders = (list(range(n_bits)), [1, 0] + list(range(2, n_bits)))
    half = row_blocks // 2
    block = (2, half, slab, width)
    kept = (n_col // 2,) + block
    split = pl.pallas_call(
        functools.partial(product_kernel, n_row, n_col, (orders[0][0], orders[1][0])),
        out_shape=[shape(kept, f32)] * 2 + [shape(kept, bf16)] * 2,
        in_specs=[SMEM, SMEM] + [VMEM] * 4,
        out_specs=[VMEM] * 4,
        scratch_shapes=[
            pltpu.VMEM((2, col_blocks, n_col, slab, width), bf16 if slab % 16 == 0 else f32),
            pltpu.VMEM((col_blocks * width, 2 * width), bf16),
        ],
        compiler_params=big,
        name="products",
    )(struct_first, struct_second, inv_first, inv_second, stored, pieces)

    linked, consts = pl.pallas_call(
        prepare_kernel,
        out_shape=[shape((width, width), f32), shape((3, slab, width), f32)],
        in_specs=[VMEM] * 3 + [ANY],
        out_specs=[VMEM] * 2,
        scratch_shapes=[pltpu.VMEM((3, width, width), f32)],
        compiler_params=big,
        name="prepare",
        cost_estimate=pl.CostEstimate(flops=6 * 10 * width**3, bytes_accessed=8 * width**2, transcendentals=0),
    )(panel_link, inv_first, inv_second, split[0])

    state = [(split[g], swapped(split[2 + g], "col", n_col, 1 << orders[g][0])) for g in range(2)]
    left = [sorted(set(range(n_bits)) - {order[0]}) for order in orders]
    for i in range(1, n_bits):
        totals, last = [], []
        for g in range(2):
            keep, came = state[g]
            bit = orders[g][i]
            inner = 1 << left[g].index(bit)
            left[g].remove(bit)
            totals.append(keep + came.astype(f32))
            keep, send = halves(totals[g].reshape((-1, 2, inner) + block), 1, ways[bit])
            keep, send = keep.reshape((-1,) + block), send.astype(bf16).reshape((-1,) + block)
            last.append((keep, swapped(send, "col", n_col, 1 << bit)))
        state = last

    sums = pl.pallas_call(
        functools.partial(sum_kernel, n_bits - 1),
        out_shape=shape((2, n_col, 3, slab, width // 2), f32),
        in_specs=[VMEM] * 4 + [ANY],
        out_specs=VMEM,
        compiler_params=big,
        name="sums",
    )(rows, *totals, linked, consts)
    keep, send = halves(sums, 0, cores)
    sums = keep + swapped(send, "row", n_row, 1)
    for bit in range(n_bits):
        keep, send = halves(sums.reshape(-1, 2, 3, slab, width // 2), 1, ways[bit])
        sums = keep + swapped(send.astype(bf16), "col", n_col, 1 << bit).astype(f32)
    mine = sums.reshape(3, slab, width // 2)
    for bit in range(1, n_row.bit_length() - 1):
        mine = mine + swapped(mine, "row", n_row, 1 << bit)

    mine, state = lax.optimization_barrier((mine, state))
    column_first, column_second = pl.pallas_call(
        functools.partial(column_kernel, n_row),
        out_shape=[shape(panel, f32)] * 2,
        in_specs=[SMEM, SMEM] + [VMEM] * 5,
        out_specs=[VMEM] * 2,
        compiler_params=big,
        name="columns",
    )(struct_first, struct_second, *[part[0] for pair in state for part in pair], linked)

    pair = jnp.stack([mine, swapped(mine, "row", n_row, 1)])
    total = jnp.concatenate([lax.dynamic_index_in_dim(pair, way, 0, keepdims=False) for way in cores], axis=-1)
    diag_first, link_block, diag_second = consts + total
    out = (row_blocks, 1, slab, width)
    return column_first.reshape(out), column_second.reshape(out), diag_first, link_block, diag_second


def solution(mesh):
    placed = (
        P(None, "row", None, "col", None, None),
        P(None, "row", "col", None),
        P(None, "row", "col", None),
        P(),
        P(),
        P(),
        P(),
        P(),
    )
    return jax.shard_map(
        body,
        mesh=mesh,
        in_specs=placed,
        out_specs=(
            P(None, "row", "col", None),
            P(None, "row", "col", None),
            P("col", None),
            P("col", None),
            P("col", None),
        ),
        check_vma=False,
    )
```

profile of v0, /device:TPU:0, one launch (start us, length us, event | category | flops | bytes accessed | tf_op | source)
XLA Modules:
  0.0 74.2 jit_solution(10791555440385257719)
XLA Ops:
  0.7 1.0 %pad_maximum_fusion.3 = bf16[2,6,32,256]{3,2,1,0:T(8,128)(2,1)S(1)} fusion(bf16[1,6,32,256]{3,2,1,0:T(8,128)(2,1)} %bitcast.101, bf16[1,6,32,256]{3,2,1,0:T(8,128)(2,1)} %bitcast.102), kind=kLoop, calls=%fused_computation.13 | loop fusion | flops 98304 | bytes 393216 | tf_op jit(solution)/shard_map/stack | solution.py:195
  1.8 0.7 collective-permute-start
  2.4 4.1 %collective-permute-start.1 = (bf16[2,3,32,256]{3,2,1,0:T(8,128)(2,1)S(1)}, bf16[2,3,32,256]{3,2,1,0:T(8,128)(2,1)S(1)}, u32[]{:S(2)}, u32[]{:S(2)}) collective-permute-start(bf16[2,3,32,256]{3,2,1,0:T(8,128)(2,1)S(1)} %get-tuple-element.79), channel_id=1, source_target_pairs={{0,4},{1,12},{2,20},{3,28},{4,0},{5,8},{6,16},{7,24},{8,5},{9,13},... | collective-permute-start | bytes 294920 | tf_op jit(solution)/shard_map/ppermute | solution.py:205
  6.5 0.1 collective-permute-start.4
  6.6 0.0 collective-permute-done
  6.6 12.4 %collective-permute-start.2 = (bf16[2,3,32,256]{3,2,1,0:T(8,128)(2,1)S(1)}, bf16[2,3,32,256]{3,2,1,0:T(8,128)(2,1)S(1)}, u32[]{:S(2)}, u32[]{:S(2)}) collective-permute-start(bf16[2,3,32,256]{3,2,1,0:T(8,128)(2,1)S(1)} %collective-permute-done), channel_id=1, source_target_pairs={{0,16},{8,24},{16,0},{24,8},{1,17},{9,25},{17,1},{25,9},{2,18},{10... | collective-permute-start | bytes 294920 | tf_op jit(solution)/shard_map/ppermute | solution.py:165
  19.0 0.0 collective-permute-done.1
  19.0 0.0 collective-permute-start.3
  19.1 3.0 %collective-permute-done.2 = bf16[2,3,32,256]{3,2,1,0:T(8,128)(2,1)S(1)} collective-permute-done((bf16[2,3,32,256]{3,2,1,0:T(8,128)(2,1)S(1)}, bf16[2,3,32,256]{3,2,1,0:T(8,128)(2,1)S(1)}, u32[]{:S(2)}, u32[]{:S(2)}) %collective-permute-start.2) | collective-permute-done | bytes 98336 | tf_op jit(solution)/shard_map/ppermute | solution.py:165
  22.1 2.5 %collective-permute-done.3 = bf16[2,3,32,256]{3,2,1,0:T(8,128)(2,1)S(1)} collective-permute-done((bf16[2,3,32,256]{3,2,1,0:T(8,128)(2,1)S(1)}, bf16[2,3,32,256]{3,2,1,0:T(8,128)(2,1)S(1)}, u32[]{:S(2)}, u32[]{:S(2)}) %collective-permute-start.3) | collective-permute-done | bytes 98336 | tf_op jit(solution)/shard_map/ppermute | solution.py:165
  24.6 0.0 collective-permute-done.4
  24.7 0.1 collective-permute-start.5
  24.8 0.0 copy-done.1
  24.8 1.5 %form.1.rows = bf16[2,2,6,32,256]{4,3,2,1,0:T(8,128)(2,1)S(1)} custom-call(s32[18]{0:T(128)S(1)} %copy-done.3, s32[12]{0:T(128)S(1)} %copy-done.4, f32[256,256]{1,0:T(8,128)S(1)} %copy-done.1, f32[256,256]{1,0:T(8,128)S(1)} %copy-done.2, bf16[2,2,6,32,256]{4,3,2,1,0:T(8,128)(2,1)S(1)} %pad_maximum_fusion.2.base), custom_call_target="tpu_custom_call" | custom-call | flops 134217728 | bytes 262144 | tf_op jit(solution)/shard_map/form/pallas_call | solution.py:216
  26.3 0.2 collective-permute-done.5
  26.5 0.1 pad_maximum_fusion
  26.6 3.3 %products.1 = (f32[4,2,3,32,256]{4,3,2,1,0:T(8,128)S(1)}, f32[4,2,3,32,256]{4,3,2,1,0:T(8,128)S(1)}, bf16[4,2,3,32,256]{4,3,2,1,0:T(8,128)(2,1)S(1)}, bf16[4,2,3,32,256]{4,3,2,1,0:T(8,128)(2,1)S(1)}) custom-call(s32[18]{0:T(128)S(1)} %copy-done.3, s32[12]{0:T(128)S(1)} %copy-done.4, f32[256,256]{1,0:T(8,128)S(1)} %copy-done.1, f32[256,256]{1,0:T(8,128)S(1)} %copy-done.2, ...), custom_call_target="tpu_custom_call" | custom-call | tf_op jit(solution)/shard_map/products/pallas_call | solution.py:232
  29.9 0.6 collective-permute-start.8
  30.5 1.1 %collective-permute-start.6 = (bf16[4,2,3,32,256]{4,3,2,1,0:T(8,128)(2,1)S(1)}, bf16[4,2,3,32,256]{4,3,2,1,0:T(8,128)(2,1)S(1)}, u32[]{:S(2)}, u32[]{:S(2)}) collective-permute-start(bf16[4,2,3,32,256]{4,3,2,1,0:T(8,128)(2,1)S(1)} %get-tuple-element.43), channel_id=1, source_target_pairs={{0,1},{1,0},{2,3},{3,2},{4,5},{5,4},{6,7},{7,6},{8,9},{9,8},{10,11... | collective-permute-start | bytes 1179656 | tf_op jit(solution)/shard_map/ppermute | solution.py:165
  31.5 2.2 %prepare.1 = (f32[256,256]{1,0:T(8,128)S(1)}, f32[3,32,256]{2,1,0:T(8,128)S(1)}) custom-call(bf16[256,256]{1,0:T(8,128)(2,1)S(1)} %copy-done.5, f32[256,256]{1,0:T(8,128)S(1)} %copy-done.1, f32[256,256]{1,0:T(8,128)S(1)} %copy-done.2, f32[4,2,3,32,256]{4,3,2,1,0:T(8,128)S(1)} %get-tuple-element.42.after), custom_call_target="tpu_custom_call" | custom-call | flops 1006632960 | bytes 524288 | tf_op jit(solution)/shard_map/prepare/pallas_call | solution.py:245
  33.7 7.5 %collective-permute-done.8 = bf16[4,2,3,32,256]{4,3,2,1,0:T(8,128)(2,1)S(1)} collective-permute-done((bf16[4,2,3,32,256]{4,3,2,1,0:T(8,128)(2,1)S(1)}, bf16[4,2,3,32,256]{4,3,2,1,0:T(8,128)(2,1)S(1)}, u32[]{:S(2)}, u32[]{:S(2)}) %collective-permute-start.8) | collective-permute-done | bytes 393248 | tf_op jit(solution)/shard_map/ppermute | solution.py:165
  41.3 0.1 convert_add_fusion
  41.5 0.5 collective-permute-start.9
  41.9 0.0 collective-permute-done.6
  41.9 0.1 convert_add_fusion.1
  42.1 1.3 %collective-permute-start.7 = (bf16[2,2,3,32,256]{4,3,2,1,0:T(8,128)(2,1)S(1)}, bf16[2,2,3,32,256]{4,3,2,1,0:T(8,128)(2,1)S(1)}, u32[]{:S(2)}, u32[]{:S(2)}) collective-permute-start(bf16[2,2,3,32,256]{4,3,2,1,0:T(8,128)(2,1)S(1)} %fusion), channel_id=1, source_target_pairs={{0,2},{1,3},{2,0},{3,1},{4,6},{5,7},{6,4},{7,5},{8,10},{9,11},{10,... | collective-permute-start | bytes 589832 | tf_op jit(solution)/shard_map/ppermute | solution.py:165
  43.4 4.5 %collective-permute-done.9 = bf16[2,2,3,32,256]{4,3,2,1,0:T(8,128)(2,1)S(1)} collective-permute-done((bf16[2,2,3,32,256]{4,3,2,1,0:T(8,128)(2,1)S(1)}, bf16[2,2,3,32,256]{4,3,2,1,0:T(8,128)(2,1)S(1)}, u32[]{:S(2)}, u32[]{:S(2)}) %collective-permute-start.9) | collective-permute-done | bytes 196640 | tf_op jit(solution)/shard_map/ppermute | solution.py:165
  47.9 0.3 collective-permute-done.7
  48.3 1.0 %sums.1 = f32[2,8,3,32,128]{4,3,2,1,0:T(8,128)S(1)} custom-call(bf16[2,2,6,32,256]{4,3,2,1,0:T(8,128)(2,1)S(1)} %form.1.rows, f32[2,2,3,32,256]{4,3,2,1,0:T(8,128)S(1)} %bitcast_add_fusion.2.total_low, f32[2,2,3,32,256]{4,3,2,1,0:T(8,128)S(1)} %bitcast_add_fusion.1.total_high, f32[256,256]{1,0:T(8,128)S(1)} %get-tuple-element.50.linked, ...), custom_call_target="tpu_custom_call" | custom-call | tf_op jit(solution)/shard_map/sums/pallas_call | solution.py:271
  49.3 0.1 collective-permute-start.10
  49.4 1.7 %collective-permute-done.10 = f32[8,3,32,128]{3,2,1,0:T(8,128)S(1)} collective-permute-done((f32[8,3,32,128]{3,2,1,0:T(8,128)S(1)}, f32[8,3,32,128]{3,2,1,0:T(8,128)S(1)}, u32[]{:S(2)}, u32[]{:S(2)}) %collective-permute-start.10) | collective-permute-done | bytes 393248 | tf_op jit(solution)/shard_map/ppermute | solution.py:165
  51.1 0.1 bitcast_add_fusion
  51.2 1.7 %collective-permute-start.11 = (bf16[4,3,32,128]{3,2,1,0:T(8,128)(2,1)S(1)}, bf16[4,3,32,128]{3,2,1,0:T(8,128)(2,1)S(1)}, u32[]{:S(2)}, u32[]{:S(2)}) collective-permute-start(bf16[4,3,32,128]{3,2,1,0:T(8,128)(2,1)S(1)} %fusion.2), channel_id=1, source_target_pairs={{0,1},{1,0},{2,3},{3,2},{4,5},{5,4},{6,7},{7,6},{8,9},{9,8},{10,11... | collective-permute-start | bytes 294920 | tf_op jit(solution)/shard_map/ppermute | solution.py:165
  52.9 2.4 %collective-permute-start.16 = (bf16[1,2,3,32,256]{4,3,2,1,0:T(8,128)(2,1)S(1)}, bf16[1,2,3,32,256]{4,3,2,1,0:T(8,128)(2,1)S(1)}, u32[]{:S(2)}, u32[]{:S(2)}) collective-permute-start(bf16[1,2,3,32,256]{4,3,2,1,0:T(8,128)(2,1)S(1)} %dynamic-slice_convert_fusion), channel_id=1, source_target_pairs={{0,4},{1,5},{2,6},{3,7},{4,0},{5,1},{6,2},{7,3},{8,12},{9,13},{10,... | collective-permute-start | bytes 294920 | tf_op jit(solution)/shard_map/ppermute | solution.py:165
  55.3 0.8 %collective-permute-done.11 = bf16[4,3,32,128]{3,2,1,0:T(8,128)(2,1)S(1)} collective-permute-done((bf16[4,3,32,128]{3,2,1,0:T(8,128)(2,1)S(1)}, bf16[4,3,32,128]{3,2,1,0:T(8,128)(2,1)S(1)}, u32[]{:S(2)}, u32[]{:S(2)}) %collective-permute-start.11) | collective-permute-done | bytes 98336 | tf_op jit(solution)/shard_map/ppermute | solution.py:165
  56.2 1.3 %collective-permute-start.12 = (bf16[2,3,32,128]{3,2,1,0:T(8,128)(2,1)S(1)}, bf16[2,3,32,128]{3,2,1,0:T(8,128)(2,1)S(1)}, u32[]{:S(2)}, u32[]{:S(2)}) collective-permute-start(bf16[2,3,32,128]{3,2,1,0:T(8,128)(2,1)S(1)} %fusion.3), channel_id=1, source_target_pairs={{0,2},{1,3},{2,0},{3,1},{4,6},{5,7},{6,4},{7,5},{8,10},{9,11},{10,... | collective-permute-start | bytes 147464 | tf_op jit(solution)/shard_map/ppermute | solution.py:165
  57.5 3.6 %collective-permute-done.12 = bf16[2,3,32,128]{3,2,1,0:T(8,128)(2,1)S(1)} collective-permute-done((bf16[2,3,32,128]{3,2,1,0:T(8,128)(2,1)S(1)}, bf16[2,3,32,128]{3,2,1,0:T(8,128)(2,1)S(1)}, u32[]{:S(2)}, u32[]{:S(2)}) %collective-permute-start.12) | collective-permute-done | bytes 49184 | tf_op jit(solution)/shard_map/ppermute | solution.py:165
  61.1 2.1 %collective-permute-start.13 = (bf16[1,3,32,128]{3,2,1,0:T(8,128)(2,1)S(1)}, bf16[1,3,32,128]{3,2,1,0:T(8,128)(2,1)S(1)}, u32[]{:S(2)}, u32[]{:S(2)}) collective-permute-start(bf16[1,3,32,128]{3,2,1,0:T(8,128)(2,1)S(1)} %dynamic-slice_convert_fusion.4), channel_id=1, source_target_pairs={{0,4},{1,5},{2,6},{3,7},{4,0},{5,1},{6,2},{7,3},{8,12},{9,13},{10,... | collective-permute-start | bytes 73736 | tf_op jit(solution)/shard_map/ppermute | solution.py:165
  63.2 1.0 %collective-permute-start.15 = (bf16[1,2,3,32,256]{4,3,2,1,0:T(8,128)(2,1)S(1)}, bf16[1,2,3,32,256]{4,3,2,1,0:T(8,128)(2,1)S(1)}, u32[]{:S(2)}, u32[]{:S(2)}) collective-permute-start(bf16[1,2,3,32,256]{4,3,2,1,0:T(8,128)(2,1)S(1)} %dynamic-slice_convert_fusion.1), channel_id=1, source_target_pairs={{0,4},{1,5},{2,6},{3,7},{4,0},{5,1},{6,2},{7,3},{8,12},{9,13},{10,... | collective-permute-start | bytes 294920 | tf_op jit(solution)/shard_map/ppermute | solution.py:165
  64.2 3.3 %collective-permute-done.13 = bf16[1,3,32,128]{3,2,1,0:T(8,128)(2,1)S(1)} collective-permute-done((bf16[1,3,32,128]{3,2,1,0:T(8,128)(2,1)S(1)}, bf16[1,3,32,128]{3,2,1,0:T(8,128)(2,1)S(1)}, u32[]{:S(2)}, u32[]{:S(2)}) %collective-permute-start.13) | collective-permute-done | bytes 24608 | tf_op jit(solution)/shard_map/ppermute | solution.py:165
  67.5 0.2 collective-permute-start.14
  67.7 3.9 %collective-permute-done.14 = f32[3,32,128]{2,1,0:T(8,128)S(1)} collective-permute-done((f32[3,32,128]{2,1,0:T(8,128)S(1)}, f32[3,32,128]{2,1,0:T(8,128)S(1)}, u32[]{:S(2)}, u32[]{:S(2)}) %collective-permute-start.14) | collective-permute-done | bytes 49184 | tf_op jit(solution)/shard_map/ppermute | solution.py:165
  71.6 0.0 collective-permute-done.16
  71.7 0.0 collective-permute-done.15
  71.7 0.1 collective-permute-start.17
  71.7 1.8 %columns.1 = (f32[6,32,256]{2,1,0:T(8,128)}, f32[6,32,256]{2,1,0:T(8,128)}) custom-call(s32[18]{0:T(128)S(1)} %copy-done.3, s32[12]{0:T(128)S(1)} %copy-done.4, f32[2,3,32,256]{3,2,1,0:T(8,128)S(1)} %bitcast.84, bf16[2,3,32,256]{3,2,1,0:T(8,128)(2,1)S(1)} %bitcast.86, f32[2,3,32,256]{3,2,1,0:T(8,128)S(1)} %bitcast.83, bf16[2,3,32,256]{3,2,1,0:T(8,128)(2,1)S(1)} %bitcast.85, ...), custom_call_target="tpu_custom_call" | custom-call | tf_op jit(solution)/shard_map/columns/pallas_call | solution.py:289
  73.5 0.0 collective-permute-done.17
  73.6 0.6 slice_bitcast_fusion
  (34 shorter events, 0.5 us)
Async XLA Ops:
  0.6 24.1 %copy-start.1 = (f32[256,256]{1,0:T(8,128)S(1)}, f32[256,256]{1,0:T(8,128)}, u32[]{:S(2)}) copy-start(f32[256,256]{1,0:T(8,128)} %inv1.5) | copy-start | bytes 786436
  0.6 24.1 %copy-start.2 = (f32[256,256]{1,0:T(8,128)S(1)}, f32[256,256]{1,0:T(8,128)}, u32[]{:S(2)}) copy-start(f32[256,256]{1,0:T(8,128)} %inv2.5) | copy-start | bytes 786436
  0.7 24.1 %copy-start.3 = (s32[18]{0:T(128)S(1)}, s32[18]{0:T(128)}, u32[]{:S(2)}) copy-start(s32[18]{0:T(128)} %struct1.5) | copy-start | bytes 220
  0.7 24.1 %copy-start.4 = (s32[12]{0:T(128)S(1)}, s32[12]{0:T(128)}, u32[]{:S(2)}) copy-start(s32[12]{0:T(128)} %struct2.5) | copy-start | bytes 148
  1.8 4.9 %collective-permute-start = (bf16[2,3,32,256]{3,2,1,0:T(8,128)(2,1)S(1)}, bf16[2,3,32,256]{3,2,1,0:T(8,128)(2,1)S(1)}, u32[]{:S(2)}, u32[]{:S(2)}) collective-permute-start(bf16[2,3,32,256]{3,2,1,0:T(8,128)(2,1)S(1)} %get-tuple-element.78), channel_id=1, source_target_pairs={{0,0},{1,8},{2,16},{3,24},{4,4},{5,12},{6,20},{7,28},{8,1},{9,9},{... | collective-permute-start | bytes 294920 | tf_op jit(solution)/shard_map/ppermute | solution.py:205
  2.4 16.6 %collective-permute-start.1 = (bf16[2,3,32,256]{3,2,1,0:T(8,128)(2,1)S(1)}, bf16[2,3,32,256]{3,2,1,0:T(8,128)(2,1)S(1)}, u32[]{:S(2)}, u32[]{:S(2)}) collective-permute-start(bf16[2,3,32,256]{3,2,1,0:T(8,128)(2,1)S(1)} %get-tuple-element.79), channel_id=1, source_target_pairs={{0,4},{1,12},{2,20},{3,28},{4,0},{5,8},{6,16},{7,24},{8,5},{9,13},... | collective-permute-start | bytes 294920 | tf_op jit(solution)/shard_map/ppermute | solution.py:205
  6.5 18.1 %collective-permute-start.4 = (bf16[2,6,32,256]{3,2,1,0:T(8,128)(2,1)S(1)}, bf16[2,6,32,256]{3,2,1,0:T(8,128)(2,1)S(1)}, u32[]{:S(2)}, u32[]{:S(2)}) collective-permute-start(bf16[2,6,32,256]{3,2,1,0:T(8,128)(2,1)S(1)} %pad_maximum_fusion.3), channel_id=1, source_target_pairs={{0,4},{1,5},{2,6},{3,7},{4,0},{5,1},{6,2},{7,3},{8,12},{9,13},{10,... | collective-permute-start | bytes 589832 | tf_op jit(solution)/shard_map/ppermute | solution.py:165
  6.6 15.4 %collective-permute-start.2 = (bf16[2,3,32,256]{3,2,1,0:T(8,128)(2,1)S(1)}, bf16[2,3,32,256]{3,2,1,0:T(8,128)(2,1)S(1)}, u32[]{:S(2)}, u32[]{:S(2)}) collective-permute-start(bf16[2,3,32,256]{3,2,1,0:T(8,128)(2,1)S(1)} %collective-permute-done), channel_id=1, source_target_pairs={{0,16},{8,24},{16,0},{24,8},{1,17},{9,25},{17,1},{25,9},{2,18},{10... | collective-permute-start | bytes 294920 | tf_op jit(solution)/shard_map/ppermute | solution.py:165
  19.0 5.5 %collective-permute-start.3 = (bf16[2,3,32,256]{3,2,1,0:T(8,128)(2,1)S(1)}, bf16[2,3,32,256]{3,2,1,0:T(8,128)(2,1)S(1)}, u32[]{:S(2)}, u32[]{:S(2)}) collective-permute-start(bf16[2,3,32,256]{3,2,1,0:T(8,128)(2,1)S(1)} %collective-permute-done.1), channel_id=1, source_target_pairs={{0,16},{8,24},{16,0},{24,8},{1,17},{9,25},{17,1},{25,9},{2,18},{10... | collective-permute-start | bytes 294920 | tf_op jit(solution)/shard_map/ppermute | solution.py:165
  24.6 2.0 %copy-start = (bf16[6,1,3,1,256,256]{5,4,3,2,1,0:T(8,128)(2,1)S(1)}, bf16[6,1,3,1,256,256]{5,4,3,2,1,0:T(8,128)(2,1)}, u32[]{:S(2)}) copy-start(bf16[6,1,3,1,256,256]{5,4,3,2,1,0:T(8,128)(2,1)} %param.8) | copy-start | bytes 7077892
  24.7 1.8 %collective-permute-start.5 = (bf16[2,2,2,3,32,256]{5,4,3,2,1,0:T(8,128)(2,1)S(1)}, bf16[2,2,2,3,32,256]{5,4,3,2,1,0:T(8,128)(2,1)S(1)}, u32[]{:S(2)}, u32[]{:S(2)}) collective-permute-start(bf16[2,2,2,3,32,256]{5,4,3,2,1,0:T(8,128)(2,1)S(1)} %pad_maximum_fusion.1), channel_id=1, source_target_pairs={{0,8},{8,0},{16,24},{24,16},{1,9},{9,1},{17,25},{25,17},{2,10},{10... | collective-permute-start | bytes 1179656 | tf_op jit(solution)/shard_map/ppermute | solution.py:165
  26.5 5.1 %copy-start.5 = (bf16[256,256]{1,0:T(8,128)(2,1)S(1)}, bf16[256,256]{1,0:T(8,128)(2,1)}, u32[]{:S(2)}) copy-start(bf16[256,256]{1,0:T(8,128)(2,1)} %link.1) | copy-start | bytes 393220
  29.9 11.4 %collective-permute-start.8 = (bf16[4,2,3,32,256]{4,3,2,1,0:T(8,128)(2,1)S(1)}, bf16[4,2,3,32,256]{4,3,2,1,0:T(8,128)(2,1)S(1)}, u32[]{:S(2)}, u32[]{:S(2)}) collective-permute-start(bf16[4,2,3,32,256]{4,3,2,1,0:T(8,128)(2,1)S(1)} %get-tuple-element.47), channel_id=1, source_target_pairs={{0,2},{1,3},{2,0},{3,1},{4,6},{5,7},{6,4},{7,5},{8,10},{9,11},{10,... | collective-permute-start | bytes 1179656 | tf_op jit(solution)/shard_map/ppermute | solution.py:165
  30.5 11.4 %collective-permute-start.6 = (bf16[4,2,3,32,256]{4,3,2,1,0:T(8,128)(2,1)S(1)}, bf16[4,2,3,32,256]{4,3,2,1,0:T(8,128)(2,1)S(1)}, u32[]{:S(2)}, u32[]{:S(2)}) collective-permute-start(bf16[4,2,3,32,256]{4,3,2,1,0:T(8,128)(2,1)S(1)} %get-tuple-element.43), channel_id=1, source_target_pairs={{0,1},{1,0},{2,3},{3,2},{4,5},{5,4},{6,7},{7,6},{8,9},{9,8},{10,11... | collective-permute-start | bytes 1179656 | tf_op jit(solution)/shard_map/ppermute | solution.py:165
  41.5 6.4 %collective-permute-start.9 = (bf16[2,2,3,32,256]{4,3,2,1,0:T(8,128)(2,1)S(1)}, bf16[2,2,3,32,256]{4,3,2,1,0:T(8,128)(2,1)S(1)}, u32[]{:S(2)}, u32[]{:S(2)}) collective-permute-start(bf16[2,2,3,32,256]{4,3,2,1,0:T(8,128)(2,1)S(1)} %fusion.1), channel_id=1, source_target_pairs={{0,1},{1,0},{2,3},{3,2},{4,5},{5,4},{6,7},{7,6},{8,9},{9,8},{10,11... | collective-permute-start | bytes 589832 | tf_op jit(solution)/shard_map/ppermute | solution.py:165
  42.1 6.1 %collective-permute-start.7 = (bf16[2,2,3,32,256]{4,3,2,1,0:T(8,128)(2,1)S(1)}, bf16[2,2,3,32,256]{4,3,2,1,0:T(8,128)(2,1)S(1)}, u32[]{:S(2)}, u32[]{:S(2)}) collective-permute-start(bf16[2,2,3,32,256]{4,3,2,1,0:T(8,128)(2,1)S(1)} %fusion), channel_id=1, source_target_pairs={{0,2},{1,3},{2,0},{3,1},{4,6},{5,7},{6,4},{7,5},{8,10},{9,11},{10,... | collective-permute-start | bytes 589832 | tf_op jit(solution)/shard_map/ppermute | solution.py:165
  49.3 1.8 %collective-permute-start.10 = (f32[8,3,32,128]{3,2,1,0:T(8,128)S(1)}, f32[8,3,32,128]{3,2,1,0:T(8,128)S(1)}, u32[]{:S(2)}, u32[]{:S(2)}) collective-permute-start(f32[8,3,32,128]{3,2,1,0:T(8,128)S(1)} %dynamic-slice_bitcast_fusion), channel_id=1, source_target_pairs={{0,8},{8,0},{16,24},{24,16},{1,9},{9,1},{17,25},{25,17},{2,10},{10... | collective-permute-start | bytes 1179656 | tf_op jit(solution)/shard_map/ppermute | solution.py:165
  51.2 4.9 %collective-permute-start.11 = (bf16[4,3,32,128]{3,2,1,0:T(8,128)(2,1)S(1)}, bf16[4,3,32,128]{3,2,1,0:T(8,128)(2,1)S(1)}, u32[]{:S(2)}, u32[]{:S(2)}) collective-permute-start(bf16[4,3,32,128]{3,2,1,0:T(8,128)(2,1)S(1)} %fusion.2), channel_id=1, source_target_pairs={{0,1},{1,0},{2,3},{3,2},{4,5},{5,4},{6,7},{7,6},{8,9},{9,8},{10,11... | collective-permute-start | bytes 294920 | tf_op jit(solution)/shard_map/ppermute | solution.py:165
  52.9 18.7 %collective-permute-start.16 = (bf16[1,2,3,32,256]{4,3,2,1,0:T(8,128)(2,1)S(1)}, bf16[1,2,3,32,256]{4,3,2,1,0:T(8,128)(2,1)S(1)}, u32[]{:S(2)}, u32[]{:S(2)}) collective-permute-start(bf16[1,2,3,32,256]{4,3,2,1,0:T(8,128)(2,1)S(1)} %dynamic-slice_convert_fusion), channel_id=1, source_target_pairs={{0,4},{1,5},{2,6},{3,7},{4,0},{5,1},{6,2},{7,3},{8,12},{9,13},{10,... | collective-permute-start | bytes 294920 | tf_op jit(solution)/shard_map/ppermute | solution.py:165
  56.2 4.9 %collective-permute-start.12 = (bf16[2,3,32,128]{3,2,1,0:T(8,128)(2,1)S(1)}, bf16[2,3,32,128]{3,2,1,0:T(8,128)(2,1)S(1)}, u32[]{:S(2)}, u32[]{:S(2)}) collective-permute-start(bf16[2,3,32,128]{3,2,1,0:T(8,128)(2,1)S(1)} %fusion.3), channel_id=1, source_target_pairs={{0,2},{1,3},{2,0},{3,1},{4,6},{5,7},{6,4},{7,5},{8,10},{9,11},{10,... | collective-permute-start | bytes 147464 | tf_op jit(solution)/shard_map/ppermute | solution.py:165
  61.1 6.3 %collective-permute-start.13 = (bf16[1,3,32,128]{3,2,1,0:T(8,128)(2,1)S(1)}, bf16[1,3,32,128]{3,2,1,0:T(8,128)(2,1)S(1)}, u32[]{:S(2)}, u32[]{:S(2)}) collective-permute-start(bf16[1,3,32,128]{3,2,1,0:T(8,128)(2,1)S(1)} %dynamic-slice_convert_fusion.4), channel_id=1, source_target_pairs={{0,4},{1,5},{2,6},{3,7},{4,0},{5,1},{6,2},{7,3},{8,12},{9,13},{10,... | collective-permute-start | bytes 73736 | tf_op jit(solution)/shard_map/ppermute | solution.py:165
  63.2 8.4 %collective-permute-start.15 = (bf16[1,2,3,32,256]{4,3,2,1,0:T(8,128)(2,1)S(1)}, bf16[1,2,3,32,256]{4,3,2,1,0:T(8,128)(2,1)S(1)}, u32[]{:S(2)}, u32[]{:S(2)}) collective-permute-start(bf16[1,2,3,32,256]{4,3,2,1,0:T(8,128)(2,1)S(1)} %dynamic-slice_convert_fusion.1), channel_id=1, source_target_pairs={{0,4},{1,5},{2,6},{3,7},{4,0},{5,1},{6,2},{7,3},{8,12},{9,13},{10,... | collective-permute-start | bytes 294920 | tf_op jit(solution)/shard_map/ppermute | solution.py:165
  67.5 4.2 %collective-permute-start.14 = (f32[3,32,128]{2,1,0:T(8,128)S(1)}, f32[3,32,128]{2,1,0:T(8,128)S(1)}, u32[]{:S(2)}, u32[]{:S(2)}) collective-permute-start(f32[3,32,128]{2,1,0:T(8,128)S(1)} %add_bitcast_fusion), channel_id=1, source_target_pairs={{0,16},{8,24},{16,0},{24,8},{1,17},{9,25},{17,1},{25,9},{2,18},{10... | collective-permute-start | bytes 147464 | tf_op jit(solution)/shard_map/ppermute | solution.py:165
  71.7 1.9 %collective-permute-start.17 = (f32[3,32,128]{2,1,0:T(8,128)S(1)}, f32[3,32,128]{2,1,0:T(8,128)S(1)}, u32[]{:S(2)}, u32[]{:S(2)}) collective-permute-start(f32[3,32,128]{2,1,0:T(8,128)S(1)} %add.58), channel_id=1, source_target_pairs={{0,8},{8,0},{16,24},{24,16},{1,9},{9,1},{17,25},{25,17},{2,10},{10... | collective-permute-start | bytes 147464 | tf_op jit(solution)/shard_map/ppermute | solution.py:165
where the time goes:
time: 74.4 us; the launch traced here: 74.2 us
  waiting for transfers between devices  31.3 us (42%)
  starting transfers between devices  29.6 us (40%)
  Pallas kernels  9.75 us (13%)
  other arithmetic  1.72 us (2%)
  between operations  1.01 us (1%)
  local copies, waits for them, and re-layouts  0.89 us (1%)
    ppermute x16, waiting for transfers between devices, swapped(): return lax.ppermute(value, axis, [(i, i ^ mask) for i in range(size)])  31.3 us
    ppermute x16, starting transfers between devices, swapped(): return lax.ppermute(value, axis, [(i, i ^ mask) for i in range(size)])  24.8 us
    ppermute x2, starting transfers between devices, body(): got.append(lax.ppermute(part, ('row', 'col'), moves))  4.77 us
    pallas_call x1, Pallas kernels, body(): pl.pallas_call(functools.partial(product_kernel, n_row, n_col, (orders[0]...  3.29 us
    pallas_call x1, Pallas kernels, body(): pl.pallas_call(prepare_kernel, out_shape=[shape((width, width), f32), sha...  2.18 us
    pallas_call x1, Pallas kernels, body(): pl.pallas_call(functools.partial(column_kernel, n_row), out_shape=[shape(...  1.77 us
  transfers between devices with their start and end apart: 18, of which 11 were waited for; matrix products, arithmetic and copies ran while one was open for 1% of the time, Pallas kernels for 7%

commit v1 on v0

--- a/solution.py
+++ b/solution.py
@@ -265,8 +265,12 @@
             totals.append(keep + came.astype(f32))
             keep, send = halves(totals[g].reshape((-1, 2, inner) + block), 1, ways[bit])
             keep, send = keep.reshape((-1,) + block), send.astype(bf16).reshape((-1,) + block)
-            last.append((keep, swapped(send, "col", n_col, 1 << bit)))
-        state = last
+            last.append((keep, send))
+        if i < n_bits - 1 and orders[0][i] != orders[1][i]:
+            state = [(keep, swapped(send, "col", n_col, 1 << order[i])) for (keep, send), order in zip(last, orders)]
+        else:
+            came = swapped(jnp.stack([send for _, send in last]), "col", n_col, 1 << orders[0][i])
+            state = [(keep, came[g]) for g, (keep, _) in enumerate(last)]
 
     sums = pl.pallas_call(
         functools.partial(sum_kernel, n_bits - 1),
@@ -278,11 +282,23 @@
     )(rows, *totals, linked, consts)
     keep, send = halves(sums, 0, cores)
     sums = keep + swapped(send, "row", n_row, 1)
-    for bit in range(n_bits):
+    view = sums.reshape(-1, 2, 2, 3, slab, width // 2)
+
+    def part(high, low):
+        return halves(halves(view, 1, ways[1])[high], 1, ways[0])[low]
+
+    sums = part(0, 0)
+    for mask in (1, 2, 3):
+        sums = sums + swapped(part(mask >> 1, mask & 1).astype(bf16), "col", n_col, mask).astype(f32)
+    for bit in range(2, n_bits - 1):
         keep, send = halves(sums.reshape(-1, 2, 3, slab, width // 2), 1, ways[bit])
         sums = keep + swapped(send.astype(bf16), "col", n_col, 1 << bit).astype(f32)
-    mine = sums.reshape(3, slab, width // 2)
-    for bit in range(1, n_row.bit_length() - 1):
+    keep, send = (part.astype(bf16) for part in halves(sums.reshape(2, 3, slab, width // 2), 0, ways[n_bits - 1]))
+    across = [(r * n_col + c, (r ^ 2) * n_col + (c ^ (n_col // 2))) for r in range(n_row) for c in range(n_col)]
+    near = keep.astype(f32) + swapped(send, "col", n_col, n_col // 2).astype(f32)
+    far = swapped(keep, "row", n_row, 2).astype(f32) + lax.ppermute(send, ("row", "col"), across).astype(f32)
+    mine = near + far
+    for bit in range(2, n_row.bit_length() - 1):
         mine = mine + swapped(mine, "row", n_row, 1 << bit)
 
     mine, state = lax.optimization_barrier((mine, state))

time: 74.4 us -> 72.8 us (0.978)
  waiting for transfers between devices: 31.3 us -> 26 us
  starting transfers between devices: 29.6 us -> 32.2 us
  other arithmetic: 1.72 us -> 2.66 us
    ppermute x16, waiting for transfers between devices: 31.3 us -> 25.1 us  [swapped(): return lax.ppermute(value, axis, [(i, i ^ mask) for i in range(size)])]
    ppermute x16, starting transfers between devices: 24.8 us -> 27.2 us  [swapped(): return lax.ppermute(value, axis, [(i, i ^ mask) for i in range(size)])]
    ppermute x0 -> x1, waiting for transfers between devices: none -> 0.95 us  [body(): lax.ppermute(send, ('row', 'col'), across).astype(f32)]
    add x4, other arithmetic: 0.37 us -> 1.3 us  [body(): totals.append(keep + came.astype(f32))]
  transfers between devices with their start and end apart: 18 -> 19, of which waited for: 11 -> 12; matrix products, arithmetic and copies ran while one was open for 1% -> 2% of each run, Pallas kernels for 7% -> 8%
where the time goes in v1:
time: 72.8 us; the launch traced here: 72.5 us
  starting transfers between devices  32.2 us (44%)
  waiting for transfers between devices  26 us (36%)
  Pallas kernels  9.76 us (13%)
  other arithmetic  2.66 us (4%)
  between operations  1.01 us (1%)
  local copies, waits for them, and re-layouts  0.92 us (1%)
    ppermute x16, starting transfers between devices, swapped(): return lax.ppermute(value, axis, [(i, i ^ mask) for i in range(size)])  27.2 us
    ppermute x16, waiting for transfers between devices, swapped(): return lax.ppermute(value, axis, [(i, i ^ mask) for i in range(size)])  25.1 us
    ppermute x2, starting transfers between devices, body(): got.append(lax.ppermute(part, ('row', 'col'), moves))  4.77 us
    pallas_call x1, Pallas kernels, body(): pl.pallas_call(functools.partial(product_kernel, n_row, n_col, (orders[0]...  3.29 us
    pallas_call x1, Pallas kernels, body(): pl.pallas_call(prepare_kernel, out_shape=[shape((width, width), f32), sha...  2.18 us
    pallas_call x1, Pallas kernels, body(): pl.pallas_call(functools.partial(column_kernel, n_row), out_shape=[shape(...  1.78 us
    pallas_call x1, Pallas kernels, body(): pl.pallas_call(functools.partial(form_kernel, n_row), out_shape=shape(bas...  1.48 us
  transfers between devices with their start and end apart: 19, of which 12 were waited for; matrix products, arithmetic and copies ran while one was open for 2% of the time, Pallas kernels for 8%

profile of v1, /device:TPU:0, one launch (start us, length us, event | category | flops | bytes accessed | tf_op | source)
XLA Modules:
  0.0 72.5 jit_solution(1737877229689681592)
XLA Ops:
  0.7 1.0 %pad_maximum_fusion.3 = bf16[2,6,32,256]{3,2,1,0:T(8,128)(2,1)S(1)} fusion(bf16[1,6,32,256]{3,2,1,0:T(8,128)(2,1)} %bitcast.120, bf16[1,6,32,256]{3,2,1,0:T(8,128)(2,1)} %bitcast.121), kind=kLoop, calls=%fused_computation.13 | loop fusion | flops 98304 | bytes 393216 | tf_op jit(solution)/shard_map/stack | solution.py:195
  1.8 0.7 collective-permute-start
  2.4 4.1 %collective-permute-start.1 = (bf16[2,3,32,256]{3,2,1,0:T(8,128)(2,1)S(1)}, bf16[2,3,32,256]{3,2,1,0:T(8,128)(2,1)S(1)}, u32[]{:S(2)}, u32[]{:S(2)}) collective-permute-start(bf16[2,3,32,256]{3,2,1,0:T(8,128)(2,1)S(1)} %get-tuple-element.79), channel_id=1, source_target_pairs={{0,4},{1,12},{2,20},{3,28},{4,0},{5,8},{6,16},{7,24},{8,5},{9,13},... | collective-permute-start | bytes 294920 | tf_op jit(solution)/shard_map/ppermute | solution.py:205
  6.5 0.1 collective-permute-start.4
  6.6 0.0 collective-permute-done
  6.6 12.4 %collective-permute-start.2 = (bf16[2,3,32,256]{3,2,1,0:T(8,128)(2,1)S(1)}, bf16[2,3,32,256]{3,2,1,0:T(8,128)(2,1)S(1)}, u32[]{:S(2)}, u32[]{:S(2)}) collective-permute-start(bf16[2,3,32,256]{3,2,1,0:T(8,128)(2,1)S(1)} %collective-permute-done), channel_id=1, source_target_pairs={{0,16},{8,24},{16,0},{24,8},{1,17},{9,25},{17,1},{25,9},{2,18},{10... | collective-permute-start | bytes 294920 | tf_op jit(solution)/shard_map/ppermute | solution.py:165
  19.0 0.0 collective-permute-done.1
  19.0 0.0 collective-permute-start.3
  19.1 3.0 %collective-permute-done.2 = bf16[2,3,32,256]{3,2,1,0:T(8,128)(2,1)S(1)} collective-permute-done((bf16[2,3,32,256]{3,2,1,0:T(8,128)(2,1)S(1)}, bf16[2,3,32,256]{3,2,1,0:T(8,128)(2,1)S(1)}, u32[]{:S(2)}, u32[]{:S(2)}) %collective-permute-start.2) | collective-permute-done | bytes 98336 | tf_op jit(solution)/shard_map/ppermute | solution.py:165
  22.1 2.5 %collective-permute-done.3 = bf16[2,3,32,256]{3,2,1,0:T(8,128)(2,1)S(1)} collective-permute-done((bf16[2,3,32,256]{3,2,1,0:T(8,128)(2,1)S(1)}, bf16[2,3,32,256]{3,2,1,0:T(8,128)(2,1)S(1)}, u32[]{:S(2)}, u32[]{:S(2)}) %collective-permute-start.3) | collective-permute-done | bytes 98336 | tf_op jit(solution)/shard_map/ppermute | solution.py:165
  24.6 0.0 collective-permute-done.4
  24.7 0.1 collective-permute-start.5
  24.8 1.5 %form.1.rows = bf16[2,2,6,32,256]{4,3,2,1,0:T(8,128)(2,1)S(1)} custom-call(s32[18]{0:T(128)S(1)} %copy-done.3, s32[12]{0:T(128)S(1)} %copy-done.4, f32[256,256]{1,0:T(8,128)S(1)} %copy-done.1, f32[256,256]{1,0:T(8,128)S(1)} %copy-done.2, bf16[2,2,6,32,256]{4,3,2,1,0:T(8,128)(2,1)S(1)} %pad_maximum_fusion.2.base), custom_call_target="tpu_custom_call" | custom-call | flops 134217728 | bytes 262144 | tf_op jit(solution)/shard_map/form/pallas_call | solution.py:216
  26.3 0.2 collective-permute-done.5
  26.5 0.1 pad_maximum_fusion
  26.6 3.3 %products.1 = (f32[4,2,3,32,256]{4,3,2,1,0:T(8,128)S(1)}, f32[4,2,3,32,256]{4,3,2,1,0:T(8,128)S(1)}, bf16[4,2,3,32,256]{4,3,2,1,0:T(8,128)(2,1)S(1)}, bf16[4,2,3,32,256]{4,3,2,1,0:T(8,128)(2,1)S(1)}) custom-call(s32[18]{0:T(128)S(1)} %copy-done.3, s32[12]{0:T(128)S(1)} %copy-done.4, f32[256,256]{1,0:T(8,128)S(1)} %copy-done.1, f32[256,256]{1,0:T(8,128)S(1)} %copy-done.2, ...), custom_call_target="tpu_custom_call" | custom-call | tf_op jit(solution)/shard_map/products/pallas_call | solution.py:232
  29.9 0.6 collective-permute-start.8
  30.5 1.1 %collective-permute-start.6 = (bf16[4,2,3,32,256]{4,3,2,1,0:T(8,128)(2,1)S(1)}, bf16[4,2,3,32,256]{4,3,2,1,0:T(8,128)(2,1)S(1)}, u32[]{:S(2)}, u32[]{:S(2)}) collective-permute-start(bf16[4,2,3,32,256]{4,3,2,1,0:T(8,128)(2,1)S(1)} %get-tuple-element.43), channel_id=1, source_target_pairs={{0,1},{1,0},{2,3},{3,2},{4,5},{5,4},{6,7},{7,6},{8,9},{9,8},{10,11... | collective-permute-start | bytes 1179656 | tf_op jit(solution)/shard_map/ppermute | solution.py:165
  31.5 2.2 %prepare.1 = (f32[256,256]{1,0:T(8,128)S(1)}, f32[3,32,256]{2,1,0:T(8,128)S(1)}) custom-call(bf16[256,256]{1,0:T(8,128)(2,1)S(1)} %copy-done.5, f32[256,256]{1,0:T(8,128)S(1)} %copy-done.1, f32[256,256]{1,0:T(8,128)S(1)} %copy-done.2, f32[4,2,3,32,256]{4,3,2,1,0:T(8,128)S(1)} %get-tuple-element.42.after), custom_call_target="tpu_custom_call" | custom-call | flops 1006632960 | bytes 524288 | tf_op jit(solution)/shard_map/prepare/pallas_call | solution.py:245
  33.7 7.7 %collective-permute-done.8 = bf16[4,2,3,32,256]{4,3,2,1,0:T(8,128)(2,1)} collective-permute-done((bf16[4,2,3,32,256]{4,3,2,1,0:T(8,128)(2,1)S(1)}, bf16[4,2,3,32,256]{4,3,2,1,0:T(8,128)(2,1)}, u32[]{:S(2)}, u32[]{:S(2)}) %collective-permute-start.8) | collective-permute-done | bytes 393248 | tf_op jit(solution)/shard_map/ppermute | solution.py:165
  41.4 1.1 %convert_add_fusion = f32[4,2,3,32,256]{4,3,2,1,0:T(8,128)S(1)} fusion(f32[4,2,3,32,256]{4,3,2,1,0:T(8,128)S(1)} %get-tuple-element.46, bf16[4,2,3,32,256]{4,3,2,1,0:T(8,128)(2,1)} %collective-permute-done.8), kind=kLoop, calls=%fused_computation.1 | loop fusion | flops 393216 | bytes 1966080 | tf_op jit(solution)/shard_map/add | solution.py:265
  42.5 0.5 collective-permute-start.9
  43.0 0.0 collective-permute-done.6
  43.0 0.1 convert_add_fusion.1
  43.2 1.3 %collective-permute-start.7 = (bf16[2,2,3,32,256]{4,3,2,1,0:T(8,128)(2,1)S(1)}, bf16[2,2,3,32,256]{4,3,2,1,0:T(8,128)(2,1)S(1)}, u32[]{:S(2)}, u32[]{:S(2)}) collective-permute-start(bf16[2,2,3,32,256]{4,3,2,1,0:T(8,128)(2,1)S(1)} %fusion), channel_id=1, source_target_pairs={{0,2},{1,3},{2,0},{3,1},{4,6},{5,7},{6,4},{7,5},{8,10},{9,11},{10,... | collective-permute-start | bytes 589832 | tf_op jit(solution)/shard_map/ppermute | solution.py:165
  44.4 4.5 %collective-permute-done.9 = bf16[2,2,3,32,256]{4,3,2,1,0:T(8,128)(2,1)S(1)} collective-permute-done((bf16[2,2,3,32,256]{4,3,2,1,0:T(8,128)(2,1)S(1)}, bf16[2,2,3,32,256]{4,3,2,1,0:T(8,128)(2,1)S(1)}, u32[]{:S(2)}, u32[]{:S(2)}) %collective-permute-start.9) | collective-permute-done | bytes 196640 | tf_op jit(solution)/shard_map/ppermute | solution.py:165
  49.0 0.3 collective-permute-done.7
  49.3 1.0 %sums.1 = f32[2,8,3,32,128]{4,3,2,1,0:T(8,128)S(1)} custom-call(bf16[2,2,6,32,256]{4,3,2,1,0:T(8,128)(2,1)S(1)} %form.1.rows, f32[2,2,3,32,256]{4,3,2,1,0:T(8,128)S(1)} %bitcast_add_fusion.2.total_low, f32[2,2,3,32,256]{4,3,2,1,0:T(8,128)S(1)} %bitcast_add_fusion.1.total_high, f32[256,256]{1,0:T(8,128)S(1)} %get-tuple-element.50.linked, ...), custom_call_target="tpu_custom_call" | custom-call | tf_op jit(solution)/shard_map/sums/pallas_call | solution.py:275
  50.4 0.1 collective-permute-start.10
  50.6 1.6 %collective-permute-done.10 = f32[8,3,32,128]{3,2,1,0:T(8,128)S(1)} collective-permute-done((f32[8,3,32,128]{3,2,1,0:T(8,128)S(1)}, f32[8,3,32,128]{3,2,1,0:T(8,128)S(1)}, u32[]{:S(2)}, u32[]{:S(2)}) %collective-permute-start.10) | collective-permute-done | bytes 393248 | tf_op jit(solution)/shard_map/ppermute | solution.py:165
  52.2 0.1 bitcast_add_fusion
  52.3 1.7 %collective-permute-start.11 = (bf16[2,3,32,128]{3,2,1,0:T(8,128)(2,1)S(1)}, bf16[2,3,32,128]{3,2,1,0:T(8,128)(2,1)S(1)}, u32[]{:S(2)}, u32[]{:S(2)}) collective-permute-start(bf16[2,3,32,128]{3,2,1,0:T(8,128)(2,1)S(1)} %get-tuple-element.73), channel_id=1, source_target_pairs={{0,1},{1,0},{2,3},{3,2},{4,5},{5,4},{6,7},{7,6},{8,9},{9,8},{10,11... | collective-permute-start | bytes 147464 | tf_op jit(solution)/shard_map/ppermute | solution.py:165
  54.0 0.5 collective-permute-start.12
  54.5 1.3 %collective-permute-start.13 = (bf16[2,3,32,128]{3,2,1,0:T(8,128)(2,1)S(1)}, bf16[2,3,32,128]{3,2,1,0:T(8,128)(2,1)S(1)}, u32[]{:S(2)}, u32[]{:S(2)}) collective-permute-start(bf16[2,3,32,128]{3,2,1,0:T(8,128)(2,1)S(1)} %get-tuple-element.74), channel_id=1, source_target_pairs={{0,3},{1,2},{2,1},{3,0},{4,7},{5,6},{6,5},{7,4},{8,11},{9,10},{10,... | collective-permute-start | bytes 147464 | tf_op jit(solution)/shard_map/ppermute | solution.py:165
  55.9 2.3 %collective-permute-start.17 = (bf16[2,1,2,3,32,256]{5,4,3,2,1,0:T(8,128)(2,1)S(1)}, bf16[2,1,2,3,32,256]{5,4,3,2,1,0:T(8,128)(2,1)S(1)}, u32[]{:S(2)}, u32[]{:S(2)}) collective-permute-start(bf16[2,1,2,3,32,256]{5,4,3,2,1,0:T(8,128)(2,1)S(1)} %pad_maximum_fusion.4), channel_id=1, source_target_pairs={{0,4},{1,5},{2,6},{3,7},{4,0},{5,1},{6,2},{7,3},{8,12},{9,13},{10,... | collective-permute-start | bytes 589832 | tf_op jit(solution)/shard_map/ppermute | solution.py:165
  58.2 0.0 collective-permute-done.11
  58.2 0.1 collective-permute-done.12
  58.2 1.3 %collective-permute-done.13 = bf16[2,3,32,128]{3,2,1,0:T(8,128)(2,1)S(1)} collective-permute-done((bf16[2,3,32,128]{3,2,1,0:T(8,128)(2,1)S(1)}, bf16[2,3,32,128]{3,2,1,0:T(8,128)(2,1)S(1)}, u32[]{:S(2)}, u32[]{:S(2)}) %collective-permute-start.13) | collective-permute-done | bytes 49184 | tf_op jit(solution)/shard_map/ppermute | solution.py:165
  59.6 3.9 %collective-permute-start.14 = (bf16[3,32,128]{2,1,0:T(8,128)(2,1)S(1)}, bf16[3,32,128]{2,1,0:T(8,128)(2,1)S(1)}, u32[]{:S(2)}, u32[]{:S(2)}) collective-permute-start(bf16[3,32,128]{2,1,0:T(8,128)(2,1)S(1)} %get-tuple-element.86), channel_id=1, source_target_pairs={{0,4},{1,5},{2,6},{3,7},{4,0},{5,1},{6,2},{7,3},{8,12},{9,13},{10,... | collective-permute-start | bytes 73736 | tf_op jit(solution)/shard_map/ppermute | solution.py:165
  63.4 0.2 collective-permute-start.16
  63.6 1.3 %collective-permute-start.15 = (bf16[3,32,128]{2,1,0:T(8,128)(2,1)S(1)}, bf16[3,32,128]{2,1,0:T(8,128)(2,1)S(1)}, u32[]{:S(2)}, u32[]{:S(2)}) collective-permute-start(bf16[3,32,128]{2,1,0:T(8,128)(2,1)S(1)} %get-tuple-element.85), channel_id=1, source_target_pairs={{0,16},{8,24},{16,0},{24,8},{1,17},{9,25},{17,1},{25,9},{2,18},{10... | collective-permute-start | bytes 73736 | tf_op jit(solution)/shard_map/ppermute | solution.py:165
  64.9 3.8 %collective-permute-done.17 = bf16[2,1,2,3,32,256]{5,4,3,2,1,0:T(8,128)(2,1)S(1)} collective-permute-done((bf16[2,1,2,3,32,256]{5,4,3,2,1,0:T(8,128)(2,1)S(1)}, bf16[2,1,2,3,32,256]{5,4,3,2,1,0:T(8,128)(2,1)S(1)}, u32[]{:S(2)}, u32[]{:S(2)}) %collective-permute-start.17) | collective-permute-done | bytes 196640 | tf_op jit(solution)/shard_map/ppermute | solution.py:165
  68.8 0.2 collective-permute-done.14
  69.0 0.0 collective-permute-done.15
  69.0 0.9 %collective-permute-done.16 = bf16[3,32,128]{2,1,0:T(8,128)(2,1)S(1)} collective-permute-done((bf16[3,32,128]{2,1,0:T(8,128)(2,1)S(1)}, bf16[3,32,128]{2,1,0:T(8,128)(2,1)S(1)}, u32[]{:S(2)}, u32[]{:S(2)}) %collective-permute-start.16) | collective-permute-done | bytes 24608 | tf_op jit(solution)/shard_map/ppermute | solution.py:299
  70.0 0.1 collective-permute-start.18
  70.1 1.8 %columns.1 = (f32[6,32,256]{2,1,0:T(8,128)}, f32[6,32,256]{2,1,0:T(8,128)}) custom-call(s32[18]{0:T(128)S(1)} %copy-done.3, s32[12]{0:T(128)S(1)} %copy-done.4, f32[2,3,32,256]{3,2,1,0:T(8,128)S(1)} %bitcast.105, bf16[2,3,32,256]{3,2,1,0:T(8,128)(2,1)S(1)} %bitcast.107, f32[2,3,32,256]{3,2,1,0:T(8,128)S(1)} %bitcast.104, ...), custom_call_target="tpu_custom_call" | custom-call | tf_op jit(solution)/shard_map/columns/pallas_call | solution.py:305
  71.9 0.6 slice_bitcast_fusion.2
  (35 shorter events, 0.6 us)
Async XLA Ops:
  0.6 24.1 %copy-start.1 = (f32[256,256]{1,0:T(8,128)S(1)}, f32[256,256]{1,0:T(8,128)}, u32[]{:S(2)}) copy-start(f32[256,256]{1,0:T(8,128)} %inv1.5) | copy-start | bytes 786436
  0.6 24.1 %copy-start.2 = (f32[256,256]{1,0:T(8,128)S(1)}, f32[256,256]{1,0:T(8,128)}, u32[]{:S(2)}) copy-start(f32[256,256]{1,0:T(8,128)} %inv2.5) | copy-start | bytes 786436
  0.7 24.1 %copy-start.3 = (s32[18]{0:T(128)S(1)}, s32[18]{0:T(128)}, u32[]{:S(2)}) copy-start(s32[18]{0:T(128)} %struct1.5) | copy-start | bytes 220
  0.7 24.1 %copy-start.4 = (s32[12]{0:T(128)S(1)}, s32[12]{0:T(128)}, u32[]{:S(2)}) copy-start(s32[12]{0:T(128)} %struct2.5) | copy-start | bytes 148
  1.8 4.9 %collective-permute-start = (bf16[2,3,32,256]{3,2,1,0:T(8,128)(2,1)S(1)}, bf16[2,3,32,256]{3,2,1,0:T(8,128)(2,1)S(1)}, u32[]{:S(2)}, u32[]{:S(2)}) collective-permute-start(bf16[2,3,32,256]{3,2,1,0:T(8,128)(2,1)S(1)} %get-tuple-element.78), channel_id=1, source_target_pairs={{0,0},{1,8},{2,16},{3,24},{4,4},{5,12},{6,20},{7,28},{8,1},{9,9},{... | collective-permute-start | bytes 294920 | tf_op jit(solution)/shard_map/ppermute | solution.py:205
  2.4 16.6 %collective-permute-start.1 = (bf16[2,3,32,256]{3,2,1,0:T(8,128)(2,1)S(1)}, bf16[2,3,32,256]{3,2,1,0:T(8,128)(2,1)S(1)}, u32[]{:S(2)}, u32[]{:S(2)}) collective-permute-start(bf16[2,3,32,256]{3,2,1,0:T(8,128)(2,1)S(1)} %get-tuple-element.79), channel_id=1, source_target_pairs={{0,4},{1,12},{2,20},{3,28},{4,0},{5,8},{6,16},{7,24},{8,5},{9,13},... | collective-permute-start | bytes 294920 | tf_op jit(solution)/shard_map/ppermute | solution.py:205
  6.5 18.1 %collective-permute-start.4 = (bf16[2,6,32,256]{3,2,1,0:T(8,128)(2,1)S(1)}, bf16[2,6,32,256]{3,2,1,0:T(8,128)(2,1)S(1)}, u32[]{:S(2)}, u32[]{:S(2)}) collective-permute-start(bf16[2,6,32,256]{3,2,1,0:T(8,128)(2,1)S(1)} %pad_maximum_fusion.3), channel_id=1, source_target_pairs={{0,4},{1,5},{2,6},{3,7},{4,0},{5,1},{6,2},{7,3},{8,12},{9,13},{10,... | collective-permute-start | bytes 589832 | tf_op jit(solution)/shard_map/ppermute | solution.py:165
  6.6 15.4 %collective-permute-start.2 = (bf16[2,3,32,256]{3,2,1,0:T(8,128)(2,1)S(1)}, bf16[2,3,32,256]{3,2,1,0:T(8,128)(2,1)S(1)}, u32[]{:S(2)}, u32[]{:S(2)}) collective-permute-start(bf16[2,3,32,256]{3,2,1,0:T(8,128)(2,1)S(1)} %collective-permute-done), channel_id=1, source_target_pairs={{0,16},{8,24},{16,0},{24,8},{1,17},{9,25},{17,1},{25,9},{2,18},{10... | collective-permute-start | bytes 294920 | tf_op jit(solution)/shard_map/ppermute | solution.py:165
  19.0 5.5 %collective-permute-start.3 = (bf16[2,3,32,256]{3,2,1,0:T(8,128)(2,1)S(1)}, bf16[2,3,32,256]{3,2,1,0:T(8,128)(2,1)S(1)}, u32[]{:S(2)}, u32[]{:S(2)}) collective-permute-start(bf16[2,3,32,256]{3,2,1,0:T(8,128)(2,1)S(1)} %collective-permute-done.1), channel_id=1, source_target_pairs={{0,16},{8,24},{16,0},{24,8},{1,17},{9,25},{17,1},{25,9},{2,18},{10... | collective-permute-start | bytes 294920 | tf_op jit(solution)/shard_map/ppermute | solution.py:165
  24.6 2.0 %copy-start = (bf16[6,1,3,1,256,256]{5,4,3,2,1,0:T(8,128)(2,1)S(1)}, bf16[6,1,3,1,256,256]{5,4,3,2,1,0:T(8,128)(2,1)}, u32[]{:S(2)}) copy-start(bf16[6,1,3,1,256,256]{5,4,3,2,1,0:T(8,128)(2,1)} %param.8) | copy-start | bytes 7077892
  24.7 1.8 %collective-permute-start.5 = (bf16[2,2,2,3,32,256]{5,4,3,2,1,0:T(8,128)(2,1)S(1)}, bf16[2,2,2,3,32,256]{5,4,3,2,1,0:T(8,128)(2,1)S(1)}, u32[]{:S(2)}, u32[]{:S(2)}) collective-permute-start(bf16[2,2,2,3,32,256]{5,4,3,2,1,0:T(8,128)(2,1)S(1)} %pad_maximum_fusion.1), channel_id=1, source_target_pairs={{0,8},{8,0},{16,24},{24,16},{1,9},{9,1},{17,25},{25,17},{2,10},{10... | collective-permute-start | bytes 1179656 | tf_op jit(solution)/shard_map/ppermute | solution.py:165
  26.5 5.1 %copy-start.5 = (bf16[256,256]{1,0:T(8,128)(2,1)S(1)}, bf16[256,256]{1,0:T(8,128)(2,1)}, u32[]{:S(2)}) copy-start(bf16[256,256]{1,0:T(8,128)(2,1)} %link.1) | copy-start | bytes 393220
  29.9 11.5 %collective-permute-start.8 = (bf16[4,2,3,32,256]{4,3,2,1,0:T(8,128)(2,1)S(1)}, bf16[4,2,3,32,256]{4,3,2,1,0:T(8,128)(2,1)}, u32[]{:S(2)}, u32[]{:S(2)}) collective-permute-start(bf16[4,2,3,32,256]{4,3,2,1,0:T(8,128)(2,1)S(1)} %get-tuple-element.47), channel_id=1, source_target_pairs={{0,2},{1,3},{2,0},{3,1},{4,6},{5,7},{6,4},{7,5},{8,10},{9,11},{10,... | collective-permute-start | bytes 1179656 | tf_op jit(solution)/shard_map/ppermute | solution.py:165
  30.5 12.5 %collective-permute-start.6 = (bf16[4,2,3,32,256]{4,3,2,1,0:T(8,128)(2,1)S(1)}, bf16[4,2,3,32,256]{4,3,2,1,0:T(8,128)(2,1)S(1)}, u32[]{:S(2)}, u32[]{:S(2)}) collective-permute-start(bf16[4,2,3,32,256]{4,3,2,1,0:T(8,128)(2,1)S(1)} %get-tuple-element.43), channel_id=1, source_target_pairs={{0,1},{1,0},{2,3},{3,2},{4,5},{5,4},{6,7},{7,6},{8,9},{9,8},{10,11... | collective-permute-start | bytes 1179656 | tf_op jit(solution)/shard_map/ppermute | solution.py:165
  42.5 6.4 %collective-permute-start.9 = (bf16[2,2,3,32,256]{4,3,2,1,0:T(8,128)(2,1)S(1)}, bf16[2,2,3,32,256]{4,3,2,1,0:T(8,128)(2,1)S(1)}, u32[]{:S(2)}, u32[]{:S(2)}) collective-permute-start(bf16[2,2,3,32,256]{4,3,2,1,0:T(8,128)(2,1)S(1)} %fusion.1), channel_id=1, source_target_pairs={{0,1},{1,0},{2,3},{3,2},{4,5},{5,4},{6,7},{7,6},{8,9},{9,8},{10,11... | collective-permute-start | bytes 589832 | tf_op jit(solution)/shard_map/ppermute | solution.py:165
  43.2 6.1 %collective-permute-start.7 = (bf16[2,2,3,32,256]{4,3,2,1,0:T(8,128)(2,1)S(1)}, bf16[2,2,3,32,256]{4,3,2,1,0:T(8,128)(2,1)S(1)}, u32[]{:S(2)}, u32[]{:S(2)}) collective-permute-start(bf16[2,2,3,32,256]{4,3,2,1,0:T(8,128)(2,1)S(1)} %fusion), channel_id=1, source_target_pairs={{0,2},{1,3},{2,0},{3,1},{4,6},{5,7},{6,4},{7,5},{8,10},{9,11},{10,... | collective-permute-start | bytes 589832 | tf_op jit(solution)/shard_map/ppermute | solution.py:165
  50.4 1.8 %collective-permute-start.10 = (f32[8,3,32,128]{3,2,1,0:T(8,128)S(1)}, f32[8,3,32,128]{3,2,1,0:T(8,128)S(1)}, u32[]{:S(2)}, u32[]{:S(2)}) collective-permute-start(f32[8,3,32,128]{3,2,1,0:T(8,128)S(1)} %dynamic-slice_bitcast_fusion), channel_id=1, source_target_pairs={{0,8},{8,0},{16,24},{24,16},{1,9},{9,1},{17,25},{25,17},{2,10},{10... | collective-permute-start | bytes 1179656 | tf_op jit(solution)/shard_map/ppermute | solution.py:165
  52.3 5.9 %collective-permute-start.11 = (bf16[2,3,32,128]{3,2,1,0:T(8,128)(2,1)S(1)}, bf16[2,3,32,128]{3,2,1,0:T(8,128)(2,1)S(1)}, u32[]{:S(2)}, u32[]{:S(2)}) collective-permute-start(bf16[2,3,32,128]{3,2,1,0:T(8,128)(2,1)S(1)} %get-tuple-element.73), channel_id=1, source_target_pairs={{0,1},{1,0},{2,3},{3,2},{4,5},{5,4},{6,7},{7,6},{8,9},{9,8},{10,11... | collective-permute-start | bytes 147464 | tf_op jit(solution)/shard_map/ppermute | solution.py:165
  54.0 4.3 %collective-permute-start.12 = (bf16[2,3,32,128]{3,2,1,0:T(8,128)(2,1)S(1)}, bf16[2,3,32,128]{3,2,1,0:T(8,128)(2,1)S(1)}, u32[]{:S(2)}, u32[]{:S(2)}) collective-permute-start(bf16[2,3,32,128]{3,2,1,0:T(8,128)(2,1)S(1)} %get-tuple-element.75), channel_id=1, source_target_pairs={{0,2},{1,3},{2,0},{3,1},{4,6},{5,7},{6,4},{7,5},{8,10},{9,11},{10,... | collective-permute-start | bytes 147464 | tf_op jit(solution)/shard_map/ppermute | solution.py:165
  54.5 5.0 %collective-permute-start.13 = (bf16[2,3,32,128]{3,2,1,0:T(8,128)(2,1)S(1)}, bf16[2,3,32,128]{3,2,1,0:T(8,128)(2,1)S(1)}, u32[]{:S(2)}, u32[]{:S(2)}) collective-permute-start(bf16[2,3,32,128]{3,2,1,0:T(8,128)(2,1)S(1)} %get-tuple-element.74), channel_id=1, source_target_pairs={{0,3},{1,2},{2,1},{3,0},{4,7},{5,6},{6,5},{7,4},{8,11},{9,10},{10,... | collective-permute-start | bytes 147464 | tf_op jit(solution)/shard_map/ppermute | solution.py:165
  55.9 12.9 %collective-permute-start.17 = (bf16[2,1,2,3,32,256]{5,4,3,2,1,0:T(8,128)(2,1)S(1)}, bf16[2,1,2,3,32,256]{5,4,3,2,1,0:T(8,128)(2,1)S(1)}, u32[]{:S(2)}, u32[]{:S(2)}) collective-permute-start(bf16[2,1,2,3,32,256]{5,4,3,2,1,0:T(8,128)(2,1)S(1)} %pad_maximum_fusion.4), channel_id=1, source_target_pairs={{0,4},{1,5},{2,6},{3,7},{4,0},{5,1},{6,2},{7,3},{8,12},{9,13},{10,... | collective-permute-start | bytes 589832 | tf_op jit(solution)/shard_map/ppermute | solution.py:165
  59.6 9.5 %collective-permute-start.14 = (bf16[3,32,128]{2,1,0:T(8,128)(2,1)S(1)}, bf16[3,32,128]{2,1,0:T(8,128)(2,1)S(1)}, u32[]{:S(2)}, u32[]{:S(2)}) collective-permute-start(bf16[3,32,128]{2,1,0:T(8,128)(2,1)S(1)} %get-tuple-element.86), channel_id=1, source_target_pairs={{0,4},{1,5},{2,6},{3,7},{4,0},{5,1},{6,2},{7,3},{8,12},{9,13},{10,... | collective-permute-start | bytes 73736 | tf_op jit(solution)/shard_map/ppermute | solution.py:165
  63.4 6.6 %collective-permute-start.16 = (bf16[3,32,128]{2,1,0:T(8,128)(2,1)S(1)}, bf16[3,32,128]{2,1,0:T(8,128)(2,1)S(1)}, u32[]{:S(2)}, u32[]{:S(2)}) collective-permute-start(bf16[3,32,128]{2,1,0:T(8,128)(2,1)S(1)} %get-tuple-element.86), channel_id=1, source_target_pairs={{0,20},{1,21},{2,22},{3,23},{4,16},{5,17},{6,18},{7,19},{8,28},{9,... | collective-permute-start | bytes 73736 | tf_op jit(solution)/shard_map/ppermute | solution.py:299
  63.6 5.4 %collective-permute-start.15 = (bf16[3,32,128]{2,1,0:T(8,128)(2,1)S(1)}, bf16[3,32,128]{2,1,0:T(8,128)(2,1)S(1)}, u32[]{:S(2)}, u32[]{:S(2)}) collective-permute-start(bf16[3,32,128]{2,1,0:T(8,128)(2,1)S(1)} %get-tuple-element.85), channel_id=1, source_target_pairs={{0,16},{8,24},{16,0},{24,8},{1,17},{9,25},{17,1},{25,9},{2,18},{10... | collective-permute-start | bytes 73736 | tf_op jit(solution)/shard_map/ppermute | solution.py:165
  70.0 1.9 %collective-permute-start.18 = (f32[3,32,128]{2,1,0:T(8,128)S(1)}, f32[3,32,128]{2,1,0:T(8,128)S(1)}, u32[]{:S(2)}, u32[]{:S(2)}) collective-permute-start(f32[3,32,128]{2,1,0:T(8,128)S(1)} %add_add_fusion), channel_id=1, source_target_pairs={{0,8},{8,0},{16,24},{24,16},{1,9},{9,1},{17,25},{25,17},{2,10},{10... | collective-permute-start | bytes 147464 | tf_op jit(solution)/shard_map/ppermute | solution.py:165

commit v2 on v1

--- a/solution.py
+++ b/solution.py
@@ -190,7 +190,9 @@
     ways = [(way.astype(jnp.uint32), (1 - way).astype(jnp.uint32)) for way in ways]
     core = lax.axis_index("row") & 1
     cores = (core.astype(jnp.uint32), (1 - core).astype(jnp.uint32))
-    panels, picks, ways, cores = lax.optimization_barrier((panels, picks, ways, cores))
+    quads = [(((here_col >> (n_bits - 1)) << 1) | ((here_col >> 1) & 1)) ^ m for m in range(4)]
+    quads = [quad.astype(jnp.uint32) for quad in quads]
+    panels, picks, ways, cores, quads = lax.optimization_barrier((panels, picks, ways, cores, quads))
 
     raw = lax.optimization_barrier(jnp.stack(panels))
     turns = raw.reshape(2, col_blocks, cycle, slab, width)
@@ -282,22 +284,20 @@
     )(rows, *totals, linked, consts)
     keep, send = halves(sums, 0, cores)
     sums = keep + swapped(send, "row", n_row, 1)
-    view = sums.reshape(-1, 2, 2, 3, slab, width // 2)
-
-    def part(high, low):
-        return halves(halves(view, 1, ways[1])[high], 1, ways[0])[low]
-
-    sums = part(0, 0)
-    for mask in (1, 2, 3):
-        sums = sums + swapped(part(mask >> 1, mask & 1).astype(bf16), "col", n_col, mask).astype(f32)
+    tail = (3, slab, width // 2)
+    keep, send = (part.astype(bf16) for part in halves(sums.reshape((-1, 2) + tail), 1, ways[0]))
+    across = [(r * n_col + c, (r ^ 2) * n_col + (c ^ 1)) for r in range(n_row) for c in range(n_col)]
+    near = keep.astype(f32) + swapped(send, "col", n_col, 1).astype(f32)
+    far = swapped(keep, "row", n_row, 2).astype(f32) + lax.ppermute(send, ("row", "col"), across).astype(f32)
+    sums = near + far
     for bit in range(2, n_bits - 1):
-        keep, send = halves(sums.reshape(-1, 2, 3, slab, width // 2), 1, ways[bit])
+        keep, send = halves(sums.reshape((-1, 2, 2) + tail), 1, ways[bit])
         sums = keep + swapped(send.astype(bf16), "col", n_col, 1 << bit).astype(f32)
-    keep, send = (part.astype(bf16) for part in halves(sums.reshape(2, 3, slab, width // 2), 0, ways[n_bits - 1]))
-    across = [(r * n_col + c, (r ^ 2) * n_col + (c ^ (n_col // 2))) for r in range(n_row) for c in range(n_col)]
-    near = keep.astype(f32) + swapped(send, "col", n_col, n_col // 2).astype(f32)
-    far = swapped(keep, "row", n_row, 2).astype(f32) + lax.ppermute(send, ("row", "col"), across).astype(f32)
-    mine = near + far
+    parts = [lax.dynamic_index_in_dim(sums.reshape((4,) + tail), quad, 0, keepdims=False) for quad in quads]
+    mine = parts[0]
+    for m in range(1, 4):
+        mask = ((m >> 1) << (n_bits - 1)) | ((m & 1) << 1)
+        mine = mine + swapped(parts[m].astype(bf16), "col", n_col, mask).astype(f32)
     for bit in range(2, n_row.bit_length() - 1):
         mine = mine + swapped(mine, "row", n_row, 1 << bit)
 

time: 72.8 us -> 73 us (level)
  waiting for transfers between devices: 26 us -> 27.6 us
  other arithmetic: 2.66 us -> 1.77 us
    ppermute x16, waiting for transfers between devices: 25.1 us -> 27.6 us  [swapped(): return lax.ppermute(value, axis, [(i, i ^ mask) for i in range(size)])]
    ppermute x16, starting transfers between devices: 27.2 us -> 25.5 us  [swapped(): return lax.ppermute(value, axis, [(i, i ^ mask) for i in range(size)])]
    ppermute x1, starting transfers between devices: 0.2 us -> 1.45 us  [body(): lax.ppermute(send, ('row', 'col'), across).astype(f32)]
    ppermute x1, waiting for transfers between devices: 0.95 us -> 0.01 us  [body(): lax.ppermute(send, ('row', 'col'), across).astype(f32)]
    add x4, other arithmetic: 1.3 us -> 0.37 us  [body(): totals.append(keep + came.astype(f32))]
  transfers between devices with their start and end apart: 19 -> 19, of which waited for: 12 -> 10; matrix products, arithmetic and copies ran while one was open for 2% -> 1% of each run, Pallas kernels for 8% -> 7%
where the time goes in v2:
time: 73 us; the launch traced here: 72.8 us
  starting transfers between devices  31.8 us (44%)
  waiting for transfers between devices  27.6 us (38%)
  Pallas kernels  9.75 us (13%)
  other arithmetic  1.77 us (2%)
  between operations  1.01 us (1%)
  local copies, waits for them, and re-layouts  0.92 us (1%)
    ppermute x16, waiting for transfers between devices, swapped(): return lax.ppermute(value, axis, [(i, i ^ mask) for i in range(size)])  27.6 us
    ppermute x16, starting transfers between devices, swapped(): return lax.ppermute(value, axis, [(i, i ^ mask) for i in range(size)])  25.5 us
    ppermute x2, starting transfers between devices, body(): got.append(lax.ppermute(part, ('row', 'col'), moves))  4.77 us
    pallas_call x1, Pallas kernels, body(): pl.pallas_call(functools.partial(product_kernel, n_row, n_col, (orders[0]...  3.29 us
    pallas_call x1, Pallas kernels, body(): pl.pallas_call(prepare_kernel, out_shape=[shape((width, width), f32), sha...  2.18 us
    pallas_call x1, Pallas kernels, body(): pl.pallas_call(functools.partial(column_kernel, n_row), out_shape=[shape(...  1.78 us
    pallas_call x1, Pallas kernels, body(): pl.pallas_call(functools.partial(form_kernel, n_row), out_shape=shape(bas...  1.48 us
  transfers between devices with their start and end apart: 19, of which 10 were waited for; matrix products, arithmetic and copies ran while one was open for 1% of the time, Pallas kernels for 7%

profile of v2, /device:TPU:0, one launch (start us, length us, event | category | flops | bytes accessed | tf_op | source)
XLA Modules:
  0.0 72.8 jit_solution(1314519761038486608)
XLA Ops:
  0.7 1.0 %pad_maximum_fusion.3 = bf16[2,6,32,256]{3,2,1,0:T(8,128)(2,1)S(1)} fusion(bf16[1,6,32,256]{3,2,1,0:T(8,128)(2,1)} %bitcast.115, bf16[1,6,32,256]{3,2,1,0:T(8,128)(2,1)} %bitcast.116), kind=kLoop, calls=%fused_computation.13 | loop fusion | flops 98304 | bytes 393216 | tf_op jit(solution)/shard_map/stack | solution.py:197
  1.8 0.7 collective-permute-start
  2.4 4.1 %collective-permute-start.1 = (bf16[2,3,32,256]{3,2,1,0:T(8,128)(2,1)S(1)}, bf16[2,3,32,256]{3,2,1,0:T(8,128)(2,1)S(1)}, u32[]{:S(2)}, u32[]{:S(2)}) collective-permute-start(bf16[2,3,32,256]{3,2,1,0:T(8,128)(2,1)S(1)} %get-tuple-element.89), channel_id=1, source_target_pairs={{0,4},{1,12},{2,20},{3,28},{4,0},{5,8},{6,16},{7,24},{8,5},{9,13},... | collective-permute-start | bytes 294920 | tf_op jit(solution)/shard_map/ppermute | solution.py:207
  6.5 0.1 collective-permute-start.4
  6.6 0.0 collective-permute-done
  6.6 12.4 %collective-permute-start.2 = (bf16[2,3,32,256]{3,2,1,0:T(8,128)(2,1)S(1)}, bf16[2,3,32,256]{3,2,1,0:T(8,128)(2,1)S(1)}, u32[]{:S(2)}, u32[]{:S(2)}) collective-permute-start(bf16[2,3,32,256]{3,2,1,0:T(8,128)(2,1)S(1)} %collective-permute-done), channel_id=1, source_target_pairs={{0,16},{8,24},{16,0},{24,8},{1,17},{9,25},{17,1},{25,9},{2,18},{10... | collective-permute-start | bytes 294920 | tf_op jit(solution)/shard_map/ppermute | solution.py:165
  19.0 0.0 collective-permute-done.1
  19.0 0.0 collective-permute-start.3
  19.1 3.0 %collective-permute-done.2 = bf16[2,3,32,256]{3,2,1,0:T(8,128)(2,1)S(1)} collective-permute-done((bf16[2,3,32,256]{3,2,1,0:T(8,128)(2,1)S(1)}, bf16[2,3,32,256]{3,2,1,0:T(8,128)(2,1)S(1)}, u32[]{:S(2)}, u32[]{:S(2)}) %collective-permute-start.2) | collective-permute-done | bytes 98336 | tf_op jit(solution)/shard_map/ppermute | solution.py:165
  22.1 2.5 %collective-permute-done.3 = bf16[2,3,32,256]{3,2,1,0:T(8,128)(2,1)S(1)} collective-permute-done((bf16[2,3,32,256]{3,2,1,0:T(8,128)(2,1)S(1)}, bf16[2,3,32,256]{3,2,1,0:T(8,128)(2,1)S(1)}, u32[]{:S(2)}, u32[]{:S(2)}) %collective-permute-start.3) | collective-permute-done | bytes 98336 | tf_op jit(solution)/shard_map/ppermute | solution.py:165
  24.6 0.0 collective-permute-done.4
  24.7 0.1 collective-permute-start.5
  24.8 1.5 %form.1.rows = bf16[2,2,6,32,256]{4,3,2,1,0:T(8,128)(2,1)S(1)} custom-call(s32[18]{0:T(128)S(1)} %copy-done.3, s32[12]{0:T(128)S(1)} %copy-done.4, f32[256,256]{1,0:T(8,128)S(1)} %copy-done.1, f32[256,256]{1,0:T(8,128)S(1)} %copy-done.2, bf16[2,2,6,32,256]{4,3,2,1,0:T(8,128)(2,1)S(1)} %pad_maximum_fusion.2.base), custom_call_target="tpu_custom_call" | custom-call | flops 134217728 | bytes 262144 | tf_op jit(solution)/shard_map/form/pallas_call | solution.py:218
  26.3 0.2 collective-permute-done.5
  26.5 0.1 pad_maximum_fusion
  26.6 3.3 %products.1 = (f32[4,2,3,32,256]{4,3,2,1,0:T(8,128)S(1)}, f32[4,2,3,32,256]{4,3,2,1,0:T(8,128)S(1)}, bf16[4,2,3,32,256]{4,3,2,1,0:T(8,128)(2,1)S(1)}, bf16[4,2,3,32,256]{4,3,2,1,0:T(8,128)(2,1)S(1)}) custom-call(s32[18]{0:T(128)S(1)} %copy-done.3, s32[12]{0:T(128)S(1)} %copy-done.4, f32[256,256]{1,0:T(8,128)S(1)} %copy-done.1, f32[256,256]{1,0:T(8,128)S(1)} %copy-done.2, ...), custom_call_target="tpu_custom_call" | custom-call | tf_op jit(solution)/shard_map/products/pallas_call | solution.py:234
  29.9 0.6 collective-permute-start.8
  30.5 1.1 %collective-permute-start.6 = (bf16[4,2,3,32,256]{4,3,2,1,0:T(8,128)(2,1)S(1)}, bf16[4,2,3,32,256]{4,3,2,1,0:T(8,128)(2,1)S(1)}, u32[]{:S(2)}, u32[]{:S(2)}) collective-permute-start(bf16[4,2,3,32,256]{4,3,2,1,0:T(8,128)(2,1)S(1)} %get-tuple-element.47), channel_id=1, source_target_pairs={{0,1},{1,0},{2,3},{3,2},{4,5},{5,4},{6,7},{7,6},{8,9},{9,8},{10,11... | collective-permute-start | bytes 1179656 | tf_op jit(solution)/shard_map/ppermute | solution.py:165
  31.6 2.2 %prepare.1 = (f32[256,256]{1,0:T(8,128)S(1)}, f32[3,32,256]{2,1,0:T(8,128)S(1)}) custom-call(bf16[256,256]{1,0:T(8,128)(2,1)S(1)} %copy-done.5, f32[256,256]{1,0:T(8,128)S(1)} %copy-done.1, f32[256,256]{1,0:T(8,128)S(1)} %copy-done.2, f32[4,2,3,32,256]{4,3,2,1,0:T(8,128)S(1)} %get-tuple-element.46.after), custom_call_target="tpu_custom_call" | custom-call | flops 1006632960 | bytes 524288 | tf_op jit(solution)/shard_map/prepare/pallas_call | solution.py:247
  33.7 7.5 %collective-permute-done.8 = bf16[4,2,3,32,256]{4,3,2,1,0:T(8,128)(2,1)S(1)} collective-permute-done((bf16[4,2,3,32,256]{4,3,2,1,0:T(8,128)(2,1)S(1)}, bf16[4,2,3,32,256]{4,3,2,1,0:T(8,128)(2,1)S(1)}, u32[]{:S(2)}, u32[]{:S(2)}) %collective-permute-start.8) | collective-permute-done | bytes 393248 | tf_op jit(solution)/shard_map/ppermute | solution.py:165
  41.3 0.1 convert_add_fusion
  41.5 0.5 collective-permute-start.9
  41.9 0.0 collective-permute-done.6
  41.9 0.1 convert_add_fusion.1
  42.1 1.3 %collective-permute-start.7 = (bf16[2,2,3,32,256]{4,3,2,1,0:T(8,128)(2,1)S(1)}, bf16[2,2,3,32,256]{4,3,2,1,0:T(8,128)(2,1)S(1)}, u32[]{:S(2)}, u32[]{:S(2)}) collective-permute-start(bf16[2,2,3,32,256]{4,3,2,1,0:T(8,128)(2,1)S(1)} %fusion), channel_id=1, source_target_pairs={{0,2},{1,3},{2,0},{3,1},{4,6},{5,7},{6,4},{7,5},{8,10},{9,11},{10,... | collective-permute-start | bytes 589832 | tf_op jit(solution)/shard_map/ppermute | solution.py:165
  43.4 4.5 %collective-permute-done.9 = bf16[2,2,3,32,256]{4,3,2,1,0:T(8,128)(2,1)S(1)} collective-permute-done((bf16[2,2,3,32,256]{4,3,2,1,0:T(8,128)(2,1)S(1)}, bf16[2,2,3,32,256]{4,3,2,1,0:T(8,128)(2,1)S(1)}, u32[]{:S(2)}, u32[]{:S(2)}) %collective-permute-start.9) | collective-permute-done | bytes 196640 | tf_op jit(solution)/shard_map/ppermute | solution.py:165
  47.9 0.3 collective-permute-done.7
  48.3 1.0 %sums.1 = f32[2,8,3,32,128]{4,3,2,1,0:T(8,128)S(1)} custom-call(bf16[2,2,6,32,256]{4,3,2,1,0:T(8,128)(2,1)S(1)} %form.1.rows, f32[2,2,3,32,256]{4,3,2,1,0:T(8,128)S(1)} %bitcast_add_fusion.2.total_low, f32[2,2,3,32,256]{4,3,2,1,0:T(8,128)S(1)} %bitcast_add_fusion.1.total_high, f32[256,256]{1,0:T(8,128)S(1)} %get-tuple-element.54.linked, ...), custom_call_target="tpu_custom_call" | custom-call | tf_op jit(solution)/shard_map/sums/pallas_call | solution.py:277
  49.3 0.1 collective-permute-start.10
  49.5 2.8 %collective-permute-start.17 = (bf16[2,1,2,3,32,256]{5,4,3,2,1,0:T(8,128)(2,1)S(1)}, bf16[2,1,2,3,32,256]{5,4,3,2,1,0:T(8,128)(2,1)S(1)}, u32[]{:S(2)}, u32[]{:S(2)}) collective-permute-start(bf16[2,1,2,3,32,256]{5,4,3,2,1,0:T(8,128)(2,1)S(1)} %pad_maximum_fusion.4), channel_id=1, source_target_pairs={{0,4},{1,5},{2,6},{3,7},{4,0},{5,1},{6,2},{7,3},{8,12},{9,13},{10,... | collective-permute-start | bytes 589832 | tf_op jit(solution)/shard_map/ppermute | solution.py:165
  52.4 0.0 collective-permute-done.10
  52.4 0.1 bitcast_add_fusion
  52.5 1.2 %collective-permute-start.11 = (bf16[4,3,32,128]{3,2,1,0:T(8,128)(2,1)S(1)}, bf16[4,3,32,128]{3,2,1,0:T(8,128)(2,1)S(1)}, u32[]{:S(2)}, u32[]{:S(2)}) collective-permute-start(bf16[4,3,32,128]{3,2,1,0:T(8,128)(2,1)S(1)} %get-tuple-element.87), channel_id=1, source_target_pairs={{0,1},{1,0},{2,3},{3,2},{4,5},{5,4},{6,7},{7,6},{8,9},{9,8},{10,11... | collective-permute-start | bytes 294920 | tf_op jit(solution)/shard_map/ppermute | solution.py:165
  53.7 1.4 %collective-permute-start.13 = (bf16[4,3,32,128]{3,2,1,0:T(8,128)(2,1)S(1)}, bf16[4,3,32,128]{3,2,1,0:T(8,128)(2,1)S(1)}, u32[]{:S(2)}, u32[]{:S(2)}) collective-permute-start(bf16[4,3,32,128]{3,2,1,0:T(8,128)(2,1)S(1)} %get-tuple-element.87), channel_id=1, source_target_pairs={{0,17},{1,16},{2,19},{3,18},{4,21},{5,20},{6,23},{7,22},{8,25},{9,... | collective-permute-start | bytes 294920 | tf_op jit(solution)/shard_map/ppermute | solution.py:291
  55.2 0.9 %collective-permute-start.12 = (bf16[4,3,32,128]{3,2,1,0:T(8,128)(2,1)S(1)}, bf16[4,3,32,128]{3,2,1,0:T(8,128)(2,1)S(1)}, u32[]{:S(2)}, u32[]{:S(2)}) collective-permute-start(bf16[4,3,32,128]{3,2,1,0:T(8,128)(2,1)S(1)} %get-tuple-element.86), channel_id=1, source_target_pairs={{0,16},{8,24},{16,0},{24,8},{1,17},{9,25},{17,1},{25,9},{2,18},{10... | collective-permute-start | bytes 294920 | tf_op jit(solution)/shard_map/ppermute | solution.py:165
  56.1 2.1 %collective-permute-done.11 = bf16[4,3,32,128]{3,2,1,0:T(8,128)(2,1)S(1)} collective-permute-done((bf16[4,3,32,128]{3,2,1,0:T(8,128)(2,1)S(1)}, bf16[4,3,32,128]{3,2,1,0:T(8,128)(2,1)S(1)}, u32[]{:S(2)}, u32[]{:S(2)}) %collective-permute-start.11) | collective-permute-done | bytes 98336 | tf_op jit(solution)/shard_map/ppermute | solution.py:165
  58.2 3.4 %collective-permute-done.12 = bf16[4,3,32,128]{3,2,1,0:T(8,128)(2,1)S(1)} collective-permute-done((bf16[4,3,32,128]{3,2,1,0:T(8,128)(2,1)S(1)}, bf16[4,3,32,128]{3,2,1,0:T(8,128)(2,1)S(1)}, u32[]{:S(2)}, u32[]{:S(2)}) %collective-permute-start.12) | collective-permute-done | bytes 98336 | tf_op jit(solution)/shard_map/ppermute | solution.py:165
  61.6 0.0 collective-permute-done.13
  61.7 1.5 %collective-permute-start.14 = (bf16[3,32,128]{2,1,0:T(8,128)(2,1)S(1)}, bf16[3,32,128]{2,1,0:T(8,128)(2,1)S(1)}, u32[]{:S(2)}, u32[]{:S(2)}) collective-permute-start(bf16[3,32,128]{2,1,0:T(8,128)(2,1)S(1)} %get-tuple-element.83), channel_id=1, source_target_pairs={{0,2},{1,3},{2,0},{3,1},{4,6},{5,7},{6,4},{7,5},{8,10},{9,11},{10,... | collective-permute-start | bytes 73736 | tf_op jit(solution)/shard_map/ppermute | solution.py:165
  63.2 1.4 %collective-permute-start.15 = (bf16[3,32,128]{2,1,0:T(8,128)(2,1)S(1)}, bf16[3,32,128]{2,1,0:T(8,128)(2,1)S(1)}, u32[]{:S(2)}, u32[]{:S(2)}) collective-permute-start(bf16[3,32,128]{2,1,0:T(8,128)(2,1)S(1)} %get-tuple-element.85), channel_id=1, source_target_pairs={{0,4},{1,5},{2,6},{3,7},{4,0},{5,1},{6,2},{7,3},{8,12},{9,13},{10,... | collective-permute-start | bytes 73736 | tf_op jit(solution)/shard_map/ppermute | solution.py:165
  64.6 1.5 %collective-permute-start.16 = (bf16[3,32,128]{2,1,0:T(8,128)(2,1)S(1)}, bf16[3,32,128]{2,1,0:T(8,128)(2,1)S(1)}, u32[]{:S(2)}, u32[]{:S(2)}) collective-permute-start(bf16[3,32,128]{2,1,0:T(8,128)(2,1)S(1)} %get-tuple-element.84), channel_id=1, source_target_pairs={{0,6},{1,7},{2,4},{3,5},{4,2},{5,3},{6,0},{7,1},{8,14},{9,15},{10,... | collective-permute-start | bytes 73736 | tf_op jit(solution)/shard_map/ppermute | solution.py:165
  66.1 0.0 collective-permute-done.17
  66.1 2.3 %collective-permute-done.15 = bf16[3,32,128]{2,1,0:T(8,128)(2,1)S(1)} collective-permute-done((bf16[3,32,128]{2,1,0:T(8,128)(2,1)S(1)}, bf16[3,32,128]{2,1,0:T(8,128)(2,1)S(1)}, u32[]{:S(2)}, u32[]{:S(2)}) %collective-permute-start.15) | collective-permute-done | bytes 24608 | tf_op jit(solution)/shard_map/ppermute | solution.py:165
  68.4 1.8 %collective-permute-done.16 = bf16[3,32,128]{2,1,0:T(8,128)(2,1)S(1)} collective-permute-done((bf16[3,32,128]{2,1,0:T(8,128)(2,1)S(1)}, bf16[3,32,128]{2,1,0:T(8,128)(2,1)S(1)}, u32[]{:S(2)}, u32[]{:S(2)}) %collective-permute-start.16) | collective-permute-done | bytes 24608 | tf_op jit(solution)/shard_map/ppermute | solution.py:165
  70.2 0.1 collective-permute-start.18
  70.3 1.8 %columns.1 = (f32[6,32,256]{2,1,0:T(8,128)}, f32[6,32,256]{2,1,0:T(8,128)}) custom-call(s32[18]{0:T(128)S(1)} %copy-done.3, s32[12]{0:T(128)S(1)} %copy-done.4, f32[2,3,32,256]{3,2,1,0:T(8,128)S(1)} %bitcast.101, bf16[2,3,32,256]{3,2,1,0:T(8,128)(2,1)S(1)} %bitcast.103, f32[2,3,32,256]{3,2,1,0:T(8,128)S(1)} %bitcast.100, ...), custom_call_target="tpu_custom_call" | custom-call | tf_op jit(solution)/shard_map/columns/pallas_call | solution.py:305
  72.1 0.0 collective-permute-done.18
  72.1 0.6 slice_bitcast_fusion.2
  (35 shorter events, 0.6 us)
Async XLA Ops:
  0.6 24.1 %copy-start.1 = (f32[256,256]{1,0:T(8,128)S(1)}, f32[256,256]{1,0:T(8,128)}, u32[]{:S(2)}) copy-start(f32[256,256]{1,0:T(8,128)} %inv1.5) | copy-start | bytes 786436
  0.6 24.1 %copy-start.2 = (f32[256,256]{1,0:T(8,128)S(1)}, f32[256,256]{1,0:T(8,128)}, u32[]{:S(2)}) copy-start(f32[256,256]{1,0:T(8,128)} %inv2.5) | copy-start | bytes 786436
  0.7 24.1 %copy-start.3 = (s32[18]{0:T(128)S(1)}, s32[18]{0:T(128)}, u32[]{:S(2)}) copy-start(s32[18]{0:T(128)} %struct1.5) | copy-start | bytes 220
  0.7 24.1 %copy-start.4 = (s32[12]{0:T(128)S(1)}, s32[12]{0:T(128)}, u32[]{:S(2)}) copy-start(s32[12]{0:T(128)} %struct2.5) | copy-start | bytes 148
  1.8 4.9 %collective-permute-start = (bf16[2,3,32,256]{3,2,1,0:T(8,128)(2,1)S(1)}, bf16[2,3,32,256]{3,2,1,0:T(8,128)(2,1)S(1)}, u32[]{:S(2)}, u32[]{:S(2)}) collective-permute-start(bf16[2,3,32,256]{3,2,1,0:T(8,128)(2,1)S(1)} %get-tuple-element.88), channel_id=1, source_target_pairs={{0,0},{1,8},{2,16},{3,24},{4,4},{5,12},{6,20},{7,28},{8,1},{9,9},{... | collective-permute-start | bytes 294920 | tf_op jit(solution)/shard_map/ppermute | solution.py:207
  2.4 16.6 %collective-permute-start.1 = (bf16[2,3,32,256]{3,2,1,0:T(8,128)(2,1)S(1)}, bf16[2,3,32,256]{3,2,1,0:T(8,128)(2,1)S(1)}, u32[]{:S(2)}, u32[]{:S(2)}) collective-permute-start(bf16[2,3,32,256]{3,2,1,0:T(8,128)(2,1)S(1)} %get-tuple-element.89), channel_id=1, source_target_pairs={{0,4},{1,12},{2,20},{3,28},{4,0},{5,8},{6,16},{7,24},{8,5},{9,13},... | collective-permute-start | bytes 294920 | tf_op jit(solution)/shard_map/ppermute | solution.py:207
  6.5 18.1 %collective-permute-start.4 = (bf16[2,6,32,256]{3,2,1,0:T(8,128)(2,1)S(1)}, bf16[2,6,32,256]{3,2,1,0:T(8,128)(2,1)S(1)}, u32[]{:S(2)}, u32[]{:S(2)}) collective-permute-start(bf16[2,6,32,256]{3,2,1,0:T(8,128)(2,1)S(1)} %pad_maximum_fusion.3), channel_id=1, source_target_pairs={{0,4},{1,5},{2,6},{3,7},{4,0},{5,1},{6,2},{7,3},{8,12},{9,13},{10,... | collective-permute-start | bytes 589832 | tf_op jit(solution)/shard_map/ppermute | solution.py:165
  6.6 15.4 %collective-permute-start.2 = (bf16[2,3,32,256]{3,2,1,0:T(8,128)(2,1)S(1)}, bf16[2,3,32,256]{3,2,1,0:T(8,128)(2,1)S(1)}, u32[]{:S(2)}, u32[]{:S(2)}) collective-permute-start(bf16[2,3,32,256]{3,2,1,0:T(8,128)(2,1)S(1)} %collective-permute-done), channel_id=1, source_target_pairs={{0,16},{8,24},{16,0},{24,8},{1,17},{9,25},{17,1},{25,9},{2,18},{10... | collective-permute-start | bytes 294920 | tf_op jit(solution)/shard_map/ppermute | solution.py:165
  19.0 5.5 %collective-permute-start.3 = (bf16[2,3,32,256]{3,2,1,0:T(8,128)(2,1)S(1)}, bf16[2,3,32,256]{3,2,1,0:T(8,128)(2,1)S(1)}, u32[]{:S(2)}, u32[]{:S(2)}) collective-permute-start(bf16[2,3,32,256]{3,2,1,0:T(8,128)(2,1)S(1)} %collective-permute-done.1), channel_id=1, source_target_pairs={{0,16},{8,24},{16,0},{24,8},{1,17},{9,25},{17,1},{25,9},{2,18},{10... | collective-permute-start | bytes 294920 | tf_op jit(solution)/shard_map/ppermute | solution.py:165
  24.6 2.0 %copy-start = (bf16[6,1,3,1,256,256]{5,4,3,2,1,0:T(8,128)(2,1)S(1)}, bf16[6,1,3,1,256,256]{5,4,3,2,1,0:T(8,128)(2,1)}, u32[]{:S(2)}) copy-start(bf16[6,1,3,1,256,256]{5,4,3,2,1,0:T(8,128)(2,1)} %param.8) | copy-start | bytes 7077892
  24.7 1.8 %collective-permute-start.5 = (bf16[2,2,2,3,32,256]{5,4,3,2,1,0:T(8,128)(2,1)S(1)}, bf16[2,2,2,3,32,256]{5,4,3,2,1,0:T(8,128)(2,1)S(1)}, u32[]{:S(2)}, u32[]{:S(2)}) collective-permute-start(bf16[2,2,2,3,32,256]{5,4,3,2,1,0:T(8,128)(2,1)S(1)} %pad_maximum_fusion.1), channel_id=1, source_target_pairs={{0,8},{8,0},{16,24},{24,16},{1,9},{9,1},{17,25},{25,17},{2,10},{10... | collective-permute-start | bytes 1179656 | tf_op jit(solution)/shard_map/ppermute | solution.py:165
  26.5 5.1 %copy-start.5 = (bf16[256,256]{1,0:T(8,128)(2,1)S(1)}, bf16[256,256]{1,0:T(8,128)(2,1)}, u32[]{:S(2)}) copy-start(bf16[256,256]{1,0:T(8,128)(2,1)} %link.1) | copy-start | bytes 393220
  29.9 11.4 %collective-permute-start.8 = (bf16[4,2,3,32,256]{4,3,2,1,0:T(8,128)(2,1)S(1)}, bf16[4,2,3,32,256]{4,3,2,1,0:T(8,128)(2,1)S(1)}, u32[]{:S(2)}, u32[]{:S(2)}) collective-permute-start(bf16[4,2,3,32,256]{4,3,2,1,0:T(8,128)(2,1)S(1)} %get-tuple-element.51), channel_id=1, source_target_pairs={{0,2},{1,3},{2,0},{3,1},{4,6},{5,7},{6,4},{7,5},{8,10},{9,11},{10,... | collective-permute-start | bytes 1179656 | tf_op jit(solution)/shard_map/ppermute | solution.py:165
  30.5 11.4 %collective-permute-start.6 = (bf16[4,2,3,32,256]{4,3,2,1,0:T(8,128)(2,1)S(1)}, bf16[4,2,3,32,256]{4,3,2,1,0:T(8,128)(2,1)S(1)}, u32[]{:S(2)}, u32[]{:S(2)}) collective-permute-start(bf16[4,2,3,32,256]{4,3,2,1,0:T(8,128)(2,1)S(1)} %get-tuple-element.47), channel_id=1, source_target_pairs={{0,1},{1,0},{2,3},{3,2},{4,5},{5,4},{6,7},{7,6},{8,9},{9,8},{10,11... | collective-permute-start | bytes 1179656 | tf_op jit(solution)/shard_map/ppermute | solution.py:165
  41.5 6.4 %collective-permute-start.9 = (bf16[2,2,3,32,256]{4,3,2,1,0:T(8,128)(2,1)S(1)}, bf16[2,2,3,32,256]{4,3,2,1,0:T(8,128)(2,1)S(1)}, u32[]{:S(2)}, u32[]{:S(2)}) collective-permute-start(bf16[2,2,3,32,256]{4,3,2,1,0:T(8,128)(2,1)S(1)} %fusion.1), channel_id=1, source_target_pairs={{0,1},{1,0},{2,3},{3,2},{4,5},{5,4},{6,7},{7,6},{8,9},{9,8},{10,11... | collective-permute-start | bytes 589832 | tf_op jit(solution)/shard_map/ppermute | solution.py:165
  42.1 6.1 %collective-permute-start.7 = (bf16[2,2,3,32,256]{4,3,2,1,0:T(8,128)(2,1)S(1)}, bf16[2,2,3,32,256]{4,3,2,1,0:T(8,128)(2,1)S(1)}, u32[]{:S(2)}, u32[]{:S(2)}) collective-permute-start(bf16[2,2,3,32,256]{4,3,2,1,0:T(8,128)(2,1)S(1)} %fusion), channel_id=1, source_target_pairs={{0,2},{1,3},{2,0},{3,1},{4,6},{5,7},{6,4},{7,5},{8,10},{9,11},{10,... | collective-permute-start | bytes 589832 | tf_op jit(solution)/shard_map/ppermute | solution.py:165
  49.3 3.0 %collective-permute-start.10 = (f32[8,3,32,128]{3,2,1,0:T(8,128)S(1)}, f32[8,3,32,128]{3,2,1,0:T(8,128)S(1)}, u32[]{:S(2)}, u32[]{:S(2)}) collective-permute-start(f32[8,3,32,128]{3,2,1,0:T(8,128)S(1)} %dynamic-slice_bitcast_fusion), channel_id=1, source_target_pairs={{0,8},{8,0},{16,24},{24,16},{1,9},{9,1},{17,25},{25,17},{2,10},{10... | collective-permute-start | bytes 1179656 | tf_op jit(solution)/shard_map/ppermute | solution.py:165
  49.5 16.6 %collective-permute-start.17 = (bf16[2,1,2,3,32,256]{5,4,3,2,1,0:T(8,128)(2,1)S(1)}, bf16[2,1,2,3,32,256]{5,4,3,2,1,0:T(8,128)(2,1)S(1)}, u32[]{:S(2)}, u32[]{:S(2)}) collective-permute-start(bf16[2,1,2,3,32,256]{5,4,3,2,1,0:T(8,128)(2,1)S(1)} %pad_maximum_fusion.4), channel_id=1, source_target_pairs={{0,4},{1,5},{2,6},{3,7},{4,0},{5,1},{6,2},{7,3},{8,12},{9,13},{10,... | collective-permute-start | bytes 589832 | tf_op jit(solution)/shard_map/ppermute | solution.py:165
  52.5 5.7 %collective-permute-start.11 = (bf16[4,3,32,128]{3,2,1,0:T(8,128)(2,1)S(1)}, bf16[4,3,32,128]{3,2,1,0:T(8,128)(2,1)S(1)}, u32[]{:S(2)}, u32[]{:S(2)}) collective-permute-start(bf16[4,3,32,128]{3,2,1,0:T(8,128)(2,1)S(1)} %get-tuple-element.87), channel_id=1, source_target_pairs={{0,1},{1,0},{2,3},{3,2},{4,5},{5,4},{6,7},{7,6},{8,9},{9,8},{10,11... | collective-permute-start | bytes 294920 | tf_op jit(solution)/shard_map/ppermute | solution.py:165
  53.7 7.9 %collective-permute-start.13 = (bf16[4,3,32,128]{3,2,1,0:T(8,128)(2,1)S(1)}, bf16[4,3,32,128]{3,2,1,0:T(8,128)(2,1)S(1)}, u32[]{:S(2)}, u32[]{:S(2)}) collective-permute-start(bf16[4,3,32,128]{3,2,1,0:T(8,128)(2,1)S(1)} %get-tuple-element.87), channel_id=1, source_target_pairs={{0,17},{1,16},{2,19},{3,18},{4,21},{5,20},{6,23},{7,22},{8,25},{9,... | collective-permute-start | bytes 294920 | tf_op jit(solution)/shard_map/ppermute | solution.py:291
  55.2 6.4 %collective-permute-start.12 = (bf16[4,3,32,128]{3,2,1,0:T(8,128)(2,1)S(1)}, bf16[4,3,32,128]{3,2,1,0:T(8,128)(2,1)S(1)}, u32[]{:S(2)}, u32[]{:S(2)}) collective-permute-start(bf16[4,3,32,128]{3,2,1,0:T(8,128)(2,1)S(1)} %get-tuple-element.86), channel_id=1, source_target_pairs={{0,16},{8,24},{16,0},{24,8},{1,17},{9,25},{17,1},{25,9},{2,18},{10... | collective-permute-start | bytes 294920 | tf_op jit(solution)/shard_map/ppermute | solution.py:165
  61.7 4.5 %collective-permute-start.14 = (bf16[3,32,128]{2,1,0:T(8,128)(2,1)S(1)}, bf16[3,32,128]{2,1,0:T(8,128)(2,1)S(1)}, u32[]{:S(2)}, u32[]{:S(2)}) collective-permute-start(bf16[3,32,128]{2,1,0:T(8,128)(2,1)S(1)} %get-tuple-element.83), channel_id=1, source_target_pairs={{0,2},{1,3},{2,0},{3,1},{4,6},{5,7},{6,4},{7,5},{8,10},{9,11},{10,... | collective-permute-start | bytes 73736 | tf_op jit(solution)/shard_map/ppermute | solution.py:165
  63.2 5.3 %collective-permute-start.15 = (bf16[3,32,128]{2,1,0:T(8,128)(2,1)S(1)}, bf16[3,32,128]{2,1,0:T(8,128)(2,1)S(1)}, u32[]{:S(2)}, u32[]{:S(2)}) collective-permute-start(bf16[3,32,128]{2,1,0:T(8,128)(2,1)S(1)} %get-tuple-element.85), channel_id=1, source_target_pairs={{0,4},{1,5},{2,6},{3,7},{4,0},{5,1},{6,2},{7,3},{8,12},{9,13},{10,... | collective-permute-start | bytes 73736 | tf_op jit(solution)/shard_map/ppermute | solution.py:165
  64.6 5.6 %collective-permute-start.16 = (bf16[3,32,128]{2,1,0:T(8,128)(2,1)S(1)}, bf16[3,32,128]{2,1,0:T(8,128)(2,1)S(1)}, u32[]{:S(2)}, u32[]{:S(2)}) collective-permute-start(bf16[3,32,128]{2,1,0:T(8,128)(2,1)S(1)} %get-tuple-element.84), channel_id=1, source_target_pairs={{0,6},{1,7},{2,4},{3,5},{4,2},{5,3},{6,0},{7,1},{8,14},{9,15},{10,... | collective-permute-start | bytes 73736 | tf_op jit(solution)/shard_map/ppermute | solution.py:165
  70.2 1.9 %collective-permute-start.18 = (f32[3,32,128]{2,1,0:T(8,128)S(1)}, f32[3,32,128]{2,1,0:T(8,128)S(1)}, u32[]{:S(2)}, u32[]{:S(2)}) collective-permute-start(f32[3,32,128]{2,1,0:T(8,128)S(1)} %fusion.11), channel_id=1, source_target_pairs={{0,8},{8,0},{16,24},{24,16},{1,9},{9,1},{17,25},{25,17},{2,10},{10... | collective-permute-start | bytes 147464 | tf_op jit(solution)/shard_map/ppermute | solution.py:165

commit v3 on v1

--- a/solution.py
+++ b/solution.py
@@ -46,10 +46,6 @@
     return found == 1
 
 
-def slice_of(row, turn, n_row):
-    return turn * n_row + row
-
-
 def place_of(piece, n_row):
     return piece % n_row, piece // n_row
 
@@ -57,26 +53,22 @@
 def product_kernel(n_row, n_col, first_bits, struct1, struct2, inv1, inv2, stored, pieces, *rest):
     cycle = n_col // n_row
     keeps, sends = rest[:2], rest[2:4]
-    loose, factor = rest[4:]
+    (factor,) = rest[4:]
     row_blocks = stored.shape[0]
-    _, col_blocks, _, slab, width = loose.shape
+    _, _, _, col_blocks, slab, width = pieces.shape
+    packed = jnp.bfloat16 if slab % 16 == 0 else jnp.float32
     here_row, here_col = lax.axis_index("row"), lax.axis_index("col")
 
     group = here_col // n_row
-    for m in range(n_row):
-        row = here_row ^ m
-        for s in range(cycle):
-            slot = slice_of(row, lax.rem(s - group + cycle, cycle), n_row)
-            for p in range(2):
-                for b in range(col_blocks):
-                    loose[p, b, slot] = pieces[m, s, p, b].astype(loose.dtype)
+    places = [(row ^ here_row, lax.rem(turn + group, cycle)) for turn in range(cycle) for row in range(n_row)]
     for p, (struct, inverse) in enumerate(((struct1, inv1), (struct2, inv2))):
 
         def look(place, found):
             return tuple(f | (struct[place] == b * n_col + here_col).astype(jnp.int32) for b, f in enumerate(found))
 
         found = lax.fori_loop(0, struct.shape[0], look, (jnp.int32(0),) * col_blocks)
-        blocks = loose[p].reshape(col_blocks * width, width).astype(jnp.bfloat16)
+        slices = [pieces[m, s, p, b].astype(packed) for b in range(col_blocks) for m, s in places]
+        blocks = jnp.concatenate(slices, axis=0).astype(jnp.bfloat16)
         product = split_dot(blocks, inverse[...])
         for b in range(col_blocks):
             place = slice(b * width, (b + 1) * width)
@@ -190,7 +182,9 @@
     ways = [(way.astype(jnp.uint32), (1 - way).astype(jnp.uint32)) for way in ways]
     core = lax.axis_index("row") & 1
     cores = (core.astype(jnp.uint32), (1 - core).astype(jnp.uint32))
-    panels, picks, ways, cores = lax.optimization_barrier((panels, picks, ways, cores))
+    quads = [(here_col & 3) ^ m for m in range(4)]
+    quads = [quad.astype(jnp.uint32) for quad in quads]
+    panels, picks, ways, cores, quads = lax.optimization_barrier((panels, picks, ways, cores, quads))
 
     raw = lax.optimization_barrier(jnp.stack(panels))
     turns = raw.reshape(2, col_blocks, cycle, slab, width)
@@ -235,7 +229,6 @@
         in_specs=[SMEM, SMEM] + [VMEM] * 4,
         out_specs=[VMEM] * 4,
         scratch_shapes=[
-            pltpu.VMEM((2, col_blocks, n_col, slab, width), bf16 if slab % 16 == 0 else f32),
             pltpu.VMEM((col_blocks * width, 2 * width), bf16),
         ],
         compiler_params=big,
@@ -282,18 +275,15 @@
     )(rows, *totals, linked, consts)
     keep, send = halves(sums, 0, cores)
     sums = keep + swapped(send, "row", n_row, 1)
-    view = sums.reshape(-1, 2, 2, 3, slab, width // 2)
-
-    def part(high, low):
-        return halves(halves(view, 1, ways[1])[high], 1, ways[0])[low]
-
-    sums = part(0, 0)
-    for mask in (1, 2, 3):
-        sums = sums + swapped(part(mask >> 1, mask & 1).astype(bf16), "col", n_col, mask).astype(f32)
+    tail = (3, slab, width // 2)
+    parts = [lax.dynamic_index_in_dim(sums.reshape((-1, 4) + tail), quad, 1, keepdims=False) for quad in quads]
+    sums = parts[0]
+    for m in range(1, 4):
+        sums = sums + swapped(parts[m].astype(bf16), "col", n_col, m).astype(f32)
     for bit in range(2, n_bits - 1):
-        keep, send = halves(sums.reshape(-1, 2, 3, slab, width // 2), 1, ways[bit])
+        keep, send = halves(sums.reshape((-1, 2) + tail), 1, ways[bit])
         sums = keep + swapped(send.astype(bf16), "col", n_col, 1 << bit).astype(f32)
-    keep, send = (part.astype(bf16) for part in halves(sums.reshape(2, 3, slab, width // 2), 0, ways[n_bits - 1]))
+    keep, send = (part.astype(bf16) for part in halves(sums.reshape((2,) + tail), 0, ways[n_bits - 1]))
     across = [(r * n_col + c, (r ^ 2) * n_col + (c ^ (n_col // 2))) for r in range(n_row) for c in range(n_col)]
     near = keep.astype(f32) + swapped(send, "col", n_col, n_col // 2).astype(f32)
     far = swapped(keep, "row", n_row, 2).astype(f32) + lax.ppermute(send, ("row", "col"), across).astype(f32)

time: 72.8 us -> 71.7 us (0.985)
  other arithmetic: 2.66 us -> 1.73 us
    add x4, other arithmetic: 1.3 us -> 0.37 us  [body(): totals.append(keep + came.astype(f32))]
  transfers between devices with their start and end apart: 19 -> 19, of which waited for: 12 -> 11; matrix products, arithmetic and copies ran while one was open for 2% -> 1% of each run, Pallas kernels for 8% -> 8%
where the time goes in v3:
time: 71.7 us; the launch traced here: 71.5 us
  starting transfers between devices  32.7 us (46%)
  waiting for transfers between devices  25.4 us (35%)
  Pallas kernels  9.69 us (14%)
  other arithmetic  1.73 us (2%)
  between operations  1.01 us (1%)
  local copies, waits for them, and re-layouts  0.92 us (1%)
    ppermute x16, starting transfers between devices, swapped(): return lax.ppermute(value, axis, [(i, i ^ mask) for i in range(size)])  27.7 us
    ppermute x16, waiting for transfers between devices, swapped(): return lax.ppermute(value, axis, [(i, i ^ mask) for i in range(size)])  24.6 us
    ppermute x2, starting transfers between devices, body(): got.append(lax.ppermute(part, ('row', 'col'), moves))  4.77 us
    pallas_call x1, Pallas kernels, body(): pl.pallas_call(functools.partial(product_kernel, n_row, n_col, (orders[0]...  3.23 us
    pallas_call x1, Pallas kernels, body(): pl.pallas_call(prepare_kernel, out_shape=[shape((width, width), f32), sha...  2.18 us
    pallas_call x1, Pallas kernels, body(): pl.pallas_call(functools.partial(column_kernel, n_row), out_shape=[shape(...  1.78 us
    pallas_call x1, Pallas kernels, body(): pl.pallas_call(functools.partial(form_kernel, n_row), out_shape=shape(bas...  1.49 us
  transfers between devices with their start and end apart: 19, of which 11 were waited for; matrix products, arithmetic and copies ran while one was open for 1% of the time, Pallas kernels for 8%

profile of v3, /device:TPU:0, one launch (start us, length us, event | category | flops | bytes accessed | tf_op | source)
XLA Modules:
  0.0 71.5 jit_solution(2885776787833426266)
XLA Ops:
  0.7 1.0 %pad_maximum_fusion.3 = bf16[2,6,32,256]{3,2,1,0:T(8,128)(2,1)S(1)} fusion(bf16[1,6,32,256]{3,2,1,0:T(8,128)(2,1)} %bitcast.120, bf16[1,6,32,256]{3,2,1,0:T(8,128)(2,1)} %bitcast.121), kind=kLoop, calls=%fused_computation.13 | loop fusion | flops 98304 | bytes 393216 | tf_op jit(solution)/shard_map/stack | solution.py:189
  1.8 0.7 collective-permute-start
  2.4 4.1 %collective-permute-start.1 = (bf16[2,3,32,256]{3,2,1,0:T(8,128)(2,1)S(1)}, bf16[2,3,32,256]{3,2,1,0:T(8,128)(2,1)S(1)}, u32[]{:S(2)}, u32[]{:S(2)}) collective-permute-start(bf16[2,3,32,256]{3,2,1,0:T(8,128)(2,1)S(1)} %get-tuple-element.87), channel_id=1, source_target_pairs={{0,4},{1,12},{2,20},{3,28},{4,0},{5,8},{6,16},{7,24},{8,5},{9,13},... | collective-permute-start | bytes 294920 | tf_op jit(solution)/shard_map/ppermute | solution.py:199
  6.5 0.1 collective-permute-start.4
  6.6 0.0 collective-permute-done
  6.6 12.4 %collective-permute-start.2 = (bf16[2,3,32,256]{3,2,1,0:T(8,128)(2,1)S(1)}, bf16[2,3,32,256]{3,2,1,0:T(8,128)(2,1)S(1)}, u32[]{:S(2)}, u32[]{:S(2)}) collective-permute-start(bf16[2,3,32,256]{3,2,1,0:T(8,128)(2,1)S(1)} %collective-permute-done), channel_id=1, source_target_pairs={{0,16},{8,24},{16,0},{24,8},{1,17},{9,25},{17,1},{25,9},{2,18},{10... | collective-permute-start | bytes 294920 | tf_op jit(solution)/shard_map/ppermute | solution.py:157
  19.0 0.0 collective-permute-done.1
  19.0 0.0 collective-permute-start.3
  19.1 3.0 %collective-permute-done.2 = bf16[2,3,32,256]{3,2,1,0:T(8,128)(2,1)S(1)} collective-permute-done((bf16[2,3,32,256]{3,2,1,0:T(8,128)(2,1)S(1)}, bf16[2,3,32,256]{3,2,1,0:T(8,128)(2,1)S(1)}, u32[]{:S(2)}, u32[]{:S(2)}) %collective-permute-start.2) | collective-permute-done | bytes 98336 | tf_op jit(solution)/shard_map/ppermute | solution.py:157
  22.1 2.5 %collective-permute-done.3 = bf16[2,3,32,256]{3,2,1,0:T(8,128)(2,1)S(1)} collective-permute-done((bf16[2,3,32,256]{3,2,1,0:T(8,128)(2,1)S(1)}, bf16[2,3,32,256]{3,2,1,0:T(8,128)(2,1)S(1)}, u32[]{:S(2)}, u32[]{:S(2)}) %collective-permute-start.3) | collective-permute-done | bytes 98336 | tf_op jit(solution)/shard_map/ppermute | solution.py:157
  24.6 0.0 collective-permute-done.4
  24.7 0.1 collective-permute-start.5
  24.8 1.5 %form.1.rows = bf16[2,2,6,32,256]{4,3,2,1,0:T(8,128)(2,1)S(1)} custom-call(s32[18]{0:T(128)S(1)} %copy-done.3, s32[12]{0:T(128)S(1)} %copy-done.4, f32[256,256]{1,0:T(8,128)S(1)} %copy-done.1, f32[256,256]{1,0:T(8,128)S(1)} %copy-done.2, bf16[2,2,6,32,256]{4,3,2,1,0:T(8,128)(2,1)S(1)} %pad_maximum_fusion.2.base), custom_call_target="tpu_custom_call" | custom-call | flops 134217728 | bytes 262144 | tf_op jit(solution)/shard_map/form/pallas_call | solution.py:210
  26.3 0.2 collective-permute-done.5
  26.5 0.1 pad_maximum_fusion
  26.6 3.2 %products.1 = (f32[4,2,3,32,256]{4,3,2,1,0:T(8,128)S(1)}, f32[4,2,3,32,256]{4,3,2,1,0:T(8,128)S(1)}, bf16[4,2,3,32,256]{4,3,2,1,0:T(8,128)(2,1)S(1)}, bf16[4,2,3,32,256]{4,3,2,1,0:T(8,128)(2,1)S(1)}) custom-call(s32[18]{0:T(128)S(1)} %copy-done.3, s32[12]{0:T(128)S(1)} %copy-done.4, f32[256,256]{1,0:T(8,128)S(1)} %copy-done.1, f32[256,256]{1,0:T(8,128)S(1)} %copy-done.2, ...), custom_call_target="tpu_custom_call" | custom-call | tf_op jit(solution)/shard_map/products/pallas_call | solution.py:226
  29.8 0.6 collective-permute-start.8
  30.4 1.1 %collective-permute-start.6 = (bf16[4,2,3,32,256]{4,3,2,1,0:T(8,128)(2,1)S(1)}, bf16[4,2,3,32,256]{4,3,2,1,0:T(8,128)(2,1)S(1)}, u32[]{:S(2)}, u32[]{:S(2)}) collective-permute-start(bf16[4,2,3,32,256]{4,3,2,1,0:T(8,128)(2,1)S(1)} %get-tuple-element.47), channel_id=1, source_target_pairs={{0,1},{1,0},{2,3},{3,2},{4,5},{5,4},{6,7},{7,6},{8,9},{9,8},{10,11... | collective-permute-start | bytes 1179656 | tf_op jit(solution)/shard_map/ppermute | solution.py:157
  31.5 2.2 %prepare.1 = (f32[256,256]{1,0:T(8,128)S(1)}, f32[3,32,256]{2,1,0:T(8,128)S(1)}) custom-call(bf16[256,256]{1,0:T(8,128)(2,1)S(1)} %copy-done.5, f32[256,256]{1,0:T(8,128)S(1)} %copy-done.1, f32[256,256]{1,0:T(8,128)S(1)} %copy-done.2, f32[4,2,3,32,256]{4,3,2,1,0:T(8,128)S(1)} %get-tuple-element.46.after), custom_call_target="tpu_custom_call" | custom-call | flops 1006632960 | bytes 524288 | tf_op jit(solution)/shard_map/prepare/pallas_call | solution.py:238
  33.7 7.5 %collective-permute-done.8 = bf16[4,2,3,32,256]{4,3,2,1,0:T(8,128)(2,1)S(1)} collective-permute-done((bf16[4,2,3,32,256]{4,3,2,1,0:T(8,128)(2,1)S(1)}, bf16[4,2,3,32,256]{4,3,2,1,0:T(8,128)(2,1)S(1)}, u32[]{:S(2)}, u32[]{:S(2)}) %collective-permute-start.8) | collective-permute-done | bytes 393248 | tf_op jit(solution)/shard_map/ppermute | solution.py:157
  41.2 0.1 convert_add_fusion
  41.4 0.5 collective-permute-start.9
  41.9 0.0 collective-permute-done.6
  41.9 0.1 convert_add_fusion.1
  42.1 1.3 %collective-permute-start.7 = (bf16[2,2,3,32,256]{4,3,2,1,0:T(8,128)(2,1)S(1)}, bf16[2,2,3,32,256]{4,3,2,1,0:T(8,128)(2,1)S(1)}, u32[]{:S(2)}, u32[]{:S(2)}) collective-permute-start(bf16[2,2,3,32,256]{4,3,2,1,0:T(8,128)(2,1)S(1)} %fusion), channel_id=1, source_target_pairs={{0,2},{1,3},{2,0},{3,1},{4,6},{5,7},{6,4},{7,5},{8,10},{9,11},{10,... | collective-permute-start | bytes 589832 | tf_op jit(solution)/shard_map/ppermute | solution.py:157
  43.3 4.5 %collective-permute-done.9 = bf16[2,2,3,32,256]{4,3,2,1,0:T(8,128)(2,1)S(1)} collective-permute-done((bf16[2,2,3,32,256]{4,3,2,1,0:T(8,128)(2,1)S(1)}, bf16[2,2,3,32,256]{4,3,2,1,0:T(8,128)(2,1)S(1)}, u32[]{:S(2)}, u32[]{:S(2)}) %collective-permute-start.9) | collective-permute-done | bytes 196640 | tf_op jit(solution)/shard_map/ppermute | solution.py:157
  47.8 0.3 collective-permute-done.7
  48.2 1.0 %sums.1 = f32[2,8,3,32,128]{4,3,2,1,0:T(8,128)S(1)} custom-call(bf16[2,2,6,32,256]{4,3,2,1,0:T(8,128)(2,1)S(1)} %form.1.rows, f32[2,2,3,32,256]{4,3,2,1,0:T(8,128)S(1)} %bitcast_add_fusion.2.total_low, f32[2,2,3,32,256]{4,3,2,1,0:T(8,128)S(1)} %bitcast_add_fusion.1.total_high, f32[256,256]{1,0:T(8,128)S(1)} %get-tuple-element.54.linked, ...), custom_call_target="tpu_custom_call" | custom-call | tf_op jit(solution)/shard_map/sums/pallas_call | solution.py:268
  49.3 0.1 collective-permute-start.10
  49.5 1.6 %collective-permute-done.10 = f32[8,3,32,128]{3,2,1,0:T(8,128)S(1)} collective-permute-done((f32[8,3,32,128]{3,2,1,0:T(8,128)S(1)}, f32[8,3,32,128]{3,2,1,0:T(8,128)S(1)}, u32[]{:S(2)}, u32[]{:S(2)}) %collective-permute-start.10) | collective-permute-done | bytes 393248 | tf_op jit(solution)/shard_map/ppermute | solution.py:157
  51.1 0.1 bitcast_add_fusion
  51.2 1.7 %collective-permute-start.11 = (bf16[2,3,32,128]{3,2,1,0:T(8,128)(2,1)S(1)}, bf16[2,3,32,128]{3,2,1,0:T(8,128)(2,1)S(1)}, u32[]{:S(2)}, u32[]{:S(2)}) collective-permute-start(bf16[2,3,32,128]{3,2,1,0:T(8,128)(2,1)S(1)} %get-tuple-element.81), channel_id=1, source_target_pairs={{0,1},{1,0},{2,3},{3,2},{4,5},{5,4},{6,7},{7,6},{8,9},{9,8},{10,11... | collective-permute-start | bytes 147464 | tf_op jit(solution)/shard_map/ppermute | solution.py:157
  52.9 0.5 collective-permute-start.12
  53.4 1.3 %collective-permute-start.13 = (bf16[2,3,32,128]{3,2,1,0:T(8,128)(2,1)S(1)}, bf16[2,3,32,128]{3,2,1,0:T(8,128)(2,1)S(1)}, u32[]{:S(2)}, u32[]{:S(2)}) collective-permute-start(bf16[2,3,32,128]{3,2,1,0:T(8,128)(2,1)S(1)} %get-tuple-element.82), channel_id=1, source_target_pairs={{0,3},{1,2},{2,1},{3,0},{4,7},{5,6},{6,5},{7,4},{8,11},{9,10},{10,... | collective-permute-start | bytes 147464 | tf_op jit(solution)/shard_map/ppermute | solution.py:157
  54.7 2.8 %collective-permute-start.17 = (bf16[2,1,2,3,32,256]{5,4,3,2,1,0:T(8,128)(2,1)S(1)}, bf16[2,1,2,3,32,256]{5,4,3,2,1,0:T(8,128)(2,1)S(1)}, u32[]{:S(2)}, u32[]{:S(2)}) collective-permute-start(bf16[2,1,2,3,32,256]{5,4,3,2,1,0:T(8,128)(2,1)S(1)} %pad_maximum_fusion.4), channel_id=1, source_target_pairs={{0,4},{1,5},{2,6},{3,7},{4,0},{5,1},{6,2},{7,3},{8,12},{9,13},{10,... | collective-permute-start | bytes 589832 | tf_op jit(solution)/shard_map/ppermute | solution.py:157
  57.6 0.0 collective-permute-done.11
  57.6 0.0 collective-permute-done.12
  57.6 0.8 %collective-permute-done.13 = bf16[2,3,32,128]{3,2,1,0:T(8,128)(2,1)S(1)} collective-permute-done((bf16[2,3,32,128]{3,2,1,0:T(8,128)(2,1)S(1)}, bf16[2,3,32,128]{3,2,1,0:T(8,128)(2,1)S(1)}, u32[]{:S(2)}, u32[]{:S(2)}) %collective-permute-start.13) | collective-permute-done | bytes 49184 | tf_op jit(solution)/shard_map/ppermute | solution.py:157
  58.4 3.8 %collective-permute-start.14 = (bf16[3,32,128]{2,1,0:T(8,128)(2,1)S(1)}, bf16[3,32,128]{2,1,0:T(8,128)(2,1)S(1)}, u32[]{:S(2)}, u32[]{:S(2)}) collective-permute-start(bf16[3,32,128]{2,1,0:T(8,128)(2,1)S(1)} %get-tuple-element.94), channel_id=1, source_target_pairs={{0,4},{1,5},{2,6},{3,7},{4,0},{5,1},{6,2},{7,3},{8,12},{9,13},{10,... | collective-permute-start | bytes 73736 | tf_op jit(solution)/shard_map/ppermute | solution.py:157
  62.3 0.2 collective-permute-start.16
  62.5 1.3 %collective-permute-start.15 = (bf16[3,32,128]{2,1,0:T(8,128)(2,1)S(1)}, bf16[3,32,128]{2,1,0:T(8,128)(2,1)S(1)}, u32[]{:S(2)}, u32[]{:S(2)}) collective-permute-start(bf16[3,32,128]{2,1,0:T(8,128)(2,1)S(1)} %get-tuple-element.93), channel_id=1, source_target_pairs={{0,16},{8,24},{16,0},{24,8},{1,17},{9,25},{17,1},{25,9},{2,18},{10... | collective-permute-start | bytes 73736 | tf_op jit(solution)/shard_map/ppermute | solution.py:157
  63.8 4.0 %collective-permute-done.17 = bf16[2,1,2,3,32,256]{5,4,3,2,1,0:T(8,128)(2,1)S(1)} collective-permute-done((bf16[2,1,2,3,32,256]{5,4,3,2,1,0:T(8,128)(2,1)S(1)}, bf16[2,1,2,3,32,256]{5,4,3,2,1,0:T(8,128)(2,1)S(1)}, u32[]{:S(2)}, u32[]{:S(2)}) %collective-permute-start.17) | collective-permute-done | bytes 196640 | tf_op jit(solution)/shard_map/ppermute | solution.py:157
  67.8 0.2 collective-permute-done.14
  68.1 0.9 %collective-permute-done.16 = bf16[3,32,128]{2,1,0:T(8,128)(2,1)S(1)} collective-permute-done((bf16[3,32,128]{2,1,0:T(8,128)(2,1)S(1)}, bf16[3,32,128]{2,1,0:T(8,128)(2,1)S(1)}, u32[]{:S(2)}, u32[]{:S(2)}) %collective-permute-start.16) | collective-permute-done | bytes 24608 | tf_op jit(solution)/shard_map/ppermute | solution.py:289
  68.9 0.1 collective-permute-start.18
  69.0 1.8 %columns.1 = (f32[6,32,256]{2,1,0:T(8,128)}, f32[6,32,256]{2,1,0:T(8,128)}) custom-call(s32[18]{0:T(128)S(1)} %copy-done.3, s32[12]{0:T(128)S(1)} %copy-done.4, f32[2,3,32,256]{3,2,1,0:T(8,128)S(1)} %bitcast.105, bf16[2,3,32,256]{3,2,1,0:T(8,128)(2,1)S(1)} %bitcast.107, f32[2,3,32,256]{3,2,1,0:T(8,128)S(1)} %bitcast.104, ...), custom_call_target="tpu_custom_call" | custom-call | tf_op jit(solution)/shard_map/columns/pallas_call | solution.py:295
  70.8 0.0 collective-permute-done.18
  70.8 0.6 slice_bitcast_fusion.2
  (35 shorter events, 0.6 us)
Async XLA Ops:
  0.6 24.1 %copy-start.1 = (f32[256,256]{1,0:T(8,128)S(1)}, f32[256,256]{1,0:T(8,128)}, u32[]{:S(2)}) copy-start(f32[256,256]{1,0:T(8,128)} %inv1.5) | copy-start | bytes 786436
  0.6 24.1 %copy-start.2 = (f32[256,256]{1,0:T(8,128)S(1)}, f32[256,256]{1,0:T(8,128)}, u32[]{:S(2)}) copy-start(f32[256,256]{1,0:T(8,128)} %inv2.5) | copy-start | bytes 786436
  0.7 24.1 %copy-start.3 = (s32[18]{0:T(128)S(1)}, s32[18]{0:T(128)}, u32[]{:S(2)}) copy-start(s32[18]{0:T(128)} %struct1.5) | copy-start | bytes 220
  0.7 24.1 %copy-start.4 = (s32[12]{0:T(128)S(1)}, s32[12]{0:T(128)}, u32[]{:S(2)}) copy-start(s32[12]{0:T(128)} %struct2.5) | copy-start | bytes 148
  1.8 4.9 %collective-permute-start = (bf16[2,3,32,256]{3,2,1,0:T(8,128)(2,1)S(1)}, bf16[2,3,32,256]{3,2,1,0:T(8,128)(2,1)S(1)}, u32[]{:S(2)}, u32[]{:S(2)}) collective-permute-start(bf16[2,3,32,256]{3,2,1,0:T(8,128)(2,1)S(1)} %get-tuple-element.86), channel_id=1, source_target_pairs={{0,0},{1,8},{2,16},{3,24},{4,4},{5,12},{6,20},{7,28},{8,1},{9,9},{... | collective-permute-start | bytes 294920 | tf_op jit(solution)/shard_map/ppermute | solution.py:199
  2.4 16.6 %collective-permute-start.1 = (bf16[2,3,32,256]{3,2,1,0:T(8,128)(2,1)S(1)}, bf16[2,3,32,256]{3,2,1,0:T(8,128)(2,1)S(1)}, u32[]{:S(2)}, u32[]{:S(2)}) collective-permute-start(bf16[2,3,32,256]{3,2,1,0:T(8,128)(2,1)S(1)} %get-tuple-element.87), channel_id=1, source_target_pairs={{0,4},{1,12},{2,20},{3,28},{4,0},{5,8},{6,16},{7,24},{8,5},{9,13},... | collective-permute-start | bytes 294920 | tf_op jit(solution)/shard_map/ppermute | solution.py:199
  6.5 18.1 %collective-permute-start.4 = (bf16[2,6,32,256]{3,2,1,0:T(8,128)(2,1)S(1)}, bf16[2,6,32,256]{3,2,1,0:T(8,128)(2,1)S(1)}, u32[]{:S(2)}, u32[]{:S(2)}) collective-permute-start(bf16[2,6,32,256]{3,2,1,0:T(8,128)(2,1)S(1)} %pad_maximum_fusion.3), channel_id=1, source_target_pairs={{0,4},{1,5},{2,6},{3,7},{4,0},{5,1},{6,2},{7,3},{8,12},{9,13},{10,... | collective-permute-start | bytes 589832 | tf_op jit(solution)/shard_map/ppermute | solution.py:157
  6.6 15.4 %collective-permute-start.2 = (bf16[2,3,32,256]{3,2,1,0:T(8,128)(2,1)S(1)}, bf16[2,3,32,256]{3,2,1,0:T(8,128)(2,1)S(1)}, u32[]{:S(2)}, u32[]{:S(2)}) collective-permute-start(bf16[2,3,32,256]{3,2,1,0:T(8,128)(2,1)S(1)} %collective-permute-done), channel_id=1, source_target_pairs={{0,16},{8,24},{16,0},{24,8},{1,17},{9,25},{17,1},{25,9},{2,18},{10... | collective-permute-start | bytes 294920 | tf_op jit(solution)/shard_map/ppermute | solution.py:157
  19.0 5.5 %collective-permute-start.3 = (bf16[2,3,32,256]{3,2,1,0:T(8,128)(2,1)S(1)}, bf16[2,3,32,256]{3,2,1,0:T(8,128)(2,1)S(1)}, u32[]{:S(2)}, u32[]{:S(2)}) collective-permute-start(bf16[2,3,32,256]{3,2,1,0:T(8,128)(2,1)S(1)} %collective-permute-done.1), channel_id=1, source_target_pairs={{0,16},{8,24},{16,0},{24,8},{1,17},{9,25},{17,1},{25,9},{2,18},{10... | collective-permute-start | bytes 294920 | tf_op jit(solution)/shard_map/ppermute | solution.py:157
  24.6 2.0 %copy-start = (bf16[6,1,3,1,256,256]{5,4,3,2,1,0:T(8,128)(2,1)S(1)}, bf16[6,1,3,1,256,256]{5,4,3,2,1,0:T(8,128)(2,1)}, u32[]{:S(2)}) copy-start(bf16[6,1,3,1,256,256]{5,4,3,2,1,0:T(8,128)(2,1)} %param.8) | copy-start | bytes 7077892
  24.7 1.8 %collective-permute-start.5 = (bf16[2,2,2,3,32,256]{5,4,3,2,1,0:T(8,128)(2,1)S(1)}, bf16[2,2,2,3,32,256]{5,4,3,2,1,0:T(8,128)(2,1)S(1)}, u32[]{:S(2)}, u32[]{:S(2)}) collective-permute-start(bf16[2,2,2,3,32,256]{5,4,3,2,1,0:T(8,128)(2,1)S(1)} %pad_maximum_fusion.1), channel_id=1, source_target_pairs={{0,8},{8,0},{16,24},{24,16},{1,9},{9,1},{17,25},{25,17},{2,10},{10... | collective-permute-start | bytes 1179656 | tf_op jit(solution)/shard_map/ppermute | solution.py:157
  26.5 5.0 %copy-start.5 = (bf16[256,256]{1,0:T(8,128)(2,1)S(1)}, bf16[256,256]{1,0:T(8,128)(2,1)}, u32[]{:S(2)}) copy-start(bf16[256,256]{1,0:T(8,128)(2,1)} %link.1) | copy-start | bytes 393220
  29.8 11.4 %collective-permute-start.8 = (bf16[4,2,3,32,256]{4,3,2,1,0:T(8,128)(2,1)S(1)}, bf16[4,2,3,32,256]{4,3,2,1,0:T(8,128)(2,1)S(1)}, u32[]{:S(2)}, u32[]{:S(2)}) collective-permute-start(bf16[4,2,3,32,256]{4,3,2,1,0:T(8,128)(2,1)S(1)} %get-tuple-element.51), channel_id=1, source_target_pairs={{0,2},{1,3},{2,0},{3,1},{4,6},{5,7},{6,4},{7,5},{8,10},{9,11},{10,... | collective-permute-start | bytes 1179656 | tf_op jit(solution)/shard_map/ppermute | solution.py:157
  30.4 11.4 %collective-permute-start.6 = (bf16[4,2,3,32,256]{4,3,2,1,0:T(8,128)(2,1)S(1)}, bf16[4,2,3,32,256]{4,3,2,1,0:T(8,128)(2,1)S(1)}, u32[]{:S(2)}, u32[]{:S(2)}) collective-permute-start(bf16[4,2,3,32,256]{4,3,2,1,0:T(8,128)(2,1)S(1)} %get-tuple-element.47), channel_id=1, source_target_pairs={{0,1},{1,0},{2,3},{3,2},{4,5},{5,4},{6,7},{7,6},{8,9},{9,8},{10,11... | collective-permute-start | bytes 1179656 | tf_op jit(solution)/shard_map/ppermute | solution.py:157
  41.4 6.4 %collective-permute-start.9 = (bf16[2,2,3,32,256]{4,3,2,1,0:T(8,128)(2,1)S(1)}, bf16[2,2,3,32,256]{4,3,2,1,0:T(8,128)(2,1)S(1)}, u32[]{:S(2)}, u32[]{:S(2)}) collective-permute-start(bf16[2,2,3,32,256]{4,3,2,1,0:T(8,128)(2,1)S(1)} %fusion.1), channel_id=1, source_target_pairs={{0,1},{1,0},{2,3},{3,2},{4,5},{5,4},{6,7},{7,6},{8,9},{9,8},{10,11... | collective-permute-start | bytes 589832 | tf_op jit(solution)/shard_map/ppermute | solution.py:157
  42.1 6.1 %collective-permute-start.7 = (bf16[2,2,3,32,256]{4,3,2,1,0:T(8,128)(2,1)S(1)}, bf16[2,2,3,32,256]{4,3,2,1,0:T(8,128)(2,1)S(1)}, u32[]{:S(2)}, u32[]{:S(2)}) collective-permute-start(bf16[2,2,3,32,256]{4,3,2,1,0:T(8,128)(2,1)S(1)} %fusion), channel_id=1, source_target_pairs={{0,2},{1,3},{2,0},{3,1},{4,6},{5,7},{6,4},{7,5},{8,10},{9,11},{10,... | collective-permute-start | bytes 589832 | tf_op jit(solution)/shard_map/ppermute | solution.py:157
  49.3 1.8 %collective-permute-start.10 = (f32[8,3,32,128]{3,2,1,0:T(8,128)S(1)}, f32[8,3,32,128]{3,2,1,0:T(8,128)S(1)}, u32[]{:S(2)}, u32[]{:S(2)}) collective-permute-start(f32[8,3,32,128]{3,2,1,0:T(8,128)S(1)} %dynamic-slice_bitcast_fusion), channel_id=1, source_target_pairs={{0,8},{8,0},{16,24},{24,16},{1,9},{9,1},{17,25},{25,17},{2,10},{10... | collective-permute-start | bytes 1179656 | tf_op jit(solution)/shard_map/ppermute | solution.py:157
  51.2 6.4 %collective-permute-start.11 = (bf16[2,3,32,128]{3,2,1,0:T(8,128)(2,1)S(1)}, bf16[2,3,32,128]{3,2,1,0:T(8,128)(2,1)S(1)}, u32[]{:S(2)}, u32[]{:S(2)}) collective-permute-start(bf16[2,3,32,128]{3,2,1,0:T(8,128)(2,1)S(1)} %get-tuple-element.81), channel_id=1, source_target_pairs={{0,1},{1,0},{2,3},{3,2},{4,5},{5,4},{6,7},{7,6},{8,9},{9,8},{10,11... | collective-permute-start | bytes 147464 | tf_op jit(solution)/shard_map/ppermute | solution.py:157
  52.9 4.7 %collective-permute-start.12 = (bf16[2,3,32,128]{3,2,1,0:T(8,128)(2,1)S(1)}, bf16[2,3,32,128]{3,2,1,0:T(8,128)(2,1)S(1)}, u32[]{:S(2)}, u32[]{:S(2)}) collective-permute-start(bf16[2,3,32,128]{3,2,1,0:T(8,128)(2,1)S(1)} %get-tuple-element.83), channel_id=1, source_target_pairs={{0,2},{1,3},{2,0},{3,1},{4,6},{5,7},{6,4},{7,5},{8,10},{9,11},{10,... | collective-permute-start | bytes 147464 | tf_op jit(solution)/shard_map/ppermute | solution.py:157
  53.4 5.0 %collective-permute-start.13 = (bf16[2,3,32,128]{3,2,1,0:T(8,128)(2,1)S(1)}, bf16[2,3,32,128]{3,2,1,0:T(8,128)(2,1)S(1)}, u32[]{:S(2)}, u32[]{:S(2)}) collective-permute-start(bf16[2,3,32,128]{3,2,1,0:T(8,128)(2,1)S(1)} %get-tuple-element.82), channel_id=1, source_target_pairs={{0,3},{1,2},{2,1},{3,0},{4,7},{5,6},{6,5},{7,4},{8,11},{9,10},{10,... | collective-permute-start | bytes 147464 | tf_op jit(solution)/shard_map/ppermute | solution.py:157
  54.7 13.0 %collective-permute-start.17 = (bf16[2,1,2,3,32,256]{5,4,3,2,1,0:T(8,128)(2,1)S(1)}, bf16[2,1,2,3,32,256]{5,4,3,2,1,0:T(8,128)(2,1)S(1)}, u32[]{:S(2)}, u32[]{:S(2)}) collective-permute-start(bf16[2,1,2,3,32,256]{5,4,3,2,1,0:T(8,128)(2,1)S(1)} %pad_maximum_fusion.4), channel_id=1, source_target_pairs={{0,4},{1,5},{2,6},{3,7},{4,0},{5,1},{6,2},{7,3},{8,12},{9,13},{10,... | collective-permute-start | bytes 589832 | tf_op jit(solution)/shard_map/ppermute | solution.py:157
  58.4 9.6 %collective-permute-start.14 = (bf16[3,32,128]{2,1,0:T(8,128)(2,1)S(1)}, bf16[3,32,128]{2,1,0:T(8,128)(2,1)S(1)}, u32[]{:S(2)}, u32[]{:S(2)}) collective-permute-start(bf16[3,32,128]{2,1,0:T(8,128)(2,1)S(1)} %get-tuple-element.94), channel_id=1, source_target_pairs={{0,4},{1,5},{2,6},{3,7},{4,0},{5,1},{6,2},{7,3},{8,12},{9,13},{10,... | collective-permute-start | bytes 73736 | tf_op jit(solution)/shard_map/ppermute | solution.py:157
  62.3 6.6 %collective-permute-start.16 = (bf16[3,32,128]{2,1,0:T(8,128)(2,1)S(1)}, bf16[3,32,128]{2,1,0:T(8,128)(2,1)S(1)}, u32[]{:S(2)}, u32[]{:S(2)}) collective-permute-start(bf16[3,32,128]{2,1,0:T(8,128)(2,1)S(1)} %get-tuple-element.94), channel_id=1, source_target_pairs={{0,20},{1,21},{2,22},{3,23},{4,16},{5,17},{6,18},{7,19},{8,28},{9,... | collective-permute-start | bytes 73736 | tf_op jit(solution)/shard_map/ppermute | solution.py:289
  62.5 5.6 %collective-permute-start.15 = (bf16[3,32,128]{2,1,0:T(8,128)(2,1)S(1)}, bf16[3,32,128]{2,1,0:T(8,128)(2,1)S(1)}, u32[]{:S(2)}, u32[]{:S(2)}) collective-permute-start(bf16[3,32,128]{2,1,0:T(8,128)(2,1)S(1)} %get-tuple-element.93), channel_id=1, source_target_pairs={{0,16},{8,24},{16,0},{24,8},{1,17},{9,25},{17,1},{25,9},{2,18},{10... | collective-permute-start | bytes 73736 | tf_op jit(solution)/shard_map/ppermute | solution.py:157
  68.9 1.9 %collective-permute-start.18 = (f32[3,32,128]{2,1,0:T(8,128)S(1)}, f32[3,32,128]{2,1,0:T(8,128)S(1)}, u32[]{:S(2)}, u32[]{:S(2)}) collective-permute-start(f32[3,32,128]{2,1,0:T(8,128)S(1)} %add_add_fusion), channel_id=1, source_target_pairs={{0,8},{8,0},{16,24},{24,16},{1,9},{9,1},{17,25},{25,17},{2,10},{10... | collective-permute-start | bytes 147464 | tf_op jit(solution)/shard_map/ppermute | solution.py:157

commit v4 on v3

--- a/solution.py
+++ b/solution.py
@@ -107,7 +107,7 @@
     out[...] = whole[:, place, :]
 
 
-def form_kernel(n_row, struct1, struct2, inv1, inv2, base, rows):
+def form_kernel(n_row, struct1, struct2, inv1, inv2, base, after, rows):
     slices, _, blocks, slab, width = base.shape
     for p, (struct, inverse) in enumerate(((struct1, inv1), (struct2, inv2))):
         keep = listed(struct, blocks, n_row)
@@ -206,17 +206,7 @@
             pieces[m ^ bit] = [swapped(part, "row", n_row, bit) for part in parts]
         bit //= 2
     pieces = jnp.stack([jnp.stack(pieces[m]) for m in sorted(pieces)])
-    pieces, base = lax.optimization_barrier((pieces, base))
-    rows = pl.pallas_call(
-        functools.partial(form_kernel, n_row),
-        out_shape=shape(base.shape, bf16),
-        in_specs=[SMEM, SMEM] + [VMEM] * 3,
-        out_specs=VMEM,
-        compiler_params=big,
-        name="form",
-        cost_estimate=pl.CostEstimate(flops=8 * width**3, bytes_accessed=4 * width**2, transcendentals=0),
-    )(struct_first, struct_second, inv_first, inv_second, base)
-    beside, rows = lax.optimization_barrier((swapped(pieces, "row", n_row, 1), rows))
+    beside = swapped(pieces, "row", n_row, 1)
     pieces = jnp.stack([pieces, beside], axis=1).reshape((n_row,) + pieces.shape[1:])
 
     orders = (list(range(n_bits)), [1, 0] + list(range(2, n_bits)))
@@ -235,6 +225,15 @@
         name="products",
     )(struct_first, struct_second, inv_first, inv_second, stored, pieces)
 
+    rows = pl.pallas_call(
+        functools.partial(form_kernel, n_row),
+        out_shape=shape(base.shape, bf16),
+        in_specs=[SMEM, SMEM] + [VMEM] * 3 + [ANY],
+        out_specs=VMEM,
+        compiler_params=big,
+        name="form",
+        cost_estimate=pl.CostEstimate(flops=100 * width**3, bytes_accessed=4 * width**2, transcendentals=0),
+    )(struct_first, struct_second, inv_first, inv_second, base, split[0])
     linked, consts = pl.pallas_call(
         prepare_kernel,
         out_shape=[shape((width, width), f32), shape((3, slab, width), f32)],
@@ -243,10 +242,11 @@
         scratch_shapes=[pltpu.VMEM((3, width, width), f32)],
         compiler_params=big,
         name="prepare",
-        cost_estimate=pl.CostEstimate(flops=6 * 10 * width**3, bytes_accessed=8 * width**2, transcendentals=0),
-    )(panel_link, inv_first, inv_second, split[0])
+        cost_estimate=pl.CostEstimate(flops=60 * width**3, bytes_accessed=8 * width**2, transcendentals=0),
+    )(panel_link, inv_first, inv_second, rows)
 
     state = [(split[g], swapped(split[2 + g], "col", n_col, 1 << orders[g][0])) for g in range(2)]
+    state = lax.optimization_barrier(state)
     left = [sorted(set(range(n_bits)) - {order[0]}) for order in orders]
     for i in range(1, n_bits):
         totals, last = [], []

time: 71.7 us -> 76 us (1.060)
  starting transfers between devices: 32.7 us -> 35.7 us
  waiting for transfers between devices: 25.4 us -> 26.6 us
    ppermute x16, starting transfers between devices: 27.7 us -> 29.7 us  [swapped(): return lax.ppermute(value, axis, [(i, i ^ mask) for i in range(size)])]
    ppermute x1, starting transfers between devices: 0.21 us -> 1.26 us  [body(): lax.ppermute(send, ('row', 'col'), across).astype(f32)]
    ppermute x1, waiting for transfers between devices: 0.86 us -> 1.72 us  [body(): lax.ppermute(send, ('row', 'col'), across).astype(f32)]
  transfers between devices with their start and end apart: 19 -> 19, of which waited for: 11 -> 11; matrix products, arithmetic and copies ran while one was open for 1% -> 0% of each run, Pallas kernels for 8% -> 11%
where the time goes in v4:
time: 76 us; the launch traced here: 75.8 us
  starting transfers between devices  35.7 us (47%)
  waiting for transfers between devices  26.6 us (35%)
  Pallas kernels  9.69 us (13%)
  other arithmetic  1.9 us (2%)
  between operations  1.02 us (1%)
  local copies, waits for them, and re-layouts  0.92 us (1%)
    ppermute x16, starting transfers between devices, swapped(): return lax.ppermute(value, axis, [(i, i ^ mask) for i in range(size)])  29.7 us
    ppermute x16, waiting for transfers between devices, swapped(): return lax.ppermute(value, axis, [(i, i ^ mask) for i in range(size)])  24.9 us
    ppermute x2, starting transfers between devices, body(): got.append(lax.ppermute(part, ('row', 'col'), moves))  4.77 us
    pallas_call x1, Pallas kernels, body(): pl.pallas_call(functools.partial(product_kernel, n_row, n_col, (orders[0]...  3.23 us
    pallas_call x1, Pallas kernels, body(): pl.pallas_call(prepare_kernel, out_shape=[shape((width, width), f32), sha...  2.18 us
    pallas_call x1, Pallas kernels, body(): pl.pallas_call(functools.partial(column_kernel, n_row), out_shape=[shape(...  1.78 us
    ppermute x1, waiting for transfers between devices, body(): lax.ppermute(send, ('row', 'col'), across).astype(f32)  1.72 us
  transfers between devices with their start and end apart: 19, of which 11 were waited for; matrix products, arithmetic and copies ran while one was open for 0% of the time, Pallas kernels for 11%

profile of v4, /device:TPU:0, one launch (start us, length us, event | category | flops | bytes accessed | tf_op | source)
XLA Modules:
  0.0 75.8 jit_solution(15852584603635065898)
XLA Ops:
  0.7 1.1 %pad_maximum_fusion.3 = bf16[2,6,32,256]{3,2,1,0:T(8,128)(2,1)S(1)} fusion(bf16[1,6,32,256]{3,2,1,0:T(8,128)(2,1)} %bitcast.120, bf16[1,6,32,256]{3,2,1,0:T(8,128)(2,1)} %bitcast.121), kind=kLoop, calls=%fused_computation.13 | loop fusion | flops 98304 | bytes 393216 | tf_op jit(solution)/shard_map/stack | solution.py:189
  1.9 0.7 collective-permute-start.1
  2.6 4.1 %collective-permute-start.2 = (bf16[2,3,32,256]{3,2,1,0:T(8,128)(2,1)S(1)}, bf16[2,3,32,256]{3,2,1,0:T(8,128)(2,1)S(1)}, u32[]{:S(2)}, u32[]{:S(2)}) collective-permute-start(bf16[2,3,32,256]{3,2,1,0:T(8,128)(2,1)S(1)} %get-tuple-element.89), channel_id=1, source_target_pairs={{0,4},{1,12},{2,20},{3,28},{4,0},{5,8},{6,16},{7,24},{8,5},{9,13},... | collective-permute-start | bytes 294920 | tf_op jit(solution)/shard_map/ppermute | solution.py:199
  6.7 0.0 collective-permute-done.1
  6.7 7.4 %collective-permute-start.3 = (bf16[2,3,32,256]{3,2,1,0:T(8,128)(2,1)S(1)}, bf16[2,3,32,256]{3,2,1,0:T(8,128)(2,1)S(1)}, u32[]{:S(2)}, u32[]{:S(2)}) collective-permute-start(bf16[2,3,32,256]{3,2,1,0:T(8,128)(2,1)S(1)} %collective-permute-done.1), channel_id=1, source_target_pairs={{0,16},{8,24},{16,0},{24,8},{1,17},{9,25},{17,1},{25,9},{2,18},{10... | collective-permute-start | bytes 294920 | tf_op jit(solution)/shard_map/ppermute | solution.py:157
  14.1 0.0 collective-permute-done.2
  14.1 3.7 %collective-permute-start.4 = (bf16[2,3,32,256]{3,2,1,0:T(8,128)(2,1)S(1)}, bf16[2,3,32,256]{3,2,1,0:T(8,128)(2,1)S(1)}, u32[]{:S(2)}, u32[]{:S(2)}) collective-permute-start(bf16[2,3,32,256]{3,2,1,0:T(8,128)(2,1)S(1)} %collective-permute-done.2), channel_id=1, source_target_pairs={{0,16},{8,24},{16,0},{24,8},{1,17},{9,25},{17,1},{25,9},{2,18},{10... | collective-permute-start | bytes 294920 | tf_op jit(solution)/shard_map/ppermute | solution.py:157
  17.8 0.0 collective-permute-done.3
  17.8 2.8 %collective-permute-done.4 = bf16[2,3,32,256]{3,2,1,0:T(8,128)(2,1)S(1)} collective-permute-done((bf16[2,3,32,256]{3,2,1,0:T(8,128)(2,1)S(1)}, bf16[2,3,32,256]{3,2,1,0:T(8,128)(2,1)S(1)}, u32[]{:S(2)}, u32[]{:S(2)}) %collective-permute-start.4) | collective-permute-done | bytes 98336 | tf_op jit(solution)/shard_map/ppermute | solution.py:157
  20.6 0.1 fusion.15
  20.7 0.1 collective-permute-start.5
  20.8 2.7 %collective-permute-start = (bf16[2,6,32,256]{3,2,1,0:T(8,128)(2,1)S(1)}, bf16[2,6,32,256]{3,2,1,0:T(8,128)(2,1)S(1)}, u32[]{:S(2)}, u32[]{:S(2)}) collective-permute-start(bf16[2,6,32,256]{3,2,1,0:T(8,128)(2,1)S(1)} %pad_maximum_fusion.3), channel_id=1, source_target_pairs={{0,4},{1,5},{2,6},{3,7},{4,0},{5,1},{6,2},{7,3},{8,12},{9,13},{10,... | collective-permute-start | bytes 589832 | tf_op jit(solution)/shard_map/ppermute | solution.py:157
  23.5 0.0 collective-permute-done.5
  23.5 0.1 pad_maximum_fusion
  23.6 3.2 %products.1 = (f32[4,2,3,32,256]{4,3,2,1,0:T(8,128)S(1)}, f32[4,2,3,32,256]{4,3,2,1,0:T(8,128)S(1)}, bf16[4,2,3,32,256]{4,3,2,1,0:T(8,128)(2,1)S(1)}, bf16[4,2,3,32,256]{4,3,2,1,0:T(8,128)(2,1)S(1)}) custom-call(s32[18]{0:T(128)S(1)} %copy-done.3, s32[12]{0:T(128)S(1)} %copy-done.4, f32[256,256]{1,0:T(8,128)S(1)} %copy-done.1, f32[256,256]{1,0:T(8,128)S(1)} %copy-done.2, ...), custom_call_target="tpu_custom_call" | custom-call | tf_op jit(solution)/shard_map/products/pallas_call | solution.py:216
  26.9 0.1 collective-permute-start.6
  26.9 3.9 %collective-permute-start.7 = (bf16[4,2,3,32,256]{4,3,2,1,0:T(8,128)(2,1)S(1)}, bf16[4,2,3,32,256]{4,3,2,1,0:T(8,128)(2,1)S(1)}, u32[]{:S(2)}, u32[]{:S(2)}) collective-permute-start(bf16[4,2,3,32,256]{4,3,2,1,0:T(8,128)(2,1)S(1)} %get-tuple-element.45), channel_id=1, source_target_pairs={{0,2},{1,3},{2,0},{3,1},{4,6},{5,7},{6,4},{7,5},{8,10},{9,11},{10,... | collective-permute-start | bytes 1179656 | tf_op jit(solution)/shard_map/ppermute | solution.py:157
  30.9 2.5 %collective-permute-done = bf16[2,6,32,256]{3,2,1,0:T(8,128)(2,1)S(1)} collective-permute-done((bf16[2,6,32,256]{3,2,1,0:T(8,128)(2,1)S(1)}, bf16[2,6,32,256]{3,2,1,0:T(8,128)(2,1)S(1)}, u32[]{:S(2)}, u32[]{:S(2)}) %collective-permute-start) | collective-permute-done | bytes 196640 | tf_op jit(solution)/shard_map/ppermute | solution.py:157
  33.4 1.5 %form.1.after.rows = bf16[2,2,6,32,256]{4,3,2,1,0:T(8,128)(2,1)S(1)} custom-call(s32[18]{0:T(128)S(1)} %copy-done.3, s32[12]{0:T(128)S(1)} %copy-done.4, f32[256,256]{1,0:T(8,128)S(1)} %copy-done.1, f32[256,256]{1,0:T(8,128)S(1)} %copy-done.2, bf16[2,2,6,32,256]{4,3,2,1,0:T(8,128)(2,1)S(1)} %pad_maximum_fusion.1.base, ...), custom_call_target="tpu_custom_call" | custom-call | flops 1677721600 | bytes 262144 | tf_op jit(solution)/shard_map/form/pallas_call | solution.py:228
  34.9 0.0 copy-start.5
  34.9 3.2 %collective-permute-done.6 = bf16[4,2,3,32,256]{4,3,2,1,0:T(8,128)(2,1)S(1)} collective-permute-done((bf16[4,2,3,32,256]{4,3,2,1,0:T(8,128)(2,1)S(1)}, bf16[4,2,3,32,256]{4,3,2,1,0:T(8,128)(2,1)S(1)}, u32[]{:S(2)}, u32[]{:S(2)}) %collective-permute-start.6) | collective-permute-done | bytes 393248 | tf_op jit(solution)/shard_map/ppermute | solution.py:157
  38.1 3.5 %collective-permute-done.7 = bf16[4,2,3,32,256]{4,3,2,1,0:T(8,128)(2,1)S(1)} collective-permute-done((bf16[4,2,3,32,256]{4,3,2,1,0:T(8,128)(2,1)S(1)}, bf16[4,2,3,32,256]{4,3,2,1,0:T(8,128)(2,1)S(1)}, u32[]{:S(2)}, u32[]{:S(2)}) %collective-permute-start.7) | collective-permute-done | bytes 393248 | tf_op jit(solution)/shard_map/ppermute | solution.py:157
  41.6 0.3 convert_add_fusion
  42.0 0.9 %collective-permute-start.9 = (bf16[2,2,3,32,256]{4,3,2,1,0:T(8,128)(2,1)S(1)}, bf16[2,2,3,32,256]{4,3,2,1,0:T(8,128)(2,1)S(1)}, u32[]{:S(2)}, u32[]{:S(2)}) collective-permute-start(bf16[2,2,3,32,256]{4,3,2,1,0:T(8,128)(2,1)S(1)} %fusion.1), channel_id=1, source_target_pairs={{0,1},{1,0},{2,3},{3,2},{4,5},{5,4},{6,7},{7,6},{8,9},{9,8},{10,11... | collective-permute-start | bytes 589832 | tf_op jit(solution)/shard_map/ppermute | solution.py:157
  43.0 2.2 %prepare.1 = (f32[256,256]{1,0:T(8,128)S(1)}, f32[3,32,256]{2,1,0:T(8,128)S(1)}) custom-call(bf16[256,256]{1,0:T(8,128)(2,1)S(1)} %copy-done.5, f32[256,256]{1,0:T(8,128)S(1)} %copy-done.1, f32[256,256]{1,0:T(8,128)S(1)} %copy-done.2, bf16[2,2,6,32,256]{4,3,2,1,0:T(8,128)(2,1)S(1)} %form.1.after.rows), custom_call_target="tpu_custom_call" | custom-call | flops 1006632960 | bytes 524288 | tf_op jit(solution)/shard_map/prepare/pallas_call | solution.py:237
  45.2 0.4 collective-permute-start.8
  45.6 3.3 %collective-permute-done.9 = bf16[2,2,3,32,256]{4,3,2,1,0:T(8,128)(2,1)S(1)} collective-permute-done((bf16[2,2,3,32,256]{4,3,2,1,0:T(8,128)(2,1)S(1)}, bf16[2,2,3,32,256]{4,3,2,1,0:T(8,128)(2,1)S(1)}, u32[]{:S(2)}, u32[]{:S(2)}) %collective-permute-start.9) | collective-permute-done | bytes 196640 | tf_op jit(solution)/shard_map/ppermute | solution.py:157
  49.0 2.8 %collective-permute-done.8 = bf16[2,2,3,32,256]{4,3,2,1,0:T(8,128)(2,1)S(1)} collective-permute-done((bf16[2,2,3,32,256]{4,3,2,1,0:T(8,128)(2,1)S(1)}, bf16[2,2,3,32,256]{4,3,2,1,0:T(8,128)(2,1)S(1)}, u32[]{:S(2)}, u32[]{:S(2)}) %collective-permute-start.8) | collective-permute-done | bytes 196640 | tf_op jit(solution)/shard_map/ppermute | solution.py:157
  51.9 1.0 %sums.1 = f32[2,8,3,32,128]{4,3,2,1,0:T(8,128)S(1)} custom-call(bf16[2,2,6,32,256]{4,3,2,1,0:T(8,128)(2,1)S(1)} %form.1.after.rows, f32[2,2,3,32,256]{4,3,2,1,0:T(8,128)S(1)} %bitcast_add_fusion.2.total_low, f32[2,2,3,32,256]{4,3,2,1,0:T(8,128)S(1)} %bitcast_add_fusion.1.total_high, f32[256,256]{1,0:T(8,128)S(1)} %get-tuple-element.54.linked, ...), custom_call_target="tpu_custom_call" | custom-call | tf_op jit(solution)/shard_map/sums/pallas_call | solution.py:268
  53.0 0.1 collective-permute-start.10
  53.1 1.6 %collective-permute-done.10 = f32[8,3,32,128]{3,2,1,0:T(8,128)S(1)} collective-permute-done((f32[8,3,32,128]{3,2,1,0:T(8,128)S(1)}, f32[8,3,32,128]{3,2,1,0:T(8,128)S(1)}, u32[]{:S(2)}, u32[]{:S(2)}) %collective-permute-start.10) | collective-permute-done | bytes 393248 | tf_op jit(solution)/shard_map/ppermute | solution.py:157
  54.7 0.1 bitcast_add_fusion
  54.8 1.2 %collective-permute-start.11 = (bf16[2,3,32,128]{3,2,1,0:T(8,128)(2,1)S(1)}, bf16[2,3,32,128]{3,2,1,0:T(8,128)(2,1)S(1)}, u32[]{:S(2)}, u32[]{:S(2)}) collective-permute-start(bf16[2,3,32,128]{3,2,1,0:T(8,128)(2,1)S(1)} %get-tuple-element.81), channel_id=1, source_target_pairs={{0,1},{1,0},{2,3},{3,2},{4,5},{5,4},{6,7},{7,6},{8,9},{9,8},{10,11... | collective-permute-start | bytes 147464 | tf_op jit(solution)/shard_map/ppermute | solution.py:157
  56.1 0.3 collective-permute-start.12
  56.3 2.1 %collective-permute-start.13 = (bf16[2,3,32,128]{3,2,1,0:T(8,128)(2,1)S(1)}, bf16[2,3,32,128]{3,2,1,0:T(8,128)(2,1)S(1)}, u32[]{:S(2)}, u32[]{:S(2)}) collective-permute-start(bf16[2,3,32,128]{3,2,1,0:T(8,128)(2,1)S(1)} %get-tuple-element.82), channel_id=1, source_target_pairs={{0,3},{1,2},{2,1},{3,0},{4,7},{5,6},{6,5},{7,4},{8,11},{9,10},{10,... | collective-permute-start | bytes 147464 | tf_op jit(solution)/shard_map/ppermute | solution.py:157
  58.4 1.8 %collective-permute-start.17 = (bf16[2,1,2,3,32,256]{5,4,3,2,1,0:T(8,128)(2,1)S(1)}, bf16[2,1,2,3,32,256]{5,4,3,2,1,0:T(8,128)(2,1)S(1)}, u32[]{:S(2)}, u32[]{:S(2)}) collective-permute-start(bf16[2,1,2,3,32,256]{5,4,3,2,1,0:T(8,128)(2,1)S(1)} %pad_maximum_fusion.4), channel_id=1, source_target_pairs={{0,4},{1,5},{2,6},{3,7},{4,0},{5,1},{6,2},{7,3},{8,12},{9,13},{10,... | collective-permute-start | bytes 589832 | tf_op jit(solution)/shard_map/ppermute | solution.py:157
  60.3 0.0 collective-permute-done.12
  60.3 1.1 %collective-permute-done.13 = bf16[2,3,32,128]{3,2,1,0:T(8,128)(2,1)S(1)} collective-permute-done((bf16[2,3,32,128]{3,2,1,0:T(8,128)(2,1)S(1)}, bf16[2,3,32,128]{3,2,1,0:T(8,128)(2,1)S(1)}, u32[]{:S(2)}, u32[]{:S(2)}) %collective-permute-start.13) | collective-permute-done | bytes 49184 | tf_op jit(solution)/shard_map/ppermute | solution.py:157
  61.4 4.4 %collective-permute-start.14 = (bf16[3,32,128]{2,1,0:T(8,128)(2,1)S(1)}, bf16[3,32,128]{2,1,0:T(8,128)(2,1)S(1)}, u32[]{:S(2)}, u32[]{:S(2)}) collective-permute-start(bf16[3,32,128]{2,1,0:T(8,128)(2,1)S(1)} %get-tuple-element.96), channel_id=1, source_target_pairs={{0,4},{1,5},{2,6},{3,7},{4,0},{5,1},{6,2},{7,3},{8,12},{9,13},{10,... | collective-permute-start | bytes 73736 | tf_op jit(solution)/shard_map/ppermute | solution.py:157
  65.8 1.3 %collective-permute-start.16 = (bf16[3,32,128]{2,1,0:T(8,128)(2,1)S(1)}, bf16[3,32,128]{2,1,0:T(8,128)(2,1)S(1)}, u32[]{:S(2)}, u32[]{:S(2)}) collective-permute-start(bf16[3,32,128]{2,1,0:T(8,128)(2,1)S(1)} %get-tuple-element.96), channel_id=1, source_target_pairs={{0,20},{1,21},{2,22},{3,23},{4,16},{5,17},{6,18},{7,19},{8,28},{9,... | collective-permute-start | bytes 73736 | tf_op jit(solution)/shard_map/ppermute | solution.py:289
  67.1 0.5 collective-permute-start.15
  67.6 3.7 %collective-permute-done.17 = bf16[2,1,2,3,32,256]{5,4,3,2,1,0:T(8,128)(2,1)S(1)} collective-permute-done((bf16[2,1,2,3,32,256]{5,4,3,2,1,0:T(8,128)(2,1)S(1)}, bf16[2,1,2,3,32,256]{5,4,3,2,1,0:T(8,128)(2,1)S(1)}, u32[]{:S(2)}, u32[]{:S(2)}) %collective-permute-start.17) | collective-permute-done | bytes 196640 | tf_op jit(solution)/shard_map/ppermute | solution.py:157
  71.3 0.2 collective-permute-done.14
  71.5 0.0 collective-permute-done.15
  71.5 1.7 %collective-permute-done.16 = bf16[3,32,128]{2,1,0:T(8,128)(2,1)S(1)} collective-permute-done((bf16[3,32,128]{2,1,0:T(8,128)(2,1)S(1)}, bf16[3,32,128]{2,1,0:T(8,128)(2,1)S(1)}, u32[]{:S(2)}, u32[]{:S(2)}) %collective-permute-start.16) | collective-permute-done | bytes 24608 | tf_op jit(solution)/shard_map/ppermute | solution.py:289
  73.3 0.1 collective-permute-start.18
  73.4 1.8 %columns.1 = (f32[6,32,256]{2,1,0:T(8,128)}, f32[6,32,256]{2,1,0:T(8,128)}) custom-call(s32[18]{0:T(128)S(1)} %copy-done.3, s32[12]{0:T(128)S(1)} %copy-done.4, f32[2,3,32,256]{3,2,1,0:T(8,128)S(1)} %bitcast.106, bf16[2,3,32,256]{3,2,1,0:T(8,128)(2,1)S(1)} %bitcast.108, f32[2,3,32,256]{3,2,1,0:T(8,128)S(1)} %bitcast.105, ...), custom_call_target="tpu_custom_call" | custom-call | tf_op jit(solution)/shard_map/columns/pallas_call | solution.py:295
  75.2 0.6 slice_bitcast_fusion.2
  (34 shorter events, 0.6 us)
Async XLA Ops:
  0.6 22.9 %copy-start = (bf16[6,1,3,1,256,256]{5,4,3,2,1,0:T(8,128)(2,1)S(1)}, bf16[6,1,3,1,256,256]{5,4,3,2,1,0:T(8,128)(2,1)}, u32[]{:S(2)}) copy-start(bf16[6,1,3,1,256,256]{5,4,3,2,1,0:T(8,128)(2,1)} %param.8) | copy-start | bytes 7077892
  0.6 22.9 %copy-start.1 = (f32[256,256]{1,0:T(8,128)S(1)}, f32[256,256]{1,0:T(8,128)}, u32[]{:S(2)}) copy-start(f32[256,256]{1,0:T(8,128)} %inv1.5) | copy-start | bytes 786436
  0.7 22.9 %copy-start.2 = (f32[256,256]{1,0:T(8,128)S(1)}, f32[256,256]{1,0:T(8,128)}, u32[]{:S(2)}) copy-start(f32[256,256]{1,0:T(8,128)} %inv2.5) | copy-start | bytes 786436
  0.7 22.9 %copy-start.3 = (s32[18]{0:T(128)S(1)}, s32[18]{0:T(128)}, u32[]{:S(2)}) copy-start(s32[18]{0:T(128)} %struct1.5) | copy-start | bytes 220
  0.7 22.9 %copy-start.4 = (s32[12]{0:T(128)S(1)}, s32[12]{0:T(128)}, u32[]{:S(2)}) copy-start(s32[12]{0:T(128)} %struct2.5) | copy-start | bytes 148
  1.9 4.8 %collective-permute-start.1 = (bf16[2,3,32,256]{3,2,1,0:T(8,128)(2,1)S(1)}, bf16[2,3,32,256]{3,2,1,0:T(8,128)(2,1)S(1)}, u32[]{:S(2)}, u32[]{:S(2)}) collective-permute-start(bf16[2,3,32,256]{3,2,1,0:T(8,128)(2,1)S(1)} %get-tuple-element.88), channel_id=1, source_target_pairs={{0,0},{1,8},{2,16},{3,24},{4,4},{5,12},{6,20},{7,28},{8,1},{9,9},{... | collective-permute-start | bytes 294920 | tf_op jit(solution)/shard_map/ppermute | solution.py:199
  2.6 11.5 %collective-permute-start.2 = (bf16[2,3,32,256]{3,2,1,0:T(8,128)(2,1)S(1)}, bf16[2,3,32,256]{3,2,1,0:T(8,128)(2,1)S(1)}, u32[]{:S(2)}, u32[]{:S(2)}) collective-permute-start(bf16[2,3,32,256]{3,2,1,0:T(8,128)(2,1)S(1)} %get-tuple-element.89), channel_id=1, source_target_pairs={{0,4},{1,12},{2,20},{3,28},{4,0},{5,8},{6,16},{7,24},{8,5},{9,13},... | collective-permute-start | bytes 294920 | tf_op jit(solution)/shard_map/ppermute | solution.py:199
  6.7 11.1 %collective-permute-start.3 = (bf16[2,3,32,256]{3,2,1,0:T(8,128)(2,1)S(1)}, bf16[2,3,32,256]{3,2,1,0:T(8,128)(2,1)S(1)}, u32[]{:S(2)}, u32[]{:S(2)}) collective-permute-start(bf16[2,3,32,256]{3,2,1,0:T(8,128)(2,1)S(1)} %collective-permute-done.1), channel_id=1, source_target_pairs={{0,16},{8,24},{16,0},{24,8},{1,17},{9,25},{17,1},{25,9},{2,18},{10... | collective-permute-start | bytes 294920 | tf_op jit(solution)/shard_map/ppermute | solution.py:157
  14.1 6.5 %collective-permute-start.4 = (bf16[2,3,32,256]{3,2,1,0:T(8,128)(2,1)S(1)}, bf16[2,3,32,256]{3,2,1,0:T(8,128)(2,1)S(1)}, u32[]{:S(2)}, u32[]{:S(2)}) collective-permute-start(bf16[2,3,32,256]{3,2,1,0:T(8,128)(2,1)S(1)} %collective-permute-done.2), channel_id=1, source_target_pairs={{0,16},{8,24},{16,0},{24,8},{1,17},{9,25},{17,1},{25,9},{2,18},{10... | collective-permute-start | bytes 294920 | tf_op jit(solution)/shard_map/ppermute | solution.py:157
  20.7 2.8 %collective-permute-start.5 = (bf16[2,2,2,3,32,256]{5,4,3,2,1,0:T(8,128)(2,1)S(1)}, bf16[2,2,2,3,32,256]{5,4,3,2,1,0:T(8,128)(2,1)S(1)}, u32[]{:S(2)}, u32[]{:S(2)}) collective-permute-start(bf16[2,2,2,3,32,256]{5,4,3,2,1,0:T(8,128)(2,1)S(1)} %get-tuple-element.85), channel_id=1, source_target_pairs={{0,8},{8,0},{16,24},{24,16},{1,9},{9,1},{17,25},{25,17},{2,10},{10... | collective-permute-start | bytes 1179656 | tf_op jit(solution)/shard_map/ppermute | solution.py:157
  20.8 12.5 %collective-permute-start = (bf16[2,6,32,256]{3,2,1,0:T(8,128)(2,1)S(1)}, bf16[2,6,32,256]{3,2,1,0:T(8,128)(2,1)S(1)}, u32[]{:S(2)}, u32[]{:S(2)}) collective-permute-start(bf16[2,6,32,256]{3,2,1,0:T(8,128)(2,1)S(1)} %pad_maximum_fusion.3), channel_id=1, source_target_pairs={{0,4},{1,5},{2,6},{3,7},{4,0},{5,1},{6,2},{7,3},{8,12},{9,13},{10,... | collective-permute-start | bytes 589832 | tf_op jit(solution)/shard_map/ppermute | solution.py:157
  26.9 11.3 %collective-permute-start.6 = (bf16[4,2,3,32,256]{4,3,2,1,0:T(8,128)(2,1)S(1)}, bf16[4,2,3,32,256]{4,3,2,1,0:T(8,128)(2,1)S(1)}, u32[]{:S(2)}, u32[]{:S(2)}) collective-permute-start(bf16[4,2,3,32,256]{4,3,2,1,0:T(8,128)(2,1)S(1)} %get-tuple-element.43), channel_id=1, source_target_pairs={{0,1},{1,0},{2,3},{3,2},{4,5},{5,4},{6,7},{7,6},{8,9},{9,8},{10,11... | collective-permute-start | bytes 1179656 | tf_op jit(solution)/shard_map/ppermute | solution.py:157
  26.9 14.7 %collective-permute-start.7 = (bf16[4,2,3,32,256]{4,3,2,1,0:T(8,128)(2,1)S(1)}, bf16[4,2,3,32,256]{4,3,2,1,0:T(8,128)(2,1)S(1)}, u32[]{:S(2)}, u32[]{:S(2)}) collective-permute-start(bf16[4,2,3,32,256]{4,3,2,1,0:T(8,128)(2,1)S(1)} %get-tuple-element.45), channel_id=1, source_target_pairs={{0,2},{1,3},{2,0},{3,1},{4,6},{5,7},{6,4},{7,5},{8,10},{9,11},{10,... | collective-permute-start | bytes 1179656 | tf_op jit(solution)/shard_map/ppermute | solution.py:157
  34.9 8.1 %copy-start.5 = (bf16[256,256]{1,0:T(8,128)(2,1)S(1)}, bf16[256,256]{1,0:T(8,128)(2,1)}, u32[]{:S(2)}) copy-start(bf16[256,256]{1,0:T(8,128)(2,1)} %link.1) | copy-start | bytes 393220
  42.0 6.9 %collective-permute-start.9 = (bf16[2,2,3,32,256]{4,3,2,1,0:T(8,128)(2,1)S(1)}, bf16[2,2,3,32,256]{4,3,2,1,0:T(8,128)(2,1)S(1)}, u32[]{:S(2)}, u32[]{:S(2)}) collective-permute-start(bf16[2,2,3,32,256]{4,3,2,1,0:T(8,128)(2,1)S(1)} %fusion.1), channel_id=1, source_target_pairs={{0,1},{1,0},{2,3},{3,2},{4,5},{5,4},{6,7},{7,6},{8,9},{9,8},{10,11... | collective-permute-start | bytes 589832 | tf_op jit(solution)/shard_map/ppermute | solution.py:157
  45.2 6.6 %collective-permute-start.8 = (bf16[2,2,3,32,256]{4,3,2,1,0:T(8,128)(2,1)S(1)}, bf16[2,2,3,32,256]{4,3,2,1,0:T(8,128)(2,1)S(1)}, u32[]{:S(2)}, u32[]{:S(2)}) collective-permute-start(bf16[2,2,3,32,256]{4,3,2,1,0:T(8,128)(2,1)S(1)} %fusion), channel_id=1, source_target_pairs={{0,2},{1,3},{2,0},{3,1},{4,6},{5,7},{6,4},{7,5},{8,10},{9,11},{10,... | collective-permute-start | bytes 589832 | tf_op jit(solution)/shard_map/ppermute | solution.py:157
  53.0 1.8 %collective-permute-start.10 = (f32[8,3,32,128]{3,2,1,0:T(8,128)S(1)}, f32[8,3,32,128]{3,2,1,0:T(8,128)S(1)}, u32[]{:S(2)}, u32[]{:S(2)}) collective-permute-start(f32[8,3,32,128]{3,2,1,0:T(8,128)S(1)} %dynamic-slice_bitcast_fusion), channel_id=1, source_target_pairs={{0,8},{8,0},{16,24},{24,16},{1,9},{9,1},{17,25},{25,17},{2,10},{10... | collective-permute-start | bytes 1179656 | tf_op jit(solution)/shard_map/ppermute | solution.py:157
  54.8 5.4 %collective-permute-start.11 = (bf16[2,3,32,128]{3,2,1,0:T(8,128)(2,1)S(1)}, bf16[2,3,32,128]{3,2,1,0:T(8,128)(2,1)S(1)}, u32[]{:S(2)}, u32[]{:S(2)}) collective-permute-start(bf16[2,3,32,128]{3,2,1,0:T(8,128)(2,1)S(1)} %get-tuple-element.81), channel_id=1, source_target_pairs={{0,1},{1,0},{2,3},{3,2},{4,5},{5,4},{6,7},{7,6},{8,9},{9,8},{10,11... | collective-permute-start | bytes 147464 | tf_op jit(solution)/shard_map/ppermute | solution.py:157
  56.1 4.2 %collective-permute-start.12 = (bf16[2,3,32,128]{3,2,1,0:T(8,128)(2,1)S(1)}, bf16[2,3,32,128]{3,2,1,0:T(8,128)(2,1)S(1)}, u32[]{:S(2)}, u32[]{:S(2)}) collective-permute-start(bf16[2,3,32,128]{3,2,1,0:T(8,128)(2,1)S(1)} %get-tuple-element.83), channel_id=1, source_target_pairs={{0,2},{1,3},{2,0},{3,1},{4,6},{5,7},{6,4},{7,5},{8,10},{9,11},{10,... | collective-permute-start | bytes 147464 | tf_op jit(solution)/shard_map/ppermute | solution.py:157
  56.3 5.0 %collective-permute-start.13 = (bf16[2,3,32,128]{3,2,1,0:T(8,128)(2,1)S(1)}, bf16[2,3,32,128]{3,2,1,0:T(8,128)(2,1)S(1)}, u32[]{:S(2)}, u32[]{:S(2)}) collective-permute-start(bf16[2,3,32,128]{3,2,1,0:T(8,128)(2,1)S(1)} %get-tuple-element.82), channel_id=1, source_target_pairs={{0,3},{1,2},{2,1},{3,0},{4,7},{5,6},{6,5},{7,4},{8,11},{9,10},{10,... | collective-permute-start | bytes 147464 | tf_op jit(solution)/shard_map/ppermute | solution.py:157
  58.4 12.9 %collective-permute-start.17 = (bf16[2,1,2,3,32,256]{5,4,3,2,1,0:T(8,128)(2,1)S(1)}, bf16[2,1,2,3,32,256]{5,4,3,2,1,0:T(8,128)(2,1)S(1)}, u32[]{:S(2)}, u32[]{:S(2)}) collective-permute-start(bf16[2,1,2,3,32,256]{5,4,3,2,1,0:T(8,128)(2,1)S(1)} %pad_maximum_fusion.4), channel_id=1, source_target_pairs={{0,4},{1,5},{2,6},{3,7},{4,0},{5,1},{6,2},{7,3},{8,12},{9,13},{10,... | collective-permute-start | bytes 589832 | tf_op jit(solution)/shard_map/ppermute | solution.py:157
  61.4 10.2 %collective-permute-start.14 = (bf16[3,32,128]{2,1,0:T(8,128)(2,1)S(1)}, bf16[3,32,128]{2,1,0:T(8,128)(2,1)S(1)}, u32[]{:S(2)}, u32[]{:S(2)}) collective-permute-start(bf16[3,32,128]{2,1,0:T(8,128)(2,1)S(1)} %get-tuple-element.96), channel_id=1, source_target_pairs={{0,4},{1,5},{2,6},{3,7},{4,0},{5,1},{6,2},{7,3},{8,12},{9,13},{10,... | collective-permute-start | bytes 73736 | tf_op jit(solution)/shard_map/ppermute | solution.py:157
  65.8 7.4 %collective-permute-start.16 = (bf16[3,32,128]{2,1,0:T(8,128)(2,1)S(1)}, bf16[3,32,128]{2,1,0:T(8,128)(2,1)S(1)}, u32[]{:S(2)}, u32[]{:S(2)}) collective-permute-start(bf16[3,32,128]{2,1,0:T(8,128)(2,1)S(1)} %get-tuple-element.96), channel_id=1, source_target_pairs={{0,20},{1,21},{2,22},{3,23},{4,16},{5,17},{6,18},{7,19},{8,28},{9,... | collective-permute-start | bytes 73736 | tf_op jit(solution)/shard_map/ppermute | solution.py:289
  67.1 4.5 %collective-permute-start.15 = (bf16[3,32,128]{2,1,0:T(8,128)(2,1)S(1)}, bf16[3,32,128]{2,1,0:T(8,128)(2,1)S(1)}, u32[]{:S(2)}, u32[]{:S(2)}) collective-permute-start(bf16[3,32,128]{2,1,0:T(8,128)(2,1)S(1)} %get-tuple-element.95), channel_id=1, source_target_pairs={{0,16},{8,24},{16,0},{24,8},{1,17},{9,25},{17,1},{25,9},{2,18},{10... | collective-permute-start | bytes 73736 | tf_op jit(solution)/shard_map/ppermute | solution.py:157
  73.3 1.9 %collective-permute-start.18 = (f32[3,32,128]{2,1,0:T(8,128)S(1)}, f32[3,32,128]{2,1,0:T(8,128)S(1)}, u32[]{:S(2)}, u32[]{:S(2)}) collective-permute-start(f32[3,32,128]{2,1,0:T(8,128)S(1)} %add_add_fusion), channel_id=1, source_target_pairs={{0,8},{8,0},{16,24},{24,16},{1,9},{9,1},{17,25},{25,17},{2,10},{10... | collective-permute-start | bytes 147464 | tf_op jit(solution)/shard_map/ppermute | solution.py:157

commit v5 on v3

--- a/solution.py
+++ b/solution.py
@@ -134,11 +134,8 @@
     cross = split_dot(u2, sum1, 0)
     top = cross.T - split_dot(first, link)
     second = split_dot(u2, gathered(1), 0) - split_dot(cross, link) - split_dot(link, top, 0)
-    across = width // 2
     for i, part in enumerate((first, top, second)):
-        part = part.reshape(width // slab, slab, width)
-        for h in range(2):
-            out[h, :, i] = part[:, :, h * across : (h + 1) * across]
+        out[:, i] = part.reshape(width // slab, slab, width)
 
 
 def column_kernel(n_row, struct1, struct2, kept_low, came_low, kept_high, came_high, linked, column1, column2):
@@ -180,11 +177,9 @@
     picks = [((s - turn + cycle) % cycle).astype(jnp.uint32) for s in range(cycle)]
     ways = [(here_col >> bit) & 1 for bit in range(n_bits)]
     ways = [(way.astype(jnp.uint32), (1 - way).astype(jnp.uint32)) for way in ways]
-    core = lax.axis_index("row") & 1
-    cores = (core.astype(jnp.uint32), (1 - core).astype(jnp.uint32))
     quads = [(here_col & 3) ^ m for m in range(4)]
     quads = [quad.astype(jnp.uint32) for quad in quads]
-    panels, picks, ways, cores, quads = lax.optimization_barrier((panels, picks, ways, cores, quads))
+    panels, picks, ways, quads = lax.optimization_barrier((panels, picks, ways, quads))
 
     raw = lax.optimization_barrier(jnp.stack(panels))
     turns = raw.reshape(2, col_blocks, cycle, slab, width)
@@ -267,15 +262,13 @@
 
     sums = pl.pallas_call(
         functools.partial(sum_kernel, n_bits - 1),
-        out_shape=shape((2, n_col, 3, slab, width // 2), f32),
+        out_shape=shape((n_col, 3, slab, width), f32),
         in_specs=[VMEM] * 4 + [ANY],
         out_specs=VMEM,
         compiler_params=big,
         name="sums",
     )(rows, *totals, linked, consts)
-    keep, send = halves(sums, 0, cores)
-    sums = keep + swapped(send, "row", n_row, 1)
-    tail = (3, slab, width // 2)
+    tail = (3, slab, width)
     parts = [lax.dynamic_index_in_dim(sums.reshape((-1, 4) + tail), quad, 1, keepdims=False) for quad in quads]
     sums = parts[0]
     for m in range(1, 4):
@@ -283,6 +276,7 @@
     for bit in range(2, n_bits - 1):
         keep, send = halves(sums.reshape((-1, 2) + tail), 1, ways[bit])
         sums = keep + swapped(send.astype(bf16), "col", n_col, 1 << bit).astype(f32)
+    sums, state = lax.optimization_barrier((sums, state))
     keep, send = (part.astype(bf16) for part in halves(sums.reshape((2,) + tail), 0, ways[n_bits - 1]))
     across = [(r * n_col + c, (r ^ 2) * n_col + (c ^ (n_col // 2))) for r in range(n_row) for c in range(n_col)]
     near = keep.astype(f32) + swapped(send, "col", n_col, n_col // 2).astype(f32)
@@ -291,7 +285,6 @@
     for bit in range(2, n_row.bit_length() - 1):
         mine = mine + swapped(mine, "row", n_row, 1 << bit)
 
-    mine, state = lax.optimization_barrier((mine, state))
     column_first, column_second = pl.pallas_call(
         functools.partial(column_kernel, n_row),
         out_shape=[shape(panel, f32)] * 2,
@@ -301,8 +294,7 @@
         name="columns",
     )(struct_first, struct_second, *[part[0] for pair in state for part in pair], linked)
 
-    pair = jnp.stack([mine, swapped(mine, "row", n_row, 1)])
-    total = jnp.concatenate([lax.dynamic_index_in_dim(pair, way, 0, keepdims=False) for way in cores], axis=-1)
+    total = mine + swapped(mine, "row", n_row, 1)
     diag_first, link_block, diag_second = consts + total
     out = (row_blocks, 1, slab, width)
     return column_first.reshape(out), column_second.reshape(out), diag_first, link_block, diag_second

time: 71.7 us -> 72.2 us (level)
  waiting for transfers between devices: 25.4 us -> 27 us
  starting transfers between devices: 32.7 us -> 31.7 us
    ppermute x16 -> x15, starting transfers between devices: 27.7 us -> 24.1 us  [swapped(): return lax.ppermute(value, axis, [(i, i ^ mask) for i in range(size)])]
    ppermute x1, starting transfers between devices: 0.21 us -> 2.8 us  [body(): lax.ppermute(send, ('row', 'col'), across).astype(f32)]
    ppermute x1, waiting for transfers between devices: 0.86 us -> 2.19 us  [body(): lax.ppermute(send, ('row', 'col'), across).astype(f32)]
    ppermute x16 -> x15, waiting for transfers between devices: 24.6 us -> 24.8 us  [swapped(): return lax.ppermute(value, axis, [(i, i ^ mask) for i in range(size)])]
  transfers between devices with their start and end apart: 19 -> 18, of which waited for: 11 -> 11; matrix products, arithmetic and copies ran while one was open for 1% -> 1% of each run, Pallas kernels for 8% -> 9%
where the time goes in v5:
time: 72.2 us; the launch traced here: 72 us
  starting transfers between devices  31.7 us (44%)
  waiting for transfers between devices  27 us (37%)
  Pallas kernels  9.7 us (13%)
  other arithmetic  1.7 us (2%)
  between operations  0.99 us (1%)
  local copies, waits for them, and re-layouts  0.89 us (1%)
    ppermute x15, waiting for transfers between devices, swapped(): return lax.ppermute(value, axis, [(i, i ^ mask) for i in range(size)])  24.8 us
    ppermute x15, starting transfers between devices, swapped(): return lax.ppermute(value, axis, [(i, i ^ mask) for i in range(size)])  24.1 us
    ppermute x2, starting transfers between devices, body(): got.append(lax.ppermute(part, ('row', 'col'), moves))  4.77 us
    pallas_call x1, Pallas kernels, body(): pl.pallas_call(functools.partial(product_kernel, n_row, n_col, (orders[0]...  3.23 us
    ppermute x1, starting transfers between devices, body(): lax.ppermute(send, ('row', 'col'), across).astype(f32)  2.8 us
    ppermute x1, waiting for transfers between devices, body(): lax.ppermute(send, ('row', 'col'), across).astype(f32)  2.19 us
    pallas_call x1, Pallas kernels, body(): pl.pallas_call(prepare_kernel, out_shape=[shape((width, width), f32), sha...  2.18 us
    pallas_call x1, Pallas kernels, body(): pl.pallas_call(functools.partial(column_kernel, n_row), out_shape=[shape(...  1.78 us
  transfers between devices with their start and end apart: 18, of which 11 were waited for; matrix products, arithmetic and copies ran while one was open for 1% of the time, Pallas kernels for 9%

profile of v5, /device:TPU:0, one launch (start us, length us, event | category | flops | bytes accessed | tf_op | source)
XLA Modules:
  0.0 72.0 jit_solution(9036913153563199661)
XLA Ops:
  0.6 0.0 copy-start.1
  0.7 1.0 %pad_maximum_fusion.3 = bf16[2,6,32,256]{3,2,1,0:T(8,128)(2,1)S(1)} fusion(bf16[1,6,32,256]{3,2,1,0:T(8,128)(2,1)} %bitcast.113, bf16[1,6,32,256]{3,2,1,0:T(8,128)(2,1)} %bitcast.114), kind=kLoop, calls=%fused_computation.11 | loop fusion | flops 98304 | bytes 393216 | tf_op jit(solution)/shard_map/stack | solution.py:184
  1.8 0.7 collective-permute-start
  2.4 4.1 %collective-permute-start.1 = (bf16[2,3,32,256]{3,2,1,0:T(8,128)(2,1)S(1)}, bf16[2,3,32,256]{3,2,1,0:T(8,128)(2,1)S(1)}, u32[]{:S(2)}, u32[]{:S(2)}) collective-permute-start(bf16[2,3,32,256]{3,2,1,0:T(8,128)(2,1)S(1)} %get-tuple-element.83), channel_id=1, source_target_pairs={{0,4},{1,12},{2,20},{3,28},{4,0},{5,8},{6,16},{7,24},{8,5},{9,13},... | collective-permute-start | bytes 294920 | tf_op jit(solution)/shard_map/ppermute | solution.py:194
  6.5 0.1 collective-permute-start.4
  6.6 0.0 collective-permute-done
  6.6 12.4 %collective-permute-start.2 = (bf16[2,3,32,256]{3,2,1,0:T(8,128)(2,1)S(1)}, bf16[2,3,32,256]{3,2,1,0:T(8,128)(2,1)S(1)}, u32[]{:S(2)}, u32[]{:S(2)}) collective-permute-start(bf16[2,3,32,256]{3,2,1,0:T(8,128)(2,1)S(1)} %collective-permute-done), channel_id=1, source_target_pairs={{0,16},{8,24},{16,0},{24,8},{1,17},{9,25},{17,1},{25,9},{2,18},{10... | collective-permute-start | bytes 294920 | tf_op jit(solution)/shard_map/ppermute | solution.py:154
  19.0 0.0 collective-permute-done.1
  19.0 0.0 collective-permute-start.3
  19.1 3.0 %collective-permute-done.2 = bf16[2,3,32,256]{3,2,1,0:T(8,128)(2,1)S(1)} collective-permute-done((bf16[2,3,32,256]{3,2,1,0:T(8,128)(2,1)S(1)}, bf16[2,3,32,256]{3,2,1,0:T(8,128)(2,1)S(1)}, u32[]{:S(2)}, u32[]{:S(2)}) %collective-permute-start.2) | collective-permute-done | bytes 98336 | tf_op jit(solution)/shard_map/ppermute | solution.py:154
  22.1 2.5 %collective-permute-done.3 = bf16[2,3,32,256]{3,2,1,0:T(8,128)(2,1)S(1)} collective-permute-done((bf16[2,3,32,256]{3,2,1,0:T(8,128)(2,1)S(1)}, bf16[2,3,32,256]{3,2,1,0:T(8,128)(2,1)S(1)}, u32[]{:S(2)}, u32[]{:S(2)}) %collective-permute-start.3) | collective-permute-done | bytes 98336 | tf_op jit(solution)/shard_map/ppermute | solution.py:154
  24.6 0.0 collective-permute-done.4
  24.7 0.1 collective-permute-start.5
  24.8 1.5 %form.1.rows = bf16[2,2,6,32,256]{4,3,2,1,0:T(8,128)(2,1)S(1)} custom-call(s32[18]{0:T(128)S(1)} %copy-done.3, s32[12]{0:T(128)S(1)} %copy-done.4, f32[256,256]{1,0:T(8,128)S(1)} %copy-done.1, f32[256,256]{1,0:T(8,128)S(1)} %copy-done.2, bf16[2,2,6,32,256]{4,3,2,1,0:T(8,128)(2,1)S(1)} %pad_maximum_fusion.2.base), custom_call_target="tpu_custom_call" | custom-call | flops 134217728 | bytes 262144 | tf_op jit(solution)/shard_map/form/pallas_call | solution.py:205
  26.3 0.2 collective-permute-done.5
  26.5 0.1 pad_maximum_fusion
  26.6 3.2 %products.1 = (f32[4,2,3,32,256]{4,3,2,1,0:T(8,128)S(1)}, f32[4,2,3,32,256]{4,3,2,1,0:T(8,128)S(1)}, bf16[4,2,3,32,256]{4,3,2,1,0:T(8,128)(2,1)S(1)}, bf16[4,2,3,32,256]{4,3,2,1,0:T(8,128)(2,1)S(1)}) custom-call(s32[18]{0:T(128)S(1)} %copy-done.3, s32[12]{0:T(128)S(1)} %copy-done.4, f32[256,256]{1,0:T(8,128)S(1)} %copy-done.1, f32[256,256]{1,0:T(8,128)S(1)} %copy-done.2, ...), custom_call_target="tpu_custom_call" | custom-call | tf_op jit(solution)/shard_map/products/pallas_call | solution.py:221
  29.8 0.6 collective-permute-start.8
  30.4 1.1 %collective-permute-start.6 = (bf16[4,2,3,32,256]{4,3,2,1,0:T(8,128)(2,1)S(1)}, bf16[4,2,3,32,256]{4,3,2,1,0:T(8,128)(2,1)S(1)}, u32[]{:S(2)}, u32[]{:S(2)}) collective-permute-start(bf16[4,2,3,32,256]{4,3,2,1,0:T(8,128)(2,1)S(1)} %get-tuple-element.45), channel_id=1, source_target_pairs={{0,1},{1,0},{2,3},{3,2},{4,5},{5,4},{6,7},{7,6},{8,9},{9,8},{10,11... | collective-permute-start | bytes 1179656 | tf_op jit(solution)/shard_map/ppermute | solution.py:154
  31.5 2.2 %prepare.1 = (f32[256,256]{1,0:T(8,128)S(1)}, f32[3,32,256]{2,1,0:T(8,128)S(1)}) custom-call(bf16[256,256]{1,0:T(8,128)(2,1)S(1)} %copy-done.5, f32[256,256]{1,0:T(8,128)S(1)} %copy-done.1, f32[256,256]{1,0:T(8,128)S(1)} %copy-done.2, f32[4,2,3,32,256]{4,3,2,1,0:T(8,128)S(1)} %get-tuple-element.44.after), custom_call_target="tpu_custom_call" | custom-call | flops 1006632960 | bytes 524288 | tf_op jit(solution)/shard_map/prepare/pallas_call | solution.py:233
  33.7 7.5 %collective-permute-done.8 = bf16[4,2,3,32,256]{4,3,2,1,0:T(8,128)(2,1)S(1)} collective-permute-done((bf16[4,2,3,32,256]{4,3,2,1,0:T(8,128)(2,1)S(1)}, bf16[4,2,3,32,256]{4,3,2,1,0:T(8,128)(2,1)S(1)}, u32[]{:S(2)}, u32[]{:S(2)}) %collective-permute-start.8) | collective-permute-done | bytes 393248 | tf_op jit(solution)/shard_map/ppermute | solution.py:154
  41.2 0.1 convert_add_fusion
  41.4 0.5 collective-permute-start.9
  41.9 0.0 collective-permute-done.6
  41.9 0.1 convert_add_fusion.1
  42.1 1.3 %collective-permute-start.7 = (bf16[2,2,3,32,256]{4,3,2,1,0:T(8,128)(2,1)S(1)}, bf16[2,2,3,32,256]{4,3,2,1,0:T(8,128)(2,1)S(1)}, u32[]{:S(2)}, u32[]{:S(2)}) collective-permute-start(bf16[2,2,3,32,256]{4,3,2,1,0:T(8,128)(2,1)S(1)} %fusion), channel_id=1, source_target_pairs={{0,2},{1,3},{2,0},{3,1},{4,6},{5,7},{6,4},{7,5},{8,10},{9,11},{10,... | collective-permute-start | bytes 589832 | tf_op jit(solution)/shard_map/ppermute | solution.py:154
  43.3 4.5 %collective-permute-done.9 = bf16[2,2,3,32,256]{4,3,2,1,0:T(8,128)(2,1)S(1)} collective-permute-done((bf16[2,2,3,32,256]{4,3,2,1,0:T(8,128)(2,1)S(1)}, bf16[2,2,3,32,256]{4,3,2,1,0:T(8,128)(2,1)S(1)}, u32[]{:S(2)}, u32[]{:S(2)}) %collective-permute-start.9) | collective-permute-done | bytes 196640 | tf_op jit(solution)/shard_map/ppermute | solution.py:154
  47.9 0.3 collective-permute-done.7
  48.3 2.8 %collective-permute-start.13 = (bf16[2,1,2,3,32,256]{5,4,3,2,1,0:T(8,128)(2,1)S(1)}, bf16[2,1,2,3,32,256]{5,4,3,2,1,0:T(8,128)(2,1)S(1)}, u32[]{:S(2)}, u32[]{:S(2)}) collective-permute-start(bf16[2,1,2,3,32,256]{5,4,3,2,1,0:T(8,128)(2,1)S(1)} %pad_maximum_fusion.4), channel_id=1, source_target_pairs={{0,4},{1,5},{2,6},{3,7},{4,0},{5,1},{6,2},{7,3},{8,12},{9,13},{10,... | collective-permute-start | bytes 589832 | tf_op jit(solution)/shard_map/ppermute | solution.py:154
  51.1 1.0 %sums.1 = f32[8,3,32,256]{3,2,1,0:T(8,128)S(1)} custom-call(bf16[2,2,6,32,256]{4,3,2,1,0:T(8,128)(2,1)S(1)} %form.1.rows, f32[2,2,3,32,256]{4,3,2,1,0:T(8,128)S(1)} %bitcast_add_fusion.1.total_low, f32[2,2,3,32,256]{4,3,2,1,0:T(8,128)S(1)} %bitcast_add_fusion.total_high, f32[256,256]{1,0:T(8,128)S(1)} %get-tuple-element.52.linked, ...), custom_call_target="tpu_custom_call" | custom-call | tf_op jit(solution)/shard_map/sums/pallas_call | solution.py:263
  52.2 1.2 %collective-permute-start.10 = (bf16[2,3,32,256]{3,2,1,0:T(8,128)(2,1)S(1)}, bf16[2,3,32,256]{3,2,1,0:T(8,128)(2,1)S(1)}, u32[]{:S(2)}, u32[]{:S(2)}) collective-permute-start(bf16[2,3,32,256]{3,2,1,0:T(8,128)(2,1)S(1)} %get-tuple-element.77), channel_id=1, source_target_pairs={{0,1},{1,0},{2,3},{3,2},{4,5},{5,4},{6,7},{7,6},{8,9},{9,8},{10,11... | collective-permute-start | bytes 294920 | tf_op jit(solution)/shard_map/ppermute | solution.py:154
  53.4 1.4 %collective-permute-start.11 = (bf16[2,3,32,256]{3,2,1,0:T(8,128)(2,1)S(1)}, bf16[2,3,32,256]{3,2,1,0:T(8,128)(2,1)S(1)}, u32[]{:S(2)}, u32[]{:S(2)}) collective-permute-start(bf16[2,3,32,256]{3,2,1,0:T(8,128)(2,1)S(1)} %get-tuple-element.78), channel_id=1, source_target_pairs={{0,2},{1,3},{2,0},{3,1},{4,6},{5,7},{6,4},{7,5},{8,10},{9,11},{10,... | collective-permute-start | bytes 294920 | tf_op jit(solution)/shard_map/ppermute | solution.py:154
  54.9 0.9 %collective-permute-start.12 = (bf16[2,3,32,256]{3,2,1,0:T(8,128)(2,1)S(1)}, bf16[2,3,32,256]{3,2,1,0:T(8,128)(2,1)S(1)}, u32[]{:S(2)}, u32[]{:S(2)}) collective-permute-start(bf16[2,3,32,256]{3,2,1,0:T(8,128)(2,1)S(1)} %get-tuple-element.79), channel_id=1, source_target_pairs={{0,3},{1,2},{2,1},{3,0},{4,7},{5,6},{6,5},{7,4},{8,11},{9,10},{10,... | collective-permute-start | bytes 294920 | tf_op jit(solution)/shard_map/ppermute | solution.py:154
  55.8 1.6 %collective-permute-done.10 = bf16[2,3,32,256]{3,2,1,0:T(8,128)(2,1)S(1)} collective-permute-done((bf16[2,3,32,256]{3,2,1,0:T(8,128)(2,1)S(1)}, bf16[2,3,32,256]{3,2,1,0:T(8,128)(2,1)S(1)}, u32[]{:S(2)}, u32[]{:S(2)}) %collective-permute-start.10) | collective-permute-done | bytes 98336 | tf_op jit(solution)/shard_map/ppermute | solution.py:154
  57.4 2.8 %collective-permute-done.11 = bf16[2,3,32,256]{3,2,1,0:T(8,128)(2,1)S(1)} collective-permute-done((bf16[2,3,32,256]{3,2,1,0:T(8,128)(2,1)S(1)}, bf16[2,3,32,256]{3,2,1,0:T(8,128)(2,1)S(1)}, u32[]{:S(2)}, u32[]{:S(2)}) %collective-permute-start.11) | collective-permute-done | bytes 98336 | tf_op jit(solution)/shard_map/ppermute | solution.py:154
  60.2 1.5 %collective-permute-done.12 = bf16[2,3,32,256]{3,2,1,0:T(8,128)(2,1)S(1)} collective-permute-done((bf16[2,3,32,256]{3,2,1,0:T(8,128)(2,1)S(1)}, bf16[2,3,32,256]{3,2,1,0:T(8,128)(2,1)S(1)}, u32[]{:S(2)}, u32[]{:S(2)}) %collective-permute-start.12) | collective-permute-done | bytes 98336 | tf_op jit(solution)/shard_map/ppermute | solution.py:154
  61.7 0.1 fusion.3
  61.8 0.0 collective-permute-done.13
  61.9 0.1 collective-permute-start.14
  61.9 1.6 %collective-permute-start.15 = (bf16[3,32,256]{2,1,0:T(8,128)(2,1)S(1)}, bf16[3,32,256]{2,1,0:T(8,128)(2,1)S(1)}, u32[]{:S(2)}, u32[]{:S(2)}) collective-permute-start(bf16[3,32,256]{2,1,0:T(8,128)(2,1)S(1)} %get-tuple-element.87), channel_id=1, source_target_pairs={{0,16},{8,24},{16,0},{24,8},{1,17},{9,25},{17,1},{25,9},{2,18},{10... | collective-permute-start | bytes 147464 | tf_op jit(solution)/shard_map/ppermute | solution.py:154
  63.5 2.8 %collective-permute-start.16 = (bf16[3,32,256]{2,1,0:T(8,128)(2,1)S(1)}, bf16[3,32,256]{2,1,0:T(8,128)(2,1)S(1)}, u32[]{:S(2)}, u32[]{:S(2)}) collective-permute-start(bf16[3,32,256]{2,1,0:T(8,128)(2,1)S(1)} %get-tuple-element.88), channel_id=1, source_target_pairs={{0,20},{1,21},{2,22},{3,23},{4,16},{5,17},{6,18},{7,19},{8,28},{9,... | collective-permute-start | bytes 147464 | tf_op jit(solution)/shard_map/ppermute | solution.py:283
  66.3 0.9 %collective-permute-done.14 = bf16[3,32,256]{2,1,0:T(8,128)(2,1)S(1)} collective-permute-done((bf16[3,32,256]{2,1,0:T(8,128)(2,1)S(1)}, bf16[3,32,256]{2,1,0:T(8,128)(2,1)S(1)}, u32[]{:S(2)}, u32[]{:S(2)}) %collective-permute-start.14) | collective-permute-done | bytes 49184 | tf_op jit(solution)/shard_map/ppermute | solution.py:154
  67.2 0.0 collective-permute-done.15
  67.2 2.2 %collective-permute-done.16 = bf16[3,32,256]{2,1,0:T(8,128)(2,1)S(1)} collective-permute-done((bf16[3,32,256]{2,1,0:T(8,128)(2,1)S(1)}, bf16[3,32,256]{2,1,0:T(8,128)(2,1)S(1)}, u32[]{:S(2)}, u32[]{:S(2)}) %collective-permute-start.16) | collective-permute-done | bytes 49184 | tf_op jit(solution)/shard_map/ppermute | solution.py:283
  69.4 0.1 collective-permute-start.17
  69.5 1.8 %columns.1 = (f32[6,32,256]{2,1,0:T(8,128)}, f32[6,32,256]{2,1,0:T(8,128)}) custom-call(s32[18]{0:T(128)S(1)} %copy-done.3, s32[12]{0:T(128)S(1)} %copy-done.4, f32[2,3,32,256]{3,2,1,0:T(8,128)S(1)} %bitcast.101, bf16[2,3,32,256]{3,2,1,0:T(8,128)(2,1)S(1)} %bitcast.103, f32[2,3,32,256]{3,2,1,0:T(8,128)S(1)} %bitcast.100, ...), custom_call_target="tpu_custom_call" | custom-call | tf_op jit(solution)/shard_map/columns/pallas_call | solution.py:288
  71.3 0.0 collective-permute-done.17
  71.3 0.6 slice_bitcast_fusion.2
  (30 shorter events, 0.5 us)
Async XLA Ops:
  0.6 24.1 %copy-start.1 = (f32[256,256]{1,0:T(8,128)S(1)}, f32[256,256]{1,0:T(8,128)}, u32[]{:S(2)}) copy-start(f32[256,256]{1,0:T(8,128)} %inv1.5) | copy-start | bytes 786436
  0.6 24.1 %copy-start.2 = (f32[256,256]{1,0:T(8,128)S(1)}, f32[256,256]{1,0:T(8,128)}, u32[]{:S(2)}) copy-start(f32[256,256]{1,0:T(8,128)} %inv2.5) | copy-start | bytes 786436
  0.7 24.1 %copy-start.3 = (s32[18]{0:T(128)S(1)}, s32[18]{0:T(128)}, u32[]{:S(2)}) copy-start(s32[18]{0:T(128)} %struct1.5) | copy-start | bytes 220
  0.7 24.1 %copy-start.4 = (s32[12]{0:T(128)S(1)}, s32[12]{0:T(128)}, u32[]{:S(2)}) copy-start(s32[12]{0:T(128)} %struct2.5) | copy-start | bytes 148
  1.8 4.9 %collective-permute-start = (bf16[2,3,32,256]{3,2,1,0:T(8,128)(2,1)S(1)}, bf16[2,3,32,256]{3,2,1,0:T(8,128)(2,1)S(1)}, u32[]{:S(2)}, u32[]{:S(2)}) collective-permute-start(bf16[2,3,32,256]{3,2,1,0:T(8,128)(2,1)S(1)} %get-tuple-element.82), channel_id=1, source_target_pairs={{0,0},{1,8},{2,16},{3,24},{4,4},{5,12},{6,20},{7,28},{8,1},{9,9},{... | collective-permute-start | bytes 294920 | tf_op jit(solution)/shard_map/ppermute | solution.py:194
  2.4 16.6 %collective-permute-start.1 = (bf16[2,3,32,256]{3,2,1,0:T(8,128)(2,1)S(1)}, bf16[2,3,32,256]{3,2,1,0:T(8,128)(2,1)S(1)}, u32[]{:S(2)}, u32[]{:S(2)}) collective-permute-start(bf16[2,3,32,256]{3,2,1,0:T(8,128)(2,1)S(1)} %get-tuple-element.83), channel_id=1, source_target_pairs={{0,4},{1,12},{2,20},{3,28},{4,0},{5,8},{6,16},{7,24},{8,5},{9,13},... | collective-permute-start | bytes 294920 | tf_op jit(solution)/shard_map/ppermute | solution.py:194
  6.5 18.1 %collective-permute-start.4 = (bf16[2,6,32,256]{3,2,1,0:T(8,128)(2,1)S(1)}, bf16[2,6,32,256]{3,2,1,0:T(8,128)(2,1)S(1)}, u32[]{:S(2)}, u32[]{:S(2)}) collective-permute-start(bf16[2,6,32,256]{3,2,1,0:T(8,128)(2,1)S(1)} %pad_maximum_fusion.3), channel_id=1, source_target_pairs={{0,4},{1,5},{2,6},{3,7},{4,0},{5,1},{6,2},{7,3},{8,12},{9,13},{10,... | collective-permute-start | bytes 589832 | tf_op jit(solution)/shard_map/ppermute | solution.py:154
  6.6 15.4 %collective-permute-start.2 = (bf16[2,3,32,256]{3,2,1,0:T(8,128)(2,1)S(1)}, bf16[2,3,32,256]{3,2,1,0:T(8,128)(2,1)S(1)}, u32[]{:S(2)}, u32[]{:S(2)}) collective-permute-start(bf16[2,3,32,256]{3,2,1,0:T(8,128)(2,1)S(1)} %collective-permute-done), channel_id=1, source_target_pairs={{0,16},{8,24},{16,0},{24,8},{1,17},{9,25},{17,1},{25,9},{2,18},{10... | collective-permute-start | bytes 294920 | tf_op jit(solution)/shard_map/ppermute | solution.py:154
  19.0 5.5 %collective-permute-start.3 = (bf16[2,3,32,256]{3,2,1,0:T(8,128)(2,1)S(1)}, bf16[2,3,32,256]{3,2,1,0:T(8,128)(2,1)S(1)}, u32[]{:S(2)}, u32[]{:S(2)}) collective-permute-start(bf16[2,3,32,256]{3,2,1,0:T(8,128)(2,1)S(1)} %collective-permute-done.1), channel_id=1, source_target_pairs={{0,16},{8,24},{16,0},{24,8},{1,17},{9,25},{17,1},{25,9},{2,18},{10... | collective-permute-start | bytes 294920 | tf_op jit(solution)/shard_map/ppermute | solution.py:154
  24.6 2.0 %copy-start = (bf16[6,1,3,1,256,256]{5,4,3,2,1,0:T(8,128)(2,1)S(1)}, bf16[6,1,3,1,256,256]{5,4,3,2,1,0:T(8,128)(2,1)}, u32[]{:S(2)}) copy-start(bf16[6,1,3,1,256,256]{5,4,3,2,1,0:T(8,128)(2,1)} %param.8) | copy-start | bytes 7077892
  24.7 1.8 %collective-permute-start.5 = (bf16[2,2,2,3,32,256]{5,4,3,2,1,0:T(8,128)(2,1)S(1)}, bf16[2,2,2,3,32,256]{5,4,3,2,1,0:T(8,128)(2,1)S(1)}, u32[]{:S(2)}, u32[]{:S(2)}) collective-permute-start(bf16[2,2,2,3,32,256]{5,4,3,2,1,0:T(8,128)(2,1)S(1)} %pad_maximum_fusion.1), channel_id=1, source_target_pairs={{0,8},{8,0},{16,24},{24,16},{1,9},{9,1},{17,25},{25,17},{2,10},{10... | collective-permute-start | bytes 1179656 | tf_op jit(solution)/shard_map/ppermute | solution.py:154
  26.5 5.0 %copy-start.5 = (bf16[256,256]{1,0:T(8,128)(2,1)S(1)}, bf16[256,256]{1,0:T(8,128)(2,1)}, u32[]{:S(2)}) copy-start(bf16[256,256]{1,0:T(8,128)(2,1)} %link.1) | copy-start | bytes 393220
  29.8 11.4 %collective-permute-start.8 = (bf16[4,2,3,32,256]{4,3,2,1,0:T(8,128)(2,1)S(1)}, bf16[4,2,3,32,256]{4,3,2,1,0:T(8,128)(2,1)S(1)}, u32[]{:S(2)}, u32[]{:S(2)}) collective-permute-start(bf16[4,2,3,32,256]{4,3,2,1,0:T(8,128)(2,1)S(1)} %get-tuple-element.49), channel_id=1, source_target_pairs={{0,2},{1,3},{2,0},{3,1},{4,6},{5,7},{6,4},{7,5},{8,10},{9,11},{10,... | collective-permute-start | bytes 1179656 | tf_op jit(solution)/shard_map/ppermute | solution.py:154
  30.4 11.4 %collective-permute-start.6 = (bf16[4,2,3,32,256]{4,3,2,1,0:T(8,128)(2,1)S(1)}, bf16[4,2,3,32,256]{4,3,2,1,0:T(8,128)(2,1)S(1)}, u32[]{:S(2)}, u32[]{:S(2)}) collective-permute-start(bf16[4,2,3,32,256]{4,3,2,1,0:T(8,128)(2,1)S(1)} %get-tuple-element.45), channel_id=1, source_target_pairs={{0,1},{1,0},{2,3},{3,2},{4,5},{5,4},{6,7},{7,6},{8,9},{9,8},{10,11... | collective-permute-start | bytes 1179656 | tf_op jit(solution)/shard_map/ppermute | solution.py:154
  41.4 6.4 %collective-permute-start.9 = (bf16[2,2,3,32,256]{4,3,2,1,0:T(8,128)(2,1)S(1)}, bf16[2,2,3,32,256]{4,3,2,1,0:T(8,128)(2,1)S(1)}, u32[]{:S(2)}, u32[]{:S(2)}) collective-permute-start(bf16[2,2,3,32,256]{4,3,2,1,0:T(8,128)(2,1)S(1)} %fusion.1), channel_id=1, source_target_pairs={{0,1},{1,0},{2,3},{3,2},{4,5},{5,4},{6,7},{7,6},{8,9},{9,8},{10,11... | collective-permute-start | bytes 589832 | tf_op jit(solution)/shard_map/ppermute | solution.py:154
  42.1 6.1 %collective-permute-start.7 = (bf16[2,2,3,32,256]{4,3,2,1,0:T(8,128)(2,1)S(1)}, bf16[2,2,3,32,256]{4,3,2,1,0:T(8,128)(2,1)S(1)}, u32[]{:S(2)}, u32[]{:S(2)}) collective-permute-start(bf16[2,2,3,32,256]{4,3,2,1,0:T(8,128)(2,1)S(1)} %fusion), channel_id=1, source_target_pairs={{0,2},{1,3},{2,0},{3,1},{4,6},{5,7},{6,4},{7,5},{8,10},{9,11},{10,... | collective-permute-start | bytes 589832 | tf_op jit(solution)/shard_map/ppermute | solution.py:154
  48.3 13.5 %collective-permute-start.13 = (bf16[2,1,2,3,32,256]{5,4,3,2,1,0:T(8,128)(2,1)S(1)}, bf16[2,1,2,3,32,256]{5,4,3,2,1,0:T(8,128)(2,1)S(1)}, u32[]{:S(2)}, u32[]{:S(2)}) collective-permute-start(bf16[2,1,2,3,32,256]{5,4,3,2,1,0:T(8,128)(2,1)S(1)} %pad_maximum_fusion.4), channel_id=1, source_target_pairs={{0,4},{1,5},{2,6},{3,7},{4,0},{5,1},{6,2},{7,3},{8,12},{9,13},{10,... | collective-permute-start | bytes 589832 | tf_op jit(solution)/shard_map/ppermute | solution.py:154
  52.2 5.2 %collective-permute-start.10 = (bf16[2,3,32,256]{3,2,1,0:T(8,128)(2,1)S(1)}, bf16[2,3,32,256]{3,2,1,0:T(8,128)(2,1)S(1)}, u32[]{:S(2)}, u32[]{:S(2)}) collective-permute-start(bf16[2,3,32,256]{3,2,1,0:T(8,128)(2,1)S(1)} %get-tuple-element.77), channel_id=1, source_target_pairs={{0,1},{1,0},{2,3},{3,2},{4,5},{5,4},{6,7},{7,6},{8,9},{9,8},{10,11... | collective-permute-start | bytes 294920 | tf_op jit(solution)/shard_map/ppermute | solution.py:154
  53.4 6.8 %collective-permute-start.11 = (bf16[2,3,32,256]{3,2,1,0:T(8,128)(2,1)S(1)}, bf16[2,3,32,256]{3,2,1,0:T(8,128)(2,1)S(1)}, u32[]{:S(2)}, u32[]{:S(2)}) collective-permute-start(bf16[2,3,32,256]{3,2,1,0:T(8,128)(2,1)S(1)} %get-tuple-element.78), channel_id=1, source_target_pairs={{0,2},{1,3},{2,0},{3,1},{4,6},{5,7},{6,4},{7,5},{8,10},{9,11},{10,... | collective-permute-start | bytes 294920 | tf_op jit(solution)/shard_map/ppermute | solution.py:154
  54.9 6.9 %collective-permute-start.12 = (bf16[2,3,32,256]{3,2,1,0:T(8,128)(2,1)S(1)}, bf16[2,3,32,256]{3,2,1,0:T(8,128)(2,1)S(1)}, u32[]{:S(2)}, u32[]{:S(2)}) collective-permute-start(bf16[2,3,32,256]{3,2,1,0:T(8,128)(2,1)S(1)} %get-tuple-element.79), channel_id=1, source_target_pairs={{0,3},{1,2},{2,1},{3,0},{4,7},{5,6},{6,5},{7,4},{8,11},{9,10},{10,... | collective-permute-start | bytes 294920 | tf_op jit(solution)/shard_map/ppermute | solution.py:154
  61.9 5.3 %collective-permute-start.14 = (bf16[3,32,256]{2,1,0:T(8,128)(2,1)S(1)}, bf16[3,32,256]{2,1,0:T(8,128)(2,1)S(1)}, u32[]{:S(2)}, u32[]{:S(2)}) collective-permute-start(bf16[3,32,256]{2,1,0:T(8,128)(2,1)S(1)} %get-tuple-element.88), channel_id=1, source_target_pairs={{0,4},{1,5},{2,6},{3,7},{4,0},{5,1},{6,2},{7,3},{8,12},{9,13},{10,... | collective-permute-start | bytes 147464 | tf_op jit(solution)/shard_map/ppermute | solution.py:154
  61.9 5.3 %collective-permute-start.15 = (bf16[3,32,256]{2,1,0:T(8,128)(2,1)S(1)}, bf16[3,32,256]{2,1,0:T(8,128)(2,1)S(1)}, u32[]{:S(2)}, u32[]{:S(2)}) collective-permute-start(bf16[3,32,256]{2,1,0:T(8,128)(2,1)S(1)} %get-tuple-element.87), channel_id=1, source_target_pairs={{0,16},{8,24},{16,0},{24,8},{1,17},{9,25},{17,1},{25,9},{2,18},{10... | collective-permute-start | bytes 147464 | tf_op jit(solution)/shard_map/ppermute | solution.py:154
  63.5 5.9 %collective-permute-start.16 = (bf16[3,32,256]{2,1,0:T(8,128)(2,1)S(1)}, bf16[3,32,256]{2,1,0:T(8,128)(2,1)S(1)}, u32[]{:S(2)}, u32[]{:S(2)}) collective-permute-start(bf16[3,32,256]{2,1,0:T(8,128)(2,1)S(1)} %get-tuple-element.88), channel_id=1, source_target_pairs={{0,20},{1,21},{2,22},{3,23},{4,16},{5,17},{6,18},{7,19},{8,28},{9,... | collective-permute-start | bytes 147464 | tf_op jit(solution)/shard_map/ppermute | solution.py:283
  69.4 1.9 %collective-permute-start.17 = (f32[3,32,256]{2,1,0:T(8,128)S(1)}, f32[3,32,256]{2,1,0:T(8,128)S(1)}, u32[]{:S(2)}, u32[]{:S(2)}) collective-permute-start(f32[3,32,256]{2,1,0:T(8,128)S(1)} %add_add_fusion.1), channel_id=1, source_target_pairs={{0,8},{8,0},{16,24},{24,16},{1,9},{9,1},{17,25},{25,17},{2,10},{10... | collective-permute-start | bytes 294920 | tf_op jit(solution)/shard_map/ppermute | solution.py:154

commit v6 on v3

--- a/solution.py
+++ b/solution.py
@@ -107,12 +107,13 @@
     out[...] = whole[:, place, :]
 
 
-def form_kernel(n_row, struct1, struct2, inv1, inv2, base, rows):
-    slices, _, blocks, slab, width = base.shape
-    for p, (struct, inverse) in enumerate(((struct1, inv1), (struct2, inv2))):
+def form_kernel(n_row, struct1, struct2, inv1, inv2, raw, other1, other2, after1, after2, rows):
+    _, blocks, slab, width = raw.shape
+    for p, (struct, inverse, other) in enumerate(((struct1, inv1, other1), (struct2, inv2, other2))):
         keep = listed(struct, blocks, n_row)
-        flat = base[:, p].astype(jnp.float32).reshape(slices * blocks * slab, width).astype(jnp.bfloat16)
-        product = split_dot(flat, inverse[...]).reshape(slices, blocks, slab, width)
+        both = [part.astype(jnp.float32).reshape(blocks * slab, width) for part in (raw[p], other[...])]
+        flat = jnp.concatenate(both, axis=0).astype(jnp.bfloat16)
+        product = split_dot(flat, inverse[...]).reshape(2, blocks, slab, width)
         rows[:, p] = jnp.where(keep[None], product, 0.0).astype(jnp.bfloat16)
 
 
@@ -197,8 +198,6 @@
                 moves.append((r * n_col + c, row * n_col + r + (s - t) % cycle * n_row))
         part = lax.dynamic_index_in_dim(turns, picks[s], 2, keepdims=False)
         got.append(lax.ppermute(part, ("row", "col"), moves))
-    base = jnp.stack([raw, swapped(raw, "col", n_col, n_col // 2)])
-
     pieces = {0: got}
     bit = n_row // 2
     while bit > 1:
@@ -206,17 +205,7 @@
             pieces[m ^ bit] = [swapped(part, "row", n_row, bit) for part in parts]
         bit //= 2
     pieces = jnp.stack([jnp.stack(pieces[m]) for m in sorted(pieces)])
-    pieces, base = lax.optimization_barrier((pieces, base))
-    rows = pl.pallas_call(
-        functools.partial(form_kernel, n_row),
-        out_shape=shape(base.shape, bf16),
-        in_specs=[SMEM, SMEM] + [VMEM] * 3,
-        out_specs=VMEM,
-        compiler_params=big,
-        name="form",
-        cost_estimate=pl.CostEstimate(flops=8 * width**3, bytes_accessed=4 * width**2, transcendentals=0),
-    )(struct_first, struct_second, inv_first, inv_second, base)
-    beside, rows = lax.optimization_barrier((swapped(pieces, "row", n_row, 1), rows))
+    beside = swapped(pieces, "row", n_row, 1)
     pieces = jnp.stack([pieces, beside], axis=1).reshape((n_row,) + pieces.shape[1:])
 
     orders = (list(range(n_bits)), [1, 0] + list(range(2, n_bits)))
@@ -247,6 +236,17 @@
     )(panel_link, inv_first, inv_second, split[0])
 
     state = [(split[g], swapped(split[2 + g], "col", n_col, 1 << orders[g][0])) for g in range(2)]
+    raw, consts = lax.optimization_barrier((raw, consts))
+    others = [swapped(panel_rows, "col", n_col, n_col // 2) for panel_rows in raw]
+    rows = pl.pallas_call(
+        functools.partial(form_kernel, n_row),
+        out_shape=shape((2,) + raw.shape, bf16),
+        in_specs=[SMEM, SMEM] + [VMEM] * 5 + [ANY] * 2,
+        out_specs=VMEM,
+        compiler_params=big,
+        name="form",
+        cost_estimate=pl.CostEstimate(flops=8 * width**3, bytes_accessed=4 * width**2, transcendentals=0),
+    )(struct_first, struct_second, inv_first, inv_second, raw, *others, state[0][1], state[1][1])
     left = [sorted(set(range(n_bits)) - {order[0]}) for order in orders]
     for i in range(1, n_bits):
         totals, last = [], []

time: 71.7 us -> 72.7 us (1.014)
  starting transfers between devices: 32.7 us -> 37.9 us
  waiting for transfers between devices: 25.4 us -> 21.1 us
    ppermute x16 -> x17, starting transfers between devices: 27.7 us -> 32.6 us  [swapped(): return lax.ppermute(value, axis, [(i, i ^ mask) for i in range(size)])]
    ppermute x16 -> x17, waiting for transfers between devices: 24.6 us -> 20.2 us  [swapped(): return lax.ppermute(value, axis, [(i, i ^ mask) for i in range(size)])]
  transfers between devices with their start and end apart: 19 -> 20, of which waited for: 11 -> 9; matrix products, arithmetic and copies ran while one was open for 1% -> 1% of each run, Pallas kernels for 8% -> 7%
where the time goes in v6:
time: 72.7 us; the launch traced here: 72.5 us
  starting transfers between devices  37.9 us (52%)
  waiting for transfers between devices  21.1 us (29%)
  Pallas kernels  9.68 us (13%)
  other arithmetic  1.83 us (3%)
  between operations  1.04 us (1%)
  local copies, waits for them, and re-layouts  0.94 us (1%)
    ppermute x17, starting transfers between devices, swapped(): return lax.ppermute(value, axis, [(i, i ^ mask) for i in range(size)])  32.6 us
    ppermute x17, waiting for transfers between devices, swapped(): return lax.ppermute(value, axis, [(i, i ^ mask) for i in range(size)])  20.2 us
    ppermute x2, starting transfers between devices, body(): got.append(lax.ppermute(part, ('row', 'col'), moves))  4.77 us
    pallas_call x1, Pallas kernels, body(): pl.pallas_call(functools.partial(product_kernel, n_row, n_col, (orders[0]...  3.23 us
    pallas_call x1, Pallas kernels, body(): pl.pallas_call(prepare_kernel, out_shape=[shape((width, width), f32), sha...  2.18 us
    pallas_call x1, Pallas kernels, body(): pl.pallas_call(functools.partial(column_kernel, n_row), out_shape=[shape(...  1.77 us
    pallas_call x1, Pallas kernels, body(): pl.pallas_call(functools.partial(form_kernel, n_row), out_shape=shape((2,...  1.49 us
  transfers between devices with their start and end apart: 20, of which 9 were waited for; matrix products, arithmetic and copies ran while one was open for 1% of the time, Pallas kernels for 7%

profile of v6, /device:TPU:0, one launch (start us, length us, event | category | flops | bytes accessed | tf_op | source)
XLA Modules:
  0.0 72.5 jit_solution(15829806430945370403)
XLA Ops:
  0.7 1.1 %pad_maximum_fusion.2.raw = bf16[2,6,32,256]{3,2,1,0:T(8,128)(2,1)S(1)} fusion(bf16[1,6,32,256]{3,2,1,0:T(8,128)(2,1)} %bitcast.120, bf16[1,6,32,256]{3,2,1,0:T(8,128)(2,1)} %bitcast.121), kind=kLoop, calls=%fused_computation.12 | loop fusion | flops 98304 | bytes 393216 | tf_op jit(solution)/shard_map/stack | solution.py:190
  1.9 0.7 collective-permute-start
  2.6 4.1 %collective-permute-start.1 = (bf16[2,3,32,256]{3,2,1,0:T(8,128)(2,1)S(1)}, bf16[2,3,32,256]{3,2,1,0:T(8,128)(2,1)S(1)}, u32[]{:S(2)}, u32[]{:S(2)}) collective-permute-start(bf16[2,3,32,256]{3,2,1,0:T(8,128)(2,1)S(1)} %get-tuple-element.87), channel_id=1, source_target_pairs={{0,4},{1,12},{2,20},{3,28},{4,0},{5,8},{6,16},{7,24},{8,5},{9,13},... | collective-permute-start | bytes 294920 | tf_op jit(solution)/shard_map/ppermute | solution.py:200
  6.7 0.0 collective-permute-done
  6.7 7.4 %collective-permute-start.2 = (bf16[2,3,32,256]{3,2,1,0:T(8,128)(2,1)S(1)}, bf16[2,3,32,256]{3,2,1,0:T(8,128)(2,1)S(1)}, u32[]{:S(2)}, u32[]{:S(2)}) collective-permute-start(bf16[2,3,32,256]{3,2,1,0:T(8,128)(2,1)S(1)} %collective-permute-done), channel_id=1, source_target_pairs={{0,16},{8,24},{16,0},{24,8},{1,17},{9,25},{17,1},{25,9},{2,18},{10... | collective-permute-start | bytes 294920 | tf_op jit(solution)/shard_map/ppermute | solution.py:158
  14.1 0.0 collective-permute-done.1
  14.1 3.7 %collective-permute-start.3 = (bf16[2,3,32,256]{3,2,1,0:T(8,128)(2,1)S(1)}, bf16[2,3,32,256]{3,2,1,0:T(8,128)(2,1)S(1)}, u32[]{:S(2)}, u32[]{:S(2)}) collective-permute-start(bf16[2,3,32,256]{3,2,1,0:T(8,128)(2,1)S(1)} %collective-permute-done.1), channel_id=1, source_target_pairs={{0,16},{8,24},{16,0},{24,8},{1,17},{9,25},{17,1},{25,9},{2,18},{10... | collective-permute-start | bytes 294920 | tf_op jit(solution)/shard_map/ppermute | solution.py:158
  17.8 0.0 collective-permute-done.2
  17.8 2.8 %collective-permute-done.3 = bf16[2,3,32,256]{3,2,1,0:T(8,128)(2,1)S(1)} collective-permute-done((bf16[2,3,32,256]{3,2,1,0:T(8,128)(2,1)S(1)}, bf16[2,3,32,256]{3,2,1,0:T(8,128)(2,1)S(1)}, u32[]{:S(2)}, u32[]{:S(2)}) %collective-permute-start.3) | collective-permute-done | bytes 98336 | tf_op jit(solution)/shard_map/ppermute | solution.py:158
  20.6 0.1 fusion.15
  20.7 0.1 collective-permute-start.4
  20.8 1.7 %collective-permute-done.4 = bf16[2,2,2,3,32,256]{5,4,3,2,1,0:T(8,128)(2,1)S(1)} collective-permute-done((bf16[2,2,2,3,32,256]{5,4,3,2,1,0:T(8,128)(2,1)S(1)}, bf16[2,2,2,3,32,256]{5,4,3,2,1,0:T(8,128)(2,1)S(1)}, u32[]{:S(2)}, u32[]{:S(2)}) %collective-permute-start.4) | collective-permute-done | bytes 393248 | tf_op jit(solution)/shard_map/ppermute | solution.py:158
  22.5 0.1 pad_maximum_fusion
  22.6 3.2 %products.1 = (f32[4,2,3,32,256]{4,3,2,1,0:T(8,128)S(1)}, f32[4,2,3,32,256]{4,3,2,1,0:T(8,128)S(1)}, bf16[4,2,3,32,256]{4,3,2,1,0:T(8,128)(2,1)S(1)}, bf16[4,2,3,32,256]{4,3,2,1,0:T(8,128)(2,1)S(1)}) custom-call(s32[18]{0:T(128)S(1)} %copy-done.3, s32[12]{0:T(128)S(1)} %copy-done.4, f32[256,256]{1,0:T(8,128)S(1)} %copy-done.1, f32[256,256]{1,0:T(8,128)S(1)} %copy-done.2, ...), custom_call_target="tpu_custom_call" | custom-call | tf_op jit(solution)/shard_map/products/pallas_call | solution.py:215
  25.9 0.6 collective-permute-start.8
  26.4 0.9 %collective-permute-start.7 = (bf16[4,2,3,32,256]{4,3,2,1,0:T(8,128)(2,1)S(1)}, bf16[4,2,3,32,256]{4,3,2,1,0:T(8,128)(2,1)S(1)}, u32[]{:S(2)}, u32[]{:S(2)}) collective-permute-start(bf16[4,2,3,32,256]{4,3,2,1,0:T(8,128)(2,1)S(1)} %get-tuple-element.43), channel_id=1, source_target_pairs={{0,1},{1,0},{2,3},{3,2},{4,5},{5,4},{6,7},{7,6},{8,9},{9,8},{10,11... | collective-permute-start | bytes 1179656 | tf_op jit(solution)/shard_map/ppermute | solution.py:158
  27.3 2.2 %prepare.1 = (f32[256,256]{1,0:T(8,128)S(1)}, f32[3,32,256]{2,1,0:T(8,128)S(1)}) custom-call(bf16[256,256]{1,0:T(8,128)(2,1)S(1)} %copy-done.5, f32[256,256]{1,0:T(8,128)S(1)} %copy-done.1, f32[256,256]{1,0:T(8,128)S(1)} %copy-done.2, f32[4,2,3,32,256]{4,3,2,1,0:T(8,128)S(1)} %get-tuple-element.40.after), custom_call_target="tpu_custom_call" | custom-call | flops 1006632960 | bytes 524288 | tf_op jit(solution)/shard_map/prepare/pallas_call | solution.py:227
  29.5 5.3 %collective-permute-start.5 = (bf16[6,32,256]{2,1,0:T(8,128)(2,1)S(1)}, bf16[6,32,256]{2,1,0:T(8,128)(2,1)S(1)}, u32[]{:S(2)}, u32[]{:S(2)}) collective-permute-start(bf16[6,32,256]{2,1,0:T(8,128)(2,1)S(1)} %get-tuple-element.85), channel_id=1, source_target_pairs={{0,4},{1,5},{2,6},{3,7},{4,0},{5,1},{6,2},{7,3},{8,12},{9,13},{10,... | collective-permute-start | bytes 294920 | tf_op jit(solution)/shard_map/ppermute | solution.py:158
  34.8 0.1 collective-permute-start.6
  34.9 6.4 %collective-permute-done.8.after2 = bf16[4,2,3,32,256]{4,3,2,1,0:T(8,128)(2,1)S(1)} collective-permute-done((bf16[4,2,3,32,256]{4,3,2,1,0:T(8,128)(2,1)S(1)}, bf16[4,2,3,32,256]{4,3,2,1,0:T(8,128)(2,1)S(1)}, u32[]{:S(2)}, u32[]{:S(2)}) %collective-permute-start.8) | collective-permute-done | bytes 393248 | tf_op jit(solution)/shard_map/ppermute | solution.py:158
  41.3 0.1 convert_add_fusion
  41.5 0.9 %collective-permute-start.10 = (bf16[2,2,3,32,256]{4,3,2,1,0:T(8,128)(2,1)S(1)}, bf16[2,2,3,32,256]{4,3,2,1,0:T(8,128)(2,1)S(1)}, u32[]{:S(2)}, u32[]{:S(2)}) collective-permute-start(bf16[2,2,3,32,256]{4,3,2,1,0:T(8,128)(2,1)S(1)} %fusion.1), channel_id=1, source_target_pairs={{0,1},{1,0},{2,3},{3,2},{4,5},{5,4},{6,7},{7,6},{8,9},{9,8},{10,11... | collective-permute-start | bytes 589832 | tf_op jit(solution)/shard_map/ppermute | solution.py:158
  42.4 0.1 convert_add_fusion.1
  42.6 0.1 collective-permute-start.9
  42.7 0.0 collective-permute-done.6.other2
  42.7 1.5 %form.1.rows = bf16[2,2,6,32,256]{4,3,2,1,0:T(8,128)(2,1)S(1)} custom-call(s32[18]{0:T(128)S(1)} %copy-done.3, s32[12]{0:T(128)S(1)} %copy-done.4, f32[256,256]{1,0:T(8,128)S(1)} %copy-done.1, f32[256,256]{1,0:T(8,128)S(1)} %copy-done.2, bf16[2,6,32,256]{3,2,1,0:T(8,128)(2,1)S(1)} %pad_maximum_fusion.2.raw, ...), custom_call_target="tpu_custom_call" | custom-call | flops 134217728 | bytes 262144 | tf_op jit(solution)/shard_map/form/pallas_call | solution.py:241
  44.2 3.3 %collective-permute-done.10 = bf16[2,2,3,32,256]{4,3,2,1,0:T(8,128)(2,1)S(1)} collective-permute-done((bf16[2,2,3,32,256]{4,3,2,1,0:T(8,128)(2,1)S(1)}, bf16[2,2,3,32,256]{4,3,2,1,0:T(8,128)(2,1)S(1)}, u32[]{:S(2)}, u32[]{:S(2)}) %collective-permute-start.10) | collective-permute-done | bytes 196640 | tf_op jit(solution)/shard_map/ppermute | solution.py:158
  47.6 0.8 %collective-permute-done.9 = bf16[2,2,3,32,256]{4,3,2,1,0:T(8,128)(2,1)S(1)} collective-permute-done((bf16[2,2,3,32,256]{4,3,2,1,0:T(8,128)(2,1)S(1)}, bf16[2,2,3,32,256]{4,3,2,1,0:T(8,128)(2,1)S(1)}, u32[]{:S(2)}, u32[]{:S(2)}) %collective-permute-start.9) | collective-permute-done | bytes 196640 | tf_op jit(solution)/shard_map/ppermute | solution.py:158
  48.4 1.0 %sums.1 = f32[2,8,3,32,128]{4,3,2,1,0:T(8,128)S(1)} custom-call(bf16[2,2,6,32,256]{4,3,2,1,0:T(8,128)(2,1)S(1)} %form.1.rows, f32[2,2,3,32,256]{4,3,2,1,0:T(8,128)S(1)} %bitcast_add_fusion.2.total_low, f32[2,2,3,32,256]{4,3,2,1,0:T(8,128)S(1)} %bitcast_add_fusion.1.total_high, f32[256,256]{1,0:T(8,128)S(1)} %get-tuple-element.50.linked, ...), custom_call_target="tpu_custom_call" | custom-call | tf_op jit(solution)/shard_map/sums/pallas_call | solution.py:268
  49.5 0.1 collective-permute-start.11
  49.7 1.6 %collective-permute-done.11 = f32[8,3,32,128]{3,2,1,0:T(8,128)S(1)} collective-permute-done((f32[8,3,32,128]{3,2,1,0:T(8,128)S(1)}, f32[8,3,32,128]{3,2,1,0:T(8,128)S(1)}, u32[]{:S(2)}, u32[]{:S(2)}) %collective-permute-start.11) | collective-permute-done | bytes 393248 | tf_op jit(solution)/shard_map/ppermute | solution.py:158
  51.3 0.1 bitcast_add_fusion
  51.4 1.2 %collective-permute-start.12 = (bf16[2,3,32,128]{3,2,1,0:T(8,128)(2,1)S(1)}, bf16[2,3,32,128]{3,2,1,0:T(8,128)(2,1)S(1)}, u32[]{:S(2)}, u32[]{:S(2)}) collective-permute-start(bf16[2,3,32,128]{3,2,1,0:T(8,128)(2,1)S(1)} %get-tuple-element.77), channel_id=1, source_target_pairs={{0,1},{1,0},{2,3},{3,2},{4,5},{5,4},{6,7},{7,6},{8,9},{9,8},{10,11... | collective-permute-start | bytes 147464 | tf_op jit(solution)/shard_map/ppermute | solution.py:158
  52.6 0.3 collective-permute-start.13
  52.9 2.0 %collective-permute-start.14 = (bf16[2,3,32,128]{3,2,1,0:T(8,128)(2,1)S(1)}, bf16[2,3,32,128]{3,2,1,0:T(8,128)(2,1)S(1)}, u32[]{:S(2)}, u32[]{:S(2)}) collective-permute-start(bf16[2,3,32,128]{3,2,1,0:T(8,128)(2,1)S(1)} %get-tuple-element.78), channel_id=1, source_target_pairs={{0,3},{1,2},{2,1},{3,0},{4,7},{5,6},{6,5},{7,4},{8,11},{9,10},{10,... | collective-permute-start | bytes 147464 | tf_op jit(solution)/shard_map/ppermute | solution.py:158
  54.9 3.4 %collective-permute-start.18 = (bf16[2,1,2,3,32,256]{5,4,3,2,1,0:T(8,128)(2,1)S(1)}, bf16[2,1,2,3,32,256]{5,4,3,2,1,0:T(8,128)(2,1)S(1)}, u32[]{:S(2)}, u32[]{:S(2)}) collective-permute-start(bf16[2,1,2,3,32,256]{5,4,3,2,1,0:T(8,128)(2,1)S(1)} %pad_maximum_fusion.3), channel_id=1, source_target_pairs={{0,4},{1,5},{2,6},{3,7},{4,0},{5,1},{6,2},{7,3},{8,12},{9,13},{10,... | collective-permute-start | bytes 589832 | tf_op jit(solution)/shard_map/ppermute | solution.py:158
  58.4 0.0 collective-permute-done.12
  58.4 0.0 collective-permute-done.13
  58.4 0.0 collective-permute-done.14
  58.4 5.5 %collective-permute-start.15 = (bf16[3,32,128]{2,1,0:T(8,128)(2,1)S(1)}, bf16[3,32,128]{2,1,0:T(8,128)(2,1)S(1)}, u32[]{:S(2)}, u32[]{:S(2)}) collective-permute-start(bf16[3,32,128]{2,1,0:T(8,128)(2,1)S(1)} %get-tuple-element.94), channel_id=1, source_target_pairs={{0,4},{1,5},{2,6},{3,7},{4,0},{5,1},{6,2},{7,3},{8,12},{9,13},{10,... | collective-permute-start | bytes 73736 | tf_op jit(solution)/shard_map/ppermute | solution.py:158
  63.9 0.5 collective-permute-start.17
  64.4 1.0 %collective-permute-start.16 = (bf16[3,32,128]{2,1,0:T(8,128)(2,1)S(1)}, bf16[3,32,128]{2,1,0:T(8,128)(2,1)S(1)}, u32[]{:S(2)}, u32[]{:S(2)}) collective-permute-start(bf16[3,32,128]{2,1,0:T(8,128)(2,1)S(1)} %get-tuple-element.93), channel_id=1, source_target_pairs={{0,16},{8,24},{16,0},{24,8},{1,17},{9,25},{17,1},{25,9},{2,18},{10... | collective-permute-start | bytes 73736 | tf_op jit(solution)/shard_map/ppermute | solution.py:158
  65.5 3.3 %collective-permute-done.18 = bf16[2,1,2,3,32,256]{5,4,3,2,1,0:T(8,128)(2,1)S(1)} collective-permute-done((bf16[2,1,2,3,32,256]{5,4,3,2,1,0:T(8,128)(2,1)S(1)}, bf16[2,1,2,3,32,256]{5,4,3,2,1,0:T(8,128)(2,1)S(1)}, u32[]{:S(2)}, u32[]{:S(2)}) %collective-permute-start.18) | collective-permute-done | bytes 196640 | tf_op jit(solution)/shard_map/ppermute | solution.py:158
  68.8 0.2 collective-permute-done.15
  69.1 0.9 %collective-permute-done.17 = bf16[3,32,128]{2,1,0:T(8,128)(2,1)S(1)} collective-permute-done((bf16[3,32,128]{2,1,0:T(8,128)(2,1)S(1)}, bf16[3,32,128]{2,1,0:T(8,128)(2,1)S(1)}, u32[]{:S(2)}, u32[]{:S(2)}) %collective-permute-start.17) | collective-permute-done | bytes 24608 | tf_op jit(solution)/shard_map/ppermute | solution.py:289
  70.0 0.1 collective-permute-start.19
  70.1 1.8 %columns.1 = (f32[6,32,256]{2,1,0:T(8,128)}, f32[6,32,256]{2,1,0:T(8,128)}) custom-call(s32[18]{0:T(128)S(1)} %copy-done.3, s32[12]{0:T(128)S(1)} %copy-done.4, f32[2,3,32,256]{3,2,1,0:T(8,128)S(1)} %bitcast.109, bf16[2,3,32,256]{3,2,1,0:T(8,128)(2,1)S(1)} %bitcast.111, f32[2,3,32,256]{3,2,1,0:T(8,128)S(1)} %bitcast.108, ...), custom_call_target="tpu_custom_call" | custom-call | tf_op jit(solution)/shard_map/columns/pallas_call | solution.py:295
  71.9 0.6 slice_bitcast_fusion.4
  (37 shorter events, 0.6 us)
Async XLA Ops:
  0.6 21.9 %copy-start = (bf16[6,1,3,1,256,256]{5,4,3,2,1,0:T(8,128)(2,1)S(1)}, bf16[6,1,3,1,256,256]{5,4,3,2,1,0:T(8,128)(2,1)}, u32[]{:S(2)}) copy-start(bf16[6,1,3,1,256,256]{5,4,3,2,1,0:T(8,128)(2,1)} %param.8) | copy-start | bytes 7077892
  0.6 21.9 %copy-start.1 = (f32[256,256]{1,0:T(8,128)S(1)}, f32[256,256]{1,0:T(8,128)}, u32[]{:S(2)}) copy-start(f32[256,256]{1,0:T(8,128)} %inv1.5) | copy-start | bytes 786436
  0.7 21.9 %copy-start.2 = (f32[256,256]{1,0:T(8,128)S(1)}, f32[256,256]{1,0:T(8,128)}, u32[]{:S(2)}) copy-start(f32[256,256]{1,0:T(8,128)} %inv2.5) | copy-start | bytes 786436
  0.7 21.9 %copy-start.3 = (s32[18]{0:T(128)S(1)}, s32[18]{0:T(128)}, u32[]{:S(2)}) copy-start(s32[18]{0:T(128)} %struct1.5) | copy-start | bytes 220
  0.7 21.9 %copy-start.4 = (s32[12]{0:T(128)S(1)}, s32[12]{0:T(128)}, u32[]{:S(2)}) copy-start(s32[12]{0:T(128)} %struct2.5) | copy-start | bytes 148
  1.9 4.8 %collective-permute-start = (bf16[2,3,32,256]{3,2,1,0:T(8,128)(2,1)S(1)}, bf16[2,3,32,256]{3,2,1,0:T(8,128)(2,1)S(1)}, u32[]{:S(2)}, u32[]{:S(2)}) collective-permute-start(bf16[2,3,32,256]{3,2,1,0:T(8,128)(2,1)S(1)} %get-tuple-element.86), channel_id=1, source_target_pairs={{0,0},{1,8},{2,16},{3,24},{4,4},{5,12},{6,20},{7,28},{8,1},{9,9},{... | collective-permute-start | bytes 294920 | tf_op jit(solution)/shard_map/ppermute | solution.py:200
  2.6 11.5 %collective-permute-start.1 = (bf16[2,3,32,256]{3,2,1,0:T(8,128)(2,1)S(1)}, bf16[2,3,32,256]{3,2,1,0:T(8,128)(2,1)S(1)}, u32[]{:S(2)}, u32[]{:S(2)}) collective-permute-start(bf16[2,3,32,256]{3,2,1,0:T(8,128)(2,1)S(1)} %get-tuple-element.87), channel_id=1, source_target_pairs={{0,4},{1,12},{2,20},{3,28},{4,0},{5,8},{6,16},{7,24},{8,5},{9,13},... | collective-permute-start | bytes 294920 | tf_op jit(solution)/shard_map/ppermute | solution.py:200
  6.7 11.1 %collective-permute-start.2 = (bf16[2,3,32,256]{3,2,1,0:T(8,128)(2,1)S(1)}, bf16[2,3,32,256]{3,2,1,0:T(8,128)(2,1)S(1)}, u32[]{:S(2)}, u32[]{:S(2)}) collective-permute-start(bf16[2,3,32,256]{3,2,1,0:T(8,128)(2,1)S(1)} %collective-permute-done), channel_id=1, source_target_pairs={{0,16},{8,24},{16,0},{24,8},{1,17},{9,25},{17,1},{25,9},{2,18},{10... | collective-permute-start | bytes 294920 | tf_op jit(solution)/shard_map/ppermute | solution.py:158
  14.1 6.5 %collective-permute-start.3 = (bf16[2,3,32,256]{3,2,1,0:T(8,128)(2,1)S(1)}, bf16[2,3,32,256]{3,2,1,0:T(8,128)(2,1)S(1)}, u32[]{:S(2)}, u32[]{:S(2)}) collective-permute-start(bf16[2,3,32,256]{3,2,1,0:T(8,128)(2,1)S(1)} %collective-permute-done.1), channel_id=1, source_target_pairs={{0,16},{8,24},{16,0},{24,8},{1,17},{9,25},{17,1},{25,9},{2,18},{10... | collective-permute-start | bytes 294920 | tf_op jit(solution)/shard_map/ppermute | solution.py:158
  20.7 1.8 %collective-permute-start.4 = (bf16[2,2,2,3,32,256]{5,4,3,2,1,0:T(8,128)(2,1)S(1)}, bf16[2,2,2,3,32,256]{5,4,3,2,1,0:T(8,128)(2,1)S(1)}, u32[]{:S(2)}, u32[]{:S(2)}) collective-permute-start(bf16[2,2,2,3,32,256]{5,4,3,2,1,0:T(8,128)(2,1)S(1)} %get-tuple-element.81), channel_id=1, source_target_pairs={{0,8},{8,0},{16,24},{24,16},{1,9},{9,1},{17,25},{25,17},{2,10},{10... | collective-permute-start | bytes 1179656 | tf_op jit(solution)/shard_map/ppermute | solution.py:158
  22.5 4.8 %copy-start.5 = (bf16[256,256]{1,0:T(8,128)(2,1)S(1)}, bf16[256,256]{1,0:T(8,128)(2,1)}, u32[]{:S(2)}) copy-start(bf16[256,256]{1,0:T(8,128)(2,1)} %link.1) | copy-start | bytes 393220
  25.9 15.4 %collective-permute-start.8 = (bf16[4,2,3,32,256]{4,3,2,1,0:T(8,128)(2,1)S(1)}, bf16[4,2,3,32,256]{4,3,2,1,0:T(8,128)(2,1)S(1)}, u32[]{:S(2)}, u32[]{:S(2)}) collective-permute-start(bf16[4,2,3,32,256]{4,3,2,1,0:T(8,128)(2,1)S(1)} %get-tuple-element.44), channel_id=1, source_target_pairs={{0,2},{1,3},{2,0},{3,1},{4,6},{5,7},{6,4},{7,5},{8,10},{9,11},{10,... | collective-permute-start | bytes 1179656 | tf_op jit(solution)/shard_map/ppermute | solution.py:158
  26.4 16.0 %collective-permute-start.7 = (bf16[4,2,3,32,256]{4,3,2,1,0:T(8,128)(2,1)S(1)}, bf16[4,2,3,32,256]{4,3,2,1,0:T(8,128)(2,1)S(1)}, u32[]{:S(2)}, u32[]{:S(2)}) collective-permute-start(bf16[4,2,3,32,256]{4,3,2,1,0:T(8,128)(2,1)S(1)} %get-tuple-element.43), channel_id=1, source_target_pairs={{0,1},{1,0},{2,3},{3,2},{4,5},{5,4},{6,7},{7,6},{8,9},{9,8},{10,11... | collective-permute-start | bytes 1179656 | tf_op jit(solution)/shard_map/ppermute | solution.py:158
  29.5 13.2 %collective-permute-start.5 = (bf16[6,32,256]{2,1,0:T(8,128)(2,1)S(1)}, bf16[6,32,256]{2,1,0:T(8,128)(2,1)S(1)}, u32[]{:S(2)}, u32[]{:S(2)}) collective-permute-start(bf16[6,32,256]{2,1,0:T(8,128)(2,1)S(1)} %get-tuple-element.85), channel_id=1, source_target_pairs={{0,4},{1,5},{2,6},{3,7},{4,0},{5,1},{6,2},{7,3},{8,12},{9,13},{10,... | collective-permute-start | bytes 294920 | tf_op jit(solution)/shard_map/ppermute | solution.py:158
  34.8 7.9 %collective-permute-start.6 = (bf16[6,32,256]{2,1,0:T(8,128)(2,1)S(1)}, bf16[6,32,256]{2,1,0:T(8,128)(2,1)S(1)}, u32[]{:S(2)}, u32[]{:S(2)}) collective-permute-start(bf16[6,32,256]{2,1,0:T(8,128)(2,1)S(1)} %get-tuple-element.84), channel_id=1, source_target_pairs={{0,4},{1,5},{2,6},{3,7},{4,0},{5,1},{6,2},{7,3},{8,12},{9,13},{10,... | collective-permute-start | bytes 294920 | tf_op jit(solution)/shard_map/ppermute | solution.py:158
  41.5 6.0 %collective-permute-start.10 = (bf16[2,2,3,32,256]{4,3,2,1,0:T(8,128)(2,1)S(1)}, bf16[2,2,3,32,256]{4,3,2,1,0:T(8,128)(2,1)S(1)}, u32[]{:S(2)}, u32[]{:S(2)}) collective-permute-start(bf16[2,2,3,32,256]{4,3,2,1,0:T(8,128)(2,1)S(1)} %fusion.1), channel_id=1, source_target_pairs={{0,1},{1,0},{2,3},{3,2},{4,5},{5,4},{6,7},{7,6},{8,9},{9,8},{10,11... | collective-permute-start | bytes 589832 | tf_op jit(solution)/shard_map/ppermute | solution.py:158
  42.6 5.7 %collective-permute-start.9 = (bf16[2,2,3,32,256]{4,3,2,1,0:T(8,128)(2,1)S(1)}, bf16[2,2,3,32,256]{4,3,2,1,0:T(8,128)(2,1)S(1)}, u32[]{:S(2)}, u32[]{:S(2)}) collective-permute-start(bf16[2,2,3,32,256]{4,3,2,1,0:T(8,128)(2,1)S(1)} %fusion), channel_id=1, source_target_pairs={{0,2},{1,3},{2,0},{3,1},{4,6},{5,7},{6,4},{7,5},{8,10},{9,11},{10,... | collective-permute-start | bytes 589832 | tf_op jit(solution)/shard_map/ppermute | solution.py:158
  49.5 1.8 %collective-permute-start.11 = (f32[8,3,32,128]{3,2,1,0:T(8,128)S(1)}, f32[8,3,32,128]{3,2,1,0:T(8,128)S(1)}, u32[]{:S(2)}, u32[]{:S(2)}) collective-permute-start(f32[8,3,32,128]{3,2,1,0:T(8,128)S(1)} %dynamic-slice_bitcast_fusion), channel_id=1, source_target_pairs={{0,8},{8,0},{16,24},{24,16},{1,9},{9,1},{17,25},{25,17},{2,10},{10... | collective-permute-start | bytes 1179656 | tf_op jit(solution)/shard_map/ppermute | solution.py:158
  51.4 7.0 %collective-permute-start.12 = (bf16[2,3,32,128]{3,2,1,0:T(8,128)(2,1)S(1)}, bf16[2,3,32,128]{3,2,1,0:T(8,128)(2,1)S(1)}, u32[]{:S(2)}, u32[]{:S(2)}) collective-permute-start(bf16[2,3,32,128]{3,2,1,0:T(8,128)(2,1)S(1)} %get-tuple-element.77), channel_id=1, source_target_pairs={{0,1},{1,0},{2,3},{3,2},{4,5},{5,4},{6,7},{7,6},{8,9},{9,8},{10,11... | collective-permute-start | bytes 147464 | tf_op jit(solution)/shard_map/ppermute | solution.py:158
  52.6 5.8 %collective-permute-start.13 = (bf16[2,3,32,128]{3,2,1,0:T(8,128)(2,1)S(1)}, bf16[2,3,32,128]{3,2,1,0:T(8,128)(2,1)S(1)}, u32[]{:S(2)}, u32[]{:S(2)}) collective-permute-start(bf16[2,3,32,128]{3,2,1,0:T(8,128)(2,1)S(1)} %get-tuple-element.79), channel_id=1, source_target_pairs={{0,2},{1,3},{2,0},{3,1},{4,6},{5,7},{6,4},{7,5},{8,10},{9,11},{10,... | collective-permute-start | bytes 147464 | tf_op jit(solution)/shard_map/ppermute | solution.py:158
  52.9 5.5 %collective-permute-start.14 = (bf16[2,3,32,128]{3,2,1,0:T(8,128)(2,1)S(1)}, bf16[2,3,32,128]{3,2,1,0:T(8,128)(2,1)S(1)}, u32[]{:S(2)}, u32[]{:S(2)}) collective-permute-start(bf16[2,3,32,128]{3,2,1,0:T(8,128)(2,1)S(1)} %get-tuple-element.78), channel_id=1, source_target_pairs={{0,3},{1,2},{2,1},{3,0},{4,7},{5,6},{6,5},{7,4},{8,11},{9,10},{10,... | collective-permute-start | bytes 147464 | tf_op jit(solution)/shard_map/ppermute | solution.py:158
  54.9 13.8 %collective-permute-start.18 = (bf16[2,1,2,3,32,256]{5,4,3,2,1,0:T(8,128)(2,1)S(1)}, bf16[2,1,2,3,32,256]{5,4,3,2,1,0:T(8,128)(2,1)S(1)}, u32[]{:S(2)}, u32[]{:S(2)}) collective-permute-start(bf16[2,1,2,3,32,256]{5,4,3,2,1,0:T(8,128)(2,1)S(1)} %pad_maximum_fusion.3), channel_id=1, source_target_pairs={{0,4},{1,5},{2,6},{3,7},{4,0},{5,1},{6,2},{7,3},{8,12},{9,13},{10,... | collective-permute-start | bytes 589832 | tf_op jit(solution)/shard_map/ppermute | solution.py:158
  58.4 10.6 %collective-permute-start.15 = (bf16[3,32,128]{2,1,0:T(8,128)(2,1)S(1)}, bf16[3,32,128]{2,1,0:T(8,128)(2,1)S(1)}, u32[]{:S(2)}, u32[]{:S(2)}) collective-permute-start(bf16[3,32,128]{2,1,0:T(8,128)(2,1)S(1)} %get-tuple-element.94), channel_id=1, source_target_pairs={{0,4},{1,5},{2,6},{3,7},{4,0},{5,1},{6,2},{7,3},{8,12},{9,13},{10,... | collective-permute-start | bytes 73736 | tf_op jit(solution)/shard_map/ppermute | solution.py:158
  63.9 6.0 %collective-permute-start.17 = (bf16[3,32,128]{2,1,0:T(8,128)(2,1)S(1)}, bf16[3,32,128]{2,1,0:T(8,128)(2,1)S(1)}, u32[]{:S(2)}, u32[]{:S(2)}) collective-permute-start(bf16[3,32,128]{2,1,0:T(8,128)(2,1)S(1)} %get-tuple-element.94), channel_id=1, source_target_pairs={{0,20},{1,21},{2,22},{3,23},{4,16},{5,17},{6,18},{7,19},{8,28},{9,... | collective-permute-start | bytes 73736 | tf_op jit(solution)/shard_map/ppermute | solution.py:289
  64.4 4.6 %collective-permute-start.16 = (bf16[3,32,128]{2,1,0:T(8,128)(2,1)S(1)}, bf16[3,32,128]{2,1,0:T(8,128)(2,1)S(1)}, u32[]{:S(2)}, u32[]{:S(2)}) collective-permute-start(bf16[3,32,128]{2,1,0:T(8,128)(2,1)S(1)} %get-tuple-element.93), channel_id=1, source_target_pairs={{0,16},{8,24},{16,0},{24,8},{1,17},{9,25},{17,1},{25,9},{2,18},{10... | collective-permute-start | bytes 73736 | tf_op jit(solution)/shard_map/ppermute | solution.py:158
  70.0 1.9 %collective-permute-start.19 = (f32[3,32,128]{2,1,0:T(8,128)S(1)}, f32[3,32,128]{2,1,0:T(8,128)S(1)}, u32[]{:S(2)}, u32[]{:S(2)}) collective-permute-start(f32[3,32,128]{2,1,0:T(8,128)S(1)} %add_add_fusion), channel_id=1, source_target_pairs={{0,8},{8,0},{16,24},{24,16},{1,9},{9,1},{17,25},{25,17},{2,10},{10... | collective-permute-start | bytes 147464 | tf_op jit(solution)/shard_map/ppermute | solution.py:158

commit v7 on v3

--- a/solution.py
+++ b/solution.py
@@ -75,23 +75,20 @@
             factor[place, p * width : (p + 1) * width] = jnp.where(found[b] == 1, product[place], 0.0).astype(jnp.bfloat16)
 
     half = row_blocks // 2
-    step = 2 if row_blocks % 2 == 0 else 1
-    for a in range(0, row_blocks, step):
-        wide = [jnp.concatenate([stored[a + i, b] for b in range(col_blocks)], axis=1) for i in range(step)]
-        totals = jnp.dot(jnp.concatenate(wide, axis=0), factor[...], preferred_element_type=jnp.float32)
-        for i in range(step):
-            total = totals[i * width : (i + 1) * width]
-            group, place = divmod(a + i, half)
-            bit = first_bits[group]
-            upper = ((here_col >> bit) & 1) == 1
-            for p in range(2):
-                for j in range(n_col // 2):
-                    low = ((j >> bit) << (bit + 1)) | (j & ((1 << bit) - 1))
-                    high = low | (1 << bit)
-                    x = total[low * slab : (low + 1) * slab, p * width : (p + 1) * width]
-                    y = total[high * slab : (high + 1) * slab, p * width : (p + 1) * width]
-                    keeps[group][j, p, place] = jnp.where(upper, y, x)
-                    sends[group][j, p, place] = jnp.where(upper, x, y).astype(jnp.bfloat16)
+    for a in range(row_blocks):
+        wide = jnp.concatenate([stored[a, b] for b in range(col_blocks)], axis=1)
+        group, place = divmod(a, half)
+        bit = first_bits[group]
+        upper = ((here_col >> bit) & 1) == 1
+        for p in range(2):
+            total = jnp.dot(wide, factor[:, p * width : (p + 1) * width], preferred_element_type=jnp.float32)
+            for j in range(n_col // 2):
+                low = ((j >> bit) << (bit + 1)) | (j & ((1 << bit) - 1))
+                high = low | (1 << bit)
+                x = total[low * slab : (low + 1) * slab]
+                y = total[high * slab : (high + 1) * slab]
+                keeps[group][j, p, place] = jnp.where(upper, y, x)
+                sends[group][j, p, place] = jnp.where(upper, x, y).astype(jnp.bfloat16)
 
 
 def prepare_kernel(link, inv1, inv2, after, linked, out, whole):

time: 71.7 us -> 71.7 us (level)
  no operation moved by 1% of the time
where the time goes in v7:
time: 71.7 us; the launch traced here: 71.5 us
  starting transfers between devices  32.7 us (46%)
  waiting for transfers between devices  25.4 us (35%)
  Pallas kernels  9.69 us (14%)
  other arithmetic  1.73 us (2%)
  between operations  1.01 us (1%)
  local copies, waits for them, and re-layouts  0.92 us (1%)
    ppermute x16, starting transfers between devices, swapped(): return lax.ppermute(value, axis, [(i, i ^ mask) for i in range(size)])  27.7 us
    ppermute x16, waiting for transfers between devices, swapped(): return lax.ppermute(value, axis, [(i, i ^ mask) for i in range(size)])  24.6 us
    ppermute x2, starting transfers between devices, body(): got.append(lax.ppermute(part, ('row', 'col'), moves))  4.77 us
    pallas_call x1, Pallas kernels, body(): pl.pallas_call(functools.partial(product_kernel, n_row, n_col, (orders[0]...  3.23 us
    pallas_call x1, Pallas kernels, body(): pl.pallas_call(prepare_kernel, out_shape=[shape((width, width), f32), sha...  2.18 us
    pallas_call x1, Pallas kernels, body(): pl.pallas_call(functools.partial(column_kernel, n_row), out_shape=[shape(...  1.78 us
    pallas_call x1, Pallas kernels, body(): pl.pallas_call(functools.partial(form_kernel, n_row), out_shape=shape(bas...  1.49 us
  transfers between devices with their start and end apart: 19, of which 11 were waited for; matrix products, arithmetic and copies ran while one was open for 1% of the time, Pallas kernels for 8%

profile of v7, /device:TPU:0, one launch (start us, length us, event | category | flops | bytes accessed | tf_op | source)
XLA Modules:
  0.0 71.5 jit_solution(15732487619358099029)
XLA Ops:
  0.7 1.0 %pad_maximum_fusion.3 = bf16[2,6,32,256]{3,2,1,0:T(8,128)(2,1)S(1)} fusion(bf16[1,6,32,256]{3,2,1,0:T(8,128)(2,1)} %bitcast.120, bf16[1,6,32,256]{3,2,1,0:T(8,128)(2,1)} %bitcast.121), kind=kLoop, calls=%fused_computation.13 | loop fusion | flops 98304 | bytes 393216 | tf_op jit(solution)/shard_map/stack | solution.py:186
  1.8 0.7 collective-permute-start
  2.4 4.1 %collective-permute-start.1 = (bf16[2,3,32,256]{3,2,1,0:T(8,128)(2,1)S(1)}, bf16[2,3,32,256]{3,2,1,0:T(8,128)(2,1)S(1)}, u32[]{:S(2)}, u32[]{:S(2)}) collective-permute-start(bf16[2,3,32,256]{3,2,1,0:T(8,128)(2,1)S(1)} %get-tuple-element.87), channel_id=1, source_target_pairs={{0,4},{1,12},{2,20},{3,28},{4,0},{5,8},{6,16},{7,24},{8,5},{9,13},... | collective-permute-start | bytes 294920 | tf_op jit(solution)/shard_map/ppermute | solution.py:196
  6.5 0.1 collective-permute-start.4
  6.6 0.0 collective-permute-done
  6.6 12.4 %collective-permute-start.2 = (bf16[2,3,32,256]{3,2,1,0:T(8,128)(2,1)S(1)}, bf16[2,3,32,256]{3,2,1,0:T(8,128)(2,1)S(1)}, u32[]{:S(2)}, u32[]{:S(2)}) collective-permute-start(bf16[2,3,32,256]{3,2,1,0:T(8,128)(2,1)S(1)} %collective-permute-done), channel_id=1, source_target_pairs={{0,16},{8,24},{16,0},{24,8},{1,17},{9,25},{17,1},{25,9},{2,18},{10... | collective-permute-start | bytes 294920 | tf_op jit(solution)/shard_map/ppermute | solution.py:154
  19.0 0.0 collective-permute-done.1
  19.0 0.0 collective-permute-start.3
  19.1 3.0 %collective-permute-done.2 = bf16[2,3,32,256]{3,2,1,0:T(8,128)(2,1)S(1)} collective-permute-done((bf16[2,3,32,256]{3,2,1,0:T(8,128)(2,1)S(1)}, bf16[2,3,32,256]{3,2,1,0:T(8,128)(2,1)S(1)}, u32[]{:S(2)}, u32[]{:S(2)}) %collective-permute-start.2) | collective-permute-done | bytes 98336 | tf_op jit(solution)/shard_map/ppermute | solution.py:154
  22.1 2.5 %collective-permute-done.3 = bf16[2,3,32,256]{3,2,1,0:T(8,128)(2,1)S(1)} collective-permute-done((bf16[2,3,32,256]{3,2,1,0:T(8,128)(2,1)S(1)}, bf16[2,3,32,256]{3,2,1,0:T(8,128)(2,1)S(1)}, u32[]{:S(2)}, u32[]{:S(2)}) %collective-permute-start.3) | collective-permute-done | bytes 98336 | tf_op jit(solution)/shard_map/ppermute | solution.py:154
  24.6 0.0 collective-permute-done.4
  24.7 0.1 collective-permute-start.5
  24.8 1.5 %form.1.rows = bf16[2,2,6,32,256]{4,3,2,1,0:T(8,128)(2,1)S(1)} custom-call(s32[18]{0:T(128)S(1)} %copy-done.3, s32[12]{0:T(128)S(1)} %copy-done.4, f32[256,256]{1,0:T(8,128)S(1)} %copy-done.1, f32[256,256]{1,0:T(8,128)S(1)} %copy-done.2, bf16[2,2,6,32,256]{4,3,2,1,0:T(8,128)(2,1)S(1)} %pad_maximum_fusion.2.base), custom_call_target="tpu_custom_call" | custom-call | flops 134217728 | bytes 262144 | tf_op jit(solution)/shard_map/form/pallas_call | solution.py:207
  26.3 0.2 collective-permute-done.5
  26.5 0.1 pad_maximum_fusion
  26.6 3.2 %products.1 = (f32[4,2,3,32,256]{4,3,2,1,0:T(8,128)S(1)}, f32[4,2,3,32,256]{4,3,2,1,0:T(8,128)S(1)}, bf16[4,2,3,32,256]{4,3,2,1,0:T(8,128)(2,1)S(1)}, bf16[4,2,3,32,256]{4,3,2,1,0:T(8,128)(2,1)S(1)}) custom-call(s32[18]{0:T(128)S(1)} %copy-done.3, s32[12]{0:T(128)S(1)} %copy-done.4, f32[256,256]{1,0:T(8,128)S(1)} %copy-done.1, f32[256,256]{1,0:T(8,128)S(1)} %copy-done.2, ...), custom_call_target="tpu_custom_call" | custom-call | tf_op jit(solution)/shard_map/products/pallas_call | solution.py:223
  29.8 0.6 collective-permute-start.8
  30.4 1.1 %collective-permute-start.6 = (bf16[4,2,3,32,256]{4,3,2,1,0:T(8,128)(2,1)S(1)}, bf16[4,2,3,32,256]{4,3,2,1,0:T(8,128)(2,1)S(1)}, u32[]{:S(2)}, u32[]{:S(2)}) collective-permute-start(bf16[4,2,3,32,256]{4,3,2,1,0:T(8,128)(2,1)S(1)} %get-tuple-element.47), channel_id=1, source_target_pairs={{0,1},{1,0},{2,3},{3,2},{4,5},{5,4},{6,7},{7,6},{8,9},{9,8},{10,11... | collective-permute-start | bytes 1179656 | tf_op jit(solution)/shard_map/ppermute | solution.py:154
  31.5 2.2 %prepare.1 = (f32[256,256]{1,0:T(8,128)S(1)}, f32[3,32,256]{2,1,0:T(8,128)S(1)}) custom-call(bf16[256,256]{1,0:T(8,128)(2,1)S(1)} %copy-done.5, f32[256,256]{1,0:T(8,128)S(1)} %copy-done.1, f32[256,256]{1,0:T(8,128)S(1)} %copy-done.2, f32[4,2,3,32,256]{4,3,2,1,0:T(8,128)S(1)} %get-tuple-element.46.after), custom_call_target="tpu_custom_call" | custom-call | flops 1006632960 | bytes 524288 | tf_op jit(solution)/shard_map/prepare/pallas_call | solution.py:235
  33.7 7.5 %collective-permute-done.8 = bf16[4,2,3,32,256]{4,3,2,1,0:T(8,128)(2,1)S(1)} collective-permute-done((bf16[4,2,3,32,256]{4,3,2,1,0:T(8,128)(2,1)S(1)}, bf16[4,2,3,32,256]{4,3,2,1,0:T(8,128)(2,1)S(1)}, u32[]{:S(2)}, u32[]{:S(2)}) %collective-permute-start.8) | collective-permute-done | bytes 393248 | tf_op jit(solution)/shard_map/ppermute | solution.py:154
  41.2 0.1 convert_add_fusion
  41.4 0.5 collective-permute-start.9
  41.9 0.0 collective-permute-done.6
  41.9 0.1 convert_add_fusion.1
  42.1 1.3 %collective-permute-start.7 = (bf16[2,2,3,32,256]{4,3,2,1,0:T(8,128)(2,1)S(1)}, bf16[2,2,3,32,256]{4,3,2,1,0:T(8,128)(2,1)S(1)}, u32[]{:S(2)}, u32[]{:S(2)}) collective-permute-start(bf16[2,2,3,32,256]{4,3,2,1,0:T(8,128)(2,1)S(1)} %fusion), channel_id=1, source_target_pairs={{0,2},{1,3},{2,0},{3,1},{4,6},{5,7},{6,4},{7,5},{8,10},{9,11},{10,... | collective-permute-start | bytes 589832 | tf_op jit(solution)/shard_map/ppermute | solution.py:154
  43.3 4.5 %collective-permute-done.9 = bf16[2,2,3,32,256]{4,3,2,1,0:T(8,128)(2,1)S(1)} collective-permute-done((bf16[2,2,3,32,256]{4,3,2,1,0:T(8,128)(2,1)S(1)}, bf16[2,2,3,32,256]{4,3,2,1,0:T(8,128)(2,1)S(1)}, u32[]{:S(2)}, u32[]{:S(2)}) %collective-permute-start.9) | collective-permute-done | bytes 196640 | tf_op jit(solution)/shard_map/ppermute | solution.py:154
  47.8 0.3 collective-permute-done.7
  48.2 1.0 %sums.1 = f32[2,8,3,32,128]{4,3,2,1,0:T(8,128)S(1)} custom-call(bf16[2,2,6,32,256]{4,3,2,1,0:T(8,128)(2,1)S(1)} %form.1.rows, f32[2,2,3,32,256]{4,3,2,1,0:T(8,128)S(1)} %bitcast_add_fusion.2.total_low, f32[2,2,3,32,256]{4,3,2,1,0:T(8,128)S(1)} %bitcast_add_fusion.1.total_high, f32[256,256]{1,0:T(8,128)S(1)} %get-tuple-element.54.linked, ...), custom_call_target="tpu_custom_call" | custom-call | tf_op jit(solution)/shard_map/sums/pallas_call | solution.py:265
  49.3 0.1 collective-permute-start.10
  49.5 1.6 %collective-permute-done.10 = f32[8,3,32,128]{3,2,1,0:T(8,128)S(1)} collective-permute-done((f32[8,3,32,128]{3,2,1,0:T(8,128)S(1)}, f32[8,3,32,128]{3,2,1,0:T(8,128)S(1)}, u32[]{:S(2)}, u32[]{:S(2)}) %collective-permute-start.10) | collective-permute-done | bytes 393248 | tf_op jit(solution)/shard_map/ppermute | solution.py:154
  51.1 0.1 bitcast_add_fusion
  51.2 1.7 %collective-permute-start.11 = (bf16[2,3,32,128]{3,2,1,0:T(8,128)(2,1)S(1)}, bf16[2,3,32,128]{3,2,1,0:T(8,128)(2,1)S(1)}, u32[]{:S(2)}, u32[]{:S(2)}) collective-permute-start(bf16[2,3,32,128]{3,2,1,0:T(8,128)(2,1)S(1)} %get-tuple-element.81), channel_id=1, source_target_pairs={{0,1},{1,0},{2,3},{3,2},{4,5},{5,4},{6,7},{7,6},{8,9},{9,8},{10,11... | collective-permute-start | bytes 147464 | tf_op jit(solution)/shard_map/ppermute | solution.py:154
  52.9 0.5 collective-permute-start.12
  53.4 1.3 %collective-permute-start.13 = (bf16[2,3,32,128]{3,2,1,0:T(8,128)(2,1)S(1)}, bf16[2,3,32,128]{3,2,1,0:T(8,128)(2,1)S(1)}, u32[]{:S(2)}, u32[]{:S(2)}) collective-permute-start(bf16[2,3,32,128]{3,2,1,0:T(8,128)(2,1)S(1)} %get-tuple-element.82), channel_id=1, source_target_pairs={{0,3},{1,2},{2,1},{3,0},{4,7},{5,6},{6,5},{7,4},{8,11},{9,10},{10,... | collective-permute-start | bytes 147464 | tf_op jit(solution)/shard_map/ppermute | solution.py:154
  54.7 2.8 %collective-permute-start.17 = (bf16[2,1,2,3,32,256]{5,4,3,2,1,0:T(8,128)(2,1)S(1)}, bf16[2,1,2,3,32,256]{5,4,3,2,1,0:T(8,128)(2,1)S(1)}, u32[]{:S(2)}, u32[]{:S(2)}) collective-permute-start(bf16[2,1,2,3,32,256]{5,4,3,2,1,0:T(8,128)(2,1)S(1)} %pad_maximum_fusion.4), channel_id=1, source_target_pairs={{0,4},{1,5},{2,6},{3,7},{4,0},{5,1},{6,2},{7,3},{8,12},{9,13},{10,... | collective-permute-start | bytes 589832 | tf_op jit(solution)/shard_map/ppermute | solution.py:154
  57.6 0.0 collective-permute-done.11
  57.6 0.0 collective-permute-done.12
  57.6 0.8 %collective-permute-done.13 = bf16[2,3,32,128]{3,2,1,0:T(8,128)(2,1)S(1)} collective-permute-done((bf16[2,3,32,128]{3,2,1,0:T(8,128)(2,1)S(1)}, bf16[2,3,32,128]{3,2,1,0:T(8,128)(2,1)S(1)}, u32[]{:S(2)}, u32[]{:S(2)}) %collective-permute-start.13) | collective-permute-done | bytes 49184 | tf_op jit(solution)/shard_map/ppermute | solution.py:154
  58.4 3.8 %collective-permute-start.14 = (bf16[3,32,128]{2,1,0:T(8,128)(2,1)S(1)}, bf16[3,32,128]{2,1,0:T(8,128)(2,1)S(1)}, u32[]{:S(2)}, u32[]{:S(2)}) collective-permute-start(bf16[3,32,128]{2,1,0:T(8,128)(2,1)S(1)} %get-tuple-element.94), channel_id=1, source_target_pairs={{0,4},{1,5},{2,6},{3,7},{4,0},{5,1},{6,2},{7,3},{8,12},{9,13},{10,... | collective-permute-start | bytes 73736 | tf_op jit(solution)/shard_map/ppermute | solution.py:154
  62.3 0.2 collective-permute-start.16
  62.5 1.3 %collective-permute-start.15 = (bf16[3,32,128]{2,1,0:T(8,128)(2,1)S(1)}, bf16[3,32,128]{2,1,0:T(8,128)(2,1)S(1)}, u32[]{:S(2)}, u32[]{:S(2)}) collective-permute-start(bf16[3,32,128]{2,1,0:T(8,128)(2,1)S(1)} %get-tuple-element.93), channel_id=1, source_target_pairs={{0,16},{8,24},{16,0},{24,8},{1,17},{9,25},{17,1},{25,9},{2,18},{10... | collective-permute-start | bytes 73736 | tf_op jit(solution)/shard_map/ppermute | solution.py:154
  63.8 4.0 %collective-permute-done.17 = bf16[2,1,2,3,32,256]{5,4,3,2,1,0:T(8,128)(2,1)S(1)} collective-permute-done((bf16[2,1,2,3,32,256]{5,4,3,2,1,0:T(8,128)(2,1)S(1)}, bf16[2,1,2,3,32,256]{5,4,3,2,1,0:T(8,128)(2,1)S(1)}, u32[]{:S(2)}, u32[]{:S(2)}) %collective-permute-start.17) | collective-permute-done | bytes 196640 | tf_op jit(solution)/shard_map/ppermute | solution.py:154
  67.8 0.2 collective-permute-done.14
  68.1 0.9 %collective-permute-done.16 = bf16[3,32,128]{2,1,0:T(8,128)(2,1)S(1)} collective-permute-done((bf16[3,32,128]{2,1,0:T(8,128)(2,1)S(1)}, bf16[3,32,128]{2,1,0:T(8,128)(2,1)S(1)}, u32[]{:S(2)}, u32[]{:S(2)}) %collective-permute-start.16) | collective-permute-done | bytes 24608 | tf_op jit(solution)/shard_map/ppermute | solution.py:286
  68.9 0.1 collective-permute-start.18
  69.0 1.8 %columns.1 = (f32[6,32,256]{2,1,0:T(8,128)}, f32[6,32,256]{2,1,0:T(8,128)}) custom-call(s32[18]{0:T(128)S(1)} %copy-done.3, s32[12]{0:T(128)S(1)} %copy-done.4, f32[2,3,32,256]{3,2,1,0:T(8,128)S(1)} %bitcast.105, bf16[2,3,32,256]{3,2,1,0:T(8,128)(2,1)S(1)} %bitcast.107, f32[2,3,32,256]{3,2,1,0:T(8,128)S(1)} %bitcast.104, ...), custom_call_target="tpu_custom_call" | custom-call | tf_op jit(solution)/shard_map/columns/pallas_call | solution.py:292
  70.8 0.0 collective-permute-done.18
  70.8 0.6 slice_bitcast_fusion.2
  (35 shorter events, 0.6 us)
Async XLA Ops:
  0.6 24.1 %copy-start.1 = (f32[256,256]{1,0:T(8,128)S(1)}, f32[256,256]{1,0:T(8,128)}, u32[]{:S(2)}) copy-start(f32[256,256]{1,0:T(8,128)} %inv1.5) | copy-start | bytes 786436
  0.6 24.1 %copy-start.2 = (f32[256,256]{1,0:T(8,128)S(1)}, f32[256,256]{1,0:T(8,128)}, u32[]{:S(2)}) copy-start(f32[256,256]{1,0:T(8,128)} %inv2.5) | copy-start | bytes 786436
  0.7 24.1 %copy-start.3 = (s32[18]{0:T(128)S(1)}, s32[18]{0:T(128)}, u32[]{:S(2)}) copy-start(s32[18]{0:T(128)} %struct1.5) | copy-start | bytes 220
  0.7 24.1 %copy-start.4 = (s32[12]{0:T(128)S(1)}, s32[12]{0:T(128)}, u32[]{:S(2)}) copy-start(s32[12]{0:T(128)} %struct2.5) | copy-start | bytes 148
  1.8 4.9 %collective-permute-start = (bf16[2,3,32,256]{3,2,1,0:T(8,128)(2,1)S(1)}, bf16[2,3,32,256]{3,2,1,0:T(8,128)(2,1)S(1)}, u32[]{:S(2)}, u32[]{:S(2)}) collective-permute-start(bf16[2,3,32,256]{3,2,1,0:T(8,128)(2,1)S(1)} %get-tuple-element.86), channel_id=1, source_target_pairs={{0,0},{1,8},{2,16},{3,24},{4,4},{5,12},{6,20},{7,28},{8,1},{9,9},{... | collective-permute-start | bytes 294920 | tf_op jit(solution)/shard_map/ppermute | solution.py:196
  2.4 16.6 %collective-permute-start.1 = (bf16[2,3,32,256]{3,2,1,0:T(8,128)(2,1)S(1)}, bf16[2,3,32,256]{3,2,1,0:T(8,128)(2,1)S(1)}, u32[]{:S(2)}, u32[]{:S(2)}) collective-permute-start(bf16[2,3,32,256]{3,2,1,0:T(8,128)(2,1)S(1)} %get-tuple-element.87), channel_id=1, source_target_pairs={{0,4},{1,12},{2,20},{3,28},{4,0},{5,8},{6,16},{7,24},{8,5},{9,13},... | collective-permute-start | bytes 294920 | tf_op jit(solution)/shard_map/ppermute | solution.py:196
  6.5 18.1 %collective-permute-start.4 = (bf16[2,6,32,256]{3,2,1,0:T(8,128)(2,1)S(1)}, bf16[2,6,32,256]{3,2,1,0:T(8,128)(2,1)S(1)}, u32[]{:S(2)}, u32[]{:S(2)}) collective-permute-start(bf16[2,6,32,256]{3,2,1,0:T(8,128)(2,1)S(1)} %pad_maximum_fusion.3), channel_id=1, source_target_pairs={{0,4},{1,5},{2,6},{3,7},{4,0},{5,1},{6,2},{7,3},{8,12},{9,13},{10,... | collective-permute-start | bytes 589832 | tf_op jit(solution)/shard_map/ppermute | solution.py:154
  6.6 15.4 %collective-permute-start.2 = (bf16[2,3,32,256]{3,2,1,0:T(8,128)(2,1)S(1)}, bf16[2,3,32,256]{3,2,1,0:T(8,128)(2,1)S(1)}, u32[]{:S(2)}, u32[]{:S(2)}) collective-permute-start(bf16[2,3,32,256]{3,2,1,0:T(8,128)(2,1)S(1)} %collective-permute-done), channel_id=1, source_target_pairs={{0,16},{8,24},{16,0},{24,8},{1,17},{9,25},{17,1},{25,9},{2,18},{10... | collective-permute-start | bytes 294920 | tf_op jit(solution)/shard_map/ppermute | solution.py:154
  19.0 5.5 %collective-permute-start.3 = (bf16[2,3,32,256]{3,2,1,0:T(8,128)(2,1)S(1)}, bf16[2,3,32,256]{3,2,1,0:T(8,128)(2,1)S(1)}, u32[]{:S(2)}, u32[]{:S(2)}) collective-permute-start(bf16[2,3,32,256]{3,2,1,0:T(8,128)(2,1)S(1)} %collective-permute-done.1), channel_id=1, source_target_pairs={{0,16},{8,24},{16,0},{24,8},{1,17},{9,25},{17,1},{25,9},{2,18},{10... | collective-permute-start | bytes 294920 | tf_op jit(solution)/shard_map/ppermute | solution.py:154
  24.6 2.0 %copy-start = (bf16[6,1,3,1,256,256]{5,4,3,2,1,0:T(8,128)(2,1)S(1)}, bf16[6,1,3,1,256,256]{5,4,3,2,1,0:T(8,128)(2,1)}, u32[]{:S(2)}) copy-start(bf16[6,1,3,1,256,256]{5,4,3,2,1,0:T(8,128)(2,1)} %param.8) | copy-start | bytes 7077892
  24.7 1.8 %collective-permute-start.5 = (bf16[2,2,2,3,32,256]{5,4,3,2,1,0:T(8,128)(2,1)S(1)}, bf16[2,2,2,3,32,256]{5,4,3,2,1,0:T(8,128)(2,1)S(1)}, u32[]{:S(2)}, u32[]{:S(2)}) collective-permute-start(bf16[2,2,2,3,32,256]{5,4,3,2,1,0:T(8,128)(2,1)S(1)} %pad_maximum_fusion.1), channel_id=1, source_target_pairs={{0,8},{8,0},{16,24},{24,16},{1,9},{9,1},{17,25},{25,17},{2,10},{10... | collective-permute-start | bytes 1179656 | tf_op jit(solution)/shard_map/ppermute | solution.py:154
  26.5 5.0 %copy-start.5 = (bf16[256,256]{1,0:T(8,128)(2,1)S(1)}, bf16[256,256]{1,0:T(8,128)(2,1)}, u32[]{:S(2)}) copy-start(bf16[256,256]{1,0:T(8,128)(2,1)} %link.1) | copy-start | bytes 393220
  29.8 11.4 %collective-permute-start.8 = (bf16[4,2,3,32,256]{4,3,2,1,0:T(8,128)(2,1)S(1)}, bf16[4,2,3,32,256]{4,3,2,1,0:T(8,128)(2,1)S(1)}, u32[]{:S(2)}, u32[]{:S(2)}) collective-permute-start(bf16[4,2,3,32,256]{4,3,2,1,0:T(8,128)(2,1)S(1)} %get-tuple-element.51), channel_id=1, source_target_pairs={{0,2},{1,3},{2,0},{3,1},{4,6},{5,7},{6,4},{7,5},{8,10},{9,11},{10,... | collective-permute-start | bytes 1179656 | tf_op jit(solution)/shard_map/ppermute | solution.py:154
  30.4 11.4 %collective-permute-start.6 = (bf16[4,2,3,32,256]{4,3,2,1,0:T(8,128)(2,1)S(1)}, bf16[4,2,3,32,256]{4,3,2,1,0:T(8,128)(2,1)S(1)}, u32[]{:S(2)}, u32[]{:S(2)}) collective-permute-start(bf16[4,2,3,32,256]{4,3,2,1,0:T(8,128)(2,1)S(1)} %get-tuple-element.47), channel_id=1, source_target_pairs={{0,1},{1,0},{2,3},{3,2},{4,5},{5,4},{6,7},{7,6},{8,9},{9,8},{10,11... | collective-permute-start | bytes 1179656 | tf_op jit(solution)/shard_map/ppermute | solution.py:154
  41.4 6.4 %collective-permute-start.9 = (bf16[2,2,3,32,256]{4,3,2,1,0:T(8,128)(2,1)S(1)}, bf16[2,2,3,32,256]{4,3,2,1,0:T(8,128)(2,1)S(1)}, u32[]{:S(2)}, u32[]{:S(2)}) collective-permute-start(bf16[2,2,3,32,256]{4,3,2,1,0:T(8,128)(2,1)S(1)} %fusion.1), channel_id=1, source_target_pairs={{0,1},{1,0},{2,3},{3,2},{4,5},{5,4},{6,7},{7,6},{8,9},{9,8},{10,11... | collective-permute-start | bytes 589832 | tf_op jit(solution)/shard_map/ppermute | solution.py:154
  42.1 6.1 %collective-permute-start.7 = (bf16[2,2,3,32,256]{4,3,2,1,0:T(8,128)(2,1)S(1)}, bf16[2,2,3,32,256]{4,3,2,1,0:T(8,128)(2,1)S(1)}, u32[]{:S(2)}, u32[]{:S(2)}) collective-permute-start(bf16[2,2,3,32,256]{4,3,2,1,0:T(8,128)(2,1)S(1)} %fusion), channel_id=1, source_target_pairs={{0,2},{1,3},{2,0},{3,1},{4,6},{5,7},{6,4},{7,5},{8,10},{9,11},{10,... | collective-permute-start | bytes 589832 | tf_op jit(solution)/shard_map/ppermute | solution.py:154
  49.3 1.8 %collective-permute-start.10 = (f32[8,3,32,128]{3,2,1,0:T(8,128)S(1)}, f32[8,3,32,128]{3,2,1,0:T(8,128)S(1)}, u32[]{:S(2)}, u32[]{:S(2)}) collective-permute-start(f32[8,3,32,128]{3,2,1,0:T(8,128)S(1)} %dynamic-slice_bitcast_fusion), channel_id=1, source_target_pairs={{0,8},{8,0},{16,24},{24,16},{1,9},{9,1},{17,25},{25,17},{2,10},{10... | collective-permute-start | bytes 1179656 | tf_op jit(solution)/shard_map/ppermute | solution.py:154
  51.2 6.4 %collective-permute-start.11 = (bf16[2,3,32,128]{3,2,1,0:T(8,128)(2,1)S(1)}, bf16[2,3,32,128]{3,2,1,0:T(8,128)(2,1)S(1)}, u32[]{:S(2)}, u32[]{:S(2)}) collective-permute-start(bf16[2,3,32,128]{3,2,1,0:T(8,128)(2,1)S(1)} %get-tuple-element.81), channel_id=1, source_target_pairs={{0,1},{1,0},{2,3},{3,2},{4,5},{5,4},{6,7},{7,6},{8,9},{9,8},{10,11... | collective-permute-start | bytes 147464 | tf_op jit(solution)/shard_map/ppermute | solution.py:154
  52.9 4.7 %collective-permute-start.12 = (bf16[2,3,32,128]{3,2,1,0:T(8,128)(2,1)S(1)}, bf16[2,3,32,128]{3,2,1,0:T(8,128)(2,1)S(1)}, u32[]{:S(2)}, u32[]{:S(2)}) collective-permute-start(bf16[2,3,32,128]{3,2,1,0:T(8,128)(2,1)S(1)} %get-tuple-element.83), channel_id=1, source_target_pairs={{0,2},{1,3},{2,0},{3,1},{4,6},{5,7},{6,4},{7,5},{8,10},{9,11},{10,... | collective-permute-start | bytes 147464 | tf_op jit(solution)/shard_map/ppermute | solution.py:154
  53.4 5.0 %collective-permute-start.13 = (bf16[2,3,32,128]{3,2,1,0:T(8,128)(2,1)S(1)}, bf16[2,3,32,128]{3,2,1,0:T(8,128)(2,1)S(1)}, u32[]{:S(2)}, u32[]{:S(2)}) collective-permute-start(bf16[2,3,32,128]{3,2,1,0:T(8,128)(2,1)S(1)} %get-tuple-element.82), channel_id=1, source_target_pairs={{0,3},{1,2},{2,1},{3,0},{4,7},{5,6},{6,5},{7,4},{8,11},{9,10},{10,... | collective-permute-start | bytes 147464 | tf_op jit(solution)/shard_map/ppermute | solution.py:154
  54.7 13.0 %collective-permute-start.17 = (bf16[2,1,2,3,32,256]{5,4,3,2,1,0:T(8,128)(2,1)S(1)}, bf16[2,1,2,3,32,256]{5,4,3,2,1,0:T(8,128)(2,1)S(1)}, u32[]{:S(2)}, u32[]{:S(2)}) collective-permute-start(bf16[2,1,2,3,32,256]{5,4,3,2,1,0:T(8,128)(2,1)S(1)} %pad_maximum_fusion.4), channel_id=1, source_target_pairs={{0,4},{1,5},{2,6},{3,7},{4,0},{5,1},{6,2},{7,3},{8,12},{9,13},{10,... | collective-permute-start | bytes 589832 | tf_op jit(solution)/shard_map/ppermute | solution.py:154
  58.4 9.6 %collective-permute-start.14 = (bf16[3,32,128]{2,1,0:T(8,128)(2,1)S(1)}, bf16[3,32,128]{2,1,0:T(8,128)(2,1)S(1)}, u32[]{:S(2)}, u32[]{:S(2)}) collective-permute-start(bf16[3,32,128]{2,1,0:T(8,128)(2,1)S(1)} %get-tuple-element.94), channel_id=1, source_target_pairs={{0,4},{1,5},{2,6},{3,7},{4,0},{5,1},{6,2},{7,3},{8,12},{9,13},{10,... | collective-permute-start | bytes 73736 | tf_op jit(solution)/shard_map/ppermute | solution.py:154
  62.3 6.6 %collective-permute-start.16 = (bf16[3,32,128]{2,1,0:T(8,128)(2,1)S(1)}, bf16[3,32,128]{2,1,0:T(8,128)(2,1)S(1)}, u32[]{:S(2)}, u32[]{:S(2)}) collective-permute-start(bf16[3,32,128]{2,1,0:T(8,128)(2,1)S(1)} %get-tuple-element.94), channel_id=1, source_target_pairs={{0,20},{1,21},{2,22},{3,23},{4,16},{5,17},{6,18},{7,19},{8,28},{9,... | collective-permute-start | bytes 73736 | tf_op jit(solution)/shard_map/ppermute | solution.py:286
  62.5 5.6 %collective-permute-start.15 = (bf16[3,32,128]{2,1,0:T(8,128)(2,1)S(1)}, bf16[3,32,128]{2,1,0:T(8,128)(2,1)S(1)}, u32[]{:S(2)}, u32[]{:S(2)}) collective-permute-start(bf16[3,32,128]{2,1,0:T(8,128)(2,1)S(1)} %get-tuple-element.93), channel_id=1, source_target_pairs={{0,16},{8,24},{16,0},{24,8},{1,17},{9,25},{17,1},{25,9},{2,18},{10... | collective-permute-start | bytes 73736 | tf_op jit(solution)/shard_map/ppermute | solution.py:154
  68.9 1.9 %collective-permute-start.18 = (f32[3,32,128]{2,1,0:T(8,128)S(1)}, f32[3,32,128]{2,1,0:T(8,128)S(1)}, u32[]{:S(2)}, u32[]{:S(2)}) collective-permute-start(f32[3,32,128]{2,1,0:T(8,128)S(1)} %add_add_fusion), channel_id=1, source_target_pairs={{0,8},{8,0},{16,24},{24,16},{1,9},{9,1},{17,25},{25,17},{2,10},{10... | collective-permute-start | bytes 147464 | tf_op jit(solution)/shard_map/ppermute | solution.py:154

commit v8 on v3

--- a/solution.py
+++ b/solution.py
@@ -60,7 +60,7 @@
     here_row, here_col = lax.axis_index("row"), lax.axis_index("col")
 
     group = here_col // n_row
-    places = [(row ^ here_row, lax.rem(turn + group, cycle)) for turn in range(cycle) for row in range(n_row)]
+    places = [(row ^ here_row, lax.rem(turn + group + cycle - 1, cycle)) for turn in range(cycle) for row in range(n_row)]
     for p, (struct, inverse) in enumerate(((struct1, inv1), (struct2, inv2))):
 
         def look(place, found):
@@ -177,7 +177,7 @@
 
     panels = [panel_first.reshape(panel), panel_second.reshape(panel)]
     _, turn = place_of(here_col, n_row)
-    picks = [((s - turn + cycle) % cycle).astype(jnp.uint32) for s in range(cycle)]
+    picks = [((s + 1 - turn + cycle) % cycle).astype(jnp.uint32) for s in range(cycle)]
     ways = [(here_col >> bit) & 1 for bit in range(n_bits)]
     ways = [(way.astype(jnp.uint32), (1 - way).astype(jnp.uint32)) for way in ways]
     core = lax.axis_index("row") & 1
@@ -194,7 +194,7 @@
         for r in range(n_row):
             for c in range(n_col):
                 row, t = place_of(c, n_row)
-                moves.append((r * n_col + c, row * n_col + r + (s - t) % cycle * n_row))
+                moves.append((r * n_col + c, row * n_col + r + (s + 1 - t) % cycle * n_row))
         part = lax.dynamic_index_in_dim(turns, picks[s], 2, keepdims=False)
         got.append(lax.ppermute(part, ("row", "col"), moves))
     base = jnp.stack([raw, swapped(raw, "col", n_col, n_col // 2)])

time: 71.7 us -> 70.2 us (0.979)
  starting transfers between devices: 32.7 us -> 30.6 us
    ppermute x16, starting transfers between devices: 27.7 us -> 24.7 us  [swapped(): return lax.ppermute(value, axis, [(i, i ^ mask) for i in range(size)])]
    ppermute x2, waiting for transfers between devices: 0.01 us -> 2.26 us  [body(): got.append(lax.ppermute(part, ('row', 'col'), moves))]
    ppermute x16, waiting for transfers between devices: 24.6 us -> 22.7 us  [swapped(): return lax.ppermute(value, axis, [(i, i ^ mask) for i in range(size)])]
    ppermute x1, starting transfers between devices: 0.21 us -> 1.11 us  [body(): lax.ppermute(send, ('row', 'col'), across).astype(f32)]
  transfers between devices with their start and end apart: 19 -> 19, of which waited for: 11 -> 12; matrix products, arithmetic and copies ran while one was open for 1% -> 1% of each run, Pallas kernels for 8% -> 8%
where the time goes in v8:
time: 70.2 us; the launch traced here: 70 us
  starting transfers between devices  30.6 us (44%)
  waiting for transfers between devices  26.1 us (37%)
  Pallas kernels  9.69 us (14%)
  other arithmetic  1.73 us (2%)
  between operations  1.01 us (1%)
  local copies, waits for them, and re-layouts  0.92 us (1%)
    ppermute x16, starting transfers between devices, swapped(): return lax.ppermute(value, axis, [(i, i ^ mask) for i in range(size)])  24.7 us
    ppermute x16, waiting for transfers between devices, swapped(): return lax.ppermute(value, axis, [(i, i ^ mask) for i in range(size)])  22.7 us
    ppermute x2, starting transfers between devices, body(): got.append(lax.ppermute(part, ('row', 'col'), moves))  4.76 us
    pallas_call x1, Pallas kernels, body(): pl.pallas_call(functools.partial(product_kernel, n_row, n_col, (orders[0]...  3.23 us
    ppermute x2, waiting for transfers between devices, body(): got.append(lax.ppermute(part, ('row', 'col'), moves))  2.26 us
    pallas_call x1, Pallas kernels, body(): pl.pallas_call(prepare_kernel, out_shape=[shape((width, width), f32), sha...  2.18 us
    pallas_call x1, Pallas kernels, body(): pl.pallas_call(functools.partial(column_kernel, n_row), out_shape=[shape(...  1.78 us
    pallas_call x1, Pallas kernels, body(): pl.pallas_call(functools.partial(form_kernel, n_row), out_shape=shape(bas...  1.49 us
  transfers between devices with their start and end apart: 19, of which 12 were waited for; matrix products, arithmetic and copies ran while one was open for 1% of the time, Pallas kernels for 8%

profile of v8, /device:TPU:0, one launch (start us, length us, event | category | flops | bytes accessed | tf_op | source)
XLA Modules:
  0.0 70.0 jit_solution(5107896057770028616)
XLA Ops:
  0.7 1.0 %pad_maximum_fusion.3 = bf16[2,6,32,256]{3,2,1,0:T(8,128)(2,1)S(1)} fusion(bf16[1,6,32,256]{3,2,1,0:T(8,128)(2,1)} %bitcast.120, bf16[1,6,32,256]{3,2,1,0:T(8,128)(2,1)} %bitcast.121), kind=kLoop, calls=%fused_computation.13 | loop fusion | flops 98304 | bytes 393216 | tf_op jit(solution)/shard_map/stack | solution.py:189
  1.8 4.1 %collective-permute-start = (bf16[2,3,32,256]{3,2,1,0:T(8,128)(2,1)S(1)}, bf16[2,3,32,256]{3,2,1,0:T(8,128)(2,1)S(1)}, u32[]{:S(2)}, u32[]{:S(2)}) collective-permute-start(bf16[2,3,32,256]{3,2,1,0:T(8,128)(2,1)S(1)} %get-tuple-element.86), channel_id=1, source_target_pairs={{0,4},{1,12},{2,20},{3,28},{4,0},{5,8},{6,16},{7,24},{8,5},{9,13},... | collective-permute-start | bytes 294920 | tf_op jit(solution)/shard_map/ppermute | solution.py:199
  5.9 0.7 collective-permute-start.1
  6.5 0.1 collective-permute-start.4
  6.6 2.3 %collective-permute-done = bf16[2,3,32,256]{3,2,1,0:T(8,128)(2,1)S(1)} collective-permute-done((bf16[2,3,32,256]{3,2,1,0:T(8,128)(2,1)S(1)}, bf16[2,3,32,256]{3,2,1,0:T(8,128)(2,1)S(1)}, u32[]{:S(2)}, u32[]{:S(2)}) %collective-permute-start) | collective-permute-done | bytes 98336 | tf_op jit(solution)/shard_map/ppermute | solution.py:199
  8.9 4.3 %collective-permute-start.2 = (bf16[2,3,32,256]{3,2,1,0:T(8,128)(2,1)S(1)}, bf16[2,3,32,256]{3,2,1,0:T(8,128)(2,1)S(1)}, u32[]{:S(2)}, u32[]{:S(2)}) collective-permute-start(bf16[2,3,32,256]{3,2,1,0:T(8,128)(2,1)S(1)} %collective-permute-done), channel_id=1, source_target_pairs={{0,16},{8,24},{16,0},{24,8},{1,17},{9,25},{17,1},{25,9},{2,18},{10... | collective-permute-start | bytes 294920 | tf_op jit(solution)/shard_map/ppermute | solution.py:157
  13.1 0.0 collective-permute-done.1
  13.1 5.7 %collective-permute-start.3 = (bf16[2,3,32,256]{3,2,1,0:T(8,128)(2,1)S(1)}, bf16[2,3,32,256]{3,2,1,0:T(8,128)(2,1)S(1)}, u32[]{:S(2)}, u32[]{:S(2)}) collective-permute-start(bf16[2,3,32,256]{3,2,1,0:T(8,128)(2,1)S(1)} %collective-permute-done.1), channel_id=1, source_target_pairs={{0,16},{8,24},{16,0},{24,8},{1,17},{9,25},{17,1},{25,9},{2,18},{10... | collective-permute-start | bytes 294920 | tf_op jit(solution)/shard_map/ppermute | solution.py:157
  18.9 0.0 collective-permute-done.2
  18.9 2.6 %collective-permute-done.3 = bf16[2,3,32,256]{3,2,1,0:T(8,128)(2,1)S(1)} collective-permute-done((bf16[2,3,32,256]{3,2,1,0:T(8,128)(2,1)S(1)}, bf16[2,3,32,256]{3,2,1,0:T(8,128)(2,1)S(1)}, u32[]{:S(2)}, u32[]{:S(2)}) %collective-permute-start.3) | collective-permute-done | bytes 98336 | tf_op jit(solution)/shard_map/ppermute | solution.py:157
  21.5 0.0 collective-permute-done.4
  21.6 0.1 collective-permute-start.5
  21.7 1.5 %form.1.rows = bf16[2,2,6,32,256]{4,3,2,1,0:T(8,128)(2,1)S(1)} custom-call(s32[18]{0:T(128)S(1)} %copy-done.3, s32[12]{0:T(128)S(1)} %copy-done.4, f32[256,256]{1,0:T(8,128)S(1)} %copy-done.1, f32[256,256]{1,0:T(8,128)S(1)} %copy-done.2, bf16[2,2,6,32,256]{4,3,2,1,0:T(8,128)(2,1)S(1)} %pad_maximum_fusion.2.base), custom_call_target="tpu_custom_call" | custom-call | flops 134217728 | bytes 262144 | tf_op jit(solution)/shard_map/form/pallas_call | solution.py:210
  23.2 0.2 collective-permute-done.5
  23.4 0.1 pad_maximum_fusion
  23.5 3.2 %products.1 = (f32[4,2,3,32,256]{4,3,2,1,0:T(8,128)S(1)}, f32[4,2,3,32,256]{4,3,2,1,0:T(8,128)S(1)}, bf16[4,2,3,32,256]{4,3,2,1,0:T(8,128)(2,1)S(1)}, bf16[4,2,3,32,256]{4,3,2,1,0:T(8,128)(2,1)S(1)}) custom-call(s32[18]{0:T(128)S(1)} %copy-done.3, s32[12]{0:T(128)S(1)} %copy-done.4, f32[256,256]{1,0:T(8,128)S(1)} %copy-done.1, f32[256,256]{1,0:T(8,128)S(1)} %copy-done.2, ...), custom_call_target="tpu_custom_call" | custom-call | tf_op jit(solution)/shard_map/products/pallas_call | solution.py:226
  26.7 2.4 %collective-permute-start.8 = (bf16[4,2,3,32,256]{4,3,2,1,0:T(8,128)(2,1)S(1)}, bf16[4,2,3,32,256]{4,3,2,1,0:T(8,128)(2,1)S(1)}, u32[]{:S(2)}, u32[]{:S(2)}) collective-permute-start(bf16[4,2,3,32,256]{4,3,2,1,0:T(8,128)(2,1)S(1)} %get-tuple-element.51), channel_id=1, source_target_pairs={{0,2},{1,3},{2,0},{3,1},{4,6},{5,7},{6,4},{7,5},{8,10},{9,11},{10,... | collective-permute-start | bytes 1179656 | tf_op jit(solution)/shard_map/ppermute | solution.py:157
  29.1 0.3 collective-permute-start.6
  29.4 2.2 %prepare.1 = (f32[256,256]{1,0:T(8,128)S(1)}, f32[3,32,256]{2,1,0:T(8,128)S(1)}) custom-call(bf16[256,256]{1,0:T(8,128)(2,1)S(1)} %copy-done.5, f32[256,256]{1,0:T(8,128)S(1)} %copy-done.1, f32[256,256]{1,0:T(8,128)S(1)} %copy-done.2, f32[4,2,3,32,256]{4,3,2,1,0:T(8,128)S(1)} %get-tuple-element.46.after), custom_call_target="tpu_custom_call" | custom-call | flops 1006632960 | bytes 524288 | tf_op jit(solution)/shard_map/prepare/pallas_call | solution.py:238
  31.6 7.1 %collective-permute-done.8 = bf16[4,2,3,32,256]{4,3,2,1,0:T(8,128)(2,1)S(1)} collective-permute-done((bf16[4,2,3,32,256]{4,3,2,1,0:T(8,128)(2,1)S(1)}, bf16[4,2,3,32,256]{4,3,2,1,0:T(8,128)(2,1)S(1)}, u32[]{:S(2)}, u32[]{:S(2)}) %collective-permute-start.8) | collective-permute-done | bytes 393248 | tf_op jit(solution)/shard_map/ppermute | solution.py:157
  38.7 0.1 convert_add_fusion
  38.9 0.8 %collective-permute-start.9 = (bf16[2,2,3,32,256]{4,3,2,1,0:T(8,128)(2,1)S(1)}, bf16[2,2,3,32,256]{4,3,2,1,0:T(8,128)(2,1)S(1)}, u32[]{:S(2)}, u32[]{:S(2)}) collective-permute-start(bf16[2,2,3,32,256]{4,3,2,1,0:T(8,128)(2,1)S(1)} %fusion.1), channel_id=1, source_target_pairs={{0,1},{1,0},{2,3},{3,2},{4,5},{5,4},{6,7},{7,6},{8,9},{9,8},{10,11... | collective-permute-start | bytes 589832 | tf_op jit(solution)/shard_map/ppermute | solution.py:157
  39.7 0.4 collective-permute-done.6
  40.2 0.1 convert_add_fusion.1
  40.4 0.9 %collective-permute-start.7 = (bf16[2,2,3,32,256]{4,3,2,1,0:T(8,128)(2,1)S(1)}, bf16[2,2,3,32,256]{4,3,2,1,0:T(8,128)(2,1)S(1)}, u32[]{:S(2)}, u32[]{:S(2)}) collective-permute-start(bf16[2,2,3,32,256]{4,3,2,1,0:T(8,128)(2,1)S(1)} %fusion), channel_id=1, source_target_pairs={{0,2},{1,3},{2,0},{3,1},{4,6},{5,7},{6,4},{7,5},{8,10},{9,11},{10,... | collective-permute-start | bytes 589832 | tf_op jit(solution)/shard_map/ppermute | solution.py:157
  41.2 4.4 %collective-permute-done.9 = bf16[2,2,3,32,256]{4,3,2,1,0:T(8,128)(2,1)S(1)} collective-permute-done((bf16[2,2,3,32,256]{4,3,2,1,0:T(8,128)(2,1)S(1)}, bf16[2,2,3,32,256]{4,3,2,1,0:T(8,128)(2,1)S(1)}, u32[]{:S(2)}, u32[]{:S(2)}) %collective-permute-start.9) | collective-permute-done | bytes 196640 | tf_op jit(solution)/shard_map/ppermute | solution.py:157
  45.6 0.8 %collective-permute-done.7 = bf16[2,2,3,32,256]{4,3,2,1,0:T(8,128)(2,1)S(1)} collective-permute-done((bf16[2,2,3,32,256]{4,3,2,1,0:T(8,128)(2,1)S(1)}, bf16[2,2,3,32,256]{4,3,2,1,0:T(8,128)(2,1)S(1)}, u32[]{:S(2)}, u32[]{:S(2)}) %collective-permute-start.7) | collective-permute-done | bytes 196640 | tf_op jit(solution)/shard_map/ppermute | solution.py:157
  46.5 1.0 %sums.1 = f32[2,8,3,32,128]{4,3,2,1,0:T(8,128)S(1)} custom-call(bf16[2,2,6,32,256]{4,3,2,1,0:T(8,128)(2,1)S(1)} %form.1.rows, f32[2,2,3,32,256]{4,3,2,1,0:T(8,128)S(1)} %bitcast_add_fusion.2.total_low, f32[2,2,3,32,256]{4,3,2,1,0:T(8,128)S(1)} %bitcast_add_fusion.1.total_high, f32[256,256]{1,0:T(8,128)S(1)} %get-tuple-element.54.linked, ...), custom_call_target="tpu_custom_call" | custom-call | tf_op jit(solution)/shard_map/sums/pallas_call | solution.py:268
  47.5 0.1 collective-permute-start.10
  47.7 1.6 %collective-permute-done.10 = f32[8,3,32,128]{3,2,1,0:T(8,128)S(1)} collective-permute-done((f32[8,3,32,128]{3,2,1,0:T(8,128)S(1)}, f32[8,3,32,128]{3,2,1,0:T(8,128)S(1)}, u32[]{:S(2)}, u32[]{:S(2)}) %collective-permute-start.10) | collective-permute-done | bytes 393248 | tf_op jit(solution)/shard_map/ppermute | solution.py:157
  49.3 0.1 bitcast_add_fusion
  49.4 1.2 %collective-permute-start.11 = (bf16[2,3,32,128]{3,2,1,0:T(8,128)(2,1)S(1)}, bf16[2,3,32,128]{3,2,1,0:T(8,128)(2,1)S(1)}, u32[]{:S(2)}, u32[]{:S(2)}) collective-permute-start(bf16[2,3,32,128]{3,2,1,0:T(8,128)(2,1)S(1)} %get-tuple-element.81), channel_id=1, source_target_pairs={{0,1},{1,0},{2,3},{3,2},{4,5},{5,4},{6,7},{7,6},{8,9},{9,8},{10,11... | collective-permute-start | bytes 147464 | tf_op jit(solution)/shard_map/ppermute | solution.py:157
  50.7 1.4 %collective-permute-start.12 = (bf16[2,3,32,128]{3,2,1,0:T(8,128)(2,1)S(1)}, bf16[2,3,32,128]{3,2,1,0:T(8,128)(2,1)S(1)}, u32[]{:S(2)}, u32[]{:S(2)}) collective-permute-start(bf16[2,3,32,128]{3,2,1,0:T(8,128)(2,1)S(1)} %get-tuple-element.83), channel_id=1, source_target_pairs={{0,2},{1,3},{2,0},{3,1},{4,6},{5,7},{6,4},{7,5},{8,10},{9,11},{10,... | collective-permute-start | bytes 147464 | tf_op jit(solution)/shard_map/ppermute | solution.py:157
  52.1 0.9 %collective-permute-start.13 = (bf16[2,3,32,128]{3,2,1,0:T(8,128)(2,1)S(1)}, bf16[2,3,32,128]{3,2,1,0:T(8,128)(2,1)S(1)}, u32[]{:S(2)}, u32[]{:S(2)}) collective-permute-start(bf16[2,3,32,128]{3,2,1,0:T(8,128)(2,1)S(1)} %get-tuple-element.82), channel_id=1, source_target_pairs={{0,3},{1,2},{2,1},{3,0},{4,7},{5,6},{6,5},{7,4},{8,11},{9,10},{10,... | collective-permute-start | bytes 147464 | tf_op jit(solution)/shard_map/ppermute | solution.py:157
  53.0 3.2 %collective-permute-start.17 = (bf16[2,1,2,3,32,256]{5,4,3,2,1,0:T(8,128)(2,1)S(1)}, bf16[2,1,2,3,32,256]{5,4,3,2,1,0:T(8,128)(2,1)S(1)}, u32[]{:S(2)}, u32[]{:S(2)}) collective-permute-start(bf16[2,1,2,3,32,256]{5,4,3,2,1,0:T(8,128)(2,1)S(1)} %pad_maximum_fusion.4), channel_id=1, source_target_pairs={{0,4},{1,5},{2,6},{3,7},{4,0},{5,1},{6,2},{7,3},{8,12},{9,13},{10,... | collective-permute-start | bytes 589832 | tf_op jit(solution)/shard_map/ppermute | solution.py:157
  56.2 0.0 collective-permute-done.11
  56.2 0.0 collective-permute-done.12
  56.2 2.1 %collective-permute-done.13 = bf16[2,3,32,128]{3,2,1,0:T(8,128)(2,1)S(1)} collective-permute-done((bf16[2,3,32,128]{3,2,1,0:T(8,128)(2,1)S(1)}, bf16[2,3,32,128]{3,2,1,0:T(8,128)(2,1)S(1)}, u32[]{:S(2)}, u32[]{:S(2)}) %collective-permute-start.13) | collective-permute-done | bytes 49184 | tf_op jit(solution)/shard_map/ppermute | solution.py:157
  58.4 1.3 %collective-permute-start.14 = (bf16[3,32,128]{2,1,0:T(8,128)(2,1)S(1)}, bf16[3,32,128]{2,1,0:T(8,128)(2,1)S(1)}, u32[]{:S(2)}, u32[]{:S(2)}) collective-permute-start(bf16[3,32,128]{2,1,0:T(8,128)(2,1)S(1)} %get-tuple-element.94), channel_id=1, source_target_pairs={{0,4},{1,5},{2,6},{3,7},{4,0},{5,1},{6,2},{7,3},{8,12},{9,13},{10,... | collective-permute-start | bytes 73736 | tf_op jit(solution)/shard_map/ppermute | solution.py:157
  59.7 1.1 %collective-permute-start.16 = (bf16[3,32,128]{2,1,0:T(8,128)(2,1)S(1)}, bf16[3,32,128]{2,1,0:T(8,128)(2,1)S(1)}, u32[]{:S(2)}, u32[]{:S(2)}) collective-permute-start(bf16[3,32,128]{2,1,0:T(8,128)(2,1)S(1)} %get-tuple-element.94), channel_id=1, source_target_pairs={{0,20},{1,21},{2,22},{3,23},{4,16},{5,17},{6,18},{7,19},{8,28},{9,... | collective-permute-start | bytes 73736 | tf_op jit(solution)/shard_map/ppermute | solution.py:289
  60.8 2.0 %collective-permute-start.15 = (bf16[3,32,128]{2,1,0:T(8,128)(2,1)S(1)}, bf16[3,32,128]{2,1,0:T(8,128)(2,1)S(1)}, u32[]{:S(2)}, u32[]{:S(2)}) collective-permute-start(bf16[3,32,128]{2,1,0:T(8,128)(2,1)S(1)} %get-tuple-element.93), channel_id=1, source_target_pairs={{0,16},{8,24},{16,0},{24,8},{1,17},{9,25},{17,1},{25,9},{2,18},{10... | collective-permute-start | bytes 73736 | tf_op jit(solution)/shard_map/ppermute | solution.py:157
  62.8 3.2 %collective-permute-done.17 = bf16[2,1,2,3,32,256]{5,4,3,2,1,0:T(8,128)(2,1)S(1)} collective-permute-done((bf16[2,1,2,3,32,256]{5,4,3,2,1,0:T(8,128)(2,1)S(1)}, bf16[2,1,2,3,32,256]{5,4,3,2,1,0:T(8,128)(2,1)S(1)}, u32[]{:S(2)}, u32[]{:S(2)}) %collective-permute-start.17) | collective-permute-done | bytes 196640 | tf_op jit(solution)/shard_map/ppermute | solution.py:157
  66.1 0.2 collective-permute-done.14
  66.3 0.0 collective-permute-done.15
  66.3 1.1 %collective-permute-done.16 = bf16[3,32,128]{2,1,0:T(8,128)(2,1)S(1)} collective-permute-done((bf16[3,32,128]{2,1,0:T(8,128)(2,1)S(1)}, bf16[3,32,128]{2,1,0:T(8,128)(2,1)S(1)}, u32[]{:S(2)}, u32[]{:S(2)}) %collective-permute-start.16) | collective-permute-done | bytes 24608 | tf_op jit(solution)/shard_map/ppermute | solution.py:289
  67.5 0.1 collective-permute-start.18
  67.6 1.8 %columns.1 = (f32[6,32,256]{2,1,0:T(8,128)}, f32[6,32,256]{2,1,0:T(8,128)}) custom-call(s32[18]{0:T(128)S(1)} %copy-done.3, s32[12]{0:T(128)S(1)} %copy-done.4, f32[2,3,32,256]{3,2,1,0:T(8,128)S(1)} %bitcast.105, bf16[2,3,32,256]{3,2,1,0:T(8,128)(2,1)S(1)} %bitcast.107, f32[2,3,32,256]{3,2,1,0:T(8,128)S(1)} %bitcast.104, ...), custom_call_target="tpu_custom_call" | custom-call | tf_op jit(solution)/shard_map/columns/pallas_call | solution.py:295
  69.4 0.6 slice_bitcast_fusion.2
  (35 shorter events, 0.6 us)
Async XLA Ops:
  0.6 21.1 %copy-start.1 = (f32[256,256]{1,0:T(8,128)S(1)}, f32[256,256]{1,0:T(8,128)}, u32[]{:S(2)}) copy-start(f32[256,256]{1,0:T(8,128)} %inv1.5) | copy-start | bytes 786436
  0.6 21.1 %copy-start.2 = (f32[256,256]{1,0:T(8,128)S(1)}, f32[256,256]{1,0:T(8,128)}, u32[]{:S(2)}) copy-start(f32[256,256]{1,0:T(8,128)} %inv2.5) | copy-start | bytes 786436
  0.7 21.1 %copy-start.3 = (s32[18]{0:T(128)S(1)}, s32[18]{0:T(128)}, u32[]{:S(2)}) copy-start(s32[18]{0:T(128)} %struct1.5) | copy-start | bytes 220
  0.7 21.1 %copy-start.4 = (s32[12]{0:T(128)S(1)}, s32[12]{0:T(128)}, u32[]{:S(2)}) copy-start(s32[12]{0:T(128)} %struct2.5) | copy-start | bytes 148
  1.8 7.1 %collective-permute-start = (bf16[2,3,32,256]{3,2,1,0:T(8,128)(2,1)S(1)}, bf16[2,3,32,256]{3,2,1,0:T(8,128)(2,1)S(1)}, u32[]{:S(2)}, u32[]{:S(2)}) collective-permute-start(bf16[2,3,32,256]{3,2,1,0:T(8,128)(2,1)S(1)} %get-tuple-element.86), channel_id=1, source_target_pairs={{0,4},{1,12},{2,20},{3,28},{4,0},{5,8},{6,16},{7,24},{8,5},{9,13},... | collective-permute-start | bytes 294920 | tf_op jit(solution)/shard_map/ppermute | solution.py:199
  5.9 7.3 %collective-permute-start.1 = (bf16[2,3,32,256]{3,2,1,0:T(8,128)(2,1)S(1)}, bf16[2,3,32,256]{3,2,1,0:T(8,128)(2,1)S(1)}, u32[]{:S(2)}, u32[]{:S(2)}) collective-permute-start(bf16[2,3,32,256]{3,2,1,0:T(8,128)(2,1)S(1)} %get-tuple-element.87), channel_id=1, source_target_pairs={{0,0},{1,8},{2,16},{3,24},{4,4},{5,12},{6,20},{7,28},{8,1},{9,9},{... | collective-permute-start | bytes 294920 | tf_op jit(solution)/shard_map/ppermute | solution.py:199
  6.5 15.0 %collective-permute-start.4 = (bf16[2,6,32,256]{3,2,1,0:T(8,128)(2,1)S(1)}, bf16[2,6,32,256]{3,2,1,0:T(8,128)(2,1)S(1)}, u32[]{:S(2)}, u32[]{:S(2)}) collective-permute-start(bf16[2,6,32,256]{3,2,1,0:T(8,128)(2,1)S(1)} %pad_maximum_fusion.3), channel_id=1, source_target_pairs={{0,4},{1,5},{2,6},{3,7},{4,0},{5,1},{6,2},{7,3},{8,12},{9,13},{10,... | collective-permute-start | bytes 589832 | tf_op jit(solution)/shard_map/ppermute | solution.py:157
  8.9 10.0 %collective-permute-start.2 = (bf16[2,3,32,256]{3,2,1,0:T(8,128)(2,1)S(1)}, bf16[2,3,32,256]{3,2,1,0:T(8,128)(2,1)S(1)}, u32[]{:S(2)}, u32[]{:S(2)}) collective-permute-start(bf16[2,3,32,256]{3,2,1,0:T(8,128)(2,1)S(1)} %collective-permute-done), channel_id=1, source_target_pairs={{0,16},{8,24},{16,0},{24,8},{1,17},{9,25},{17,1},{25,9},{2,18},{10... | collective-permute-start | bytes 294920 | tf_op jit(solution)/shard_map/ppermute | solution.py:157
  13.1 8.3 %collective-permute-start.3 = (bf16[2,3,32,256]{3,2,1,0:T(8,128)(2,1)S(1)}, bf16[2,3,32,256]{3,2,1,0:T(8,128)(2,1)S(1)}, u32[]{:S(2)}, u32[]{:S(2)}) collective-permute-start(bf16[2,3,32,256]{3,2,1,0:T(8,128)(2,1)S(1)} %collective-permute-done.1), channel_id=1, source_target_pairs={{0,16},{8,24},{16,0},{24,8},{1,17},{9,25},{17,1},{25,9},{2,18},{10... | collective-permute-start | bytes 294920 | tf_op jit(solution)/shard_map/ppermute | solution.py:157
  21.5 2.0 %copy-start = (bf16[6,1,3,1,256,256]{5,4,3,2,1,0:T(8,128)(2,1)S(1)}, bf16[6,1,3,1,256,256]{5,4,3,2,1,0:T(8,128)(2,1)}, u32[]{:S(2)}) copy-start(bf16[6,1,3,1,256,256]{5,4,3,2,1,0:T(8,128)(2,1)} %param.8) | copy-start | bytes 7077892
  21.6 1.8 %collective-permute-start.5 = (bf16[2,2,2,3,32,256]{5,4,3,2,1,0:T(8,128)(2,1)S(1)}, bf16[2,2,2,3,32,256]{5,4,3,2,1,0:T(8,128)(2,1)S(1)}, u32[]{:S(2)}, u32[]{:S(2)}) collective-permute-start(bf16[2,2,2,3,32,256]{5,4,3,2,1,0:T(8,128)(2,1)S(1)} %pad_maximum_fusion.1), channel_id=1, source_target_pairs={{0,8},{8,0},{16,24},{24,16},{1,9},{9,1},{17,25},{25,17},{2,10},{10... | collective-permute-start | bytes 1179656 | tf_op jit(solution)/shard_map/ppermute | solution.py:157
  23.4 6.0 %copy-start.5 = (bf16[256,256]{1,0:T(8,128)(2,1)S(1)}, bf16[256,256]{1,0:T(8,128)(2,1)}, u32[]{:S(2)}) copy-start(bf16[256,256]{1,0:T(8,128)(2,1)} %link.1) | copy-start | bytes 393220
  26.7 12.0 %collective-permute-start.8 = (bf16[4,2,3,32,256]{4,3,2,1,0:T(8,128)(2,1)S(1)}, bf16[4,2,3,32,256]{4,3,2,1,0:T(8,128)(2,1)S(1)}, u32[]{:S(2)}, u32[]{:S(2)}) collective-permute-start(bf16[4,2,3,32,256]{4,3,2,1,0:T(8,128)(2,1)S(1)} %get-tuple-element.51), channel_id=1, source_target_pairs={{0,2},{1,3},{2,0},{3,1},{4,6},{5,7},{6,4},{7,5},{8,10},{9,11},{10,... | collective-permute-start | bytes 1179656 | tf_op jit(solution)/shard_map/ppermute | solution.py:157
  29.1 11.1 %collective-permute-start.6 = (bf16[4,2,3,32,256]{4,3,2,1,0:T(8,128)(2,1)S(1)}, bf16[4,2,3,32,256]{4,3,2,1,0:T(8,128)(2,1)S(1)}, u32[]{:S(2)}, u32[]{:S(2)}) collective-permute-start(bf16[4,2,3,32,256]{4,3,2,1,0:T(8,128)(2,1)S(1)} %get-tuple-element.47), channel_id=1, source_target_pairs={{0,1},{1,0},{2,3},{3,2},{4,5},{5,4},{6,7},{7,6},{8,9},{9,8},{10,11... | collective-permute-start | bytes 1179656 | tf_op jit(solution)/shard_map/ppermute | solution.py:157
  38.9 6.7 %collective-permute-start.9 = (bf16[2,2,3,32,256]{4,3,2,1,0:T(8,128)(2,1)S(1)}, bf16[2,2,3,32,256]{4,3,2,1,0:T(8,128)(2,1)S(1)}, u32[]{:S(2)}, u32[]{:S(2)}) collective-permute-start(bf16[2,2,3,32,256]{4,3,2,1,0:T(8,128)(2,1)S(1)} %fusion.1), channel_id=1, source_target_pairs={{0,1},{1,0},{2,3},{3,2},{4,5},{5,4},{6,7},{7,6},{8,9},{9,8},{10,11... | collective-permute-start | bytes 589832 | tf_op jit(solution)/shard_map/ppermute | solution.py:157
  40.4 6.1 %collective-permute-start.7 = (bf16[2,2,3,32,256]{4,3,2,1,0:T(8,128)(2,1)S(1)}, bf16[2,2,3,32,256]{4,3,2,1,0:T(8,128)(2,1)S(1)}, u32[]{:S(2)}, u32[]{:S(2)}) collective-permute-start(bf16[2,2,3,32,256]{4,3,2,1,0:T(8,128)(2,1)S(1)} %fusion), channel_id=1, source_target_pairs={{0,2},{1,3},{2,0},{3,1},{4,6},{5,7},{6,4},{7,5},{8,10},{9,11},{10,... | collective-permute-start | bytes 589832 | tf_op jit(solution)/shard_map/ppermute | solution.py:157
  47.5 1.8 %collective-permute-start.10 = (f32[8,3,32,128]{3,2,1,0:T(8,128)S(1)}, f32[8,3,32,128]{3,2,1,0:T(8,128)S(1)}, u32[]{:S(2)}, u32[]{:S(2)}) collective-permute-start(f32[8,3,32,128]{3,2,1,0:T(8,128)S(1)} %dynamic-slice_bitcast_fusion), channel_id=1, source_target_pairs={{0,8},{8,0},{16,24},{24,16},{1,9},{9,1},{17,25},{25,17},{2,10},{10... | collective-permute-start | bytes 1179656 | tf_op jit(solution)/shard_map/ppermute | solution.py:157
  49.4 6.8 %collective-permute-start.11 = (bf16[2,3,32,128]{3,2,1,0:T(8,128)(2,1)S(1)}, bf16[2,3,32,128]{3,2,1,0:T(8,128)(2,1)S(1)}, u32[]{:S(2)}, u32[]{:S(2)}) collective-permute-start(bf16[2,3,32,128]{3,2,1,0:T(8,128)(2,1)S(1)} %get-tuple-element.81), channel_id=1, source_target_pairs={{0,1},{1,0},{2,3},{3,2},{4,5},{5,4},{6,7},{7,6},{8,9},{9,8},{10,11... | collective-permute-start | bytes 147464 | tf_op jit(solution)/shard_map/ppermute | solution.py:157
  50.7 5.5 %collective-permute-start.12 = (bf16[2,3,32,128]{3,2,1,0:T(8,128)(2,1)S(1)}, bf16[2,3,32,128]{3,2,1,0:T(8,128)(2,1)S(1)}, u32[]{:S(2)}, u32[]{:S(2)}) collective-permute-start(bf16[2,3,32,128]{3,2,1,0:T(8,128)(2,1)S(1)} %get-tuple-element.83), channel_id=1, source_target_pairs={{0,2},{1,3},{2,0},{3,1},{4,6},{5,7},{6,4},{7,5},{8,10},{9,11},{10,... | collective-permute-start | bytes 147464 | tf_op jit(solution)/shard_map/ppermute | solution.py:157
  52.1 6.2 %collective-permute-start.13 = (bf16[2,3,32,128]{3,2,1,0:T(8,128)(2,1)S(1)}, bf16[2,3,32,128]{3,2,1,0:T(8,128)(2,1)S(1)}, u32[]{:S(2)}, u32[]{:S(2)}) collective-permute-start(bf16[2,3,32,128]{3,2,1,0:T(8,128)(2,1)S(1)} %get-tuple-element.82), channel_id=1, source_target_pairs={{0,3},{1,2},{2,1},{3,0},{4,7},{5,6},{6,5},{7,4},{8,11},{9,10},{10,... | collective-permute-start | bytes 147464 | tf_op jit(solution)/shard_map/ppermute | solution.py:157
  53.0 13.1 %collective-permute-start.17 = (bf16[2,1,2,3,32,256]{5,4,3,2,1,0:T(8,128)(2,1)S(1)}, bf16[2,1,2,3,32,256]{5,4,3,2,1,0:T(8,128)(2,1)S(1)}, u32[]{:S(2)}, u32[]{:S(2)}) collective-permute-start(bf16[2,1,2,3,32,256]{5,4,3,2,1,0:T(8,128)(2,1)S(1)} %pad_maximum_fusion.4), channel_id=1, source_target_pairs={{0,4},{1,5},{2,6},{3,7},{4,0},{5,1},{6,2},{7,3},{8,12},{9,13},{10,... | collective-permute-start | bytes 589832 | tf_op jit(solution)/shard_map/ppermute | solution.py:157
  58.4 8.0 %collective-permute-start.14 = (bf16[3,32,128]{2,1,0:T(8,128)(2,1)S(1)}, bf16[3,32,128]{2,1,0:T(8,128)(2,1)S(1)}, u32[]{:S(2)}, u32[]{:S(2)}) collective-permute-start(bf16[3,32,128]{2,1,0:T(8,128)(2,1)S(1)} %get-tuple-element.94), channel_id=1, source_target_pairs={{0,4},{1,5},{2,6},{3,7},{4,0},{5,1},{6,2},{7,3},{8,12},{9,13},{10,... | collective-permute-start | bytes 73736 | tf_op jit(solution)/shard_map/ppermute | solution.py:157
  59.7 7.8 %collective-permute-start.16 = (bf16[3,32,128]{2,1,0:T(8,128)(2,1)S(1)}, bf16[3,32,128]{2,1,0:T(8,128)(2,1)S(1)}, u32[]{:S(2)}, u32[]{:S(2)}) collective-permute-start(bf16[3,32,128]{2,1,0:T(8,128)(2,1)S(1)} %get-tuple-element.94), channel_id=1, source_target_pairs={{0,20},{1,21},{2,22},{3,23},{4,16},{5,17},{6,18},{7,19},{8,28},{9,... | collective-permute-start | bytes 73736 | tf_op jit(solution)/shard_map/ppermute | solution.py:289
  60.8 5.5 %collective-permute-start.15 = (bf16[3,32,128]{2,1,0:T(8,128)(2,1)S(1)}, bf16[3,32,128]{2,1,0:T(8,128)(2,1)S(1)}, u32[]{:S(2)}, u32[]{:S(2)}) collective-permute-start(bf16[3,32,128]{2,1,0:T(8,128)(2,1)S(1)} %get-tuple-element.93), channel_id=1, source_target_pairs={{0,16},{8,24},{16,0},{24,8},{1,17},{9,25},{17,1},{25,9},{2,18},{10... | collective-permute-start | bytes 73736 | tf_op jit(solution)/shard_map/ppermute | solution.py:157
  67.5 1.9 %collective-permute-start.18 = (f32[3,32,128]{2,1,0:T(8,128)S(1)}, f32[3,32,128]{2,1,0:T(8,128)S(1)}, u32[]{:S(2)}, u32[]{:S(2)}) collective-permute-start(f32[3,32,128]{2,1,0:T(8,128)S(1)} %add_add_fusion), channel_id=1, source_target_pairs={{0,8},{8,0},{16,24},{24,16},{1,9},{9,1},{17,25},{25,17},{2,10},{10... | collective-permute-start | bytes 147464 | tf_op jit(solution)/shard_map/ppermute | solution.py:157

commit v9 on v8

--- a/solution.py
+++ b/solution.py
@@ -278,16 +278,16 @@
     tail = (3, slab, width // 2)
     parts = [lax.dynamic_index_in_dim(sums.reshape((-1, 4) + tail), quad, 1, keepdims=False) for quad in quads]
     sums = parts[0]
-    for m in range(1, 4):
+    for m in (3, 2, 1):
         sums = sums + swapped(parts[m].astype(bf16), "col", n_col, m).astype(f32)
     for bit in range(2, n_bits - 1):
         keep, send = halves(sums.reshape((-1, 2) + tail), 1, ways[bit])
         sums = keep + swapped(send.astype(bf16), "col", n_col, 1 << bit).astype(f32)
     keep, send = (part.astype(bf16) for part in halves(sums.reshape((2,) + tail), 0, ways[n_bits - 1]))
     across = [(r * n_col + c, (r ^ 2) * n_col + (c ^ (n_col // 2))) for r in range(n_row) for c in range(n_col)]
+    far = lax.ppermute(send, ("row", "col"), across).astype(f32)
     near = keep.astype(f32) + swapped(send, "col", n_col, n_col // 2).astype(f32)
-    far = swapped(keep, "row", n_row, 2).astype(f32) + lax.ppermute(send, ("row", "col"), across).astype(f32)
-    mine = near + far
+    mine = near + (swapped(keep, "row", n_row, 2).astype(f32) + far)
     for bit in range(2, n_row.bit_length() - 1):
         mine = mine + swapped(mine, "row", n_row, 1 << bit)
 

time: 70.2 us -> 70.2 us (level)
  transfers between devices with their start and end apart: 19 -> 19, of which waited for: 12 -> 11; matrix products, arithmetic and copies ran while one was open for 1% -> 1% of each run, Pallas kernels for 8% -> 8%
where the time goes in v9:
time: 70.2 us; the launch traced here: 70 us
  starting transfers between devices  30.6 us (44%)
  waiting for transfers between devices  26.1 us (37%)
  Pallas kernels  9.69 us (14%)
  other arithmetic  1.73 us (2%)
  between operations  1.01 us (1%)
  local copies, waits for them, and re-layouts  0.92 us (1%)
    ppermute x16, starting transfers between devices, swapped(): return lax.ppermute(value, axis, [(i, i ^ mask) for i in range(size)])  24.6 us
    ppermute x16, waiting for transfers between devices, swapped(): return lax.ppermute(value, axis, [(i, i ^ mask) for i in range(size)])  22.9 us
    ppermute x2, starting transfers between devices, body(): got.append(lax.ppermute(part, ('row', 'col'), moves))  4.76 us
    pallas_call x1, Pallas kernels, body(): pl.pallas_call(functools.partial(product_kernel, n_row, n_col, (orders[0]...  3.23 us
    ppermute x2, waiting for transfers between devices, body(): got.append(lax.ppermute(part, ('row', 'col'), moves))  2.26 us
    pallas_call x1, Pallas kernels, body(): pl.pallas_call(prepare_kernel, out_shape=[shape((width, width), f32), sha...  2.18 us
    pallas_call x1, Pallas kernels, body(): pl.pallas_call(functools.partial(column_kernel, n_row), out_shape=[shape(...  1.78 us
    pallas_call x1, Pallas kernels, body(): pl.pallas_call(functools.partial(form_kernel, n_row), out_shape=shape(bas...  1.49 us
  transfers between devices with their start and end apart: 19, of which 11 were waited for; matrix products, arithmetic and copies ran while one was open for 1% of the time, Pallas kernels for 8%

profile of v9, /device:TPU:0, one launch (start us, length us, event | category | flops | bytes accessed | tf_op | source)
XLA Modules:
  0.0 70.0 jit_solution(14962970890506254215)
XLA Ops:
  0.7 1.0 %pad_maximum_fusion.3 = bf16[2,6,32,256]{3,2,1,0:T(8,128)(2,1)S(1)} fusion(bf16[1,6,32,256]{3,2,1,0:T(8,128)(2,1)} %bitcast.120, bf16[1,6,32,256]{3,2,1,0:T(8,128)(2,1)} %bitcast.121), kind=kLoop, calls=%fused_computation.13 | loop fusion | flops 98304 | bytes 393216 | tf_op jit(solution)/shard_map/stack | solution.py:189
  1.8 4.1 %collective-permute-start = (bf16[2,3,32,256]{3,2,1,0:T(8,128)(2,1)S(1)}, bf16[2,3,32,256]{3,2,1,0:T(8,128)(2,1)S(1)}, u32[]{:S(2)}, u32[]{:S(2)}) collective-permute-start(bf16[2,3,32,256]{3,2,1,0:T(8,128)(2,1)S(1)} %get-tuple-element.86), channel_id=1, source_target_pairs={{0,4},{1,12},{2,20},{3,28},{4,0},{5,8},{6,16},{7,24},{8,5},{9,13},... | collective-permute-start | bytes 294920 | tf_op jit(solution)/shard_map/ppermute | solution.py:199
  5.9 0.7 collective-permute-start.1
  6.5 0.1 collective-permute-start.4
  6.6 2.3 %collective-permute-done = bf16[2,3,32,256]{3,2,1,0:T(8,128)(2,1)S(1)} collective-permute-done((bf16[2,3,32,256]{3,2,1,0:T(8,128)(2,1)S(1)}, bf16[2,3,32,256]{3,2,1,0:T(8,128)(2,1)S(1)}, u32[]{:S(2)}, u32[]{:S(2)}) %collective-permute-start) | collective-permute-done | bytes 98336 | tf_op jit(solution)/shard_map/ppermute | solution.py:199
  8.9 4.3 %collective-permute-start.2 = (bf16[2,3,32,256]{3,2,1,0:T(8,128)(2,1)S(1)}, bf16[2,3,32,256]{3,2,1,0:T(8,128)(2,1)S(1)}, u32[]{:S(2)}, u32[]{:S(2)}) collective-permute-start(bf16[2,3,32,256]{3,2,1,0:T(8,128)(2,1)S(1)} %collective-permute-done), channel_id=1, source_target_pairs={{0,16},{8,24},{16,0},{24,8},{1,17},{9,25},{17,1},{25,9},{2,18},{10... | collective-permute-start | bytes 294920 | tf_op jit(solution)/shard_map/ppermute | solution.py:157
  13.1 0.0 collective-permute-done.1
  13.1 5.7 %collective-permute-start.3 = (bf16[2,3,32,256]{3,2,1,0:T(8,128)(2,1)S(1)}, bf16[2,3,32,256]{3,2,1,0:T(8,128)(2,1)S(1)}, u32[]{:S(2)}, u32[]{:S(2)}) collective-permute-start(bf16[2,3,32,256]{3,2,1,0:T(8,128)(2,1)S(1)} %collective-permute-done.1), channel_id=1, source_target_pairs={{0,16},{8,24},{16,0},{24,8},{1,17},{9,25},{17,1},{25,9},{2,18},{10... | collective-permute-start | bytes 294920 | tf_op jit(solution)/shard_map/ppermute | solution.py:157
  18.9 0.0 collective-permute-done.2
  18.9 2.6 %collective-permute-done.3 = bf16[2,3,32,256]{3,2,1,0:T(8,128)(2,1)S(1)} collective-permute-done((bf16[2,3,32,256]{3,2,1,0:T(8,128)(2,1)S(1)}, bf16[2,3,32,256]{3,2,1,0:T(8,128)(2,1)S(1)}, u32[]{:S(2)}, u32[]{:S(2)}) %collective-permute-start.3) | collective-permute-done | bytes 98336 | tf_op jit(solution)/shard_map/ppermute | solution.py:157
  21.5 0.0 collective-permute-done.4
  21.6 0.1 collective-permute-start.5
  21.7 1.5 %form.1.rows = bf16[2,2,6,32,256]{4,3,2,1,0:T(8,128)(2,1)S(1)} custom-call(s32[18]{0:T(128)S(1)} %copy-done.3, s32[12]{0:T(128)S(1)} %copy-done.4, f32[256,256]{1,0:T(8,128)S(1)} %copy-done.1, f32[256,256]{1,0:T(8,128)S(1)} %copy-done.2, bf16[2,2,6,32,256]{4,3,2,1,0:T(8,128)(2,1)S(1)} %pad_maximum_fusion.2.base), custom_call_target="tpu_custom_call" | custom-call | flops 134217728 | bytes 262144 | tf_op jit(solution)/shard_map/form/pallas_call | solution.py:210
  23.2 0.2 collective-permute-done.5
  23.4 0.1 pad_maximum_fusion
  23.5 3.2 %products.1 = (f32[4,2,3,32,256]{4,3,2,1,0:T(8,128)S(1)}, f32[4,2,3,32,256]{4,3,2,1,0:T(8,128)S(1)}, bf16[4,2,3,32,256]{4,3,2,1,0:T(8,128)(2,1)S(1)}, bf16[4,2,3,32,256]{4,3,2,1,0:T(8,128)(2,1)S(1)}) custom-call(s32[18]{0:T(128)S(1)} %copy-done.3, s32[12]{0:T(128)S(1)} %copy-done.4, f32[256,256]{1,0:T(8,128)S(1)} %copy-done.1, f32[256,256]{1,0:T(8,128)S(1)} %copy-done.2, ...), custom_call_target="tpu_custom_call" | custom-call | tf_op jit(solution)/shard_map/products/pallas_call | solution.py:226
  26.7 2.4 %collective-permute-start.8 = (bf16[4,2,3,32,256]{4,3,2,1,0:T(8,128)(2,1)S(1)}, bf16[4,2,3,32,256]{4,3,2,1,0:T(8,128)(2,1)S(1)}, u32[]{:S(2)}, u32[]{:S(2)}) collective-permute-start(bf16[4,2,3,32,256]{4,3,2,1,0:T(8,128)(2,1)S(1)} %get-tuple-element.51), channel_id=1, source_target_pairs={{0,2},{1,3},{2,0},{3,1},{4,6},{5,7},{6,4},{7,5},{8,10},{9,11},{10,... | collective-permute-start | bytes 1179656 | tf_op jit(solution)/shard_map/ppermute | solution.py:157
  29.1 0.3 collective-permute-start.6
  29.4 2.2 %prepare.1 = (f32[256,256]{1,0:T(8,128)S(1)}, f32[3,32,256]{2,1,0:T(8,128)S(1)}) custom-call(bf16[256,256]{1,0:T(8,128)(2,1)S(1)} %copy-done.5, f32[256,256]{1,0:T(8,128)S(1)} %copy-done.1, f32[256,256]{1,0:T(8,128)S(1)} %copy-done.2, f32[4,2,3,32,256]{4,3,2,1,0:T(8,128)S(1)} %get-tuple-element.46.after), custom_call_target="tpu_custom_call" | custom-call | flops 1006632960 | bytes 524288 | tf_op jit(solution)/shard_map/prepare/pallas_call | solution.py:238
  31.6 7.1 %collective-permute-done.8 = bf16[4,2,3,32,256]{4,3,2,1,0:T(8,128)(2,1)S(1)} collective-permute-done((bf16[4,2,3,32,256]{4,3,2,1,0:T(8,128)(2,1)S(1)}, bf16[4,2,3,32,256]{4,3,2,1,0:T(8,128)(2,1)S(1)}, u32[]{:S(2)}, u32[]{:S(2)}) %collective-permute-start.8) | collective-permute-done | bytes 393248 | tf_op jit(solution)/shard_map/ppermute | solution.py:157
  38.7 0.1 convert_add_fusion
  38.9 0.8 %collective-permute-start.9 = (bf16[2,2,3,32,256]{4,3,2,1,0:T(8,128)(2,1)S(1)}, bf16[2,2,3,32,256]{4,3,2,1,0:T(8,128)(2,1)S(1)}, u32[]{:S(2)}, u32[]{:S(2)}) collective-permute-start(bf16[2,2,3,32,256]{4,3,2,1,0:T(8,128)(2,1)S(1)} %fusion.1), channel_id=1, source_target_pairs={{0,1},{1,0},{2,3},{3,2},{4,5},{5,4},{6,7},{7,6},{8,9},{9,8},{10,11... | collective-permute-start | bytes 589832 | tf_op jit(solution)/shard_map/ppermute | solution.py:157
  39.7 0.4 collective-permute-done.6
  40.2 0.1 convert_add_fusion.1
  40.4 0.9 %collective-permute-start.7 = (bf16[2,2,3,32,256]{4,3,2,1,0:T(8,128)(2,1)S(1)}, bf16[2,2,3,32,256]{4,3,2,1,0:T(8,128)(2,1)S(1)}, u32[]{:S(2)}, u32[]{:S(2)}) collective-permute-start(bf16[2,2,3,32,256]{4,3,2,1,0:T(8,128)(2,1)S(1)} %fusion), channel_id=1, source_target_pairs={{0,2},{1,3},{2,0},{3,1},{4,6},{5,7},{6,4},{7,5},{8,10},{9,11},{10,... | collective-permute-start | bytes 589832 | tf_op jit(solution)/shard_map/ppermute | solution.py:157
  41.2 4.4 %collective-permute-done.9 = bf16[2,2,3,32,256]{4,3,2,1,0:T(8,128)(2,1)S(1)} collective-permute-done((bf16[2,2,3,32,256]{4,3,2,1,0:T(8,128)(2,1)S(1)}, bf16[2,2,3,32,256]{4,3,2,1,0:T(8,128)(2,1)S(1)}, u32[]{:S(2)}, u32[]{:S(2)}) %collective-permute-start.9) | collective-permute-done | bytes 196640 | tf_op jit(solution)/shard_map/ppermute | solution.py:157
  45.6 0.8 %collective-permute-done.7 = bf16[2,2,3,32,256]{4,3,2,1,0:T(8,128)(2,1)S(1)} collective-permute-done((bf16[2,2,3,32,256]{4,3,2,1,0:T(8,128)(2,1)S(1)}, bf16[2,2,3,32,256]{4,3,2,1,0:T(8,128)(2,1)S(1)}, u32[]{:S(2)}, u32[]{:S(2)}) %collective-permute-start.7) | collective-permute-done | bytes 196640 | tf_op jit(solution)/shard_map/ppermute | solution.py:157
  46.5 1.0 %sums.1 = f32[2,8,3,32,128]{4,3,2,1,0:T(8,128)S(1)} custom-call(bf16[2,2,6,32,256]{4,3,2,1,0:T(8,128)(2,1)S(1)} %form.1.rows, f32[2,2,3,32,256]{4,3,2,1,0:T(8,128)S(1)} %bitcast_add_fusion.2.total_low, f32[2,2,3,32,256]{4,3,2,1,0:T(8,128)S(1)} %bitcast_add_fusion.1.total_high, f32[256,256]{1,0:T(8,128)S(1)} %get-tuple-element.54.linked, ...), custom_call_target="tpu_custom_call" | custom-call | tf_op jit(solution)/shard_map/sums/pallas_call | solution.py:268
  47.5 0.1 collective-permute-start.10
  47.7 1.6 %collective-permute-done.10 = f32[8,3,32,128]{3,2,1,0:T(8,128)S(1)} collective-permute-done((f32[8,3,32,128]{3,2,1,0:T(8,128)S(1)}, f32[8,3,32,128]{3,2,1,0:T(8,128)S(1)}, u32[]{:S(2)}, u32[]{:S(2)}) %collective-permute-start.10) | collective-permute-done | bytes 393248 | tf_op jit(solution)/shard_map/ppermute | solution.py:157
  49.3 0.1 bitcast_add_fusion
  49.4 2.1 %collective-permute-start.11 = (bf16[2,3,32,128]{3,2,1,0:T(8,128)(2,1)S(1)}, bf16[2,3,32,128]{3,2,1,0:T(8,128)(2,1)S(1)}, u32[]{:S(2)}, u32[]{:S(2)}) collective-permute-start(bf16[2,3,32,128]{3,2,1,0:T(8,128)(2,1)S(1)} %get-tuple-element.81), channel_id=1, source_target_pairs={{0,3},{1,2},{2,1},{3,0},{4,7},{5,6},{6,5},{7,4},{8,11},{9,10},{10,... | collective-permute-start | bytes 147464 | tf_op jit(solution)/shard_map/ppermute | solution.py:157
  51.5 0.6 collective-permute-start.12
  52.1 0.8 %collective-permute-start.13 = (bf16[2,3,32,128]{3,2,1,0:T(8,128)(2,1)S(1)}, bf16[2,3,32,128]{3,2,1,0:T(8,128)(2,1)S(1)}, u32[]{:S(2)}, u32[]{:S(2)}) collective-permute-start(bf16[2,3,32,128]{3,2,1,0:T(8,128)(2,1)S(1)} %get-tuple-element.82), channel_id=1, source_target_pairs={{0,1},{1,0},{2,3},{3,2},{4,5},{5,4},{6,7},{7,6},{8,9},{9,8},{10,11... | collective-permute-start | bytes 147464 | tf_op jit(solution)/shard_map/ppermute | solution.py:157
  53.0 3.2 %collective-permute-start.17 = (bf16[2,1,2,3,32,256]{5,4,3,2,1,0:T(8,128)(2,1)S(1)}, bf16[2,1,2,3,32,256]{5,4,3,2,1,0:T(8,128)(2,1)S(1)}, u32[]{:S(2)}, u32[]{:S(2)}) collective-permute-start(bf16[2,1,2,3,32,256]{5,4,3,2,1,0:T(8,128)(2,1)S(1)} %pad_maximum_fusion.4), channel_id=1, source_target_pairs={{0,4},{1,5},{2,6},{3,7},{4,0},{5,1},{6,2},{7,3},{8,12},{9,13},{10,... | collective-permute-start | bytes 589832 | tf_op jit(solution)/shard_map/ppermute | solution.py:157
  56.2 0.0 collective-permute-done.11
  56.2 0.0 collective-permute-done.12
  56.2 0.0 collective-permute-done.13
  56.3 2.6 %collective-permute-start.14 = (bf16[3,32,128]{2,1,0:T(8,128)(2,1)S(1)}, bf16[3,32,128]{2,1,0:T(8,128)(2,1)S(1)}, u32[]{:S(2)}, u32[]{:S(2)}) collective-permute-start(bf16[3,32,128]{2,1,0:T(8,128)(2,1)S(1)} %get-tuple-element.94), channel_id=1, source_target_pairs={{0,4},{1,5},{2,6},{3,7},{4,0},{5,1},{6,2},{7,3},{8,12},{9,13},{10,... | collective-permute-start | bytes 73736 | tf_op jit(solution)/shard_map/ppermute | solution.py:157
  58.9 1.3 %collective-permute-start.16 = (bf16[3,32,128]{2,1,0:T(8,128)(2,1)S(1)}, bf16[3,32,128]{2,1,0:T(8,128)(2,1)S(1)}, u32[]{:S(2)}, u32[]{:S(2)}) collective-permute-start(bf16[3,32,128]{2,1,0:T(8,128)(2,1)S(1)} %get-tuple-element.94), channel_id=1, source_target_pairs={{0,20},{1,21},{2,22},{3,23},{4,16},{5,17},{6,18},{7,19},{8,28},{9,... | collective-permute-start | bytes 73736 | tf_op jit(solution)/shard_map/ppermute | solution.py:288
  60.2 0.6 collective-permute-start.15
  60.7 5.6 %collective-permute-done.17 = bf16[2,1,2,3,32,256]{5,4,3,2,1,0:T(8,128)(2,1)S(1)} collective-permute-done((bf16[2,1,2,3,32,256]{5,4,3,2,1,0:T(8,128)(2,1)S(1)}, bf16[2,1,2,3,32,256]{5,4,3,2,1,0:T(8,128)(2,1)S(1)}, u32[]{:S(2)}, u32[]{:S(2)}) %collective-permute-start.17) | collective-permute-done | bytes 196640 | tf_op jit(solution)/shard_map/ppermute | solution.py:157
  66.4 0.2 collective-permute-done.14
  66.6 0.8 %collective-permute-done.16 = bf16[3,32,128]{2,1,0:T(8,128)(2,1)S(1)} collective-permute-done((bf16[3,32,128]{2,1,0:T(8,128)(2,1)S(1)}, bf16[3,32,128]{2,1,0:T(8,128)(2,1)S(1)}, u32[]{:S(2)}, u32[]{:S(2)}) %collective-permute-start.16) | collective-permute-done | bytes 24608 | tf_op jit(solution)/shard_map/ppermute | solution.py:288
  67.5 0.1 collective-permute-start.18
  67.6 1.8 %columns.1 = (f32[6,32,256]{2,1,0:T(8,128)}, f32[6,32,256]{2,1,0:T(8,128)}) custom-call(s32[18]{0:T(128)S(1)} %copy-done.3, s32[12]{0:T(128)S(1)} %copy-done.4, f32[2,3,32,256]{3,2,1,0:T(8,128)S(1)} %bitcast.105, bf16[2,3,32,256]{3,2,1,0:T(8,128)(2,1)S(1)} %bitcast.107, f32[2,3,32,256]{3,2,1,0:T(8,128)S(1)} %bitcast.104, ...), custom_call_target="tpu_custom_call" | custom-call | tf_op jit(solution)/shard_map/columns/pallas_call | solution.py:295
  69.3 0.0 collective-permute-done.18
  69.4 0.6 slice_bitcast_fusion.2
  (35 shorter events, 0.6 us)
Async XLA Ops:
  0.6 21.1 %copy-start.1 = (f32[256,256]{1,0:T(8,128)S(1)}, f32[256,256]{1,0:T(8,128)}, u32[]{:S(2)}) copy-start(f32[256,256]{1,0:T(8,128)} %inv1.5) | copy-start | bytes 786436
  0.6 21.1 %copy-start.2 = (f32[256,256]{1,0:T(8,128)S(1)}, f32[256,256]{1,0:T(8,128)}, u32[]{:S(2)}) copy-start(f32[256,256]{1,0:T(8,128)} %inv2.5) | copy-start | bytes 786436
  0.7 21.1 %copy-start.3 = (s32[18]{0:T(128)S(1)}, s32[18]{0:T(128)}, u32[]{:S(2)}) copy-start(s32[18]{0:T(128)} %struct1.5) | copy-start | bytes 220
  0.7 21.1 %copy-start.4 = (s32[12]{0:T(128)S(1)}, s32[12]{0:T(128)}, u32[]{:S(2)}) copy-start(s32[12]{0:T(128)} %struct2.5) | copy-start | bytes 148
  1.8 7.1 %collective-permute-start = (bf16[2,3,32,256]{3,2,1,0:T(8,128)(2,1)S(1)}, bf16[2,3,32,256]{3,2,1,0:T(8,128)(2,1)S(1)}, u32[]{:S(2)}, u32[]{:S(2)}) collective-permute-start(bf16[2,3,32,256]{3,2,1,0:T(8,128)(2,1)S(1)} %get-tuple-element.86), channel_id=1, source_target_pairs={{0,4},{1,12},{2,20},{3,28},{4,0},{5,8},{6,16},{7,24},{8,5},{9,13},... | collective-permute-start | bytes 294920 | tf_op jit(solution)/shard_map/ppermute | solution.py:199
  5.9 7.3 %collective-permute-start.1 = (bf16[2,3,32,256]{3,2,1,0:T(8,128)(2,1)S(1)}, bf16[2,3,32,256]{3,2,1,0:T(8,128)(2,1)S(1)}, u32[]{:S(2)}, u32[]{:S(2)}) collective-permute-start(bf16[2,3,32,256]{3,2,1,0:T(8,128)(2,1)S(1)} %get-tuple-element.87), channel_id=1, source_target_pairs={{0,0},{1,8},{2,16},{3,24},{4,4},{5,12},{6,20},{7,28},{8,1},{9,9},{... | collective-permute-start | bytes 294920 | tf_op jit(solution)/shard_map/ppermute | solution.py:199
  6.5 15.0 %collective-permute-start.4 = (bf16[2,6,32,256]{3,2,1,0:T(8,128)(2,1)S(1)}, bf16[2,6,32,256]{3,2,1,0:T(8,128)(2,1)S(1)}, u32[]{:S(2)}, u32[]{:S(2)}) collective-permute-start(bf16[2,6,32,256]{3,2,1,0:T(8,128)(2,1)S(1)} %pad_maximum_fusion.3), channel_id=1, source_target_pairs={{0,4},{1,5},{2,6},{3,7},{4,0},{5,1},{6,2},{7,3},{8,12},{9,13},{10,... | collective-permute-start | bytes 589832 | tf_op jit(solution)/shard_map/ppermute | solution.py:157
  8.9 10.0 %collective-permute-start.2 = (bf16[2,3,32,256]{3,2,1,0:T(8,128)(2,1)S(1)}, bf16[2,3,32,256]{3,2,1,0:T(8,128)(2,1)S(1)}, u32[]{:S(2)}, u32[]{:S(2)}) collective-permute-start(bf16[2,3,32,256]{3,2,1,0:T(8,128)(2,1)S(1)} %collective-permute-done), channel_id=1, source_target_pairs={{0,16},{8,24},{16,0},{24,8},{1,17},{9,25},{17,1},{25,9},{2,18},{10... | collective-permute-start | bytes 294920 | tf_op jit(solution)/shard_map/ppermute | solution.py:157
  13.1 8.3 %collective-permute-start.3 = (bf16[2,3,32,256]{3,2,1,0:T(8,128)(2,1)S(1)}, bf16[2,3,32,256]{3,2,1,0:T(8,128)(2,1)S(1)}, u32[]{:S(2)}, u32[]{:S(2)}) collective-permute-start(bf16[2,3,32,256]{3,2,1,0:T(8,128)(2,1)S(1)} %collective-permute-done.1), channel_id=1, source_target_pairs={{0,16},{8,24},{16,0},{24,8},{1,17},{9,25},{17,1},{25,9},{2,18},{10... | collective-permute-start | bytes 294920 | tf_op jit(solution)/shard_map/ppermute | solution.py:157
  21.5 2.0 %copy-start = (bf16[6,1,3,1,256,256]{5,4,3,2,1,0:T(8,128)(2,1)S(1)}, bf16[6,1,3,1,256,256]{5,4,3,2,1,0:T(8,128)(2,1)}, u32[]{:S(2)}) copy-start(bf16[6,1,3,1,256,256]{5,4,3,2,1,0:T(8,128)(2,1)} %param.8) | copy-start | bytes 7077892
  21.6 1.8 %collective-permute-start.5 = (bf16[2,2,2,3,32,256]{5,4,3,2,1,0:T(8,128)(2,1)S(1)}, bf16[2,2,2,3,32,256]{5,4,3,2,1,0:T(8,128)(2,1)S(1)}, u32[]{:S(2)}, u32[]{:S(2)}) collective-permute-start(bf16[2,2,2,3,32,256]{5,4,3,2,1,0:T(8,128)(2,1)S(1)} %pad_maximum_fusion.1), channel_id=1, source_target_pairs={{0,8},{8,0},{16,24},{24,16},{1,9},{9,1},{17,25},{25,17},{2,10},{10... | collective-permute-start | bytes 1179656 | tf_op jit(solution)/shard_map/ppermute | solution.py:157
  23.4 6.0 %copy-start.5 = (bf16[256,256]{1,0:T(8,128)(2,1)S(1)}, bf16[256,256]{1,0:T(8,128)(2,1)}, u32[]{:S(2)}) copy-start(bf16[256,256]{1,0:T(8,128)(2,1)} %link.1) | copy-start | bytes 393220
  26.7 12.0 %collective-permute-start.8 = (bf16[4,2,3,32,256]{4,3,2,1,0:T(8,128)(2,1)S(1)}, bf16[4,2,3,32,256]{4,3,2,1,0:T(8,128)(2,1)S(1)}, u32[]{:S(2)}, u32[]{:S(2)}) collective-permute-start(bf16[4,2,3,32,256]{4,3,2,1,0:T(8,128)(2,1)S(1)} %get-tuple-element.51), channel_id=1, source_target_pairs={{0,2},{1,3},{2,0},{3,1},{4,6},{5,7},{6,4},{7,5},{8,10},{9,11},{10,... | collective-permute-start | bytes 1179656 | tf_op jit(solution)/shard_map/ppermute | solution.py:157
  29.1 11.1 %collective-permute-start.6 = (bf16[4,2,3,32,256]{4,3,2,1,0:T(8,128)(2,1)S(1)}, bf16[4,2,3,32,256]{4,3,2,1,0:T(8,128)(2,1)S(1)}, u32[]{:S(2)}, u32[]{:S(2)}) collective-permute-start(bf16[4,2,3,32,256]{4,3,2,1,0:T(8,128)(2,1)S(1)} %get-tuple-element.47), channel_id=1, source_target_pairs={{0,1},{1,0},{2,3},{3,2},{4,5},{5,4},{6,7},{7,6},{8,9},{9,8},{10,11... | collective-permute-start | bytes 1179656 | tf_op jit(solution)/shard_map/ppermute | solution.py:157
  38.9 6.7 %collective-permute-start.9 = (bf16[2,2,3,32,256]{4,3,2,1,0:T(8,128)(2,1)S(1)}, bf16[2,2,3,32,256]{4,3,2,1,0:T(8,128)(2,1)S(1)}, u32[]{:S(2)}, u32[]{:S(2)}) collective-permute-start(bf16[2,2,3,32,256]{4,3,2,1,0:T(8,128)(2,1)S(1)} %fusion.1), channel_id=1, source_target_pairs={{0,1},{1,0},{2,3},{3,2},{4,5},{5,4},{6,7},{7,6},{8,9},{9,8},{10,11... | collective-permute-start | bytes 589832 | tf_op jit(solution)/shard_map/ppermute | solution.py:157
  40.4 6.1 %collective-permute-start.7 = (bf16[2,2,3,32,256]{4,3,2,1,0:T(8,128)(2,1)S(1)}, bf16[2,2,3,32,256]{4,3,2,1,0:T(8,128)(2,1)S(1)}, u32[]{:S(2)}, u32[]{:S(2)}) collective-permute-start(bf16[2,2,3,32,256]{4,3,2,1,0:T(8,128)(2,1)S(1)} %fusion), channel_id=1, source_target_pairs={{0,2},{1,3},{2,0},{3,1},{4,6},{5,7},{6,4},{7,5},{8,10},{9,11},{10,... | collective-permute-start | bytes 589832 | tf_op jit(solution)/shard_map/ppermute | solution.py:157
  47.5 1.8 %collective-permute-start.10 = (f32[8,3,32,128]{3,2,1,0:T(8,128)S(1)}, f32[8,3,32,128]{3,2,1,0:T(8,128)S(1)}, u32[]{:S(2)}, u32[]{:S(2)}) collective-permute-start(f32[8,3,32,128]{3,2,1,0:T(8,128)S(1)} %dynamic-slice_bitcast_fusion), channel_id=1, source_target_pairs={{0,8},{8,0},{16,24},{24,16},{1,9},{9,1},{17,25},{25,17},{2,10},{10... | collective-permute-start | bytes 1179656 | tf_op jit(solution)/shard_map/ppermute | solution.py:157
  49.4 6.8 %collective-permute-start.11 = (bf16[2,3,32,128]{3,2,1,0:T(8,128)(2,1)S(1)}, bf16[2,3,32,128]{3,2,1,0:T(8,128)(2,1)S(1)}, u32[]{:S(2)}, u32[]{:S(2)}) collective-permute-start(bf16[2,3,32,128]{3,2,1,0:T(8,128)(2,1)S(1)} %get-tuple-element.81), channel_id=1, source_target_pairs={{0,3},{1,2},{2,1},{3,0},{4,7},{5,6},{6,5},{7,4},{8,11},{9,10},{10,... | collective-permute-start | bytes 147464 | tf_op jit(solution)/shard_map/ppermute | solution.py:157
  51.5 4.7 %collective-permute-start.12 = (bf16[2,3,32,128]{3,2,1,0:T(8,128)(2,1)S(1)}, bf16[2,3,32,128]{3,2,1,0:T(8,128)(2,1)S(1)}, u32[]{:S(2)}, u32[]{:S(2)}) collective-permute-start(bf16[2,3,32,128]{3,2,1,0:T(8,128)(2,1)S(1)} %get-tuple-element.83), channel_id=1, source_target_pairs={{0,2},{1,3},{2,0},{3,1},{4,6},{5,7},{6,4},{7,5},{8,10},{9,11},{10,... | collective-permute-start | bytes 147464 | tf_op jit(solution)/shard_map/ppermute | solution.py:157
  52.1 4.1 %collective-permute-start.13 = (bf16[2,3,32,128]{3,2,1,0:T(8,128)(2,1)S(1)}, bf16[2,3,32,128]{3,2,1,0:T(8,128)(2,1)S(1)}, u32[]{:S(2)}, u32[]{:S(2)}) collective-permute-start(bf16[2,3,32,128]{3,2,1,0:T(8,128)(2,1)S(1)} %get-tuple-element.82), channel_id=1, source_target_pairs={{0,1},{1,0},{2,3},{3,2},{4,5},{5,4},{6,7},{7,6},{8,9},{9,8},{10,11... | collective-permute-start | bytes 147464 | tf_op jit(solution)/shard_map/ppermute | solution.py:157
  53.0 13.3 %collective-permute-start.17 = (bf16[2,1,2,3,32,256]{5,4,3,2,1,0:T(8,128)(2,1)S(1)}, bf16[2,1,2,3,32,256]{5,4,3,2,1,0:T(8,128)(2,1)S(1)}, u32[]{:S(2)}, u32[]{:S(2)}) collective-permute-start(bf16[2,1,2,3,32,256]{5,4,3,2,1,0:T(8,128)(2,1)S(1)} %pad_maximum_fusion.4), channel_id=1, source_target_pairs={{0,4},{1,5},{2,6},{3,7},{4,0},{5,1},{6,2},{7,3},{8,12},{9,13},{10,... | collective-permute-start | bytes 589832 | tf_op jit(solution)/shard_map/ppermute | solution.py:157
  56.3 10.3 %collective-permute-start.14 = (bf16[3,32,128]{2,1,0:T(8,128)(2,1)S(1)}, bf16[3,32,128]{2,1,0:T(8,128)(2,1)S(1)}, u32[]{:S(2)}, u32[]{:S(2)}) collective-permute-start(bf16[3,32,128]{2,1,0:T(8,128)(2,1)S(1)} %get-tuple-element.94), channel_id=1, source_target_pairs={{0,4},{1,5},{2,6},{3,7},{4,0},{5,1},{6,2},{7,3},{8,12},{9,13},{10,... | collective-permute-start | bytes 73736 | tf_op jit(solution)/shard_map/ppermute | solution.py:157
  58.9 8.5 %collective-permute-start.16 = (bf16[3,32,128]{2,1,0:T(8,128)(2,1)S(1)}, bf16[3,32,128]{2,1,0:T(8,128)(2,1)S(1)}, u32[]{:S(2)}, u32[]{:S(2)}) collective-permute-start(bf16[3,32,128]{2,1,0:T(8,128)(2,1)S(1)} %get-tuple-element.94), channel_id=1, source_target_pairs={{0,20},{1,21},{2,22},{3,23},{4,16},{5,17},{6,18},{7,19},{8,28},{9,... | collective-permute-start | bytes 73736 | tf_op jit(solution)/shard_map/ppermute | solution.py:288
  60.2 6.4 %collective-permute-start.15 = (bf16[3,32,128]{2,1,0:T(8,128)(2,1)S(1)}, bf16[3,32,128]{2,1,0:T(8,128)(2,1)S(1)}, u32[]{:S(2)}, u32[]{:S(2)}) collective-permute-start(bf16[3,32,128]{2,1,0:T(8,128)(2,1)S(1)} %get-tuple-element.93), channel_id=1, source_target_pairs={{0,16},{8,24},{16,0},{24,8},{1,17},{9,25},{17,1},{25,9},{2,18},{10... | collective-permute-start | bytes 73736 | tf_op jit(solution)/shard_map/ppermute | solution.py:157
  67.5 1.9 %collective-permute-start.18 = (f32[3,32,128]{2,1,0:T(8,128)S(1)}, f32[3,32,128]{2,1,0:T(8,128)S(1)}, u32[]{:S(2)}, u32[]{:S(2)}) collective-permute-start(f32[3,32,128]{2,1,0:T(8,128)S(1)} %add_add_fusion), channel_id=1, source_target_pairs={{0,8},{8,0},{16,24},{24,16},{1,9},{9,1},{17,25},{25,17},{2,10},{10... | collective-permute-start | bytes 147464 | tf_op jit(solution)/shard_map/ppermute | solution.py:157

commit v10 on v8

--- a/solution.py
+++ b/solution.py
@@ -279,7 +279,7 @@
     parts = [lax.dynamic_index_in_dim(sums.reshape((-1, 4) + tail), quad, 1, keepdims=False) for quad in quads]
     sums = parts[0]
     for m in range(1, 4):
-        sums = sums + swapped(parts[m].astype(bf16), "col", n_col, m).astype(f32)
+        sums = sums + swapped(parts[m], "col", n_col, m)
     for bit in range(2, n_bits - 1):
         keep, send = halves(sums.reshape((-1, 2) + tail), 1, ways[bit])
         sums = keep + swapped(send.astype(bf16), "col", n_col, 1 << bit).astype(f32)

time: 70.2 us -> 73.5 us (1.047)
  waiting for transfers between devices: 26.1 us -> 29.4 us
    ppermute x16, waiting for transfers between devices: 22.7 us -> 27.1 us  [swapped(): return lax.ppermute(value, axis, [(i, i ^ mask) for i in range(size)])]
    ppermute x16, starting transfers between devices: 24.7 us -> 21.6 us  [swapped(): return lax.ppermute(value, axis, [(i, i ^ mask) for i in range(size)])]
    ppermute x1, starting transfers between devices: 1.11 us -> 4.29 us  [body(): lax.ppermute(send, ('row', 'col'), across).astype(f32)]
    ppermute x1, waiting for transfers between devices: 1.11 us -> 0.01 us  [body(): lax.ppermute(send, ('row', 'col'), across).astype(f32)]
  transfers between devices with their start and end apart: 19 -> 19, of which waited for: 12 -> 12; matrix products, arithmetic and copies ran while one was open for 1% -> 1% of each run, Pallas kernels for 8% -> 7%
where the time goes in v10:
time: 73.5 us; the launch traced here: 73.3 us
  starting transfers between devices  30.6 us (42%)
  waiting for transfers between devices  29.4 us (40%)
  Pallas kernels  9.69 us (13%)
  other arithmetic  1.74 us (2%)
  between operations  1.02 us (1%)
  local copies, waits for them, and re-layouts  0.9 us (1%)
    ppermute x16, waiting for transfers between devices, swapped(): return lax.ppermute(value, axis, [(i, i ^ mask) for i in range(size)])  27.1 us
    ppermute x16, starting transfers between devices, swapped(): return lax.ppermute(value, axis, [(i, i ^ mask) for i in range(size)])  21.6 us
    ppermute x2, starting transfers between devices, body(): got.append(lax.ppermute(part, ('row', 'col'), moves))  4.76 us
    ppermute x1, starting transfers between devices, body(): lax.ppermute(send, ('row', 'col'), across).astype(f32)  4.29 us
    pallas_call x1, Pallas kernels, body(): pl.pallas_call(functools.partial(product_kernel, n_row, n_col, (orders[0]...  3.23 us
    ppermute x2, waiting for transfers between devices, body(): got.append(lax.ppermute(part, ('row', 'col'), moves))  2.26 us
    pallas_call x1, Pallas kernels, body(): pl.pallas_call(prepare_kernel, out_shape=[shape((width, width), f32), sha...  2.18 us
    pallas_call x1, Pallas kernels, body(): pl.pallas_call(functools.partial(column_kernel, n_row), out_shape=[shape(...  1.78 us
  transfers between devices with their start and end apart: 19, of which 12 were waited for; matrix products, arithmetic and copies ran while one was open for 1% of the time, Pallas kernels for 7%

profile of v10, /device:TPU:0, one launch (start us, length us, event | category | flops | bytes accessed | tf_op | source)
XLA Modules:
  0.0 73.3 jit_solution(14296189420515800934)
XLA Ops:
  0.7 1.0 %pad_maximum_fusion.3 = bf16[2,6,32,256]{3,2,1,0:T(8,128)(2,1)S(1)} fusion(bf16[1,6,32,256]{3,2,1,0:T(8,128)(2,1)} %bitcast.112, bf16[1,6,32,256]{3,2,1,0:T(8,128)(2,1)} %bitcast.113), kind=kLoop, calls=%fused_computation.13 | loop fusion | flops 98304 | bytes 393216 | tf_op jit(solution)/shard_map/stack | solution.py:189
  1.8 4.1 %collective-permute-start = (bf16[2,3,32,256]{3,2,1,0:T(8,128)(2,1)S(1)}, bf16[2,3,32,256]{3,2,1,0:T(8,128)(2,1)S(1)}, u32[]{:S(2)}, u32[]{:S(2)}) collective-permute-start(bf16[2,3,32,256]{3,2,1,0:T(8,128)(2,1)S(1)} %get-tuple-element.86), channel_id=1, source_target_pairs={{0,4},{1,12},{2,20},{3,28},{4,0},{5,8},{6,16},{7,24},{8,5},{9,13},... | collective-permute-start | bytes 294920 | tf_op jit(solution)/shard_map/ppermute | solution.py:199
  5.9 0.7 collective-permute-start.1
  6.5 0.1 collective-permute-start.4
  6.6 2.3 %collective-permute-done = bf16[2,3,32,256]{3,2,1,0:T(8,128)(2,1)S(1)} collective-permute-done((bf16[2,3,32,256]{3,2,1,0:T(8,128)(2,1)S(1)}, bf16[2,3,32,256]{3,2,1,0:T(8,128)(2,1)S(1)}, u32[]{:S(2)}, u32[]{:S(2)}) %collective-permute-start) | collective-permute-done | bytes 98336 | tf_op jit(solution)/shard_map/ppermute | solution.py:199
  8.9 4.3 %collective-permute-start.2 = (bf16[2,3,32,256]{3,2,1,0:T(8,128)(2,1)S(1)}, bf16[2,3,32,256]{3,2,1,0:T(8,128)(2,1)S(1)}, u32[]{:S(2)}, u32[]{:S(2)}) collective-permute-start(bf16[2,3,32,256]{3,2,1,0:T(8,128)(2,1)S(1)} %collective-permute-done), channel_id=1, source_target_pairs={{0,16},{8,24},{16,0},{24,8},{1,17},{9,25},{17,1},{25,9},{2,18},{10... | collective-permute-start | bytes 294920 | tf_op jit(solution)/shard_map/ppermute | solution.py:157
  13.1 0.0 collective-permute-done.1
  13.1 5.7 %collective-permute-start.3 = (bf16[2,3,32,256]{3,2,1,0:T(8,128)(2,1)S(1)}, bf16[2,3,32,256]{3,2,1,0:T(8,128)(2,1)S(1)}, u32[]{:S(2)}, u32[]{:S(2)}) collective-permute-start(bf16[2,3,32,256]{3,2,1,0:T(8,128)(2,1)S(1)} %collective-permute-done.1), channel_id=1, source_target_pairs={{0,16},{8,24},{16,0},{24,8},{1,17},{9,25},{17,1},{25,9},{2,18},{10... | collective-permute-start | bytes 294920 | tf_op jit(solution)/shard_map/ppermute | solution.py:157
  18.9 0.0 collective-permute-done.2
  18.9 2.6 %collective-permute-done.3 = bf16[2,3,32,256]{3,2,1,0:T(8,128)(2,1)S(1)} collective-permute-done((bf16[2,3,32,256]{3,2,1,0:T(8,128)(2,1)S(1)}, bf16[2,3,32,256]{3,2,1,0:T(8,128)(2,1)S(1)}, u32[]{:S(2)}, u32[]{:S(2)}) %collective-permute-start.3) | collective-permute-done | bytes 98336 | tf_op jit(solution)/shard_map/ppermute | solution.py:157
  21.5 0.0 collective-permute-done.4
  21.6 0.1 collective-permute-start.5
  21.7 1.5 %form.1.rows = bf16[2,2,6,32,256]{4,3,2,1,0:T(8,128)(2,1)S(1)} custom-call(s32[18]{0:T(128)S(1)} %copy-done.3, s32[12]{0:T(128)S(1)} %copy-done.4, f32[256,256]{1,0:T(8,128)S(1)} %copy-done.1, f32[256,256]{1,0:T(8,128)S(1)} %copy-done.2, bf16[2,2,6,32,256]{4,3,2,1,0:T(8,128)(2,1)S(1)} %pad_maximum_fusion.2.base), custom_call_target="tpu_custom_call" | custom-call | flops 134217728 | bytes 262144 | tf_op jit(solution)/shard_map/form/pallas_call | solution.py:210
  23.2 0.2 collective-permute-done.5
  23.4 0.1 pad_maximum_fusion
  23.5 3.2 %products.1 = (f32[4,2,3,32,256]{4,3,2,1,0:T(8,128)S(1)}, f32[4,2,3,32,256]{4,3,2,1,0:T(8,128)S(1)}, bf16[4,2,3,32,256]{4,3,2,1,0:T(8,128)(2,1)S(1)}, bf16[4,2,3,32,256]{4,3,2,1,0:T(8,128)(2,1)S(1)}) custom-call(s32[18]{0:T(128)S(1)} %copy-done.3, s32[12]{0:T(128)S(1)} %copy-done.4, f32[256,256]{1,0:T(8,128)S(1)} %copy-done.1, f32[256,256]{1,0:T(8,128)S(1)} %copy-done.2, ...), custom_call_target="tpu_custom_call" | custom-call | tf_op jit(solution)/shard_map/products/pallas_call | solution.py:226
  26.7 2.4 %collective-permute-start.8 = (bf16[4,2,3,32,256]{4,3,2,1,0:T(8,128)(2,1)S(1)}, bf16[4,2,3,32,256]{4,3,2,1,0:T(8,128)(2,1)S(1)}, u32[]{:S(2)}, u32[]{:S(2)}) collective-permute-start(bf16[4,2,3,32,256]{4,3,2,1,0:T(8,128)(2,1)S(1)} %get-tuple-element.51), channel_id=1, source_target_pairs={{0,2},{1,3},{2,0},{3,1},{4,6},{5,7},{6,4},{7,5},{8,10},{9,11},{10,... | collective-permute-start | bytes 1179656 | tf_op jit(solution)/shard_map/ppermute | solution.py:157
  29.1 0.3 collective-permute-start.6
  29.4 2.2 %prepare.1 = (f32[256,256]{1,0:T(8,128)S(1)}, f32[3,32,256]{2,1,0:T(8,128)S(1)}) custom-call(bf16[256,256]{1,0:T(8,128)(2,1)S(1)} %copy-done.5, f32[256,256]{1,0:T(8,128)S(1)} %copy-done.1, f32[256,256]{1,0:T(8,128)S(1)} %copy-done.2, f32[4,2,3,32,256]{4,3,2,1,0:T(8,128)S(1)} %get-tuple-element.46.after), custom_call_target="tpu_custom_call" | custom-call | flops 1006632960 | bytes 524288 | tf_op jit(solution)/shard_map/prepare/pallas_call | solution.py:238
  31.6 7.1 %collective-permute-done.8 = bf16[4,2,3,32,256]{4,3,2,1,0:T(8,128)(2,1)S(1)} collective-permute-done((bf16[4,2,3,32,256]{4,3,2,1,0:T(8,128)(2,1)S(1)}, bf16[4,2,3,32,256]{4,3,2,1,0:T(8,128)(2,1)S(1)}, u32[]{:S(2)}, u32[]{:S(2)}) %collective-permute-start.8) | collective-permute-done | bytes 393248 | tf_op jit(solution)/shard_map/ppermute | solution.py:157
  38.7 0.1 convert_add_fusion
  38.9 0.8 %collective-permute-start.9 = (bf16[2,2,3,32,256]{4,3,2,1,0:T(8,128)(2,1)S(1)}, bf16[2,2,3,32,256]{4,3,2,1,0:T(8,128)(2,1)S(1)}, u32[]{:S(2)}, u32[]{:S(2)}) collective-permute-start(bf16[2,2,3,32,256]{4,3,2,1,0:T(8,128)(2,1)S(1)} %fusion.1), channel_id=1, source_target_pairs={{0,1},{1,0},{2,3},{3,2},{4,5},{5,4},{6,7},{7,6},{8,9},{9,8},{10,11... | collective-permute-start | bytes 589832 | tf_op jit(solution)/shard_map/ppermute | solution.py:157
  39.7 0.4 collective-permute-done.6
  40.2 0.1 convert_add_fusion.1
  40.4 0.9 %collective-permute-start.7 = (bf16[2,2,3,32,256]{4,3,2,1,0:T(8,128)(2,1)S(1)}, bf16[2,2,3,32,256]{4,3,2,1,0:T(8,128)(2,1)S(1)}, u32[]{:S(2)}, u32[]{:S(2)}) collective-permute-start(bf16[2,2,3,32,256]{4,3,2,1,0:T(8,128)(2,1)S(1)} %fusion), channel_id=1, source_target_pairs={{0,2},{1,3},{2,0},{3,1},{4,6},{5,7},{6,4},{7,5},{8,10},{9,11},{10,... | collective-permute-start | bytes 589832 | tf_op jit(solution)/shard_map/ppermute | solution.py:157
  41.2 4.4 %collective-permute-done.9 = bf16[2,2,3,32,256]{4,3,2,1,0:T(8,128)(2,1)S(1)} collective-permute-done((bf16[2,2,3,32,256]{4,3,2,1,0:T(8,128)(2,1)S(1)}, bf16[2,2,3,32,256]{4,3,2,1,0:T(8,128)(2,1)S(1)}, u32[]{:S(2)}, u32[]{:S(2)}) %collective-permute-start.9) | collective-permute-done | bytes 196640 | tf_op jit(solution)/shard_map/ppermute | solution.py:157
  45.6 0.8 %collective-permute-done.7 = bf16[2,2,3,32,256]{4,3,2,1,0:T(8,128)(2,1)S(1)} collective-permute-done((bf16[2,2,3,32,256]{4,3,2,1,0:T(8,128)(2,1)S(1)}, bf16[2,2,3,32,256]{4,3,2,1,0:T(8,128)(2,1)S(1)}, u32[]{:S(2)}, u32[]{:S(2)}) %collective-permute-start.7) | collective-permute-done | bytes 196640 | tf_op jit(solution)/shard_map/ppermute | solution.py:157
  46.5 1.0 %sums.1 = f32[2,8,3,32,128]{4,3,2,1,0:T(8,128)S(1)} custom-call(bf16[2,2,6,32,256]{4,3,2,1,0:T(8,128)(2,1)S(1)} %form.1.rows, f32[2,2,3,32,256]{4,3,2,1,0:T(8,128)S(1)} %bitcast_add_fusion.2.total_low, f32[2,2,3,32,256]{4,3,2,1,0:T(8,128)S(1)} %bitcast_add_fusion.1.total_high, f32[256,256]{1,0:T(8,128)S(1)} %get-tuple-element.54.linked, ...), custom_call_target="tpu_custom_call" | custom-call | tf_op jit(solution)/shard_map/sums/pallas_call | solution.py:268
  47.5 0.1 collective-permute-start.10
  47.7 3.2 %collective-permute-start.17 = (bf16[2,1,2,3,32,256]{5,4,3,2,1,0:T(8,128)(2,1)S(1)}, bf16[2,1,2,3,32,256]{5,4,3,2,1,0:T(8,128)(2,1)S(1)}, u32[]{:S(2)}, u32[]{:S(2)}) collective-permute-start(bf16[2,1,2,3,32,256]{5,4,3,2,1,0:T(8,128)(2,1)S(1)} %pad_maximum_fusion.4), channel_id=1, source_target_pairs={{0,4},{1,5},{2,6},{3,7},{4,0},{5,1},{6,2},{7,3},{8,12},{9,13},{10,... | collective-permute-start | bytes 589832 | tf_op jit(solution)/shard_map/ppermute | solution.py:157
  50.9 0.0 collective-permute-done.10
  50.9 0.1 bitcast_add_fusion
  51.0 0.7 collective-permute-start.11
  51.7 0.8 %collective-permute-start.12 = (f32[2,3,32,128]{3,2,1,0:T(8,128)S(1)}, f32[2,3,32,128]{3,2,1,0:T(8,128)S(1)}, u32[]{:S(2)}, u32[]{:S(2)}) collective-permute-start(f32[2,3,32,128]{3,2,1,0:T(8,128)S(1)} %get-tuple-element.83), channel_id=1, source_target_pairs={{0,2},{1,3},{2,0},{3,1},{4,6},{5,7},{6,4},{7,5},{8,10},{9,11},{10,... | collective-permute-start | bytes 294920 | tf_op jit(solution)/shard_map/ppermute | solution.py:157
  52.5 2.0 %collective-permute-start.13 = (f32[2,3,32,128]{3,2,1,0:T(8,128)S(1)}, f32[2,3,32,128]{3,2,1,0:T(8,128)S(1)}, u32[]{:S(2)}, u32[]{:S(2)}) collective-permute-start(f32[2,3,32,128]{3,2,1,0:T(8,128)S(1)} %get-tuple-element.82), channel_id=1, source_target_pairs={{0,3},{1,2},{2,1},{3,0},{4,7},{5,6},{6,5},{7,4},{8,11},{9,10},{10,... | collective-permute-start | bytes 294920 | tf_op jit(solution)/shard_map/ppermute | solution.py:157
  54.6 1.4 %collective-permute-done.11 = f32[2,3,32,128]{3,2,1,0:T(8,128)S(1)} collective-permute-done((f32[2,3,32,128]{3,2,1,0:T(8,128)S(1)}, f32[2,3,32,128]{3,2,1,0:T(8,128)S(1)}, u32[]{:S(2)}, u32[]{:S(2)}) %collective-permute-start.11) | collective-permute-done | bytes 98336 | tf_op jit(solution)/shard_map/ppermute | solution.py:157
  56.0 5.4 %collective-permute-done.12 = f32[2,3,32,128]{3,2,1,0:T(8,128)S(1)} collective-permute-done((f32[2,3,32,128]{3,2,1,0:T(8,128)S(1)}, f32[2,3,32,128]{3,2,1,0:T(8,128)S(1)}, u32[]{:S(2)}, u32[]{:S(2)}) %collective-permute-start.12) | collective-permute-done | bytes 98336 | tf_op jit(solution)/shard_map/ppermute | solution.py:157
  61.4 1.1 %collective-permute-done.13 = f32[2,3,32,128]{3,2,1,0:T(8,128)S(1)} collective-permute-done((f32[2,3,32,128]{3,2,1,0:T(8,128)S(1)}, f32[2,3,32,128]{3,2,1,0:T(8,128)S(1)}, u32[]{:S(2)}, u32[]{:S(2)}) %collective-permute-start.13) | collective-permute-done | bytes 98336 | tf_op jit(solution)/shard_map/ppermute | solution.py:157
  62.6 0.1 collective-permute-start.14
  62.7 4.3 %collective-permute-start.16 = (bf16[3,32,128]{2,1,0:T(8,128)(2,1)S(1)}, bf16[3,32,128]{2,1,0:T(8,128)(2,1)S(1)}, u32[]{:S(2)}, u32[]{:S(2)}) collective-permute-start(bf16[3,32,128]{2,1,0:T(8,128)(2,1)S(1)} %get-tuple-element.94), channel_id=1, source_target_pairs={{0,20},{1,21},{2,22},{3,23},{4,16},{5,17},{6,18},{7,19},{8,28},{9,... | collective-permute-start | bytes 73736 | tf_op jit(solution)/shard_map/ppermute | solution.py:289
  66.9 0.1 collective-permute-start.15
  67.1 0.4 collective-permute-done.14
  67.4 3.4 %collective-permute-done.15 = bf16[3,32,128]{2,1,0:T(8,128)(2,1)S(1)} collective-permute-done((bf16[3,32,128]{2,1,0:T(8,128)(2,1)S(1)}, bf16[3,32,128]{2,1,0:T(8,128)(2,1)S(1)}, u32[]{:S(2)}, u32[]{:S(2)}) %collective-permute-start.15) | collective-permute-done | bytes 24608 | tf_op jit(solution)/shard_map/ppermute | solution.py:157
  70.8 0.0 collective-permute-done.16
  70.8 0.1 collective-permute-start.18
  70.9 1.8 %columns.1 = (f32[6,32,256]{2,1,0:T(8,128)}, f32[6,32,256]{2,1,0:T(8,128)}) custom-call(s32[18]{0:T(128)S(1)} %copy-done.3, s32[12]{0:T(128)S(1)} %copy-done.4, f32[2,3,32,256]{3,2,1,0:T(8,128)S(1)} %bitcast.97, bf16[2,3,32,256]{3,2,1,0:T(8,128)(2,1)S(1)} %bitcast.99, f32[2,3,32,256]{3,2,1,0:T(8,128)S(1)} %bitcast.96, bf16[2,3,32,256]{3,2,1,0:T(8,128)(2,1)S(1)} %bitcast.98, ...), custom_call_target="tpu_custom_call" | custom-call | tf_op jit(solution)/shard_map/columns/pallas_call | solution.py:295
  72.6 0.0 collective-permute-done.18
  72.7 0.6 slice_bitcast_fusion.2
  (35 shorter events, 0.6 us)
Async XLA Ops:
  0.6 21.1 %copy-start.1 = (f32[256,256]{1,0:T(8,128)S(1)}, f32[256,256]{1,0:T(8,128)}, u32[]{:S(2)}) copy-start(f32[256,256]{1,0:T(8,128)} %inv1.5) | copy-start | bytes 786436
  0.6 21.1 %copy-start.2 = (f32[256,256]{1,0:T(8,128)S(1)}, f32[256,256]{1,0:T(8,128)}, u32[]{:S(2)}) copy-start(f32[256,256]{1,0:T(8,128)} %inv2.5) | copy-start | bytes 786436
  0.7 21.1 %copy-start.3 = (s32[18]{0:T(128)S(1)}, s32[18]{0:T(128)}, u32[]{:S(2)}) copy-start(s32[18]{0:T(128)} %struct1.5) | copy-start | bytes 220
  0.7 21.1 %copy-start.4 = (s32[12]{0:T(128)S(1)}, s32[12]{0:T(128)}, u32[]{:S(2)}) copy-start(s32[12]{0:T(128)} %struct2.5) | copy-start | bytes 148
  1.8 7.1 %collective-permute-start = (bf16[2,3,32,256]{3,2,1,0:T(8,128)(2,1)S(1)}, bf16[2,3,32,256]{3,2,1,0:T(8,128)(2,1)S(1)}, u32[]{:S(2)}, u32[]{:S(2)}) collective-permute-start(bf16[2,3,32,256]{3,2,1,0:T(8,128)(2,1)S(1)} %get-tuple-element.86), channel_id=1, source_target_pairs={{0,4},{1,12},{2,20},{3,28},{4,0},{5,8},{6,16},{7,24},{8,5},{9,13},... | collective-permute-start | bytes 294920 | tf_op jit(solution)/shard_map/ppermute | solution.py:199
  5.9 7.3 %collective-permute-start.1 = (bf16[2,3,32,256]{3,2,1,0:T(8,128)(2,1)S(1)}, bf16[2,3,32,256]{3,2,1,0:T(8,128)(2,1)S(1)}, u32[]{:S(2)}, u32[]{:S(2)}) collective-permute-start(bf16[2,3,32,256]{3,2,1,0:T(8,128)(2,1)S(1)} %get-tuple-element.87), channel_id=1, source_target_pairs={{0,0},{1,8},{2,16},{3,24},{4,4},{5,12},{6,20},{7,28},{8,1},{9,9},{... | collective-permute-start | bytes 294920 | tf_op jit(solution)/shard_map/ppermute | solution.py:199
  6.5 15.0 %collective-permute-start.4 = (bf16[2,6,32,256]{3,2,1,0:T(8,128)(2,1)S(1)}, bf16[2,6,32,256]{3,2,1,0:T(8,128)(2,1)S(1)}, u32[]{:S(2)}, u32[]{:S(2)}) collective-permute-start(bf16[2,6,32,256]{3,2,1,0:T(8,128)(2,1)S(1)} %pad_maximum_fusion.3), channel_id=1, source_target_pairs={{0,4},{1,5},{2,6},{3,7},{4,0},{5,1},{6,2},{7,3},{8,12},{9,13},{10,... | collective-permute-start | bytes 589832 | tf_op jit(solution)/shard_map/ppermute | solution.py:157
  8.9 10.0 %collective-permute-start.2 = (bf16[2,3,32,256]{3,2,1,0:T(8,128)(2,1)S(1)}, bf16[2,3,32,256]{3,2,1,0:T(8,128)(2,1)S(1)}, u32[]{:S(2)}, u32[]{:S(2)}) collective-permute-start(bf16[2,3,32,256]{3,2,1,0:T(8,128)(2,1)S(1)} %collective-permute-done), channel_id=1, source_target_pairs={{0,16},{8,24},{16,0},{24,8},{1,17},{9,25},{17,1},{25,9},{2,18},{10... | collective-permute-start | bytes 294920 | tf_op jit(solution)/shard_map/ppermute | solution.py:157
  13.1 8.3 %collective-permute-start.3 = (bf16[2,3,32,256]{3,2,1,0:T(8,128)(2,1)S(1)}, bf16[2,3,32,256]{3,2,1,0:T(8,128)(2,1)S(1)}, u32[]{:S(2)}, u32[]{:S(2)}) collective-permute-start(bf16[2,3,32,256]{3,2,1,0:T(8,128)(2,1)S(1)} %collective-permute-done.1), channel_id=1, source_target_pairs={{0,16},{8,24},{16,0},{24,8},{1,17},{9,25},{17,1},{25,9},{2,18},{10... | collective-permute-start | bytes 294920 | tf_op jit(solution)/shard_map/ppermute | solution.py:157
  21.5 2.0 %copy-start = (bf16[6,1,3,1,256,256]{5,4,3,2,1,0:T(8,128)(2,1)S(1)}, bf16[6,1,3,1,256,256]{5,4,3,2,1,0:T(8,128)(2,1)}, u32[]{:S(2)}) copy-start(bf16[6,1,3,1,256,256]{5,4,3,2,1,0:T(8,128)(2,1)} %param.8) | copy-start | bytes 7077892
  21.6 1.8 %collective-permute-start.5 = (bf16[2,2,2,3,32,256]{5,4,3,2,1,0:T(8,128)(2,1)S(1)}, bf16[2,2,2,3,32,256]{5,4,3,2,1,0:T(8,128)(2,1)S(1)}, u32[]{:S(2)}, u32[]{:S(2)}) collective-permute-start(bf16[2,2,2,3,32,256]{5,4,3,2,1,0:T(8,128)(2,1)S(1)} %pad_maximum_fusion.1), channel_id=1, source_target_pairs={{0,8},{8,0},{16,24},{24,16},{1,9},{9,1},{17,25},{25,17},{2,10},{10... | collective-permute-start | bytes 1179656 | tf_op jit(solution)/shard_map/ppermute | solution.py:157
  23.4 6.0 %copy-start.5 = (bf16[256,256]{1,0:T(8,128)(2,1)S(1)}, bf16[256,256]{1,0:T(8,128)(2,1)}, u32[]{:S(2)}) copy-start(bf16[256,256]{1,0:T(8,128)(2,1)} %link.1) | copy-start | bytes 393220
  26.7 12.0 %collective-permute-start.8 = (bf16[4,2,3,32,256]{4,3,2,1,0:T(8,128)(2,1)S(1)}, bf16[4,2,3,32,256]{4,3,2,1,0:T(8,128)(2,1)S(1)}, u32[]{:S(2)}, u32[]{:S(2)}) collective-permute-start(bf16[4,2,3,32,256]{4,3,2,1,0:T(8,128)(2,1)S(1)} %get-tuple-element.51), channel_id=1, source_target_pairs={{0,2},{1,3},{2,0},{3,1},{4,6},{5,7},{6,4},{7,5},{8,10},{9,11},{10,... | collective-permute-start | bytes 1179656 | tf_op jit(solution)/shard_map/ppermute | solution.py:157
  29.1 11.1 %collective-permute-start.6 = (bf16[4,2,3,32,256]{4,3,2,1,0:T(8,128)(2,1)S(1)}, bf16[4,2,3,32,256]{4,3,2,1,0:T(8,128)(2,1)S(1)}, u32[]{:S(2)}, u32[]{:S(2)}) collective-permute-start(bf16[4,2,3,32,256]{4,3,2,1,0:T(8,128)(2,1)S(1)} %get-tuple-element.47), channel_id=1, source_target_pairs={{0,1},{1,0},{2,3},{3,2},{4,5},{5,4},{6,7},{7,6},{8,9},{9,8},{10,11... | collective-permute-start | bytes 1179656 | tf_op jit(solution)/shard_map/ppermute | solution.py:157
  38.9 6.7 %collective-permute-start.9 = (bf16[2,2,3,32,256]{4,3,2,1,0:T(8,128)(2,1)S(1)}, bf16[2,2,3,32,256]{4,3,2,1,0:T(8,128)(2,1)S(1)}, u32[]{:S(2)}, u32[]{:S(2)}) collective-permute-start(bf16[2,2,3,32,256]{4,3,2,1,0:T(8,128)(2,1)S(1)} %fusion.1), channel_id=1, source_target_pairs={{0,1},{1,0},{2,3},{3,2},{4,5},{5,4},{6,7},{7,6},{8,9},{9,8},{10,11... | collective-permute-start | bytes 589832 | tf_op jit(solution)/shard_map/ppermute | solution.py:157
  40.4 6.1 %collective-permute-start.7 = (bf16[2,2,3,32,256]{4,3,2,1,0:T(8,128)(2,1)S(1)}, bf16[2,2,3,32,256]{4,3,2,1,0:T(8,128)(2,1)S(1)}, u32[]{:S(2)}, u32[]{:S(2)}) collective-permute-start(bf16[2,2,3,32,256]{4,3,2,1,0:T(8,128)(2,1)S(1)} %fusion), channel_id=1, source_target_pairs={{0,2},{1,3},{2,0},{3,1},{4,6},{5,7},{6,4},{7,5},{8,10},{9,11},{10,... | collective-permute-start | bytes 589832 | tf_op jit(solution)/shard_map/ppermute | solution.py:157
  47.5 3.4 %collective-permute-start.10 = (f32[8,3,32,128]{3,2,1,0:T(8,128)S(1)}, f32[8,3,32,128]{3,2,1,0:T(8,128)S(1)}, u32[]{:S(2)}, u32[]{:S(2)}) collective-permute-start(f32[8,3,32,128]{3,2,1,0:T(8,128)S(1)} %dynamic-slice_bitcast_fusion), channel_id=1, source_target_pairs={{0,8},{8,0},{16,24},{24,16},{1,9},{9,1},{17,25},{25,17},{2,10},{10... | collective-permute-start | bytes 1179656 | tf_op jit(solution)/shard_map/ppermute | solution.py:157
  47.7 19.3 %collective-permute-start.17 = (bf16[2,1,2,3,32,256]{5,4,3,2,1,0:T(8,128)(2,1)S(1)}, bf16[2,1,2,3,32,256]{5,4,3,2,1,0:T(8,128)(2,1)S(1)}, u32[]{:S(2)}, u32[]{:S(2)}) collective-permute-start(bf16[2,1,2,3,32,256]{5,4,3,2,1,0:T(8,128)(2,1)S(1)} %pad_maximum_fusion.4), channel_id=1, source_target_pairs={{0,4},{1,5},{2,6},{3,7},{4,0},{5,1},{6,2},{7,3},{8,12},{9,13},{10,... | collective-permute-start | bytes 589832 | tf_op jit(solution)/shard_map/ppermute | solution.py:157
  51.0 5.0 %collective-permute-start.11 = (f32[2,3,32,128]{3,2,1,0:T(8,128)S(1)}, f32[2,3,32,128]{3,2,1,0:T(8,128)S(1)}, u32[]{:S(2)}, u32[]{:S(2)}) collective-permute-start(f32[2,3,32,128]{3,2,1,0:T(8,128)S(1)} %get-tuple-element.81), channel_id=1, source_target_pairs={{0,1},{1,0},{2,3},{3,2},{4,5},{5,4},{6,7},{7,6},{8,9},{9,8},{10,11... | collective-permute-start | bytes 294920 | tf_op jit(solution)/shard_map/ppermute | solution.py:157
  51.7 9.7 %collective-permute-start.12 = (f32[2,3,32,128]{3,2,1,0:T(8,128)S(1)}, f32[2,3,32,128]{3,2,1,0:T(8,128)S(1)}, u32[]{:S(2)}, u32[]{:S(2)}) collective-permute-start(f32[2,3,32,128]{3,2,1,0:T(8,128)S(1)} %get-tuple-element.83), channel_id=1, source_target_pairs={{0,2},{1,3},{2,0},{3,1},{4,6},{5,7},{6,4},{7,5},{8,10},{9,11},{10,... | collective-permute-start | bytes 294920 | tf_op jit(solution)/shard_map/ppermute | solution.py:157
  52.5 10.0 %collective-permute-start.13 = (f32[2,3,32,128]{3,2,1,0:T(8,128)S(1)}, f32[2,3,32,128]{3,2,1,0:T(8,128)S(1)}, u32[]{:S(2)}, u32[]{:S(2)}) collective-permute-start(f32[2,3,32,128]{3,2,1,0:T(8,128)S(1)} %get-tuple-element.82), channel_id=1, source_target_pairs={{0,3},{1,2},{2,1},{3,0},{4,7},{5,6},{6,5},{7,4},{8,11},{9,10},{10,... | collective-permute-start | bytes 294920 | tf_op jit(solution)/shard_map/ppermute | solution.py:157
  62.6 4.8 %collective-permute-start.14 = (bf16[3,32,128]{2,1,0:T(8,128)(2,1)S(1)}, bf16[3,32,128]{2,1,0:T(8,128)(2,1)S(1)}, u32[]{:S(2)}, u32[]{:S(2)}) collective-permute-start(bf16[3,32,128]{2,1,0:T(8,128)(2,1)S(1)} %get-tuple-element.94), channel_id=1, source_target_pairs={{0,4},{1,5},{2,6},{3,7},{4,0},{5,1},{6,2},{7,3},{8,12},{9,13},{10,... | collective-permute-start | bytes 73736 | tf_op jit(solution)/shard_map/ppermute | solution.py:157
  62.7 8.1 %collective-permute-start.16 = (bf16[3,32,128]{2,1,0:T(8,128)(2,1)S(1)}, bf16[3,32,128]{2,1,0:T(8,128)(2,1)S(1)}, u32[]{:S(2)}, u32[]{:S(2)}) collective-permute-start(bf16[3,32,128]{2,1,0:T(8,128)(2,1)S(1)} %get-tuple-element.94), channel_id=1, source_target_pairs={{0,20},{1,21},{2,22},{3,23},{4,16},{5,17},{6,18},{7,19},{8,28},{9,... | collective-permute-start | bytes 73736 | tf_op jit(solution)/shard_map/ppermute | solution.py:289
  66.9 3.8 %collective-permute-start.15 = (bf16[3,32,128]{2,1,0:T(8,128)(2,1)S(1)}, bf16[3,32,128]{2,1,0:T(8,128)(2,1)S(1)}, u32[]{:S(2)}, u32[]{:S(2)}) collective-permute-start(bf16[3,32,128]{2,1,0:T(8,128)(2,1)S(1)} %get-tuple-element.93), channel_id=1, source_target_pairs={{0,16},{8,24},{16,0},{24,8},{1,17},{9,25},{17,1},{25,9},{2,18},{10... | collective-permute-start | bytes 73736 | tf_op jit(solution)/shard_map/ppermute | solution.py:157
  70.8 1.9 %collective-permute-start.18 = (f32[3,32,128]{2,1,0:T(8,128)S(1)}, f32[3,32,128]{2,1,0:T(8,128)S(1)}, u32[]{:S(2)}, u32[]{:S(2)}) collective-permute-start(f32[3,32,128]{2,1,0:T(8,128)S(1)} %add_add_fusion), channel_id=1, source_target_pairs={{0,8},{8,0},{16,24},{24,16},{1,9},{9,1},{17,25},{25,17},{2,10},{10... | collective-permute-start | bytes 147464 | tf_op jit(solution)/shard_map/ppermute | solution.py:157

commit v11 on v8

--- a/solution.py
+++ b/solution.py
@@ -283,6 +283,7 @@
     for bit in range(2, n_bits - 1):
         keep, send = halves(sums.reshape((-1, 2) + tail), 1, ways[bit])
         sums = keep + swapped(send.astype(bf16), "col", n_col, 1 << bit).astype(f32)
+    sums, state = lax.optimization_barrier((sums, state))
     keep, send = (part.astype(bf16) for part in halves(sums.reshape((2,) + tail), 0, ways[n_bits - 1]))
     across = [(r * n_col + c, (r ^ 2) * n_col + (c ^ (n_col // 2))) for r in range(n_row) for c in range(n_col)]
     near = keep.astype(f32) + swapped(send, "col", n_col, n_col // 2).astype(f32)
@@ -291,7 +292,6 @@
     for bit in range(2, n_row.bit_length() - 1):
         mine = mine + swapped(mine, "row", n_row, 1 << bit)
 
-    mine, state = lax.optimization_barrier((mine, state))
     column_first, column_second = pl.pallas_call(
         functools.partial(column_kernel, n_row),
         out_shape=[shape(panel, f32)] * 2,

time: 70.2 us -> 71.6 us (1.020)
  waiting for transfers between devices: 26.1 us -> 27.2 us
    ppermute x1, waiting for transfers between devices: 1.11 us -> 3.11 us  [body(): lax.ppermute(send, ('row', 'col'), across).astype(f32)]
    ppermute x1, starting transfers between devices: 1.11 us -> 2.29 us  [body(): lax.ppermute(send, ('row', 'col'), across).astype(f32)]
    ppermute x16, starting transfers between devices: 24.7 us -> 23.7 us  [swapped(): return lax.ppermute(value, axis, [(i, i ^ mask) for i in range(size)])]
    ppermute x16, waiting for transfers between devices: 22.7 us -> 21.8 us  [swapped(): return lax.ppermute(value, axis, [(i, i ^ mask) for i in range(size)])]
  transfers between devices with their start and end apart: 19 -> 19, of which waited for: 12 -> 10; matrix products, arithmetic and copies ran while one was open for 1% -> 1% of each run, Pallas kernels for 8% -> 8%
where the time goes in v11:
time: 71.6 us; the launch traced here: 71.4 us
  starting transfers between devices  30.8 us (43%)
  waiting for transfers between devices  27.2 us (38%)
  Pallas kernels  9.69 us (14%)
  other arithmetic  1.75 us (2%)
  between operations  1.05 us (1%)
  local copies, waits for them, and re-layouts  0.91 us (1%)
    ppermute x16, starting transfers between devices, swapped(): return lax.ppermute(value, axis, [(i, i ^ mask) for i in range(size)])  23.7 us
    ppermute x16, waiting for transfers between devices, swapped(): return lax.ppermute(value, axis, [(i, i ^ mask) for i in range(size)])  21.8 us
    ppermute x2, starting transfers between devices, body(): got.append(lax.ppermute(part, ('row', 'col'), moves))  4.76 us
    pallas_call x1, Pallas kernels, body(): pl.pallas_call(functools.partial(product_kernel, n_row, n_col, (orders[0]...  3.23 us
    ppermute x1, waiting for transfers between devices, body(): lax.ppermute(send, ('row', 'col'), across).astype(f32)  3.11 us
    ppermute x1, starting transfers between devices, body(): lax.ppermute(send, ('row', 'col'), across).astype(f32)  2.29 us
    ppermute x2, waiting for transfers between devices, body(): got.append(lax.ppermute(part, ('row', 'col'), moves))  2.26 us
    pallas_call x1, Pallas kernels, body(): pl.pallas_call(prepare_kernel, out_shape=[shape((width, width), f32), sha...  2.18 us
  transfers between devices with their start and end apart: 19, of which 10 were waited for; matrix products, arithmetic and copies ran while one was open for 1% of the time, Pallas kernels for 8%

profile of v11, /device:TPU:0, one launch (start us, length us, event | category | flops | bytes accessed | tf_op | source)
XLA Modules:
  0.0 71.4 jit_solution(10782637626542786828)
XLA Ops:
  0.7 1.0 %pad_maximum_fusion.3 = bf16[2,6,32,256]{3,2,1,0:T(8,128)(2,1)S(1)} fusion(bf16[1,6,32,256]{3,2,1,0:T(8,128)(2,1)} %bitcast.120, bf16[1,6,32,256]{3,2,1,0:T(8,128)(2,1)} %bitcast.121), kind=kLoop, calls=%fused_computation.13 | loop fusion | flops 98304 | bytes 393216 | tf_op jit(solution)/shard_map/stack | solution.py:189
  1.8 4.1 %collective-permute-start = (bf16[2,3,32,256]{3,2,1,0:T(8,128)(2,1)S(1)}, bf16[2,3,32,256]{3,2,1,0:T(8,128)(2,1)S(1)}, u32[]{:S(2)}, u32[]{:S(2)}) collective-permute-start(bf16[2,3,32,256]{3,2,1,0:T(8,128)(2,1)S(1)} %get-tuple-element.86), channel_id=1, source_target_pairs={{0,4},{1,12},{2,20},{3,28},{4,0},{5,8},{6,16},{7,24},{8,5},{9,13},... | collective-permute-start | bytes 294920 | tf_op jit(solution)/shard_map/ppermute | solution.py:199
  5.9 0.7 collective-permute-start.1
  6.5 0.1 collective-permute-start.4
  6.6 2.3 %collective-permute-done = bf16[2,3,32,256]{3,2,1,0:T(8,128)(2,1)S(1)} collective-permute-done((bf16[2,3,32,256]{3,2,1,0:T(8,128)(2,1)S(1)}, bf16[2,3,32,256]{3,2,1,0:T(8,128)(2,1)S(1)}, u32[]{:S(2)}, u32[]{:S(2)}) %collective-permute-start) | collective-permute-done | bytes 98336 | tf_op jit(solution)/shard_map/ppermute | solution.py:199
  8.9 4.3 %collective-permute-start.2 = (bf16[2,3,32,256]{3,2,1,0:T(8,128)(2,1)S(1)}, bf16[2,3,32,256]{3,2,1,0:T(8,128)(2,1)S(1)}, u32[]{:S(2)}, u32[]{:S(2)}) collective-permute-start(bf16[2,3,32,256]{3,2,1,0:T(8,128)(2,1)S(1)} %collective-permute-done), channel_id=1, source_target_pairs={{0,16},{8,24},{16,0},{24,8},{1,17},{9,25},{17,1},{25,9},{2,18},{10... | collective-permute-start | bytes 294920 | tf_op jit(solution)/shard_map/ppermute | solution.py:157
  13.1 0.0 collective-permute-done.1
  13.1 5.7 %collective-permute-start.3 = (bf16[2,3,32,256]{3,2,1,0:T(8,128)(2,1)S(1)}, bf16[2,3,32,256]{3,2,1,0:T(8,128)(2,1)S(1)}, u32[]{:S(2)}, u32[]{:S(2)}) collective-permute-start(bf16[2,3,32,256]{3,2,1,0:T(8,128)(2,1)S(1)} %collective-permute-done.1), channel_id=1, source_target_pairs={{0,16},{8,24},{16,0},{24,8},{1,17},{9,25},{17,1},{25,9},{2,18},{10... | collective-permute-start | bytes 294920 | tf_op jit(solution)/shard_map/ppermute | solution.py:157
  18.9 0.0 collective-permute-done.2
  18.9 2.6 %collective-permute-done.3 = bf16[2,3,32,256]{3,2,1,0:T(8,128)(2,1)S(1)} collective-permute-done((bf16[2,3,32,256]{3,2,1,0:T(8,128)(2,1)S(1)}, bf16[2,3,32,256]{3,2,1,0:T(8,128)(2,1)S(1)}, u32[]{:S(2)}, u32[]{:S(2)}) %collective-permute-start.3) | collective-permute-done | bytes 98336 | tf_op jit(solution)/shard_map/ppermute | solution.py:157
  21.5 0.0 collective-permute-done.4
  21.6 0.1 collective-permute-start.5
  21.7 1.5 %form.1.rows = bf16[2,2,6,32,256]{4,3,2,1,0:T(8,128)(2,1)S(1)} custom-call(s32[18]{0:T(128)S(1)} %copy-done.3, s32[12]{0:T(128)S(1)} %copy-done.4, f32[256,256]{1,0:T(8,128)S(1)} %copy-done.1, f32[256,256]{1,0:T(8,128)S(1)} %copy-done.2, bf16[2,2,6,32,256]{4,3,2,1,0:T(8,128)(2,1)S(1)} %pad_maximum_fusion.2.base), custom_call_target="tpu_custom_call" | custom-call | flops 134217728 | bytes 262144 | tf_op jit(solution)/shard_map/form/pallas_call | solution.py:210
  23.2 0.2 collective-permute-done.5
  23.4 0.1 pad_maximum_fusion
  23.5 3.2 %products.1 = (f32[4,2,3,32,256]{4,3,2,1,0:T(8,128)S(1)}, f32[4,2,3,32,256]{4,3,2,1,0:T(8,128)S(1)}, bf16[4,2,3,32,256]{4,3,2,1,0:T(8,128)(2,1)S(1)}, bf16[4,2,3,32,256]{4,3,2,1,0:T(8,128)(2,1)S(1)}) custom-call(s32[18]{0:T(128)S(1)} %copy-done.3, s32[12]{0:T(128)S(1)} %copy-done.4, f32[256,256]{1,0:T(8,128)S(1)} %copy-done.1, f32[256,256]{1,0:T(8,128)S(1)} %copy-done.2, ...), custom_call_target="tpu_custom_call" | custom-call | tf_op jit(solution)/shard_map/products/pallas_call | solution.py:226
  26.7 2.4 %collective-permute-start.8 = (bf16[4,2,3,32,256]{4,3,2,1,0:T(8,128)(2,1)S(1)}, bf16[4,2,3,32,256]{4,3,2,1,0:T(8,128)(2,1)S(1)}, u32[]{:S(2)}, u32[]{:S(2)}) collective-permute-start(bf16[4,2,3,32,256]{4,3,2,1,0:T(8,128)(2,1)S(1)} %get-tuple-element.51), channel_id=1, source_target_pairs={{0,2},{1,3},{2,0},{3,1},{4,6},{5,7},{6,4},{7,5},{8,10},{9,11},{10,... | collective-permute-start | bytes 1179656 | tf_op jit(solution)/shard_map/ppermute | solution.py:157
  29.1 0.3 collective-permute-start.6
  29.4 2.2 %prepare.1 = (f32[256,256]{1,0:T(8,128)S(1)}, f32[3,32,256]{2,1,0:T(8,128)S(1)}) custom-call(bf16[256,256]{1,0:T(8,128)(2,1)S(1)} %copy-done.5, f32[256,256]{1,0:T(8,128)S(1)} %copy-done.1, f32[256,256]{1,0:T(8,128)S(1)} %copy-done.2, f32[4,2,3,32,256]{4,3,2,1,0:T(8,128)S(1)} %get-tuple-element.46.after), custom_call_target="tpu_custom_call" | custom-call | flops 1006632960 | bytes 524288 | tf_op jit(solution)/shard_map/prepare/pallas_call | solution.py:238
  31.6 7.1 %collective-permute-done.8 = bf16[4,2,3,32,256]{4,3,2,1,0:T(8,128)(2,1)S(1)} collective-permute-done((bf16[4,2,3,32,256]{4,3,2,1,0:T(8,128)(2,1)S(1)}, bf16[4,2,3,32,256]{4,3,2,1,0:T(8,128)(2,1)S(1)}, u32[]{:S(2)}, u32[]{:S(2)}) %collective-permute-start.8) | collective-permute-done | bytes 393248 | tf_op jit(solution)/shard_map/ppermute | solution.py:157
  38.7 0.1 convert_add_fusion
  38.9 0.8 %collective-permute-start.9 = (bf16[2,2,3,32,256]{4,3,2,1,0:T(8,128)(2,1)S(1)}, bf16[2,2,3,32,256]{4,3,2,1,0:T(8,128)(2,1)S(1)}, u32[]{:S(2)}, u32[]{:S(2)}) collective-permute-start(bf16[2,2,3,32,256]{4,3,2,1,0:T(8,128)(2,1)S(1)} %fusion.1), channel_id=1, source_target_pairs={{0,1},{1,0},{2,3},{3,2},{4,5},{5,4},{6,7},{7,6},{8,9},{9,8},{10,11... | collective-permute-start | bytes 589832 | tf_op jit(solution)/shard_map/ppermute | solution.py:157
  39.7 0.4 collective-permute-done.6
  40.2 0.1 convert_add_fusion.1
  40.4 0.9 %collective-permute-start.7 = (bf16[2,2,3,32,256]{4,3,2,1,0:T(8,128)(2,1)S(1)}, bf16[2,2,3,32,256]{4,3,2,1,0:T(8,128)(2,1)S(1)}, u32[]{:S(2)}, u32[]{:S(2)}) collective-permute-start(bf16[2,2,3,32,256]{4,3,2,1,0:T(8,128)(2,1)S(1)} %fusion), channel_id=1, source_target_pairs={{0,2},{1,3},{2,0},{3,1},{4,6},{5,7},{6,4},{7,5},{8,10},{9,11},{10,... | collective-permute-start | bytes 589832 | tf_op jit(solution)/shard_map/ppermute | solution.py:157
  41.2 4.4 %collective-permute-done.9 = bf16[2,2,3,32,256]{4,3,2,1,0:T(8,128)(2,1)S(1)} collective-permute-done((bf16[2,2,3,32,256]{4,3,2,1,0:T(8,128)(2,1)S(1)}, bf16[2,2,3,32,256]{4,3,2,1,0:T(8,128)(2,1)S(1)}, u32[]{:S(2)}, u32[]{:S(2)}) %collective-permute-start.9) | collective-permute-done | bytes 196640 | tf_op jit(solution)/shard_map/ppermute | solution.py:157
  45.7 0.7 %collective-permute-done.7 = bf16[2,2,3,32,256]{4,3,2,1,0:T(8,128)(2,1)S(1)} collective-permute-done((bf16[2,2,3,32,256]{4,3,2,1,0:T(8,128)(2,1)S(1)}, bf16[2,2,3,32,256]{4,3,2,1,0:T(8,128)(2,1)S(1)}, u32[]{:S(2)}, u32[]{:S(2)}) %collective-permute-start.7) | collective-permute-done | bytes 196640 | tf_op jit(solution)/shard_map/ppermute | solution.py:157
  46.5 1.0 %sums.1 = f32[2,8,3,32,128]{4,3,2,1,0:T(8,128)S(1)} custom-call(bf16[2,2,6,32,256]{4,3,2,1,0:T(8,128)(2,1)S(1)} %form.1.rows, f32[2,2,3,32,256]{4,3,2,1,0:T(8,128)S(1)} %bitcast_add_fusion.2.total_low, f32[2,2,3,32,256]{4,3,2,1,0:T(8,128)S(1)} %bitcast_add_fusion.1.total_high, f32[256,256]{1,0:T(8,128)S(1)} %get-tuple-element.54.linked, ...), custom_call_target="tpu_custom_call" | custom-call | tf_op jit(solution)/shard_map/sums/pallas_call | solution.py:268
  47.6 0.1 collective-permute-start.10
  47.7 3.2 %collective-permute-start.14 = (bf16[2,1,2,3,32,256]{5,4,3,2,1,0:T(8,128)(2,1)S(1)}, bf16[2,1,2,3,32,256]{5,4,3,2,1,0:T(8,128)(2,1)S(1)}, u32[]{:S(2)}, u32[]{:S(2)}) collective-permute-start(bf16[2,1,2,3,32,256]{5,4,3,2,1,0:T(8,128)(2,1)S(1)} %pad_maximum_fusion.4), channel_id=1, source_target_pairs={{0,4},{1,5},{2,6},{3,7},{4,0},{5,1},{6,2},{7,3},{8,12},{9,13},{10,... | collective-permute-start | bytes 589832 | tf_op jit(solution)/shard_map/ppermute | solution.py:157
  50.9 0.0 collective-permute-done.10
  50.9 0.1 bitcast_add_fusion
  51.0 0.7 collective-permute-start.11
  51.7 0.8 %collective-permute-start.12 = (bf16[2,3,32,128]{3,2,1,0:T(8,128)(2,1)S(1)}, bf16[2,3,32,128]{3,2,1,0:T(8,128)(2,1)S(1)}, u32[]{:S(2)}, u32[]{:S(2)}) collective-permute-start(bf16[2,3,32,128]{3,2,1,0:T(8,128)(2,1)S(1)} %get-tuple-element.83), channel_id=1, source_target_pairs={{0,2},{1,3},{2,0},{3,1},{4,6},{5,7},{6,4},{7,5},{8,10},{9,11},{10,... | collective-permute-start | bytes 147464 | tf_op jit(solution)/shard_map/ppermute | solution.py:157
  52.5 2.0 %collective-permute-start.13 = (bf16[2,3,32,128]{3,2,1,0:T(8,128)(2,1)S(1)}, bf16[2,3,32,128]{3,2,1,0:T(8,128)(2,1)S(1)}, u32[]{:S(2)}, u32[]{:S(2)}) collective-permute-start(bf16[2,3,32,128]{3,2,1,0:T(8,128)(2,1)S(1)} %get-tuple-element.82), channel_id=1, source_target_pairs={{0,3},{1,2},{2,1},{3,0},{4,7},{5,6},{6,5},{7,4},{8,11},{9,10},{10,... | collective-permute-start | bytes 147464 | tf_op jit(solution)/shard_map/ppermute | solution.py:157
  54.6 6.1 %collective-permute-done.14 = bf16[2,1,2,3,32,256]{5,4,3,2,1,0:T(8,128)(2,1)S(1)} collective-permute-done((bf16[2,1,2,3,32,256]{5,4,3,2,1,0:T(8,128)(2,1)S(1)}, bf16[2,1,2,3,32,256]{5,4,3,2,1,0:T(8,128)(2,1)S(1)}, u32[]{:S(2)}, u32[]{:S(2)}) %collective-permute-start.14) | collective-permute-done | bytes 196640 | tf_op jit(solution)/shard_map/ppermute | solution.py:157
  60.7 0.0 collective-permute-done.11
  60.8 0.0 collective-permute-done.12
  60.8 0.0 collective-permute-done.13
  60.8 0.1 collective-permute-start.15
  60.9 2.3 %collective-permute-start.16 = (bf16[3,32,128]{2,1,0:T(8,128)(2,1)S(1)}, bf16[3,32,128]{2,1,0:T(8,128)(2,1)S(1)}, u32[]{:S(2)}, u32[]{:S(2)}) collective-permute-start(bf16[3,32,128]{2,1,0:T(8,128)(2,1)S(1)} %get-tuple-element.93), channel_id=1, source_target_pairs={{0,16},{8,24},{16,0},{24,8},{1,17},{9,25},{17,1},{25,9},{2,18},{10... | collective-permute-start | bytes 73736 | tf_op jit(solution)/shard_map/ppermute | solution.py:157
  63.2 2.3 %collective-permute-start.17 = (bf16[3,32,128]{2,1,0:T(8,128)(2,1)S(1)}, bf16[3,32,128]{2,1,0:T(8,128)(2,1)S(1)}, u32[]{:S(2)}, u32[]{:S(2)}) collective-permute-start(bf16[3,32,128]{2,1,0:T(8,128)(2,1)S(1)} %get-tuple-element.94), channel_id=1, source_target_pairs={{0,20},{1,21},{2,22},{3,23},{4,16},{5,17},{6,18},{7,19},{8,28},{9,... | collective-permute-start | bytes 73736 | tf_op jit(solution)/shard_map/ppermute | solution.py:290
  65.5 0.2 collective-permute-done.15
  65.7 3.1 %collective-permute-done.17 = bf16[3,32,128]{2,1,0:T(8,128)(2,1)S(1)} collective-permute-done((bf16[3,32,128]{2,1,0:T(8,128)(2,1)S(1)}, bf16[3,32,128]{2,1,0:T(8,128)(2,1)S(1)}, u32[]{:S(2)}, u32[]{:S(2)}) %collective-permute-start.17) | collective-permute-done | bytes 24608 | tf_op jit(solution)/shard_map/ppermute | solution.py:290
  68.8 0.1 collective-permute-start.18
  68.9 1.8 %columns.1 = (f32[6,32,256]{2,1,0:T(8,128)}, f32[6,32,256]{2,1,0:T(8,128)}) custom-call(s32[18]{0:T(128)S(1)} %copy-done.3, s32[12]{0:T(128)S(1)} %copy-done.4, f32[2,3,32,256]{3,2,1,0:T(8,128)S(1)} %bitcast.105, bf16[2,3,32,256]{3,2,1,0:T(8,128)(2,1)S(1)} %bitcast.107, f32[2,3,32,256]{3,2,1,0:T(8,128)S(1)} %bitcast.104, ...), custom_call_target="tpu_custom_call" | custom-call | tf_op jit(solution)/shard_map/columns/pallas_call | solution.py:295
  70.7 0.0 collective-permute-done.18
  70.7 0.6 slice_bitcast_fusion.2
  (35 shorter events, 0.6 us)
Async XLA Ops:
  0.6 21.1 %copy-start.1 = (f32[256,256]{1,0:T(8,128)S(1)}, f32[256,256]{1,0:T(8,128)}, u32[]{:S(2)}) copy-start(f32[256,256]{1,0:T(8,128)} %inv1.5) | copy-start | bytes 786436
  0.6 21.1 %copy-start.2 = (f32[256,256]{1,0:T(8,128)S(1)}, f32[256,256]{1,0:T(8,128)}, u32[]{:S(2)}) copy-start(f32[256,256]{1,0:T(8,128)} %inv2.5) | copy-start | bytes 786436
  0.7 21.1 %copy-start.3 = (s32[18]{0:T(128)S(1)}, s32[18]{0:T(128)}, u32[]{:S(2)}) copy-start(s32[18]{0:T(128)} %struct1.5) | copy-start | bytes 220
  0.7 21.1 %copy-start.4 = (s32[12]{0:T(128)S(1)}, s32[12]{0:T(128)}, u32[]{:S(2)}) copy-start(s32[12]{0:T(128)} %struct2.5) | copy-start | bytes 148
  1.8 7.1 %collective-permute-start = (bf16[2,3,32,256]{3,2,1,0:T(8,128)(2,1)S(1)}, bf16[2,3,32,256]{3,2,1,0:T(8,128)(2,1)S(1)}, u32[]{:S(2)}, u32[]{:S(2)}) collective-permute-start(bf16[2,3,32,256]{3,2,1,0:T(8,128)(2,1)S(1)} %get-tuple-element.86), channel_id=1, source_target_pairs={{0,4},{1,12},{2,20},{3,28},{4,0},{5,8},{6,16},{7,24},{8,5},{9,13},... | collective-permute-start | bytes 294920 | tf_op jit(solution)/shard_map/ppermute | solution.py:199
  5.9 7.3 %collective-permute-start.1 = (bf16[2,3,32,256]{3,2,1,0:T(8,128)(2,1)S(1)}, bf16[2,3,32,256]{3,2,1,0:T(8,128)(2,1)S(1)}, u32[]{:S(2)}, u32[]{:S(2)}) collective-permute-start(bf16[2,3,32,256]{3,2,1,0:T(8,128)(2,1)S(1)} %get-tuple-element.87), channel_id=1, source_target_pairs={{0,0},{1,8},{2,16},{3,24},{4,4},{5,12},{6,20},{7,28},{8,1},{9,9},{... | collective-permute-start | bytes 294920 | tf_op jit(solution)/shard_map/ppermute | solution.py:199
  6.5 15.0 %collective-permute-start.4 = (bf16[2,6,32,256]{3,2,1,0:T(8,128)(2,1)S(1)}, bf16[2,6,32,256]{3,2,1,0:T(8,128)(2,1)S(1)}, u32[]{:S(2)}, u32[]{:S(2)}) collective-permute-start(bf16[2,6,32,256]{3,2,1,0:T(8,128)(2,1)S(1)} %pad_maximum_fusion.3), channel_id=1, source_target_pairs={{0,4},{1,5},{2,6},{3,7},{4,0},{5,1},{6,2},{7,3},{8,12},{9,13},{10,... | collective-permute-start | bytes 589832 | tf_op jit(solution)/shard_map/ppermute | solution.py:157
  8.9 10.0 %collective-permute-start.2 = (bf16[2,3,32,256]{3,2,1,0:T(8,128)(2,1)S(1)}, bf16[2,3,32,256]{3,2,1,0:T(8,128)(2,1)S(1)}, u32[]{:S(2)}, u32[]{:S(2)}) collective-permute-start(bf16[2,3,32,256]{3,2,1,0:T(8,128)(2,1)S(1)} %collective-permute-done), channel_id=1, source_target_pairs={{0,16},{8,24},{16,0},{24,8},{1,17},{9,25},{17,1},{25,9},{2,18},{10... | collective-permute-start | bytes 294920 | tf_op jit(solution)/shard_map/ppermute | solution.py:157
  13.1 8.3 %collective-permute-start.3 = (bf16[2,3,32,256]{3,2,1,0:T(8,128)(2,1)S(1)}, bf16[2,3,32,256]{3,2,1,0:T(8,128)(2,1)S(1)}, u32[]{:S(2)}, u32[]{:S(2)}) collective-permute-start(bf16[2,3,32,256]{3,2,1,0:T(8,128)(2,1)S(1)} %collective-permute-done.1), channel_id=1, source_target_pairs={{0,16},{8,24},{16,0},{24,8},{1,17},{9,25},{17,1},{25,9},{2,18},{10... | collective-permute-start | bytes 294920 | tf_op jit(solution)/shard_map/ppermute | solution.py:157
  21.5 2.0 %copy-start = (bf16[6,1,3,1,256,256]{5,4,3,2,1,0:T(8,128)(2,1)S(1)}, bf16[6,1,3,1,256,256]{5,4,3,2,1,0:T(8,128)(2,1)}, u32[]{:S(2)}) copy-start(bf16[6,1,3,1,256,256]{5,4,3,2,1,0:T(8,128)(2,1)} %param.8) | copy-start | bytes 7077892
  21.6 1.8 %collective-permute-start.5 = (bf16[2,2,2,3,32,256]{5,4,3,2,1,0:T(8,128)(2,1)S(1)}, bf16[2,2,2,3,32,256]{5,4,3,2,1,0:T(8,128)(2,1)S(1)}, u32[]{:S(2)}, u32[]{:S(2)}) collective-permute-start(bf16[2,2,2,3,32,256]{5,4,3,2,1,0:T(8,128)(2,1)S(1)} %pad_maximum_fusion.1), channel_id=1, source_target_pairs={{0,8},{8,0},{16,24},{24,16},{1,9},{9,1},{17,25},{25,17},{2,10},{10... | collective-permute-start | bytes 1179656 | tf_op jit(solution)/shard_map/ppermute | solution.py:157
  23.4 6.0 %copy-start.5 = (bf16[256,256]{1,0:T(8,128)(2,1)S(1)}, bf16[256,256]{1,0:T(8,128)(2,1)}, u32[]{:S(2)}) copy-start(bf16[256,256]{1,0:T(8,128)(2,1)} %link.1) | copy-start | bytes 393220
  26.7 12.0 %collective-permute-start.8 = (bf16[4,2,3,32,256]{4,3,2,1,0:T(8,128)(2,1)S(1)}, bf16[4,2,3,32,256]{4,3,2,1,0:T(8,128)(2,1)S(1)}, u32[]{:S(2)}, u32[]{:S(2)}) collective-permute-start(bf16[4,2,3,32,256]{4,3,2,1,0:T(8,128)(2,1)S(1)} %get-tuple-element.51), channel_id=1, source_target_pairs={{0,2},{1,3},{2,0},{3,1},{4,6},{5,7},{6,4},{7,5},{8,10},{9,11},{10,... | collective-permute-start | bytes 1179656 | tf_op jit(solution)/shard_map/ppermute | solution.py:157
  29.1 11.1 %collective-permute-start.6 = (bf16[4,2,3,32,256]{4,3,2,1,0:T(8,128)(2,1)S(1)}, bf16[4,2,3,32,256]{4,3,2,1,0:T(8,128)(2,1)S(1)}, u32[]{:S(2)}, u32[]{:S(2)}) collective-permute-start(bf16[4,2,3,32,256]{4,3,2,1,0:T(8,128)(2,1)S(1)} %get-tuple-element.47), channel_id=1, source_target_pairs={{0,1},{1,0},{2,3},{3,2},{4,5},{5,4},{6,7},{7,6},{8,9},{9,8},{10,11... | collective-permute-start | bytes 1179656 | tf_op jit(solution)/shard_map/ppermute | solution.py:157
  38.9 6.7 %collective-permute-start.9 = (bf16[2,2,3,32,256]{4,3,2,1,0:T(8,128)(2,1)S(1)}, bf16[2,2,3,32,256]{4,3,2,1,0:T(8,128)(2,1)S(1)}, u32[]{:S(2)}, u32[]{:S(2)}) collective-permute-start(bf16[2,2,3,32,256]{4,3,2,1,0:T(8,128)(2,1)S(1)} %fusion.1), channel_id=1, source_target_pairs={{0,1},{1,0},{2,3},{3,2},{4,5},{5,4},{6,7},{7,6},{8,9},{9,8},{10,11... | collective-permute-start | bytes 589832 | tf_op jit(solution)/shard_map/ppermute | solution.py:157
  40.4 6.1 %collective-permute-start.7 = (bf16[2,2,3,32,256]{4,3,2,1,0:T(8,128)(2,1)S(1)}, bf16[2,2,3,32,256]{4,3,2,1,0:T(8,128)(2,1)S(1)}, u32[]{:S(2)}, u32[]{:S(2)}) collective-permute-start(bf16[2,2,3,32,256]{4,3,2,1,0:T(8,128)(2,1)S(1)} %fusion), channel_id=1, source_target_pairs={{0,2},{1,3},{2,0},{3,1},{4,6},{5,7},{6,4},{7,5},{8,10},{9,11},{10,... | collective-permute-start | bytes 589832 | tf_op jit(solution)/shard_map/ppermute | solution.py:157
  47.6 3.4 %collective-permute-start.10 = (f32[8,3,32,128]{3,2,1,0:T(8,128)S(1)}, f32[8,3,32,128]{3,2,1,0:T(8,128)S(1)}, u32[]{:S(2)}, u32[]{:S(2)}) collective-permute-start(f32[8,3,32,128]{3,2,1,0:T(8,128)S(1)} %dynamic-slice_bitcast_fusion), channel_id=1, source_target_pairs={{0,8},{8,0},{16,24},{24,16},{1,9},{9,1},{17,25},{25,17},{2,10},{10... | collective-permute-start | bytes 1179656 | tf_op jit(solution)/shard_map/ppermute | solution.py:157
  47.7 13.0 %collective-permute-start.14 = (bf16[2,1,2,3,32,256]{5,4,3,2,1,0:T(8,128)(2,1)S(1)}, bf16[2,1,2,3,32,256]{5,4,3,2,1,0:T(8,128)(2,1)S(1)}, u32[]{:S(2)}, u32[]{:S(2)}) collective-permute-start(bf16[2,1,2,3,32,256]{5,4,3,2,1,0:T(8,128)(2,1)S(1)} %pad_maximum_fusion.4), channel_id=1, source_target_pairs={{0,4},{1,5},{2,6},{3,7},{4,0},{5,1},{6,2},{7,3},{8,12},{9,13},{10,... | collective-permute-start | bytes 589832 | tf_op jit(solution)/shard_map/ppermute | solution.py:157
  51.0 9.7 %collective-permute-start.11 = (bf16[2,3,32,128]{3,2,1,0:T(8,128)(2,1)S(1)}, bf16[2,3,32,128]{3,2,1,0:T(8,128)(2,1)S(1)}, u32[]{:S(2)}, u32[]{:S(2)}) collective-permute-start(bf16[2,3,32,128]{3,2,1,0:T(8,128)(2,1)S(1)} %get-tuple-element.81), channel_id=1, source_target_pairs={{0,1},{1,0},{2,3},{3,2},{4,5},{5,4},{6,7},{7,6},{8,9},{9,8},{10,11... | collective-permute-start | bytes 147464 | tf_op jit(solution)/shard_map/ppermute | solution.py:157
  51.7 9.0 %collective-permute-start.12 = (bf16[2,3,32,128]{3,2,1,0:T(8,128)(2,1)S(1)}, bf16[2,3,32,128]{3,2,1,0:T(8,128)(2,1)S(1)}, u32[]{:S(2)}, u32[]{:S(2)}) collective-permute-start(bf16[2,3,32,128]{3,2,1,0:T(8,128)(2,1)S(1)} %get-tuple-element.83), channel_id=1, source_target_pairs={{0,2},{1,3},{2,0},{3,1},{4,6},{5,7},{6,4},{7,5},{8,10},{9,11},{10,... | collective-permute-start | bytes 147464 | tf_op jit(solution)/shard_map/ppermute | solution.py:157
  52.5 8.2 %collective-permute-start.13 = (bf16[2,3,32,128]{3,2,1,0:T(8,128)(2,1)S(1)}, bf16[2,3,32,128]{3,2,1,0:T(8,128)(2,1)S(1)}, u32[]{:S(2)}, u32[]{:S(2)}) collective-permute-start(bf16[2,3,32,128]{3,2,1,0:T(8,128)(2,1)S(1)} %get-tuple-element.82), channel_id=1, source_target_pairs={{0,3},{1,2},{2,1},{3,0},{4,7},{5,6},{6,5},{7,4},{8,11},{9,10},{10,... | collective-permute-start | bytes 147464 | tf_op jit(solution)/shard_map/ppermute | solution.py:157
  60.8 4.8 %collective-permute-start.15 = (bf16[3,32,128]{2,1,0:T(8,128)(2,1)S(1)}, bf16[3,32,128]{2,1,0:T(8,128)(2,1)S(1)}, u32[]{:S(2)}, u32[]{:S(2)}) collective-permute-start(bf16[3,32,128]{2,1,0:T(8,128)(2,1)S(1)} %get-tuple-element.94), channel_id=1, source_target_pairs={{0,4},{1,5},{2,6},{3,7},{4,0},{5,1},{6,2},{7,3},{8,12},{9,13},{10,... | collective-permute-start | bytes 73736 | tf_op jit(solution)/shard_map/ppermute | solution.py:157
  60.9 4.8 %collective-permute-start.16 = (bf16[3,32,128]{2,1,0:T(8,128)(2,1)S(1)}, bf16[3,32,128]{2,1,0:T(8,128)(2,1)S(1)}, u32[]{:S(2)}, u32[]{:S(2)}) collective-permute-start(bf16[3,32,128]{2,1,0:T(8,128)(2,1)S(1)} %get-tuple-element.93), channel_id=1, source_target_pairs={{0,16},{8,24},{16,0},{24,8},{1,17},{9,25},{17,1},{25,9},{2,18},{10... | collective-permute-start | bytes 73736 | tf_op jit(solution)/shard_map/ppermute | solution.py:157
  63.2 5.6 %collective-permute-start.17 = (bf16[3,32,128]{2,1,0:T(8,128)(2,1)S(1)}, bf16[3,32,128]{2,1,0:T(8,128)(2,1)S(1)}, u32[]{:S(2)}, u32[]{:S(2)}) collective-permute-start(bf16[3,32,128]{2,1,0:T(8,128)(2,1)S(1)} %get-tuple-element.94), channel_id=1, source_target_pairs={{0,20},{1,21},{2,22},{3,23},{4,16},{5,17},{6,18},{7,19},{8,28},{9,... | collective-permute-start | bytes 73736 | tf_op jit(solution)/shard_map/ppermute | solution.py:290
  68.8 1.9 %collective-permute-start.18 = (f32[3,32,128]{2,1,0:T(8,128)S(1)}, f32[3,32,128]{2,1,0:T(8,128)S(1)}, u32[]{:S(2)}, u32[]{:S(2)}) collective-permute-start(f32[3,32,128]{2,1,0:T(8,128)S(1)} %add_add_fusion), channel_id=1, source_target_pairs={{0,8},{8,0},{16,24},{24,16},{1,9},{9,1},{17,25},{25,17},{2,10},{10... | collective-permute-start | bytes 147464 | tf_op jit(solution)/shard_map/ppermute | solution.py:157
